TPU v7x, 32 devices: a whole 2x2x4 slice. The times are simulated.
32 devices in a mesh: ctx: 4 (over y, x), fsdp: 8 (over z, core).
Axes of the slice: x: 2, y: 2, z: 4, core: 2. Of those that a mesh axis runs over, the one named last changes fastest.
Arguments:
- tokens: bfloat16 [8, 1728, 1280], P('fsdp', 'ctx'), may hold values from -7.2 to 7.2
- cotangent: bfloat16 [8, 1728, 1280], P('fsdp', 'ctx'), may hold values from -7.2 to 7.2
- segments: int32 [8, 1728], P('fsdp'), may hold values from 0 to 7, as said below
- valid: int32 [8, 1728], P('fsdp'), may hold values from 0 to 1, as said below
- norm_one: bfloat16 [1280], P('fsdp'), may hold values from 0.5 to 1.5
- w_query: bfloat16 [1280, 1280], P('fsdp'), may hold values from -0.25 to 0.25
- w_key: bfloat16 [1280, 320], P('fsdp'), may hold values from -0.25 to 0.25
- w_value: bfloat16 [1280, 320], P('fsdp'), may hold values from -0.15625 to 0.15625
- w_out: bfloat16 [1280, 1280], P('fsdp'), may hold values from -0.5 to 0.5
- norm_two: bfloat16 [1280], P('fsdp'), may hold values from 0.5 to 1.5
- w_gate: bfloat16 [1280, 3584], P('fsdp'), may hold values from -0.15625 to 0.15625
- w_up: bfloat16 [1280, 3584], P('fsdp'), may hold values from -0.15625 to 0.15625
- w_down: bfloat16 [3584, 1280], P('fsdp'), may hold values from -0.09375 to 0.09375
Outputs:
- output: bfloat16 [8, 1728, 1280], P('fsdp', 'ctx')
- grad_tokens: bfloat16 [8, 1728, 1280], P('fsdp', 'ctx')
- grad_norm_one: float32 [1280], P('fsdp')
- grad_query: float32 [1280, 1280], P('fsdp')
- grad_key: float32 [1280, 320], P('fsdp')
- grad_value: float32 [1280, 320], P('fsdp')
- grad_out: float32 [1280, 1280], P('fsdp')
- grad_norm_two: float32 [1280], P('fsdp')
- grad_gate: float32 [1280, 3584], P('fsdp')
- grad_up: float32 [1280, 3584], P('fsdp')
- grad_down: float32 [3584, 1280], P('fsdp')
- spreads: float32 [5], replicated
Inputs may be any that keep to these rules, and one draw needn't show every extreme that they name: `segments`: within a sequence the numbers never fall; the first document covers at least three quarters of the 1728 positions. `valid`: each sequence ends with 1 to 216 padding positions and has no others.
All inputs are finite; a program needn't handle non-finite values.
Results may differ from a plain program's by a relative error of at most 0.019.
Values may be sent and summed in bfloat16 or wider, within the bound.
No kernel may reach another device: no remote copies, remote signals or barrier semaphores. Data moves between devices by JAX's collectives and lax.ppermute only.
A program may use at most 256 MiB of HBM per device.

v0:
```python
import math

import jax
import jax.numpy as jnp
from jax import lax
from jax.sharding import PartitionSpec as P

HEADS = 20
KV_HEADS = 5
HEAD_DIM = 64
WINDOW = 1024


EPSILON = 1e-05
MASKED = -1e30
ROPE_BASE = 10000.0


def dealt_place(owner_index, within, block_rows, ctx_count):
    return jnp.where(
        within < block_rows,
        owner_index * block_rows + within,
        (2 * ctx_count - 1 - owner_index) * block_rows + within - block_rows,
    )


def rope_tables(places, half_dim):
    freqs = jnp.exp(jnp.arange(half_dim, dtype=jnp.float32) * (-math.log(ROPE_BASE) / half_dim))
    angles = places.astype(jnp.float32)[:, None] * freqs[None, :]
    return (jnp.cos(angles)[:, None, :], jnp.sin(angles)[:, None, :])


def rotate(value_rows, cosine, sine):
    half_dim = value_rows.shape[-1] // 2
    first_half = value_rows[..., :half_dim]
    second_half = value_rows[..., half_dim:]
    return jnp.concatenate(
        [first_half * cosine - second_half * sine, first_half * sine + second_half * cosine],
        axis=-1,
    )


def unrotate(grad_rows, cosine, sine):
    half_dim = grad_rows.shape[-1] // 2
    first_half = grad_rows[..., :half_dim]
    second_half = grad_rows[..., half_dim:]
    return jnp.concatenate(
        [first_half * cosine + second_half * sine, second_half * cosine - first_half * sine],
        axis=-1,
    )


def norm_forward(value_rows, gain):
    inverse = lax.rsqrt(jnp.mean(value_rows * value_rows, axis=-1, keepdims=True) + EPSILON)
    normed = value_rows * inverse
    return (normed * gain, normed, inverse)


def norm_backward(upstream, gain, normed, inverse):
    scaled = upstream * gain
    grad_in = inverse * (scaled - normed * jnp.mean(scaled * normed, axis=-1, keepdims=True))
    return (grad_in, jnp.sum(upstream * normed, axis=0))


def matmul(left, right):
    return jnp.dot(left, right, preferred_element_type=jnp.float32)


def left_outer(left, right):
    return lax.dot_general(
        left, right, (((0,), (0,)), ((), ())), preferred_element_type=jnp.float32
    )


def right_inner(left, right):
    return lax.dot_general(
        left, right, (((1,), (1,)), ((), ())), preferred_element_type=jnp.float32
    )


def head_scores(query_head, key_head, allowed, score_scale):
    scores = (
        jnp.einsum("rgd,ld->grl", query_head, key_head, preferred_element_type=jnp.float32)
        * score_scale
    )
    return jnp.where(allowed[None], scores, MASKED)


def head_forward(query_head, key_head, value_head, allowed, score_scale):
    scores = head_scores(query_head, key_head, allowed, score_scale)
    row_peak = jnp.max(scores, axis=-1, keepdims=True)
    exponent = jnp.exp(scores - row_peak)
    row_total = jnp.sum(exponent, axis=-1, keepdims=True)
    probabilities = (exponent / row_total).astype(jnp.bfloat16)
    mixed_heads = jnp.einsum(
        "grl,ld->rgd", probabilities, value_head, preferred_element_type=jnp.float32
    )
    return (mixed_heads, row_peak[..., 0] + jnp.log(row_total[..., 0]))


def head_backward(query_head, key_head, value_head, grad_head, log_total, allowed, score_scale):
    scores = head_scores(query_head, key_head, allowed, score_scale)
    probabilities = jnp.exp(scores - log_total[..., None])
    grad_probs = jnp.einsum(
        "rgd,ld->grl", grad_head, value_head, preferred_element_type=jnp.float32
    )
    center = jnp.sum(probabilities * grad_probs, axis=-1, keepdims=True)
    grad_scores = (probabilities * (grad_probs - center)).astype(jnp.bfloat16)
    grad_queries = (
        jnp.einsum("grl,ld->rgd", grad_scores, key_head, preferred_element_type=jnp.float32)
        * score_scale
    )
    grad_keys = (
        jnp.einsum("grl,rgd->ld", grad_scores, query_head, preferred_element_type=jnp.float32)
        * score_scale
    )
    grad_values = jnp.einsum(
        "grl,rgd->ld",
        probabilities.astype(jnp.bfloat16),
        grad_head,
        preferred_element_type=jnp.float32,
    )
    return (grad_queries, grad_keys, grad_values)


def per_device(
    tokens,
    cotangent,
    segments,
    valid,
    norm_one,
    w_query,
    w_key,
    w_value,
    w_out,
    norm_two,
    w_gate,
    w_up,
    w_down,
):
    ctx_count = lax.axis_size("ctx")
    owner_index = lax.axis_index("ctx")
    row_count = tokens.shape[1]
    block_rows = row_count // 2
    model_width = tokens.shape[2]
    seq_length = 2 * ctx_count * block_rows
    group_size = HEADS // KV_HEADS
    kv_width = KV_HEADS * HEAD_DIM
    score_scale = 1.0 / math.sqrt(HEAD_DIM)
    local_places = dealt_place(
        owner_index, jnp.arange(row_count, dtype=jnp.int32), block_rows, ctx_count
    )
    every = jnp.arange(seq_length, dtype=jnp.int32)
    key_places = dealt_place(every // row_count, every % row_count, block_rows, ctx_count)
    seg_row = segments[0]
    valid_row = valid[0]
    query_segs = seg_row[local_places]
    key_segs = seg_row[key_places]
    key_valid = valid_row[key_places]
    query_valid = valid_row[local_places]
    distance = local_places[:, None] - key_places[None, :]
    allowed = (
        (query_segs[:, None] == key_segs[None, :])
        & (distance >= 0)
        & (distance < WINDOW)
        & ((key_valid[None, :] == 1) | (distance == 0))
    )
    attn_weights = (
        lax.all_gather(norm_one, "fsdp", axis=0, tiled=True),
        lax.all_gather(w_query, "fsdp", axis=0, tiled=True),
        lax.all_gather(w_key, "fsdp", axis=0, tiled=True),
        lax.all_gather(w_value, "fsdp", axis=0, tiled=True),
        lax.all_gather(w_out, "fsdp", axis=0, tiled=True),
    )
    ffn_weights = (
        lax.all_gather(norm_two, "fsdp", axis=0, tiled=True),
        lax.all_gather(w_gate, "fsdp", axis=0, tiled=True),
        lax.all_gather(w_up, "fsdp", axis=0, tiled=True),
        lax.all_gather(w_down, "fsdp", axis=0, tiled=True),
    )
    gain_one, query_w, key_w, value_w, out_w = attn_weights
    gain_two, gate_w, up_w, down_w = ffn_weights
    inputs = tokens[0].astype(jnp.float32)
    normed_one, unit_one, inverse_one = norm_forward(inputs, gain_one.astype(jnp.float32))
    first_in = normed_one.astype(jnp.bfloat16)
    cosine, sine = rope_tables(local_places, HEAD_DIM // 2)
    query_rot = rotate(
        matmul(first_in, query_w).reshape(row_count, HEADS, HEAD_DIM), cosine, sine
    ).astype(jnp.bfloat16)
    key_rot = (
        rotate(matmul(first_in, key_w).reshape(row_count, KV_HEADS, HEAD_DIM), cosine, sine)
        .astype(jnp.bfloat16)
        .reshape(row_count, kv_width)
    )
    value_rows = matmul(first_in, value_w).astype(jnp.bfloat16)
    key_all, value_all = (
        lax.all_gather(key_rot, "ctx", axis=0, tiled=True),
        lax.all_gather(value_rows, "ctx", axis=0, tiled=True),
    )
    query_heads = query_rot.reshape(row_count, KV_HEADS, group_size, HEAD_DIM).transpose(1, 0, 2, 3)
    key_heads = key_all.reshape(seq_length, KV_HEADS, HEAD_DIM).transpose(1, 0, 2)
    value_heads = value_all.reshape(seq_length, KV_HEADS, HEAD_DIM).transpose(1, 0, 2)
    mixed_heads, log_total = lax.map(
        lambda packed: head_forward(packed[0], packed[1], packed[2], allowed, score_scale),
        (query_heads, key_heads, value_heads),
    )
    attended = (
        mixed_heads.transpose(1, 0, 2, 3).reshape(row_count, model_width).astype(jnp.bfloat16)
    )
    branch_attn = matmul(attended, out_w)
    middle = inputs + branch_attn
    normed_two, unit_two, inverse_two = norm_forward(middle, gain_two.astype(jnp.float32))
    second_in = normed_two.astype(jnp.bfloat16)
    gate_pre = matmul(second_in, gate_w)
    up_pre = matmul(second_in, up_w)
    sigmoid_gate = jax.nn.sigmoid(gate_pre)
    swish_gate = gate_pre * sigmoid_gate
    hidden = (swish_gate * up_pre).astype(jnp.bfloat16)
    branch_ffn = matmul(hidden, down_w)
    result = middle + branch_ffn
    attn_back = (
        lax.all_gather(norm_one, "fsdp", axis=0, tiled=True),
        lax.all_gather(w_query, "fsdp", axis=0, tiled=True),
        lax.all_gather(w_key, "fsdp", axis=0, tiled=True),
        lax.all_gather(w_value, "fsdp", axis=0, tiled=True),
        lax.all_gather(w_out, "fsdp", axis=0, tiled=True),
    )
    ffn_back = (
        lax.all_gather(norm_two, "fsdp", axis=0, tiled=True),
        lax.all_gather(w_gate, "fsdp", axis=0, tiled=True),
        lax.all_gather(w_up, "fsdp", axis=0, tiled=True),
        lax.all_gather(w_down, "fsdp", axis=0, tiled=True),
    )
    gain_one_b, query_wb, key_wb, value_wb, out_wb = attn_back
    gain_two_b, gate_wb, up_wb, down_wb = ffn_back
    grad_output = cotangent[0]
    grad_hidden = right_inner(grad_output, down_wb)
    grad_down = left_outer(hidden, grad_output)
    slope = sigmoid_gate * (1.0 + gate_pre * (1.0 - sigmoid_gate))
    grad_gate_pre = (grad_hidden * up_pre * slope).astype(jnp.bfloat16)
    grad_up_pre = (grad_hidden * swish_gate).astype(jnp.bfloat16)
    grad_gate_w = left_outer(second_in, grad_gate_pre)
    grad_up_w = left_outer(second_in, grad_up_pre)
    grad_second = right_inner(grad_gate_pre, gate_wb) + right_inner(grad_up_pre, up_wb)
    grad_mid_norm, grad_gain_two = norm_backward(
        grad_second, gain_two_b.astype(jnp.float32), unit_two, inverse_two
    )
    grad_middle = grad_output.astype(jnp.float32) + grad_mid_norm
    ffn_shards = (
        lax.psum_scatter(grad_gain_two, "fsdp", scatter_dimension=0, tiled=True),
        lax.psum_scatter(grad_gate_w, "fsdp", scatter_dimension=0, tiled=True),
        lax.psum_scatter(grad_up_w, "fsdp", scatter_dimension=0, tiled=True),
        lax.psum_scatter(grad_down, "fsdp", scatter_dimension=0, tiled=True),
    )
    grad_branch = grad_middle.astype(jnp.bfloat16)
    grad_out_w = left_outer(attended, grad_branch)
    grad_attended = right_inner(grad_branch, out_wb).astype(jnp.bfloat16)
    grad_heads = grad_attended.reshape(row_count, KV_HEADS, group_size, HEAD_DIM).transpose(
        1, 0, 2, 3
    )
    grad_q_heads, grad_k_heads, grad_v_heads = lax.map(
        lambda packed: head_backward(
            packed[0], packed[1], packed[2], packed[3], packed[4], allowed, score_scale
        ),
        (query_heads, key_heads, value_heads, grad_heads, log_total),
    )
    grad_q_rot = grad_q_heads.transpose(1, 0, 2, 3).reshape(row_count, HEADS, HEAD_DIM)
    grad_k_all = grad_k_heads.transpose(1, 0, 2).reshape(seq_length, kv_width)
    grad_v_all = grad_v_heads.transpose(1, 0, 2).reshape(seq_length, kv_width)
    grad_k_local, grad_v_local = (
        lax.psum_scatter(
            grad_k_all.astype(jnp.bfloat16), "ctx", scatter_dimension=0, tiled=True
        ).astype(jnp.float32),
        lax.psum_scatter(
            grad_v_all.astype(jnp.bfloat16), "ctx", scatter_dimension=0, tiled=True
        ).astype(jnp.float32),
    )
    grad_q = unrotate(grad_q_rot, cosine, sine).reshape(row_count, model_width).astype(jnp.bfloat16)
    grad_k = (
        unrotate(grad_k_local.reshape(row_count, KV_HEADS, HEAD_DIM), cosine, sine)
        .reshape(row_count, kv_width)
        .astype(jnp.bfloat16)
    )
    grad_v = grad_v_local.astype(jnp.bfloat16)
    grad_query_w = left_outer(first_in, grad_q)
    grad_key_w = left_outer(first_in, grad_k)
    grad_value_w = left_outer(first_in, grad_v)
    grad_first = (
        right_inner(grad_q, query_wb) + right_inner(grad_k, key_wb) + right_inner(grad_v, value_wb)
    )
    grad_in_norm, grad_gain_one = norm_backward(
        grad_first, gain_one_b.astype(jnp.float32), unit_one, inverse_one
    )
    grad_inputs = grad_middle + grad_in_norm
    attn_shards = (
        lax.psum_scatter(grad_gain_one, "fsdp", scatter_dimension=0, tiled=True),
        lax.psum_scatter(grad_query_w, "fsdp", scatter_dimension=0, tiled=True),
        lax.psum_scatter(grad_key_w, "fsdp", scatter_dimension=0, tiled=True),
        lax.psum_scatter(grad_value_w, "fsdp", scatter_dimension=0, tiled=True),
        lax.psum_scatter(grad_out_w, "fsdp", scatter_dimension=0, tiled=True),
    )
    shard_rows = attn_shards[0].shape[0]
    shard_gain_one = jnp.broadcast_to(attn_shards[0][:, None], (shard_rows, ctx_count))
    shard_gain_two = jnp.broadcast_to(ffn_shards[0][:, None], (shard_rows, ctx_count))
    column_sums = (
        lax.psum_scatter(
            shard_gain_one.astype(jnp.bfloat16), "ctx", scatter_dimension=1, tiled=True
        ).astype(jnp.float32),
        lax.psum_scatter(
            attn_shards[1].astype(jnp.bfloat16), "ctx", scatter_dimension=1, tiled=True
        ).astype(jnp.float32),
        lax.psum_scatter(
            attn_shards[2].astype(jnp.bfloat16), "ctx", scatter_dimension=1, tiled=True
        ).astype(jnp.float32),
        lax.psum_scatter(
            attn_shards[3].astype(jnp.bfloat16), "ctx", scatter_dimension=1, tiled=True
        ).astype(jnp.float32),
        lax.psum_scatter(
            attn_shards[4].astype(jnp.bfloat16), "ctx", scatter_dimension=1, tiled=True
        ).astype(jnp.float32),
        lax.psum_scatter(
            shard_gain_two.astype(jnp.bfloat16), "ctx", scatter_dimension=1, tiled=True
        ).astype(jnp.float32),
        lax.psum_scatter(
            ffn_shards[1].astype(jnp.bfloat16), "ctx", scatter_dimension=1, tiled=True
        ).astype(jnp.float32),
        lax.psum_scatter(
            ffn_shards[2].astype(jnp.bfloat16), "ctx", scatter_dimension=1, tiled=True
        ).astype(jnp.float32),
        lax.psum_scatter(
            ffn_shards[3].astype(jnp.bfloat16), "ctx", scatter_dimension=1, tiled=True
        ).astype(jnp.float32),
    )
    whole_columns = (
        lax.all_gather(column_sums[1].astype(jnp.bfloat16), "ctx", axis=1, tiled=True).astype(
            jnp.float32
        ),
        lax.all_gather(column_sums[2].astype(jnp.bfloat16), "ctx", axis=1, tiled=True).astype(
            jnp.float32
        ),
        lax.all_gather(column_sums[3].astype(jnp.bfloat16), "ctx", axis=1, tiled=True).astype(
            jnp.float32
        ),
        lax.all_gather(column_sums[4].astype(jnp.bfloat16), "ctx", axis=1, tiled=True).astype(
            jnp.float32
        ),
        lax.all_gather(column_sums[6].astype(jnp.bfloat16), "ctx", axis=1, tiled=True).astype(
            jnp.float32
        ),
        lax.all_gather(column_sums[7].astype(jnp.bfloat16), "ctx", axis=1, tiled=True).astype(
            jnp.float32
        ),
        lax.all_gather(column_sums[8].astype(jnp.bfloat16), "ctx", axis=1, tiled=True).astype(
            jnp.float32
        ),
    )
    summed = (
        column_sums[0][:, 0],
        whole_columns[0],
        whole_columns[1],
        whole_columns[2],
        whole_columns[3],
        column_sums[5][:, 0],
        whole_columns[4],
        whole_columns[5],
        whole_columns[6],
    )
    live_rows = query_valid.astype(jnp.float32)[:, None]
    squares = jnp.stack(
        [
            jnp.sum(live_rows * member * member)
            for member in (result, grad_inputs, branch_attn, branch_ffn, middle)
        ]
    )
    live_count = jnp.sum(query_valid.astype(jnp.float32))
    total_squares, total_count = lax.psum((squares, live_count), ("ctx", "fsdp"))
    spreads = jnp.sqrt(total_squares / (total_count * model_width))
    return (
        result[None].astype(jnp.bfloat16),
        grad_inputs[None].astype(jnp.bfloat16),
        summed[0],
        summed[1],
        summed[2],
        summed[3],
        summed[4],
        summed[5],
        summed[6],
        summed[7],
        summed[8],
        spreads,
    )


def solution(mesh):
    placed = (
        P("fsdp", "ctx", None),
        P("fsdp", "ctx", None),
        P("fsdp", None),
        P("fsdp", None),
        P("fsdp"),
        P("fsdp", None),
        P("fsdp", None),
        P("fsdp", None),
        P("fsdp", None),
        P("fsdp"),
        P("fsdp", None),
        P("fsdp", None),
        P("fsdp", None),
    )
    return jax.shard_map(
        per_device,
        mesh=mesh,
        in_specs=placed,
        out_specs=(
            P("fsdp", "ctx", None),
            P("fsdp", "ctx", None),
            P("fsdp"),
            P("fsdp", None),
            P("fsdp", None),
            P("fsdp", None),
            P("fsdp", None),
            P("fsdp"),
            P("fsdp", None),
            P("fsdp", None),
            P("fsdp", None),
            P(),
        ),
        check_vma=False,
    )
```

profile of v0, /device:TPU:0, one launch (start us, length us, event | category | flops | bytes accessed | tf_op | source)
XLA Modules:
  0.0 1811.9 jit_solution(4668168186258539506)
XLA Ops:
  7.3 18.2 %all_gather.64 = bf16[1280,320]{1,0:T(8,128)(2,1)S(1)} all-gather(bf16[160,320]{1,0:T(8,128)(2,1)} %param.24), channel_id=1, replica_groups=mesh['ctx'=4,'fsdp'=8] {'fsdp'}, dimensions={0}, use_global_device_ids=true | all-gather | bytes 921600 | tf_op jit(solution)/shard_map/all_gather | solution.py:172
  29.2 17.7 all-reduce.10
  50.1 16.1 all_gather.66
  113.0 36.5 %all-gather.15.cloned.1.call-done = bf16[1280,1280]{1,0:T(8,128)(2,1)} async-done(((bf16[160,1280]{1,0:T(8,128)(2,1)}), bf16[1280,1280]{1,0:T(8,128)(2,1)}) %all-gather.15.cloned.1.call-update) | async-done | bytes 3276816 | tf_op jit(solution)/shard_map/all_gather | solution.py:170
  160.9 81.7 %while.30 = (s32[]{:T(128)}, bf16[5,432,4,64]{1,3,2,0:T(8,128)(2,1)}, f32[5,4,432]{2,1,0:T(4,128)S(1)}, bf16[5,1728,64]{1,2,0:T(8,128)(2,1)}, bf16[5,1728,64]{1,...) while((s32[]{:T(128)}, ...), condition=%wide.region_4.5_spmd.clone.clone, body=%wide.region_1.4_spmd.clone.sunk.clone | while | flops 806960448 | bytes 43156948 | solution.py:203
  248.7 29.5 %all-gather.19.cloned.1.call-done = bf16[1280,3584]{1,0:T(8,128)(2,1)} async-done(((bf16[160,3584]{1,0:T(8,128)(2,1)}), bf16[1280,3584]{1,0:T(8,128)(2,1)}) %all-gather.19.cloned.1.call-update) | async-done | bytes 9175056 | tf_op jit(solution)/shard_map/all_gather | solution.py:177
  287.7 79.0 %all-gather.21.cloned.1.call-done = bf16[1280,3584]{1,0:T(8,128)(2,1)} async-done(((bf16[160,3584]{1,0:T(8,128)(2,1)}), bf16[1280,3584]{1,0:T(8,128)(2,1)}) %all-gather.21.cloned.1.call-update) | async-done | bytes 9175056 | tf_op jit(solution)/shard_map/all_gather | solution.py:178
  377.8 77.7 %all-gather.23.cloned.1.call-done = bf16[3584,1280]{1,0:T(8,128)(2,1)} async-done(((bf16[448,1280]{1,0:T(8,128)(2,1)}), bf16[3584,1280]{1,0:T(8,128)(2,1)}) %all-gather.23.cloned.1.call-update) | async-done | bytes 9175056 | tf_op jit(solution)/shard_map/all_gather | solution.py:179
  502.3 148.3 %while.31 = (s32[]{:T(128)}, f32[5,432,4,64]{1,3,2,0:T(8,128)}, bf16[5,1728,64]{1,2,0:T(8,128)(2,1)}, bf16[5,1728,64]{1,2,0:T(8,128)(2,1)}, bf16[5,1728,64]{1,2,...) while((s32[]{:T(128)}, f32[5,432,4,64]{1,3,2,0:T(8,128)}, ...), condition=%wide.region_9.10_spmd.clone.clone, body=%wide.region_7.9_spmd.clone.sunk.clone | while | flops 1962757376 | bytes 96759248 | solution.py:261
  688.9 33.5 %all-reduce.15.cloned.1.call-done = (bf16[1728,320]{0,1:T(8,128)(2,1)}, bf16[1728,320]{0,1:T(8,128)(2,1)}) async-done(((bf16[1728,320]{0,1:T(8,128)(2,1)}, bf16[1728,320]{0,1:T(8,128)(2,1)}), (bf16[1728,320]{0,1:T(8,128)(2,1)}, bf16[1728,320]{0,1:T(8,128)(2,1)})) %all-reduce.15.cloned.1.call-update) | async-done | bytes 2211856
  746.8 161.1 %reduce-scatter.39.cloned.1.call-done = f32[160,3584]{1,0:T(8,128)} async-done(((f32[1280,3584]{1,0:T(8,128)}), f32[160,3584]{1,0:T(8,128)}) %reduce-scatter.39.cloned.1.call-update) | async-done | bytes 2293776 | tf_op jit(solution)/shard_map/reduce_scatter | solution.py:251
  913.4 178.1 %reduce-scatter.41.cloned.1.call-done = f32[160,3584]{1,0:T(8,128)} async-done(((f32[1280,3584]{1,0:T(8,128)}), f32[160,3584]{1,0:T(8,128)}) %reduce-scatter.41.cloned.1.call-update) | async-done | bytes 2293776 | tf_op jit(solution)/shard_map/reduce_scatter | solution.py:252
  1097.1 178.3 %reduce-scatter.43.cloned.1.call-done = f32[448,1280]{1,0:T(8,128)} async-done(((f32[3584,1280]{1,0:T(8,128)}), f32[448,1280]{1,0:T(8,128)}) %reduce-scatter.43.cloned.1.call-update) | async-done | bytes 2293776 | tf_op jit(solution)/shard_map/reduce_scatter | solution.py:253
  1280.7 31.3 %reduce-scatter.33.cloned.1.call-done = f32[160,320]{1,0:T(8,128)} async-done(((f32[1280,320]{1,0:T(8,128)}), f32[160,320]{1,0:T(8,128)}) %reduce-scatter.33.cloned.1.call-update) | async-done | bytes 204816 | tf_op jit(solution)/shard_map/reduce_scatter | solution.py:298
  1313.8 35.0 %reduce-scatter.35.cloned.1.call-done = f32[160,320]{1,0:T(8,128)} async-done(((f32[1280,320]{1,0:T(8,128)}), f32[160,320]{1,0:T(8,128)}) %reduce-scatter.35.cloned.1.call-update) | async-done | bytes 204816 | tf_op jit(solution)/shard_map/reduce_scatter | solution.py:299
  1350.7 71.0 %reduce-scatter.31.cloned.1.call-done = f32[160,1280]{1,0:T(8,128)} async-done(((f32[1280,1280]{1,0:T(8,128)}), f32[160,1280]{1,0:T(8,128)}) %reduce-scatter.31.cloned.1.call-update) | async-done | bytes 819216 | tf_op jit(solution)/shard_map/reduce_scatter | solution.py:297
  1425.8 68.8 %reduce-scatter.37.cloned.1.call-done = f32[160,1280]{1,0:T(8,128)} async-done(((f32[1280,1280]{1,0:T(8,128)}), f32[160,1280]{1,0:T(8,128)}) %reduce-scatter.37.cloned.1.call-update) | async-done | bytes 819216 | tf_op jit(solution)/shard_map/reduce_scatter | solution.py:300
  1498.6 30.8 %reduce-scatter.53.cloned.1.call-done = bf16[896,160]{1,0:T(8,128)(2,1)} async-done(((bf16[3584,160]{1,0:T(8,128)(2,1)}), bf16[896,160]{1,0:T(8,128)(2,1)}) %reduce-scatter.53.cloned.1.call-update) | async-done | bytes 286736
  1531.4 33.9 %reduce-scatter.55.cloned.1.call-done = bf16[896,160]{1,0:T(8,128)(2,1)} async-done(((bf16[3584,160]{1,0:T(8,128)(2,1)}), bf16[896,160]{1,0:T(8,128)(2,1)}) %reduce-scatter.55.cloned.1.call-update) | async-done | bytes 286736
  1573.8 23.6 %reduce-scatter.57.cloned.1.call-done = bf16[320,448]{1,0:T(8,128)(2,1)} async-done(((bf16[1280,448]{1,0:T(8,128)(2,1)}), bf16[320,448]{1,0:T(8,128)(2,1)}) %reduce-scatter.57.cloned.1.call-update) | async-done | bytes 286736
  1609.3 39.6 %all-reduce.8 = (f32[5]{0:T(128)S(1)}, f32[]{:T(128)}) all-reduce(f32[5]{0:T(128)S(1)} %stack.23, f32[]{:T(128)} %convert_reduce_fusion), channel_id=1, replica_groups=mesh['ctx'=4,'fsdp'=8] {'ctx','fsdp'}, use_global_device_ids=true, to_apply=%region_38.39 | all-reduce | flops 6 | bytes 48 | tf_op jit(solution)/shard_map/psum | solution.py:376
  1648.9 26.8 %all-reduce.9 = (bf16[1280]{0:T(1024)(128)(2,1)S(1)}, bf16[1280]{0:T(1024)(128)(2,1)S(1)}) all-reduce(f32[1280]{0:T(1024)S(1)} %get-tuple-element.199, f32[1280]{0:T(1024)S(1)} %copy-done.31), channel_id=4, replica_groups=mesh['ctx'=4,'fsdp'=8] {'fsdp'}, use_global_device_ids=true, to_apply=%region_14.15.clone | all-reduce | flops 2560 | bytes 15360
  1745.4 26.3 %all-gather.27.cloned.1.call-done = bf16[160,3584]{1,0:T(8,128)(2,1)} async-done(((bf16[160,896]{1,0:T(8,128)(2,1)}), bf16[160,3584]{1,0:T(8,128)(2,1)}) %all-gather.27.cloned.1.call-update) | async-done | bytes 1146896 | tf_op jit(solution)/shard_map/all_gather | solution.py:350
  1774.6 27.8 %all-gather.29.cloned.1.call-done = bf16[448,1280]{0,1:T(8,128)(2,1)} async-done(((bf16[448,320]{0,1:T(8,128)(2,1)}), bf16[448,1280]{0,1:T(8,128)(2,1)}) %all-gather.29.cloned.1.call-update) | async-done | bytes 1146896 | tf_op jit(solution)/shard_map/all_gather | solution.py:353
  (324 shorter events, 552.2 us)
Async XLA Ops:
  7.2 91.7 %all-gather.31.cloned.1.call-start = ((), (), s32[]{:S(2)}) async-start(), calls=%async_computation.29 | async-start | bytes 1638400 | tf_op jit(solution)/shard_map/all_gather | solution.py:198
  68.8 80.7 %all-gather.15.cloned.1.call-start = ((), (), s32[]{:S(2)}) async-start(), calls=%async_computation.14 | async-start | bytes 3686400 | tf_op jit(solution)/shard_map/all_gather | solution.py:170
  69.5 173.1 %all-gather.17.cloned.1.call-start = ((), (), s32[]{:S(2)}) async-start(), calls=%async_computation.15 | async-start | bytes 3686400 | tf_op jit(solution)/shard_map/all_gather | solution.py:173
  70.1 208.1 %all-gather.19.cloned.1.call-start = ((), (), s32[]{:S(2)}) async-start(), calls=%async_computation.16 | async-start | bytes 10321920 | tf_op jit(solution)/shard_map/all_gather | solution.py:177
  70.7 296.0 %all-gather.21.cloned.1.call-start = ((), (), s32[]{:S(2)}) async-start(), calls=%async_computation.17 | async-start | bytes 10321920 | tf_op jit(solution)/shard_map/all_gather | solution.py:178
  71.3 384.2 %all-gather.23.cloned.1.call-start = ((), (), s32[]{:S(2)}) async-start(), calls=%async_computation.18 | async-start | bytes 10321920 | tf_op jit(solution)/shard_map/all_gather | solution.py:179
  72.0 650.4 %all-reduce.15.cloned.1.call-start = ((), (), s32[]{:S(2)}) async-start(), calls=%async_computation.38 | async-start | bytes 4587520
  650.6 257.2 %reduce-scatter.39.cloned.1.call-start = ((), (), s32[]{:S(2)}) async-start(), calls=%async_computation.23 | async-start | bytes 20643840 | tf_op jit(solution)/shard_map/reduce_scatter | solution.py:251
  662.9 428.6 %reduce-scatter.41.cloned.1.call-start = ((), (), s32[]{:S(2)}) async-start(), calls=%async_computation.25 | async-start | bytes 20643840 | tf_op jit(solution)/shard_map/reduce_scatter | solution.py:252
  673.8 601.5 %reduce-scatter.43.cloned.1.call-start = ((), (), s32[]{:S(2)}) async-start(), calls=%async_computation.27 | async-start | bytes 20643840 | tf_op jit(solution)/shard_map/reduce_scatter | solution.py:253
  687.1 624.9 %reduce-scatter.33.cloned.1.call-start = ((), (), s32[]{:S(2)}) async-start(), calls=%async_computation.20 | async-start | bytes 2211840 | tf_op jit(solution)/shard_map/reduce_scatter | solution.py:298
  726.9 622.0 %reduce-scatter.35.cloned.1.call-start = ((), (), s32[]{:S(2)}) async-start(), calls=%async_computation.21 | async-start | bytes 2211840 | tf_op jit(solution)/shard_map/reduce_scatter | solution.py:299
  730.4 691.3 %reduce-scatter.31.cloned.1.call-start = ((), (), s32[]{:S(2)}) async-start(), calls=%async_computation.19 | async-start | bytes 7372800 | tf_op jit(solution)/shard_map/reduce_scatter | solution.py:297
  739.2 755.3 %reduce-scatter.37.cloned.1.call-start = ((), (), s32[]{:S(2)}) async-start(), calls=%async_computation.22 | async-start | bytes 7372800 | tf_op jit(solution)/shard_map/reduce_scatter | solution.py:300
  746.7 782.7 %reduce-scatter.53.cloned.1.call-start = ((), (), s32[]{:S(2)}) async-start(), calls=%async_computation.35 | async-start | bytes 2293760
  913.3 652.0 %reduce-scatter.55.cloned.1.call-start = ((), (), s32[]{:S(2)}) async-start(), calls=%async_computation.36 | async-start | bytes 2293760
  1097.0 500.4 %reduce-scatter.57.cloned.1.call-start = ((), (), s32[]{:S(2)}) async-start(), calls=%async_computation.37 | async-start | bytes 1638400
  1280.6 408.8 %reduce-scatter.47.cloned.1.call-start = ((), (), s32[]{:S(2)}) async-start(), calls=%async_computation.32 | async-start | bytes 204800
  1313.8 385.8 %reduce-scatter.49.cloned.1.call-start = ((), (), s32[]{:S(2)}) async-start(), calls=%async_computation.33 | async-start | bytes 204800
  1350.6 358.9 %reduce-scatter.45.cloned.1.call-start = ((), (), s32[]{:S(2)}) async-start(), calls=%async_computation.31 | async-start | bytes 819200
  1425.7 296.3 %reduce-scatter.51.cloned.1.call-start = ((), (), s32[]{:S(2)}) async-start(), calls=%async_computation.34 | async-start | bytes 819200
  1498.6 244.0 %all-gather.25.cloned.1.call-start = ((), (), s32[]{:S(2)}) async-start(), calls=%async_computation.24 | async-start | bytes 1433600 | tf_op jit(solution)/shard_map/all_gather | solution.py:347
  1531.3 240.4 %all-gather.27.cloned.1.call-start = ((), (), s32[]{:S(2)}) async-start(), calls=%async_computation.26 | async-start | bytes 1433600 | tf_op jit(solution)/shard_map/all_gather | solution.py:350
  1567.2 235.2 %all-gather.29.cloned.1.call-start = ((), (), s32[]{:S(2)}) async-start(), calls=%async_computation.28 | async-start | bytes 1638400 | tf_op jit(solution)/shard_map/all_gather | solution.py:353
  (43 other events, 1338.2 us)
Sparse Core Ops, SparseCore 0:
  50.1 27.0 all-gather.30
  79.6 28.7 all-gather.32
  110.1 39.3 all-gather.14
  151.0 38.2 all-gather.16
  190.7 87.4 all-gather.18
  279.6 87.0 all-gather.20
  368.4 87.0 all-gather.22
  650.8 71.5 all-reduce.14
  724.8 183.0 reduce-scatter.38
  910.1 181.3 reduce-scatter.40
  1093.9 181.3 reduce-scatter.42
  1278.1 33.8 reduce-scatter.32
  1315.0 33.7 reduce-scatter.34
  1351.0 70.5 reduce-scatter.30
  1423.8 70.6 reduce-scatter.36
  1498.0 31.3 reduce-scatter.52
  1532.3 32.9 reduce-scatter.54
  1568.1 29.2 reduce-scatter.56
  1600.8 23.9 reduce-scatter.46
  1654.8 25.4 reduce-scatter.44
  1684.0 27.0 reduce-scatter.50
  1713.5 28.9 all-gather.24
  1744.2 27.4 all-gather.26
  1773.6 28.7 all-gather.28
  (1 shorter events, 23.9 us)
where the time goes:
time: 1820 us; the launch traced here: 1810 us
  waiting for transfers between devices  1140 us (63%)
  matrix products  292 us (16%)
  blocking collectives  166 us (9%)
  other arithmetic  110 us (6%)
  local copies, waits for them, and re-layouts  84.4 us (5%)
    reduce_scatter x1, waiting for transfers between devices, per_device(): lax.psum_scatter(grad_down, 'fsdp', scatter_dimension=0, tiled=True)  178 us
    reduce_scatter x1, waiting for transfers between devices, per_device(): lax.psum_scatter(grad_up_w, 'fsdp', scatter_dimension=0, tiled=True)  178 us
    reduce_scatter x1, waiting for transfers between devices, per_device(): lax.psum_scatter(grad_gate_w, 'fsdp', scatter_dimension=0, tiled=True)  161 us
    unnamed x33, waiting for transfers between devices  125 us
    all_gather x1, waiting for transfers between devices, per_device(): lax.all_gather(w_up, 'fsdp', axis=0, tiled=True)  79 us
    all_gather x1, waiting for transfers between devices, per_device(): lax.all_gather(w_down, 'fsdp', axis=0, tiled=True)  77.7 us
    reduce_scatter x1, waiting for transfers between devices, per_device(): lax.psum_scatter(grad_query_w, 'fsdp', scatter_dimension=0, tiled=True)  71 us
    reduce_scatter x1, waiting for transfers between devices, per_device(): lax.psum_scatter(grad_out_w, 'fsdp', scatter_dimension=0, tiled=True)  68.8 us
  transfers between devices with their start and end apart: 25, of which 19 were waited for; matrix products, arithmetic and copies ran while one was open for 15% of the time, Pallas kernels for 0%

commit v1 on v0

v1 whole, which is shorter than its diff:
```python
import functools
import math

import jax
import jax.numpy as jnp
from jax import lax
from jax.experimental import pallas as pl
from jax.experimental.pallas import tpu as pltpu
from jax.sharding import PartitionSpec as P

HEADS = 20
KV_HEADS = 5
HEAD_DIM = 64
GROUP = HEADS // KV_HEADS
WINDOW = 1024
EPSILON = 1e-05
MASKED = -1e30
ROPE_BASE = 10000.0
PARTS = 2
BF16 = jnp.bfloat16
F32 = jnp.float32


def core_swap(v):
    n = lax.axis_size("fsdp")
    return lax.ppermute(v, "fsdp", [(i, i ^ 1) for i in range(n)])


def swap_x(v):
    return lax.ppermute(v, "ctx", [(i, i ^ 1) for i in range(4)])


def swap_y(v):
    return lax.ppermute(v, "ctx", [(i, i ^ 2) for i in range(4)])


def put(buffer, piece, index, axis):
    return lax.dynamic_update_slice_in_dim(
        buffer, jnp.expand_dims(piece, axis), index, axis
    )


def take(v, index, axis):
    return lax.dynamic_index_in_dim(v, index, axis, keepdims=False)


def place(pieces, axis):
    first = pieces[0][1]
    shape = first.shape[:axis] + (len(pieces),) + first.shape[axis:]
    buffer = jnp.zeros(shape, first.dtype)
    for index, piece in pieces:
        buffer = put(buffer, piece, index, axis)
    return buffer


def z_groups(n):
    return [list(range(0, n, 2)), list(range(1, n, 2))]


def z_gather(piece):
    n = lax.axis_size("fsdp")
    nz = n // 2
    if nz != 4:
        return lax.all_gather(piece, "fsdp", axis=0, axis_index_groups=z_groups(n))
    z = lax.axis_index("fsdp") // 2
    pieces = [(z, piece)]
    for d in (1, 2, 3):
        got = lax.ppermute(piece, "fsdp", [(i, (i + 2 * d) % n) for i in range(n)])
        pieces.append(((z - d) % nz, got))
    return place(pieces, 0)


def z_scatter(pieces):
    n = lax.axis_size("fsdp")
    nz = n // 2
    if nz != 4:
        return lax.psum_scatter(
            pieces, "fsdp", scatter_dimension=0, axis_index_groups=z_groups(n)
        ).astype(F32)
    z = lax.axis_index("fsdp") // 2
    total = take(pieces, z, 0).astype(F32)
    for d in (1, 2, 3):
        sent = take(pieces, (z + d) % nz, 0)
        got = lax.ppermute(sent, "fsdp", [(i, (i + 2 * d) % n) for i in range(n)])
        total = total + got.astype(F32)
    return total


def half_perm(nz, s):
    return [(k * nz + (z + s) % nz, 2 * z + k) for z in range(nz) for k in range(2)]


def half_gather(piece):
    n = lax.axis_size("fsdp")
    nz = n // 2
    f = lax.axis_index("fsdp")
    z, k = f // 2, f % 2
    if nz != 4:
        every = lax.all_gather(piece, "fsdp", axis=0)
        return lax.dynamic_slice_in_dim(every, k * nz, nz, 0)
    pieces = []
    for s in range(nz):
        pieces.append(((z + s) % nz, lax.ppermute(piece, "fsdp", half_perm(nz, s))))
    return place(pieces, 0)


def half_scatter(pieces):
    n = lax.axis_size("fsdp")
    nz = n // 2
    f = lax.axis_index("fsdp")
    z, k = f // 2, f % 2
    if nz != 4:
        both = lax.dynamic_update_slice_in_dim(
            jnp.zeros((n,) + pieces.shape[1:], pieces.dtype), pieces, k * nz, 0
        )
        return lax.psum_scatter(both, "fsdp", scatter_dimension=0).astype(F32)
    total = None
    for s in range(nz):
        back = [(b, a) for a, b in half_perm(nz, s)]
        got = lax.ppermute(take(pieces, (z + s) % nz, 0), "fsdp", back).astype(F32)
        total = got if total is None else total + got
    return total


def ctx_gather(piece, axis):
    c = lax.axis_index("ctx")
    half = piece.shape[0] // 2
    from_x = swap_x(piece)
    from_y = swap_y(piece)
    from_d = jnp.concatenate([swap_y(from_x[:half]), swap_x(from_y[half:])], axis=0)
    return place([(c, piece), (c ^ 1, from_x), (c ^ 2, from_y), (c ^ 3, from_d)], axis)


def ctx_scatter(whole, axis):
    c = lax.axis_index("ctx")
    half = whole.shape[0] // 2
    low, high = whole[:half], whole[half:]
    low_got = swap_x(jnp.stack([take(low, c ^ 1, axis), take(low, c ^ 3, axis)]))
    high_got = swap_y(jnp.stack([take(high, c ^ 2, axis), take(high, c ^ 3, axis)]))
    low_own = take(low, c, axis).astype(F32) + low_got[0].astype(F32)
    low_pass = (take(low, c ^ 2, axis).astype(F32) + low_got[1].astype(F32)).astype(BF16)
    high_own = take(high, c, axis).astype(F32) + high_got[0].astype(F32)
    high_pass = (take(high, c ^ 1, axis).astype(F32) + high_got[1].astype(F32)).astype(BF16)
    low_sum = low_own + swap_y(low_pass).astype(F32)
    high_sum = high_own + swap_x(high_pass).astype(F32)
    return jnp.concatenate([low_sum, high_sum], axis=0)


def pair_bias(q_block, k_block, rows, seg_q, seg_k, valid_k):
    key_at = k_block * rows + lax.broadcasted_iota(jnp.int32, (rows, rows), 0)
    query_at = q_block * rows + lax.broadcasted_iota(jnp.int32, (rows, rows), 1)
    distance = query_at - key_at
    allowed = (
        (seg_q == seg_k)
        & (distance >= 0)
        & (distance < WINDOW)
        & ((valid_k == 1) | (distance == 0))
    )
    return jnp.where(allowed, 0.0, MASKED).astype(F32)


def first_block(q_block, rows):
    reach = (WINDOW + rows - 2) // rows
    return jnp.maximum(q_block - reach, 0)


def dot(a, b, dims):
    return lax.dot_general(a, b, (dims, ((), ())), preferred_element_type=F32)


def fill_bias(blocks_ref, seg_q_ref, seg_k_ref, valid_k_ref, bias_ref, rows):
    for side in range(2):
        b = blocks_ref[side]
        lo = first_block(b, rows)

        def body(kb, _):
            bias_ref[side, kb - lo] = pair_bias(
                b, kb, rows, seg_q_ref[side], seg_k_ref[kb], valid_k_ref[kb]
            )
            return 0

        lax.fori_loop(lo, b + 1, body, 0)


def forward_kernel(
    blocks_ref, seg_q_ref, seg_k_ref, valid_k_ref, q_ref, k_ref, v_ref,
    o_ref, lse_ref, bias_ref, acc_ref, peak_ref, total_ref,
):
    rows = q_ref.shape[-1]

    @pl.when(pl.program_id(0) == 0)
    def _():
        fill_bias(blocks_ref, seg_q_ref, seg_k_ref, valid_k_ref, bias_ref, rows)

    for side in range(2):
        b = blocks_ref[side]
        lo = first_block(b, rows)
        acc_ref[...] = jnp.zeros_like(acc_ref)
        total_ref[...] = jnp.zeros_like(total_ref)
        peak_ref[...] = jnp.full_like(peak_ref, -jnp.inf)

        def body(kb, _):
            keys = k_ref[kb, 0].T
            values_t = v_ref[kb, 0]
            bias = bias_ref[side, kb - lo]
            for h in range(GROUP):
                query = q_ref[side, h] * 0.125
                s = dot(keys, query, ((1,), (0,))) + bias
                peak_old = peak_ref[h : h + 1]
                peak = jnp.maximum(peak_old, jnp.max(s, axis=0, keepdims=True))
                p = jnp.exp(s - peak)
                shrink = jnp.exp(peak_old - peak)
                peak_ref[h : h + 1] = peak
                total_ref[h : h + 1] = total_ref[h : h + 1] * shrink + jnp.sum(
                    p, axis=0, keepdims=True
                )
                acc_ref[h] = acc_ref[h] * shrink + dot(values_t, p.astype(BF16), ((1,), (0,)))
            return 0

        body(b, 0)
        lax.fori_loop(lo, b, body, 0)
        for h in range(GROUP):
            total = total_ref[h : h + 1]
            o_ref[side, h] = (acc_ref[h] / total).astype(BF16)
            lse_ref[side, 0, h : h + 1] = peak_ref[h : h + 1] + jnp.log(total)


def backward_kernel(
    blocks_ref, seg_q_ref, seg_k_ref, valid_k_ref, q_ref, k_ref, v_ref, o_ref, do_ref, lse_ref,
    dq_ref, dk_ref, dv_ref, bias_ref, acc_ref, center_ref,
):
    rows = q_ref.shape[-1]

    @pl.when(pl.program_id(0) == 0)
    def _():
        fill_bias(blocks_ref, seg_q_ref, seg_k_ref, valid_k_ref, bias_ref, rows)

    dk_ref[...] = jnp.zeros_like(dk_ref)
    dv_ref[...] = jnp.zeros_like(dv_ref)
    for side in range(2):
        b = blocks_ref[side]
        lo = first_block(b, rows)
        acc_ref[...] = jnp.zeros_like(acc_ref)
        for h in range(GROUP):
            center_ref[h : h + 1] = jnp.sum(
                o_ref[side, h].astype(F32) * do_ref[side, h].astype(F32), axis=0, keepdims=True
            )

        def body(kb, _):
            keys_t = k_ref[kb, 0]
            keys = keys_t.T
            values = v_ref[kb, 0].T
            bias = bias_ref[side, kb - lo]
            for h in range(GROUP):
                query_t = q_ref[side, h] * 0.125
                grad_t = do_ref[side, h]
                s = dot(keys, query_t, ((1,), (0,))) + bias
                p = jnp.exp(s - lse_ref[side, 0, h : h + 1])
                dp = dot(values, grad_t, ((1,), (0,)))
                ds = (p * (dp - center_ref[h : h + 1])).astype(BF16)
                dv_ref[kb, 0] += dot(grad_t, p.astype(BF16), ((1,), (1,)))
                dk_ref[kb, 0] += dot(query_t, ds, ((1,), (1,)))
                acc_ref[h] += dot(keys_t, ds, ((1,), (0,)))
            return 0

        lax.fori_loop(lo, b + 1, body, 0)
        for h in range(GROUP):
            dq_ref[side, h] = acc_ref[h] * 0.125


def kernel_specs(blocks, rows):
    q_spec = pl.BlockSpec((2, GROUP, HEAD_DIM, rows), lambda g, s: (0, g, 0, 0))
    k_spec = pl.BlockSpec((blocks, 1, HEAD_DIM, rows), lambda g, s: (0, g, 0, 0))
    v_spec = pl.BlockSpec((blocks, 1, HEAD_DIM, rows), lambda g, s: (0, KV_HEADS + g, 0, 0))
    stat_spec = pl.BlockSpec((2, 1, GROUP, rows), lambda g, s: (0, g, 0, 0))
    seg_specs = [
        pl.BlockSpec((2, 1, rows), lambda g, s: (0, 0, 0)),
        pl.BlockSpec((blocks, rows, 1), lambda g, s: (0, 0, 0)),
        pl.BlockSpec((blocks, rows, 1), lambda g, s: (0, 0, 0)),
    ]
    return q_spec, k_spec, v_spec, stat_spec, seg_specs


def attention_forward(q_blocks, seg_q, seg_k, valid_k, q_t, kv_t):
    blocks, _, _, rows = kv_t.shape
    q_spec, k_spec, v_spec, stat_spec, seg_specs = kernel_specs(blocks, rows)
    reach = (WINDOW + rows - 2) // rows + 1
    return pl.pallas_call(
        forward_kernel,
        grid_spec=pltpu.PrefetchScalarGridSpec(
            num_scalar_prefetch=1,
            grid=(KV_HEADS,),
            in_specs=seg_specs + [q_spec, k_spec, v_spec],
            out_specs=[q_spec, stat_spec],
            scratch_shapes=[
                pltpu.VMEM((2, reach, rows, rows), F32),
                pltpu.VMEM((GROUP, HEAD_DIM, rows), F32),
                pltpu.VMEM((GROUP, rows), F32),
                pltpu.VMEM((GROUP, rows), F32),
            ],
        ),
        out_shape=[
            jax.ShapeDtypeStruct(q_t.shape, BF16),
            jax.ShapeDtypeStruct((2, KV_HEADS, GROUP, rows), F32),
        ],
        compiler_params=pltpu.CompilerParams(vmem_limit_bytes=40 * 2**20),
        cost_estimate=pl.CostEstimate(
            flops=20_000_000_000, bytes_accessed=6_000_000, transcendentals=0
        ),
    )(q_blocks, seg_q, seg_k, valid_k, q_t, kv_t, kv_t)


def attention_backward(q_blocks, seg_q, seg_k, valid_k, q_t, kv_t, o_t, do_t, lse):
    blocks, _, _, rows = kv_t.shape
    q_spec, k_spec, v_spec, stat_spec, seg_specs = kernel_specs(blocks, rows)
    reach = (WINDOW + rows - 2) // rows + 1
    return pl.pallas_call(
        backward_kernel,
        grid_spec=pltpu.PrefetchScalarGridSpec(
            num_scalar_prefetch=1,
            grid=(KV_HEADS,),
            in_specs=seg_specs + [q_spec, k_spec, v_spec, q_spec, q_spec, stat_spec],
            out_specs=[q_spec, k_spec, k_spec],
            scratch_shapes=[
                pltpu.VMEM((2, reach, rows, rows), F32),
                pltpu.VMEM((GROUP, HEAD_DIM, rows), F32),
                pltpu.VMEM((GROUP, rows), F32),
            ],
        ),
        out_shape=[
            jax.ShapeDtypeStruct(q_t.shape, F32),
            jax.ShapeDtypeStruct((blocks, KV_HEADS, HEAD_DIM, rows), F32),
            jax.ShapeDtypeStruct((blocks, KV_HEADS, HEAD_DIM, rows), F32),
        ],
        compiler_params=pltpu.CompilerParams(vmem_limit_bytes=48 * 2**20),
        cost_estimate=pl.CostEstimate(
            flops=40_000_000_000, bytes_accessed=16_000_000, transcendentals=0
        ),
    )(q_blocks, seg_q, seg_k, valid_k, q_t, kv_t, kv_t, o_t, do_t, lse)


def norm_forward(value_rows, gain):
    inverse = lax.rsqrt(jnp.mean(value_rows * value_rows, axis=-1, keepdims=True) + EPSILON)
    normed = value_rows * inverse
    return (normed * gain, normed, inverse)


def norm_backward(upstream, gain, normed, inverse):
    scaled = upstream * gain
    grad_in = inverse * (scaled - normed * jnp.mean(scaled * normed, axis=-1, keepdims=True))
    return (grad_in, jnp.sum(upstream * normed, axis=0))


def ein(spec, left, right):
    return jnp.einsum(spec, left, right, preferred_element_type=F32)


def turn(v, cosine, sine):
    half = HEAD_DIM // 2
    a, b = v[:, :, :half], v[:, :, half:]
    return jnp.concatenate([a * cosine - b * sine, a * sine + b * cosine], axis=2)


def order(n, own, other):
    k = lax.axis_index("fsdp") % 2
    return jnp.stack([jnp.where(k == 0, own, other), jnp.where(k == 0, other, own)])


def gather_rows(shard):
    n = lax.axis_size("fsdp")
    c = lax.axis_index("ctx")
    r, cols = shard.shape
    quarter = lax.dynamic_slice_in_dim(shard, c * (r // 4), r // 4, 0)
    mine = ctx_gather(z_gather(quarter), 1)
    other = core_swap(mine)
    k = lax.axis_index("fsdp") % 2
    whole = place([(k, mine), (k ^ 1, other)], 1)
    return whole.reshape(n * r, cols)


def scatter_rows(whole):
    n = lax.axis_size("fsdp")
    nz = n // 2
    k = lax.axis_index("fsdp") % 2
    rows, cols = whole.shape
    r = rows // n
    parts = whole.reshape(nz, 2, 4, r // 4, cols)
    got = core_swap(take(parts, k ^ 1, 1))
    pair = (take(parts, k, 1).astype(F32) + got.astype(F32)).astype(BF16)
    mine = z_scatter(ctx_scatter(pair, 1).astype(BF16))
    return ctx_gather(mine.astype(BF16), 0).reshape(r, cols).astype(F32)


def per_device(
    tokens, cotangent, segments, valid, norm_one, w_query, w_key, w_value, w_out,
    norm_two, w_gate, w_up, w_down,
):
    c = lax.axis_index("ctx")
    n = lax.axis_size("fsdp")
    nz = n // 2
    f = lax.axis_index("fsdp")
    k = f % 2
    row_count = tokens.shape[1]
    rows = row_count // 2
    width = tokens.shape[2]
    blocks = 8
    q_width, kv_width = w_query.shape[1], w_key.shape[1]
    ff = w_gate.shape[1]
    r = w_query.shape[0]
    r4 = r // 4

    q_blocks = jnp.stack([c, blocks - 1 - c]).astype(jnp.int32)
    seg_blocks = segments[0].reshape(blocks, rows)
    valid_blocks = valid[0].reshape(blocks, rows)
    seg_q = jnp.stack([take(seg_blocks, q_blocks[0], 0), take(seg_blocks, q_blocks[1], 0)])
    live = jnp.stack([take(valid_blocks, q_blocks[0], 0), take(valid_blocks, q_blocks[1], 0)])
    seg_q = seg_q[:, None, :]
    seg_k = seg_blocks[:, :, None]
    valid_k = valid_blocks[:, :, None]
    places = q_blocks[:, None] * rows + jnp.arange(rows, dtype=jnp.int32)[None, :]
    half = HEAD_DIM // 2
    freqs = jnp.exp(jnp.arange(half, dtype=F32) * (-math.log(ROPE_BASE) / half))
    angles = places.astype(F32)[:, None, None, :] * freqs[None, None, :, None]
    cosine, sine = jnp.cos(angles), jnp.sin(angles)

    gains = jnp.stack([norm_one, norm_two], axis=1)
    gains = jnp.concatenate([gains, jnp.zeros((r, 126), BF16)], axis=1)
    qkv_w = gather_rows(jnp.concatenate([w_query, w_key, w_value, gains], axis=1))
    out_w = gather_rows(w_out)
    gain_one = qkv_w[:, -128].astype(F32)
    gain_two = qkv_w[:, -127].astype(F32)

    d_rows = w_down.shape[0]
    d4 = d_rows // 4
    strip = d_rows // PARTS
    s4 = strip // 4

    def columns(shard):
        quarter = lax.dynamic_slice_in_dim(shard, c * r4, r4, 0)
        cut = quarter.reshape(r4, 2, nz, PARTS, strip).transpose(1, 3, 0, 2, 4)
        return cut.reshape(2, PARTS, r4, nz * strip)

    pairs = jnp.concatenate([columns(w_gate), columns(w_up)], axis=3)
    cut = nz * strip
    gu_w, down_w = [], []
    for part in range(PARTS):
        keep = take(pairs[:, part], k, 0)
        other = core_swap(take(pairs[:, part], k ^ 1, 0))
        both = order(n, keep, other)
        gu_w.append(ctx_gather(z_gather(both), 2).reshape(n * r, 2 * cut))
        piece = lax.dynamic_slice_in_dim(w_down, part * strip + c * s4, s4, 0)
        down_w.append(ctx_gather(half_gather(piece), 1).reshape(cut, width))

    inputs = tokens[0].astype(F32)
    normed_one, unit_one, inverse_one = norm_forward(inputs, gain_one)
    first_in = normed_one.astype(BF16)
    first_sides = first_in.reshape(2, rows, width)
    qkv_t = ein("if,bri->bfr", qkv_w[:, : q_width + 2 * kv_width], first_sides)
    q_t = turn(qkv_t[:, :q_width].reshape(2, HEADS, HEAD_DIM, rows), cosine, sine).astype(BF16)
    k_t = turn(
        qkv_t[:, q_width : q_width + kv_width].reshape(2, KV_HEADS, HEAD_DIM, rows), cosine, sine
    ).astype(BF16)
    v_t = qkv_t[:, q_width + kv_width :].reshape(2, KV_HEADS, HEAD_DIM, rows).astype(BF16)
    kv_own = jnp.concatenate([k_t, v_t], axis=1)
    kv_x, kv_y = swap_x(kv_own), swap_y(kv_own)
    kv_d = jnp.stack([swap_y(kv_x[0]), swap_x(kv_y[1])])
    kv_all = jnp.zeros((blocks,) + kv_own.shape[1:], BF16)
    for owner, piece in ((c, kv_own), (c ^ 1, kv_x), (c ^ 2, kv_y), (c ^ 3, kv_d)):
        kv_all = put(kv_all, piece[0], owner, 0)
        kv_all = put(kv_all, piece[1], blocks - 1 - owner, 0)
    o_t, lse = attention_forward(q_blocks, seg_q, seg_k, valid_k, q_t, kv_all)
    attended_t = o_t.reshape(2, width, rows)
    branch_attn = ein("bfr,fo->bro", attended_t, out_w).reshape(row_count, width)
    middle = inputs + branch_attn

    normed_two, unit_two, inverse_two = norm_forward(middle, gain_two)
    second_in = normed_two.astype(BF16)
    grad_output = cotangent[0]
    x2 = jnp.concatenate([second_in, core_swap(second_in)], axis=0)
    dy2 = jnp.concatenate([grad_output, core_swap(grad_output)], axis=0)
    ffn2 = 0.0
    d_second2 = 0.0
    grad_gu, grad_d = [], []
    for part in range(PARTS):
        gu = ein("ri,if->rf", x2, gu_w[part])
        gate_pre, up_pre = gu[:, :cut], gu[:, cut:]
        sig = jax.nn.sigmoid(gate_pre)
        swish = gate_pre * sig
        hidden = (swish * up_pre).astype(BF16)
        d_hidden = ein("ro,fo->rf", dy2, down_w[part])
        slope = sig * (1.0 + gate_pre * (1.0 - sig))
        d_gu = jnp.concatenate(
            [(d_hidden * up_pre * slope).astype(BF16), (d_hidden * swish).astype(BF16)], axis=1
        )
        grad_d.append(ein("rf,ro->fo", hidden, dy2).astype(BF16))
        grad_gu.append(ein("ri,rf->if", x2, d_gu).astype(BF16))
        ffn2 = ffn2 + ein("rf,fo->ro", hidden, down_w[part])
        d_second2 = d_second2 + ein("rf,if->ri", d_gu, gu_w[part])
    d_second = d_second2[:row_count] + core_swap(d_second2[row_count:].astype(BF16)).astype(F32)
    branch_ffn = ffn2[:row_count] + core_swap(ffn2[row_count:].astype(BF16)).astype(F32)
    result = middle + branch_ffn

    quarter_gu, shard_down = [], []
    for part in range(PARTS):
        whole = grad_gu[part].reshape(nz, 2, 4, r4, 2 * cut)
        mine = z_scatter(ctx_scatter(whole, 2).astype(BF16))
        own = take(mine, k, 0).astype(BF16)
        other = core_swap(take(mine, k ^ 1, 0).astype(BF16))
        quarter_gu.append(order(n, own, other))
        down = half_scatter(ctx_scatter(grad_d[part].reshape(nz, 4, s4, width), 1).astype(BF16))
        shard_down.append(ctx_gather(down.astype(BF16), 0).reshape(strip, width))
    quarters = jnp.stack(quarter_gu, axis=1).reshape(2, PARTS, r4, 2, nz, strip)
    quarters = quarters.transpose(3, 2, 0, 4, 1, 5).reshape(2, r4, ff)
    whole_gu = ctx_gather(quarters, 1).reshape(2, r, ff).astype(F32)
    grad_gate_w, grad_up_w = whole_gu[0], whole_gu[1]
    grad_down_w = jnp.concatenate(shard_down, axis=0).astype(F32)

    grad_mid_norm, grad_gain_two = norm_backward(d_second, gain_two, unit_two, inverse_two)
    grad_middle = grad_output.astype(F32) + grad_mid_norm
    d_branch = grad_middle.astype(BF16).reshape(2, rows, width)
    grad_out_w = scatter_rows(ein("bfr,bro->fo", attended_t, d_branch).astype(BF16))
    do_t = ein("fo,bro->bfr", out_w, d_branch).astype(BF16).reshape(2, HEADS, HEAD_DIM, rows)
    dq_t, dk_t, dv_t = attention_backward(
        q_blocks, seg_q, seg_k, valid_k, q_t, kv_all, o_t, do_t, lse
    )
    dkv = jnp.concatenate([dk_t, dv_t], axis=1).astype(BF16)

    def of(owner, side):
        return take(dkv, owner if side == 0 else blocks - 1 - owner, 0)

    low = swap_x(jnp.stack([of(c ^ 1, 0), of(c ^ 3, 0)])).astype(F32)
    high = swap_y(jnp.stack([of(c ^ 2, 1), of(c ^ 3, 1)])).astype(F32)
    low_own = of(c, 0).astype(F32) + low[0]
    low_pass = (of(c ^ 2, 0).astype(F32) + low[1]).astype(BF16)
    high_own = of(c, 1).astype(F32) + high[0]
    high_pass = (of(c ^ 1, 1).astype(F32) + high[1]).astype(BF16)
    dkv_own = jnp.stack(
        [low_own + swap_y(low_pass).astype(F32), high_own + swap_x(high_pass).astype(F32)]
    )
    d_q = turn(dq_t, cosine, -sine).astype(BF16)
    d_k = turn(dkv_own[:, :KV_HEADS], cosine, -sine).astype(BF16)
    d_v = dkv_own[:, KV_HEADS:].astype(BF16)
    d_qkv = jnp.concatenate([d_q, d_k, d_v], axis=1).reshape(2, q_width + 2 * kv_width, rows)
    grad_qkv = scatter_rows(ein("bri,bfr->if", first_sides, d_qkv).astype(BF16))
    d_first = ein("bfr,if->bri", d_qkv, qkv_w[:, : q_width + 2 * kv_width])
    grad_in_norm, grad_gain_one = norm_backward(
        d_first.reshape(row_count, width), gain_one, unit_one, inverse_one
    )
    grad_inputs = grad_middle + grad_in_norm

    live_rows = live.reshape(row_count, 1).astype(F32)
    squares = jnp.stack(
        [
            jnp.sum(live_rows * member * member)
            for member in (result, grad_inputs, branch_attn, branch_ffn, middle)
        ]
        + [jnp.sum(live_rows)]
    )
    small = lax.psum(jnp.concatenate([grad_gain_one, grad_gain_two, squares]), ("ctx", "fsdp"))
    gain_sums = lax.dynamic_slice_in_dim(small[: 2 * width].reshape(2, width), f * r, r, 1)
    squares = small[2 * width :]
    spreads = jnp.sqrt(squares[:5] / (squares[5] * width))
    return (
        result[None].astype(BF16),
        grad_inputs[None].astype(BF16),
        gain_sums[0],
        grad_qkv[:, :q_width],
        grad_qkv[:, q_width : q_width + kv_width],
        grad_qkv[:, q_width + kv_width :],
        grad_out_w,
        gain_sums[1],
        grad_gate_w,
        grad_up_w,
        grad_down_w,
        spreads,
    )


def solution(mesh):
    rows, shard, vector = P("fsdp", "ctx", None), P("fsdp", None), P("fsdp")
    return jax.shard_map(
        per_device,
        mesh=mesh,
        in_specs=(
            rows, rows, shard, shard, vector, shard, shard, shard, shard, vector,
            shard, shard, shard,
        ),
        out_specs=(
            rows, rows, vector, shard, shard, shard, shard, vector, shard, shard, shard, P(),
        ),
        check_vma=False,
    )
```

time: 1820 us -> 880 us (0.48)
  waiting for transfers between devices: 1140 us -> 260 us
  starting transfers between devices: 1.49 us -> 215 us
  matrix products: 292 us -> 93.1 us
  blocking collectives: 166 us -> 41.1 us
  Pallas kernels: 0 us -> 86.1 us
  other arithmetic: 110 us -> 67.7 us
  local copies, waits for them, and re-layouts: 84.4 us -> 103 us
    reduce_scatter x7 -> x0, waiting for transfers between devices: 724 us -> none  [the longest x1 178 us: per_device(): lax.psum_scatter(grad_down, 'fsdp', scatter_dimension=0, tiled=True)]
    all_gather x10 -> x0, waiting for transfers between devices: 290 us -> none  [the longest x1 79 us: per_device(): lax.all_gather(w_up, 'fsdp', axis=0, tiled=True)]
    ppermute x0 -> x128, waiting for transfers between devices: none -> 260 us  [the longest x38 127 us: swap_x(): return lax.ppermute(v, 'ctx', [(i, i ^ 1) for i in range(4)])]
    ppermute x0 -> x128, starting transfers between devices: none -> 215 us  [the longest x38 71.3 us: swap_y(): return lax.ppermute(v, 'ctx', [(i, i ^ 2) for i in range(4)])]
    dot_general x56 -> x18, matrix products: 292 us -> 93.1 us  [ein(): return jnp.einsum(spec, left, right, preferred_element_type=F32)]
    unnamed x33 -> x0, waiting for transfers between devices: 125 us -> none
    pallas_call x0 -> x2, Pallas kernels: none -> 86.1 us  [the longest x1 43.7 us: attention_backward(): pl.pallas_call(backward_kernel, grid_spec=pltpu.PrefetchScalarGridSpec(nu...]
    all_gather x6 -> x0, blocking collectives: 72.3 us -> none  [the longest x1 18.2 us: per_device(): lax.all_gather(w_value, 'fsdp', axis=0, tiled=True)]
  transfers between devices with their start and end apart: 25 -> 128, of which waited for: 19 -> 51; matrix products, arithmetic and copies ran while one was open for 15% -> 24% of each run, Pallas kernels for 0% -> 10%
where the time goes in v1:
time: 880 us; the launch traced here: 871 us
  waiting for transfers between devices  260 us (30%)
  starting transfers between devices  215 us (24%)
  local copies, waits for them, and re-layouts  103 us (12%)
  matrix products  93.1 us (11%)
  Pallas kernels  86.1 us (10%)
  other arithmetic  67.7 us (8%)
  blocking collectives  41.1 us (5%)
    ppermute x38, waiting for transfers between devices, swap_x(): return lax.ppermute(v, 'ctx', [(i, i ^ 1) for i in range(4)])  127 us
    dot_general x18, matrix products, ein(): return jnp.einsum(spec, left, right, preferred_element_type=F32)  93.1 us
    ppermute x38, starting transfers between devices, swap_y(): return lax.ppermute(v, 'ctx', [(i, i ^ 2) for i in range(4)])  71.3 us
    ppermute x38, waiting for transfers between devices, swap_y(): return lax.ppermute(v, 'ctx', [(i, i ^ 2) for i in range(4)])  65.5 us
    pallas_call x1, Pallas kernels, attention_backward(): pl.pallas_call(backward_kernel, grid_spec=pltpu.PrefetchScalarGridSpec(nu...  43.7 us
    ppermute x38, starting transfers between devices, swap_x(): return lax.ppermute(v, 'ctx', [(i, i ^ 1) for i in range(4)])  43.4 us
    pallas_call x1, Pallas kernels, attention_forward(): pl.pallas_call(forward_kernel, grid_spec=pltpu.PrefetchScalarGridSpec(num...  42.5 us
    psum x1, blocking collectives, per_device(): lax.psum(jnp.concatenate([grad_gain_one, grad_gain_two, squares]), ('ctx'...  41.1 us
  transfers between devices with their start and end apart: 128, of which 51 were waited for; matrix products, arithmetic and copies ran while one was open for 24% of the time, Pallas kernels for 10%

profile of v1, /device:TPU:0, one launch (start us, length us, event | category | flops | bytes accessed | tf_op | source)
XLA Modules:
  0.0 870.8 jit_solution(5793630866485631754)
XLA Ops:
  95.0 9.9 %collective-permute-done.39 = bf16[2,40,1792]{2,1,0:T(8,128)(2,1)S(1)} collective-permute-done((bf16[2,40,1792]{2,1,0:T(8,128)(2,1)S(1)}, bf16[2,40,1792]{2,1,0:T(8,128)(2,1)S(1)}, u32[]{:S(2)}, u32[]{:S(2)}) %collective-permute-start.39) | collective-permute-done | bytes 286752 | tf_op jit(solution)/shard_map/ppermute | solution.py:68
  120.2 12.1 %collective-permute-done.23 = bf16[2,40,1792]{2,1,0:T(8,128)(2,1)S(1)} collective-permute-done((bf16[2,40,1792]{2,1,0:T(8,128)(2,1)S(1)}, bf16[2,40,1792]{2,1,0:T(8,128)(2,1)S(1)}, u32[]{:S(2)}, u32[]{:S(2)}) %collective-permute-start.23) | collective-permute-done | bytes 286752 | tf_op jit(solution)/shard_map/ppermute | solution.py:68
  149.6 8.1 collective-permute-done.18
  164.1 11.3 %collective-permute-done.3 = bf16[4,40,2048]{2,1,0:T(8,128)(2,1)S(1)} collective-permute-done((bf16[4,40,2048]{2,1,0:T(8,128)(2,1)S(1)}, bf16[4,40,2048]{2,1,0:T(8,128)(2,1)S(1)}, u32[]{:S(2)}, u32[]{:S(2)}) %collective-permute-start.3) | collective-permute-done | bytes 655392 | tf_op jit(solution)/shard_map/ppermute | solution.py:30
  185.4 20.7 %collective-permute-done.52 = bf16[2,56,1280]{2,1,0:T(8,128)(2,1)S(1)} collective-permute-done((bf16[2,56,1280]{2,1,0:T(8,128)(2,1)S(1)}, bf16[2,56,1280]{2,1,0:T(8,128)(2,1)S(1)}, u32[]{:S(2)}, u32[]{:S(2)}) %collective-permute-start.52) | collective-permute-done | bytes 286752 | tf_op jit(solution)/shard_map/ppermute | solution.py:30
  215.7 24.5 %collective-permute-done.6 = bf16[2,40,2048]{2,1,0:T(8,128)(2,1)S(1)} collective-permute-done((bf16[2,40,2048]{2,1,0:T(8,128)(2,1)S(1)}, bf16[2,40,2048]{2,1,0:T(8,128)(2,1)S(1)}, u32[]{:S(2)}, u32[]{:S(2)}) %collective-permute-start.6) | collective-permute-done | bytes 327712 | tf_op jit(solution)/shard_map/ppermute | solution.py:30
  248.0 8.8 %collective-permute-done.26 = bf16[4,2,40,1792]{3,2,1,0:T(8,128)(2,1)S(1)} collective-permute-done((bf16[4,2,40,1792]{3,2,1,0:T(8,128)(2,1)S(1)}, bf16[4,2,40,1792]{3,2,1,0:T(8,128)(2,1)S(1)}, u32[]{:S(2)}, u32[]{:S(2)}) %collective-permute-start.26) | collective-permute-done | bytes 1146912 | tf_op jit(solution)/shard_map/ppermute | solution.py:34
  285.3 8.3 collective-permute-done.9
  304.2 42.5 %shard_map.220 = (bf16[2,20,64,216]{3,2,1,0:T(8,128)(2,1)S(1)}, f32[2,5,4,216]{3,2,1,0:T(4,128)S(1)}) custom-call(s32[2]{0:T(128)S(1)} %get-tuple-element.51.blocks_ref, s32[2,1,216]{2,1,0:T(1,128)S(1)} %broadcast_in_dim.257.seg_q_ref, s32[8,216,1]{2,1,0:T(8,128)S(1)} %broadcast_in_dim_reshape_squeeze.8.seg_k_ref, s32[8,216,1]{2,1,0:T(8,128)S(1)} %copy-done.6, ...), custom_call_target="tpu_custom_call" | custom-call | flops 20000000000 | bytes 6000000 | tf_op jit(solution)/shard_map/pallas_call | solution.py:288
  361.7 9.6 %fusion.177 = f32[864,1792]{1,0:T(8,128)} fusion(bf16[1280,1792]{1,0:T(8,128)(2,1)} %bitcast.802, bf16[432,1280]{1,0:T(8,128)(2,1)S(1)} %collective-permute-done.20, bf16[432,1280]{1,0:T(8,128)(2,1)S(1)} %multiply_convert_fusion.6), kind=kOutput, calls=%fused_computation.528 | convolution fusion | flops 3968040960 | bytes 12992512 | tf_op jit(solution)/shard_map/ri,if->rf/dot_general | solution.py:355
  415.4 13.6 %collective-permute-start.106 = (bf16[2,2,56,1280]{3,2,1,0:T(8,128)(2,1)}, bf16[2,2,56,1280]{3,2,1,0:T(8,128)(2,1)}, u32[]{:S(2)}, u32[]{:S(2)}) collective-permute-start(bf16[2,2,56,1280]{3,2,1,0:T(8,128)(2,1)} %pad_maximum_fusion.21), channel_id=1, source_target_pairs={{0,16},{8,24},{16,0},{24,8},{1,17},{9,25},{17,1},{25,9},{2,18},{10... | collective-permute-start | bytes 1720328 | tf_op jit(solution)/shard_map/ppermute | solution.py:34
  435.9 7.5 convolution_convert_fusion.1
  445.9 7.5 convolution_convert_fusion
  465.9 9.4 %collective-permute-done.116 = bf16[2,2,56,1280]{3,2,1,0:T(8,128)(2,1)S(1)} collective-permute-done((bf16[2,2,56,1280]{3,2,1,0:T(8,128)(2,1)S(1)}, bf16[2,2,56,1280]{3,2,1,0:T(8,128)(2,1)S(1)}, u32[]{:S(2)}, u32[]{:S(2)}) %collective-permute-start.116) | collective-permute-done | bytes 573472 | tf_op jit(solution)/shard_map/ppermute | solution.py:30
  534.6 43.7 %shard_map.221 = (f32[2,20,64,216]{3,2,1,0:T(8,128)}, f32[8,5,64,216]{3,2,1,0:T(8,128)}, f32[8,5,64,216]{3,2,1,0:T(8,128)}) custom-call(s32[2]{0:T(128)S(1)} %get-tuple-element.51.blocks_ref, s32[2,1,216]{2,1,0:T(1,128)S(1)} %broadcast_in_dim.257.seg_q_ref, s32[8,216,1]{2,1,0:T(8,128)S(1)} %broadcast_in_dim_reshape_squeeze.8.seg_k_ref, ...), custom_call_target="tpu_custom_call" | custom-call | flops 40000000000 | bytes 16000000 | tf_op jit(solution)/shard_map/pallas_call | solution.py:317
  587.1 12.5 %collective-permute-start.113 = (bf16[56,1280]{1,0:T(8,128)(2,1)}, bf16[56,1280]{1,0:T(8,128)(2,1)S(1)}, u32[]{:S(2)}, u32[]{:S(2)}) collective-permute-start(bf16[56,1280]{1,0:T(8,128)(2,1)} %get-tuple-element.35), channel_id=1, source_target_pairs={{0,16},{8,24},{16,0},{24,8},{1,17},{9,25},{17,1},{25,9},{2,18},{10... | collective-permute-start | bytes 430088 | tf_op jit(solution)/shard_map/ppermute | solution.py:34
  613.2 10.5 %collective-permute-done.114 = bf16[28,1280]{1,0:T(8,128)(2,1)S(1)} collective-permute-done((bf16[28,1280]{1,0:T(8,128)(2,1)S(1)}, bf16[28,1280]{1,0:T(8,128)(2,1)S(1)}, u32[]{:S(2)}, u32[]{:S(2)}) %collective-permute-start.114) | collective-permute-done | bytes 71712 | tf_op jit(solution)/shard_map/ppermute | solution.py:34
  636.4 7.8 collective-permute-done.87
  682.7 41.1 %psum.7 = f32[2566]{0:T(1024)S(1)} all-reduce(f32[2566]{0:T(1024)S(1)} %concatenate.133), channel_id=1, replica_groups=mesh['ctx'=4,'fsdp'=8] {'ctx','fsdp'}, use_global_device_ids=true, to_apply=%region_12.13 | all-reduce | flops 2566 | bytes 20528 | tf_op jit(solution)/shard_map/psum | solution.py:559
  725.6 7.1 bitcast_convert_fusion
  742.1 10.2 %collective-permute-done.97 = bf16[2,40,1792]{2,1,0:T(8,128)(2,1)S(1)} collective-permute-done((bf16[2,40,1792]{2,1,0:T(8,128)(2,1)S(1)}, bf16[2,40,1792]{2,1,0:T(8,128)(2,1)S(1)}, u32[]{:S(2)}, u32[]{:S(2)}) %collective-permute-start.97) | collective-permute-done | bytes 286752 | tf_op jit(solution)/shard_map/ppermute | solution.py:84
  763.0 12.1 %collective-permute-done.100 = bf16[2,40,3584]{2,1,0:T(8,128)(2,1)S(1)} collective-permute-done((bf16[2,40,3584]{2,1,0:T(8,128)(2,1)S(1)}, bf16[2,40,3584]{2,1,0:T(8,128)(2,1)S(1)}, u32[]{:S(2)}, u32[]{:S(2)}) %collective-permute-start.100) | collective-permute-done | bytes 573472 | tf_op jit(solution)/shard_map/ppermute | solution.py:30
  782.2 9.9 %collective-permute-done.75 = bf16[2,2,40,1280]{3,2,1,0:T(8,128)(2,1)S(1)} collective-permute-done((bf16[2,2,40,1280]{3,2,1,0:T(8,128)(2,1)S(1)}, bf16[2,2,40,1280]{3,2,1,0:T(8,128)(2,1)S(1)}, u32[]{:S(2)}, u32[]{:S(2)}) %collective-permute-start.75) | collective-permute-done | bytes 409632 | tf_op jit(solution)/shard_map/ppermute | solution.py:34
  825.5 10.6 %collective-permute-done.63 = bf16[2,2,40,1920]{3,2,1,0:T(8,128)(2,1)S(1)} collective-permute-done((bf16[2,2,40,1920]{3,2,1,0:T(8,128)(2,1)S(1)}, bf16[2,2,40,1920]{3,2,1,0:T(8,128)(2,1)S(1)}, u32[]{:S(2)}, u32[]{:S(2)}) %collective-permute-start.63) | collective-permute-done | bytes 614432 | tf_op jit(solution)/shard_map/ppermute | solution.py:34
  (738 shorter events, 507.2 us)
Async XLA Ops:
  12.9 67.4 %collective-permute-start = (bf16[40,2048]{1,0:T(8,128)(2,1)}, bf16[40,2048]{1,0:T(8,128)(2,1)}, u32[]{:S(2)}, u32[]{:S(2)}) collective-permute-start(bf16[40,2048]{1,0:T(8,128)(2,1)} %get-tuple-element.53), channel_id=1, source_target_pairs={{0,2},{1,3},{2,4},{3,5},{4,6},{5,7},{6,0},{7,1},{8,10},{9,11},{10,... | collective-permute-start | bytes 491528 | tf_op jit(solution)/shard_map/ppermute | solution.py:68
  13.6 69.5 %collective-permute-start.1 = (bf16[40,2048]{1,0:T(8,128)(2,1)}, bf16[40,2048]{1,0:T(8,128)(2,1)}, u32[]{:S(2)}, u32[]{:S(2)}) collective-permute-start(bf16[40,2048]{1,0:T(8,128)(2,1)} %get-tuple-element.53), channel_id=1, source_target_pairs={{0,4},{1,5},{2,6},{3,7},{4,0},{5,1},{6,2},{7,3},{8,12},{9,13},{10,... | collective-permute-start | bytes 491528 | tf_op jit(solution)/shard_map/ppermute | solution.py:68
  75.0 66.7 %collective-permute-start.15 = (bf16[4,40,1280]{2,1,0:T(8,128)(2,1)S(1)}, bf16[4,40,1280]{2,1,0:T(8,128)(2,1)S(1)}, u32[]{:S(2)}, u32[]{:S(2)}) collective-permute-start(bf16[4,40,1280]{2,1,0:T(8,128)(2,1)S(1)} %bitcast_dynamic-update-slice_fusion.59), channel_id=1, source_target_pairs={{0,8},{8,0},{16,24},{24,16},{1,9},{9,1},{17,25},{25,17},{2,10},{10... | collective-permute-start | bytes 1228808 | tf_op jit(solution)/shard_map/ppermute | solution.py:30
  78.5 65.4 %collective-permute-start.16 = (bf16[4,40,1280]{2,1,0:T(8,128)(2,1)S(1)}, bf16[4,40,1280]{2,1,0:T(8,128)(2,1)S(1)}, u32[]{:S(2)}, u32[]{:S(2)}) collective-permute-start(bf16[4,40,1280]{2,1,0:T(8,128)(2,1)S(1)} %bitcast_dynamic-update-slice_fusion.59), channel_id=1, source_target_pairs={{0,16},{8,24},{16,0},{24,8},{1,17},{9,25},{17,1},{25,9},{2,18},{10... | collective-permute-start | bytes 1228808 | tf_op jit(solution)/shard_map/ppermute | solution.py:34
  93.4 65.7 %collective-permute-start.49 = (bf16[4,56,1280]{2,1,0:T(8,128)(2,1)S(1)}, bf16[4,56,1280]{2,1,0:T(8,128)(2,1)S(1)}, u32[]{:S(2)}, u32[]{:S(2)}) collective-permute-start(bf16[4,56,1280]{2,1,0:T(8,128)(2,1)S(1)} %bitcast_dynamic-update-slice_fusion.48), channel_id=1, source_target_pairs={{0,8},{8,0},{16,24},{24,16},{1,9},{9,1},{17,25},{25,17},{2,10},{10... | collective-permute-start | bytes 1720328 | tf_op jit(solution)/shard_map/ppermute | solution.py:30
  104.9 56.7 %collective-permute-start.50 = (bf16[4,56,1280]{2,1,0:T(8,128)(2,1)S(1)}, bf16[4,56,1280]{2,1,0:T(8,128)(2,1)S(1)}, u32[]{:S(2)}, u32[]{:S(2)}) collective-permute-start(bf16[4,56,1280]{2,1,0:T(8,128)(2,1)S(1)} %bitcast_dynamic-update-slice_fusion.48), channel_id=1, source_target_pairs={{0,16},{8,24},{16,0},{24,8},{1,17},{9,25},{17,1},{25,9},{2,18},{10... | collective-permute-start | bytes 1720328 | tf_op jit(solution)/shard_map/ppermute | solution.py:34
  161.6 78.7 %collective-permute-start.41 = (bf16[4,2,40,1792]{3,2,1,0:T(8,128)(2,1)S(1)}, bf16[4,2,40,1792]{3,2,1,0:T(8,128)(2,1)S(1)}, u32[]{:S(2)}, u32[]{:S(2)}) collective-permute-start(bf16[4,2,40,1792]{3,2,1,0:T(8,128)(2,1)S(1)} %bitcast_dynamic-update-slice_fusion.27), channel_id=1, source_target_pairs={{0,8},{8,0},{16,24},{24,16},{1,9},{9,1},{17,25},{25,17},{2,10},{10... | collective-permute-start | bytes 3440648 | tf_op jit(solution)/shard_map/ppermute | solution.py:30
  242.7 113.4 %collective-permute-start.43 = (bf16[2,2,40,1792]{3,2,1,0:T(8,128)(2,1)}, bf16[2,2,40,1792]{3,2,1,0:T(8,128)(2,1)}, u32[]{:S(2)}, u32[]{:S(2)}) collective-permute-start(bf16[2,2,40,1792]{3,2,1,0:T(8,128)(2,1)} %slice.489), channel_id=1, source_target_pairs={{0,16},{8,24},{16,0},{24,8},{1,17},{9,25},{17,1},{25,9},{2,18},{10... | collective-permute-start | bytes 1720328 | tf_op jit(solution)/shard_map/ppermute | solution.py:34
  245.6 111.0 %collective-permute-start.44 = (bf16[2,2,40,1792]{3,2,1,0:T(8,128)(2,1)}, bf16[2,2,40,1792]{3,2,1,0:T(8,128)(2,1)}, u32[]{:S(2)}, u32[]{:S(2)}) collective-permute-start(bf16[2,2,40,1792]{3,2,1,0:T(8,128)(2,1)} %slice.490), channel_id=1, source_target_pairs={{0,8},{8,0},{16,24},{24,16},{1,9},{9,1},{17,25},{25,17},{2,10},{10... | collective-permute-start | bytes 1720328 | tf_op jit(solution)/shard_map/ppermute | solution.py:30
  256.7 102.2 %collective-permute-start.27 = (bf16[2,2,40,1792]{3,2,1,0:T(8,128)(2,1)}, bf16[2,2,40,1792]{3,2,1,0:T(8,128)(2,1)}, u32[]{:S(2)}, u32[]{:S(2)}) collective-permute-start(bf16[2,2,40,1792]{3,2,1,0:T(8,128)(2,1)} %slice.482), channel_id=1, source_target_pairs={{0,16},{8,24},{16,0},{24,8},{1,17},{9,25},{17,1},{25,9},{2,18},{10... | collective-permute-start | bytes 1720328 | tf_op jit(solution)/shard_map/ppermute | solution.py:34
  297.2 61.8 %collective-permute-start.28 = (bf16[2,2,40,1792]{3,2,1,0:T(8,128)(2,1)}, bf16[2,2,40,1792]{3,2,1,0:T(8,128)(2,1)}, u32[]{:S(2)}, u32[]{:S(2)}) collective-permute-start(bf16[2,2,40,1792]{3,2,1,0:T(8,128)(2,1)} %slice.483), channel_id=1, source_target_pairs={{0,8},{8,0},{16,24},{24,16},{1,9},{9,1},{17,25},{25,17},{2,10},{10... | collective-permute-start | bytes 1720328 | tf_op jit(solution)/shard_map/ppermute | solution.py:30
  405.9 110.5 %collective-permute-start.55 = (bf16[432,1280]{1,0:T(8,128)(2,1)S(1)}, bf16[432,1280]{1,0:T(8,128)(2,1)S(1)}, u32[]{:S(2)}, u32[]{:S(2)}) collective-permute-start(bf16[432,1280]{1,0:T(8,128)(2,1)S(1)} %slice.753), channel_id=1, source_target_pairs={{0,1},{1,0},{2,3},{3,2},{4,5},{5,4},{6,7},{7,6},{8,9},{9,8},{10,11... | collective-permute-start | bytes 3317768 | tf_op jit(solution)/shard_map/ppermute | solution.py:26
  411.5 105.4 %collective-permute-start.53 = (bf16[432,1280]{1,0:T(8,128)(2,1)S(1)}, bf16[432,1280]{1,0:T(8,128)(2,1)}, u32[]{:S(2)}, u32[]{:S(2)}) collective-permute-start(bf16[432,1280]{1,0:T(8,128)(2,1)S(1)} %slice.754), channel_id=1, source_target_pairs={{0,1},{1,0},{2,3},{3,2},{4,5},{5,4},{6,7},{7,6},{8,9},{9,8},{10,11... | collective-permute-start | bytes 3317768 | tf_op jit(solution)/shard_map/ppermute | solution.py:26
  509.0 78.1 %collective-permute-start.86 = (bf16[2,2,2,40,1792]{4,3,2,1,0:T(8,128)(2,1)}, bf16[2,2,2,40,1792]{4,3,2,1,0:T(8,128)(2,1)}, u32[]{:S(2)}, u32[]{:S(2)}) collective-permute-start(bf16[2,2,2,40,1792]{4,3,2,1,0:T(8,128)(2,1)} %pad_maximum_fusion.11), channel_id=1, source_target_pairs={{0,16},{8,24},{16,0},{24,8},{1,17},{9,25},{17,1},{25,9},{2,18},{10... | collective-permute-start | bytes 3440648 | tf_op jit(solution)/shard_map/ppermute | solution.py:34
  512.6 88.3 %collective-permute-start.84 = (bf16[2,2,2,40,1792]{4,3,2,1,0:T(8,128)(2,1)}, bf16[2,2,2,40,1792]{4,3,2,1,0:T(8,128)(2,1)}, u32[]{:S(2)}, u32[]{:S(2)}) collective-permute-start(bf16[2,2,2,40,1792]{4,3,2,1,0:T(8,128)(2,1)} %pad_maximum_fusion.10), channel_id=1, source_target_pairs={{0,8},{8,0},{16,24},{24,16},{1,9},{9,1},{17,25},{25,17},{2,10},{10... | collective-permute-start | bytes 3440648 | tf_op jit(solution)/shard_map/ppermute | solution.py:30
  514.8 88.1 %collective-permute-start.94 = (bf16[2,2,2,40,1792]{4,3,2,1,0:T(8,128)(2,1)}, bf16[2,2,2,40,1792]{4,3,2,1,0:T(8,128)(2,1)}, u32[]{:S(2)}, u32[]{:S(2)}) collective-permute-start(bf16[2,2,2,40,1792]{4,3,2,1,0:T(8,128)(2,1)} %pad_maximum_fusion.13), channel_id=1, source_target_pairs={{0,16},{8,24},{16,0},{24,8},{1,17},{9,25},{17,1},{25,9},{2,18},{10... | collective-permute-start | bytes 3440648 | tf_op jit(solution)/shard_map/ppermute | solution.py:34
  516.3 89.3 %collective-permute-start.92 = (bf16[2,2,2,40,1792]{4,3,2,1,0:T(8,128)(2,1)}, bf16[2,2,2,40,1792]{4,3,2,1,0:T(8,128)(2,1)}, u32[]{:S(2)}, u32[]{:S(2)}) collective-permute-start(bf16[2,2,2,40,1792]{4,3,2,1,0:T(8,128)(2,1)} %pad_maximum_fusion.12), channel_id=1, source_target_pairs={{0,8},{8,0},{16,24},{24,16},{1,9},{9,1},{17,25},{25,17},{2,10},{10... | collective-permute-start | bytes 3440648 | tf_op jit(solution)/shard_map/ppermute | solution.py:30
  516.9 90.5 %collective-permute-start.112 = (bf16[56,1280]{1,0:T(8,128)(2,1)}, bf16[56,1280]{1,0:T(8,128)(2,1)}, u32[]{:S(2)}, u32[]{:S(2)}) collective-permute-start(bf16[56,1280]{1,0:T(8,128)(2,1)} %get-tuple-element.35), channel_id=1, source_target_pairs={{0,8},{8,0},{16,24},{24,16},{1,9},{9,1},{17,25},{25,17},{2,10},{10... | collective-permute-start | bytes 430088 | tf_op jit(solution)/shard_map/ppermute | solution.py:30
  609.9 168.3 %collective-permute-start.72 = (bf16[4,4,40,1280]{3,2,1,0:T(8,128)(2,1)}, bf16[4,4,40,1280]{3,2,1,0:T(8,128)(2,1)}, u32[]{:S(2)}, u32[]{:S(2)}) collective-permute-start(bf16[4,4,40,1280]{3,2,1,0:T(8,128)(2,1)} %dynamic-slice_bitcast_fusion.1), channel_id=1, source_target_pairs={{0,1},{1,0},{2,3},{3,2},{4,5},{5,4},{6,7},{7,6},{8,9},{9,8},{10,11... | collective-permute-start | bytes 4915208 | tf_op jit(solution)/shard_map/ppermute | solution.py:26
  656.4 80.3 %collective-permute-start.88 = (bf16[2,40,1792]{2,1,0:T(8,128)(2,1)}, bf16[2,40,1792]{2,1,0:T(8,128)(2,1)S(1)}, u32[]{:S(2)}, u32[]{:S(2)}) collective-permute-start(bf16[2,40,1792]{2,1,0:T(8,128)(2,1)} %get-tuple-element.111), channel_id=1, source_target_pairs={{0,2},{1,3},{2,4},{3,5},{4,6},{5,7},{6,0},{7,1},{8,10},{9,11},{10,... | collective-permute-start | bytes 860168 | tf_op jit(solution)/shard_map/ppermute | solution.py:84
  658.3 80.3 %collective-permute-start.89 = (bf16[2,40,1792]{2,1,0:T(8,128)(2,1)}, bf16[2,40,1792]{2,1,0:T(8,128)(2,1)}, u32[]{:S(2)}, u32[]{:S(2)}) collective-permute-start(bf16[2,40,1792]{2,1,0:T(8,128)(2,1)} %get-tuple-element.112), channel_id=1, source_target_pairs={{0,4},{1,5},{2,6},{3,7},{4,0},{5,1},{6,2},{7,3},{8,12},{9,13},{10,... | collective-permute-start | bytes 860168 | tf_op jit(solution)/shard_map/ppermute | solution.py:84
  662.2 78.0 %collective-permute-start.90 = (bf16[2,40,1792]{2,1,0:T(8,128)(2,1)}, bf16[2,40,1792]{2,1,0:T(8,128)(2,1)}, u32[]{:S(2)}, u32[]{:S(2)}) collective-permute-start(bf16[2,40,1792]{2,1,0:T(8,128)(2,1)} %get-tuple-element.113), channel_id=1, source_target_pairs={{0,6},{1,7},{2,0},{3,1},{4,2},{5,3},{6,4},{7,5},{8,14},{9,15},{10,... | collective-permute-start | bytes 860168 | tf_op jit(solution)/shard_map/ppermute | solution.py:84
  664.1 77.4 %collective-permute-start.96 = (bf16[2,40,1792]{2,1,0:T(8,128)(2,1)}, bf16[2,40,1792]{2,1,0:T(8,128)(2,1)}, u32[]{:S(2)}, u32[]{:S(2)}) collective-permute-start(bf16[2,40,1792]{2,1,0:T(8,128)(2,1)} %get-tuple-element.114), channel_id=1, source_target_pairs={{0,2},{1,3},{2,4},{3,5},{4,6},{5,7},{6,0},{7,1},{8,10},{9,11},{10,... | collective-permute-start | bytes 860168 | tf_op jit(solution)/shard_map/ppermute | solution.py:84
  740.2 80.3 %collective-permute-start.60 = (bf16[4,4,40,1920]{3,2,1,0:T(8,128)(2,1)}, bf16[4,4,40,1920]{3,2,1,0:T(8,128)(2,1)}, u32[]{:S(2)}, u32[]{:S(2)}) collective-permute-start(bf16[4,4,40,1920]{3,2,1,0:T(8,128)(2,1)} %dynamic-slice_bitcast_fusion), channel_id=1, source_target_pairs={{0,1},{1,0},{2,3},{3,2},{4,5},{5,4},{6,7},{7,6},{8,9},{9,8},{10,11... | collective-permute-start | bytes 7372808 | tf_op jit(solution)/shard_map/ppermute | solution.py:26
  (199 other events, 3013.0 us)

commit v2 on v1

v2 whole, which is shorter than its diff:
```python
import functools
import math

import jax
import jax.numpy as jnp
from jax import lax
from jax.experimental import pallas as pl
from jax.experimental.pallas import tpu as pltpu
from jax.sharding import PartitionSpec as P

HEADS = 20
KV_HEADS = 5
HEAD_DIM = 64
GROUP = HEADS // KV_HEADS
WINDOW = 1024
EPSILON = 1e-05
MASKED = -1e30
ROPE_BASE = 10000.0
BF16 = jnp.bfloat16
F32 = jnp.float32


def core_swap(v):
    n = lax.axis_size("fsdp")
    return lax.ppermute(v, "fsdp", [(i, i ^ 1) for i in range(n)])


def swap_x(v):
    return lax.ppermute(v, "ctx", [(i, i ^ 1) for i in range(4)])


def swap_y(v):
    return lax.ppermute(v, "ctx", [(i, i ^ 2) for i in range(4)])


def put(buffer, piece, index, axis):
    return lax.dynamic_update_slice_in_dim(
        buffer, jnp.expand_dims(piece, axis), index, axis
    )


def take(v, index, axis):
    return lax.dynamic_index_in_dim(v, index, axis, keepdims=False)


def place(pieces, axis):
    first = pieces[0][1]
    shape = first.shape[:axis] + (len(pieces),) + first.shape[axis:]
    buffer = jnp.zeros(shape, first.dtype)
    for index, piece in pieces:
        buffer = put(buffer, piece, index, axis)
    return buffer


def z_fetch(piece):
    n = lax.axis_size("fsdp")
    nz = n // 2
    if nz != 4:
        groups = [list(range(0, n, 2)), list(range(1, n, 2))]
        every = lax.all_gather(piece, "fsdp", axis=0, axis_index_groups=groups)
        z = lax.axis_index("fsdp") // 2
        return jnp.take(every, (z - jnp.arange(nz)) % nz, axis=0)
    pieces = [piece]
    for d in (1, 2, 3):
        pieces.append(lax.ppermute(piece, "fsdp", [(i, (i + 2 * d) % n) for i in range(n)]))
    return jnp.stack(pieces)


def z_scatter(pieces):
    n = lax.axis_size("fsdp")
    nz = n // 2
    if nz != 4:
        groups = [list(range(0, n, 2)), list(range(1, n, 2))]
        return lax.psum_scatter(
            pieces, "fsdp", scatter_dimension=0, axis_index_groups=groups
        ).astype(F32)
    z = lax.axis_index("fsdp") // 2
    total = take(pieces, z, 0).astype(F32)
    for d in (1, 2, 3):
        sent = take(pieces, (z + d) % nz, 0)
        got = lax.ppermute(sent, "fsdp", [(i, (i + 2 * d) % n) for i in range(n)])
        total = total + got.astype(F32)
    return total


def sync(*values):
    return lax.optimization_barrier(values)


def ctx_fetch(piece):
    half = piece.shape[0] // 2
    from_x = swap_x(piece)
    from_y = swap_y(piece)
    from_d = jnp.concatenate([swap_y(from_x[:half]), swap_x(from_y[half:])], axis=0)
    return [piece, from_x, from_y, from_d]


def after(v, *earlier):
    return lax.optimization_barrier((v, earlier))[0]


def ctx_fetch_direct(piece):
    diagonal = lax.ppermute(piece, "ctx", [(i, i ^ 3) for i in range(4)])
    return [piece, swap_x(piece), swap_y(piece), diagonal]


def ctx_gather(piece, axis):
    c = lax.axis_index("ctx")
    return place([(c ^ i, v) for i, v in enumerate(ctx_fetch(piece))], axis)


def scatter_first(parts):
    half = parts[0].shape[0] // 2
    low_got = swap_x(jnp.concatenate([parts[1][:half], parts[3][:half]]))
    high_got = swap_y(jnp.concatenate([parts[2][half:], parts[3][half:]]))
    return low_got, high_got


def scatter_pass(parts, got):
    half = parts[0].shape[0] // 2
    low_got, high_got = got[0].astype(F32), got[1].astype(F32)
    low_pass = (parts[2][:half].astype(F32) + low_got[half:]).astype(BF16)
    high_pass = (parts[1][half:].astype(F32) + high_got[half:]).astype(BF16)
    low_own = parts[0][:half].astype(F32) + low_got[:half]
    high_own = parts[0][half:].astype(F32) + high_got[:half]
    return low_own, high_own, low_pass, high_pass


def scatter_last(low_own, high_own, low_pass, high_pass):
    from_y, from_x = swap_y(low_pass), swap_x(high_pass)
    return jnp.concatenate([low_own + from_y.astype(F32), high_own + from_x.astype(F32)])


def exchange_first(parts):
    to_x = jnp.concatenate([parts[1], parts[3][:1]], axis=0)
    to_y = jnp.concatenate([parts[2], parts[3][1:]], axis=0)
    return swap_x(to_x), swap_y(to_y)


def exchange_second(parts, got_x, got_y):
    from_d = jnp.concatenate([swap_y(got_x[2:]), swap_x(got_y[2:])], axis=0)
    return [parts[0], got_x[:2], got_y[:2], from_d]


def small_sum(v):
    n = lax.axis_size("fsdp")
    bit = 1
    while bit < n:
        v = v + lax.ppermute(v, "fsdp", [(i, i ^ bit) for i in range(n)])
        bit *= 2
    v = v + swap_x(v)
    return v + swap_y(v)


def pick_columns(c, gate, up, count):
    r, ff = gate.shape
    group = ff // count
    strip = group // 4

    def kernel(c_ref, gate_ref, up_ref, out_ref):
        for own in range(4):

            @pl.when(c_ref[0] == own)
            def _():
                for j in range(count):
                    at = j * group + own * strip
                    out_ref[:, j * strip : (j + 1) * strip] = gate_ref[:, at : at + strip]
                    to = ff // 4 + j * strip
                    out_ref[:, to : to + strip] = up_ref[:, at : at + strip]

    whole = pl.BlockSpec((r, ff), lambda i, s: (0, 0))
    return pl.pallas_call(
        kernel,
        grid_spec=pltpu.PrefetchScalarGridSpec(
            num_scalar_prefetch=1,
            grid=(1,),
            in_specs=[whole, whole],
            out_specs=pl.BlockSpec((r, ff // 2), lambda i, s: (0, 0)),
        ),
        out_shape=jax.ShapeDtypeStruct((r, ff // 2), BF16),
        cost_estimate=pl.CostEstimate(flops=0, bytes_accessed=6 * r * ff, transcendentals=0),
    )(c, gate, up)


def unpick_columns(c, pieces, count):
    r, half = pieces[0].shape
    ff = 2 * half
    group = ff // count
    strip = group // 4

    def kernel(c_ref, *refs):
        gate_ref, up_ref = refs[4:]
        for own in range(4):

            @pl.when(c_ref[0] == own)
            def _():
                for step in range(4):
                    for j in range(count):
                        at = j * group + (own ^ step) * strip
                        piece = refs[step]
                        gate_ref[:, at : at + strip] = piece[
                            :, j * strip : (j + 1) * strip
                        ].astype(F32)
                        frm = ff // 4 + j * strip
                        up_ref[:, at : at + strip] = piece[:, frm : frm + strip].astype(F32)

    whole = pl.BlockSpec((r, ff), lambda i, s: (0, 0))
    return pl.pallas_call(
        kernel,
        grid_spec=pltpu.PrefetchScalarGridSpec(
            num_scalar_prefetch=1,
            grid=(1,),
            in_specs=[pl.BlockSpec((r, half), lambda i, s: (0, 0))] * 4,
            out_specs=[whole, whole],
        ),
        out_shape=[jax.ShapeDtypeStruct((r, ff), F32)] * 2,
        compiler_params=pltpu.CompilerParams(vmem_limit_bytes=40 * 2**20),
        cost_estimate=pl.CostEstimate(flops=0, bytes_accessed=12 * r * ff, transcendentals=0),
    )(c, *pieces)


def pair_bias(q_block, k_block, rows, seg_q, seg_k, valid_k):
    key_at = k_block * rows + lax.broadcasted_iota(jnp.int32, (rows, rows), 0)
    query_at = q_block * rows + lax.broadcasted_iota(jnp.int32, (rows, rows), 1)
    distance = query_at - key_at
    allowed = (
        (seg_q == seg_k)
        & (distance >= 0)
        & (distance < WINDOW)
        & ((valid_k == 1) | (distance == 0))
    )
    return jnp.where(allowed, 0.0, MASKED).astype(F32)


def first_block(q_block, rows):
    reach = (WINDOW + rows - 2) // rows
    return jnp.maximum(q_block - reach, 0)


def dot(a, b, dims):
    return lax.dot_general(a, b, (dims, ((), ())), preferred_element_type=F32)


def fill_bias(blocks_ref, seg_q_ref, seg_k_ref, valid_k_ref, bias_ref, rows):
    for side in range(2):
        b = blocks_ref[side]
        lo = first_block(b, rows)

        def body(kb, _):
            bias_ref[side, kb - lo] = pair_bias(
                b, kb, rows, seg_q_ref[side], seg_k_ref[kb], valid_k_ref[kb]
            )
            return 0

        lax.fori_loop(lo, b + 1, body, 0)


def forward_kernel(
    blocks_ref, slots_ref, seg_q_ref, seg_k_ref, valid_k_ref, q_ref, k_ref, v_ref,
    o_ref, lse_ref, bias_ref, acc_ref, peak_ref, total_ref,
):
    rows = q_ref.shape[-1]

    @pl.when(pl.program_id(0) == 0)
    def _():
        fill_bias(blocks_ref, seg_q_ref, seg_k_ref, valid_k_ref, bias_ref, rows)

    for side in range(2):
        b = blocks_ref[side]
        lo = first_block(b, rows)
        acc_ref[...] = jnp.zeros_like(acc_ref)
        total_ref[...] = jnp.zeros_like(total_ref)
        peak_ref[...] = jnp.full_like(peak_ref, -jnp.inf)

        def body(kb, _):
            slot = slots_ref[kb]
            keys = k_ref[slot, 0].T
            values_t = v_ref[slot, 0]
            bias = bias_ref[side, kb - lo]
            for h in range(GROUP):
                query = q_ref[side, h]
                s = dot(keys, query, ((1,), (0,))) + bias
                peak_old = peak_ref[h : h + 1]
                peak = jnp.maximum(peak_old, jnp.max(s, axis=0, keepdims=True))
                p = jnp.exp(s - peak)
                shrink = jnp.exp(peak_old - peak)
                peak_ref[h : h + 1] = peak
                total_ref[h : h + 1] = total_ref[h : h + 1] * shrink + jnp.sum(
                    p, axis=0, keepdims=True
                )
                acc_ref[h] = acc_ref[h] * shrink + dot(values_t, p.astype(BF16), ((1,), (0,)))
            return 0

        body(b, 0)
        lax.fori_loop(lo, b, body, 0)
        for h in range(GROUP):
            total = total_ref[h : h + 1]
            o_ref[side, h] = (acc_ref[h] / total).astype(BF16)
            lse_ref[side, 0, h : h + 1] = peak_ref[h : h + 1] + jnp.log(total)


def backward_kernel(
    blocks_ref, slots_ref, seg_q_ref, seg_k_ref, valid_k_ref, cos_ref, sin_ref, q_ref, k_ref, v_ref,
    o_ref, do_ref, lse_ref,
    dq_ref, dkv_ref, bias_ref, acc_ref, center_ref, dk_ref, dv_ref,
):
    rows = q_ref.shape[-1]

    @pl.when(pl.program_id(0) == 0)
    def _():
        fill_bias(blocks_ref, seg_q_ref, seg_k_ref, valid_k_ref, bias_ref, rows)

    dk_ref[...] = jnp.zeros_like(dk_ref)
    dv_ref[...] = jnp.zeros_like(dv_ref)
    for side in range(2):
        b = blocks_ref[side]
        lo = first_block(b, rows)
        acc_ref[...] = jnp.zeros_like(acc_ref)
        for h in range(GROUP):
            center_ref[h : h + 1] = jnp.sum(
                o_ref[side, h].astype(F32) * do_ref[side, h].astype(F32), axis=0, keepdims=True
            )

        def body(kb, _):
            slot = slots_ref[kb]
            keys_t = k_ref[slot, 0]
            keys = keys_t.T
            values = v_ref[slot, 0].T
            bias = bias_ref[side, kb - lo]
            for h in range(GROUP):
                query_t = q_ref[side, h]
                grad_t = do_ref[side, h]
                s = dot(keys, query_t, ((1,), (0,))) + bias
                p = jnp.exp(s - lse_ref[side, 0, h : h + 1])
                dp = dot(values, grad_t, ((1,), (0,)))
                ds = (p * (dp - center_ref[h : h + 1])).astype(BF16)
                dv_ref[slot] += dot(grad_t, p.astype(BF16), ((1,), (1,)))
                dk_ref[slot] += dot(query_t, ds, ((1,), (1,)))
                acc_ref[h] += dot(keys_t, ds, ((1,), (0,)))
            return 0

        lax.fori_loop(lo, b + 1, body, 0)
        half = HEAD_DIM // 2
        cos, sin = cos_ref[side], sin_ref[side]
        for h in range(GROUP):
            a, b = acc_ref[h, :half] * 0.125, acc_ref[h, half:] * 0.125
            turned = jnp.concatenate([a * cos + b * sin, b * cos - a * sin], axis=0)
            dq_ref[side, h] = turned.astype(BF16)
    dkv_ref[:, 0, 0] = dk_ref[...].astype(BF16)
    dkv_ref[:, 1, 0] = dv_ref[...].astype(BF16)


def project(c, f, tokens_all, mine, other, cosine, sine, q_width):
    blocks, rows, width = tokens_all.shape
    _, nz, r, cols = mine.shape
    half = HEAD_DIM // 2
    kv_heads = 2 * KV_HEADS
    gains_at = q_width + kv_heads * HEAD_DIM

    def turned(flat_t, at, cos, sin):
        a, b = flat_t[at : at + half], flat_t[at + half : at + HEAD_DIM]
        return jnp.concatenate([a * cos - b * sin, a * sin + b * cos], axis=0)

    def kernel(
        at_ref, x_ref, mine_ref, other_ref, cos_ref, sin_ref,
        first_ref, q_ref, kv_ref, w_ref, gain_ref,
    ):
        @pl.when(pl.program_id(0) == 0)
        def _():
            for core in range(2):

                @pl.when(at_ref[1] % 2 == core)
                def _():
                    for z in range(nz):
                        step = (at_ref[1] // 2 - z + nz) % nz
                        for q in range(4):
                            for kk in range(2):
                                source = mine_ref if kk == core else other_ref
                                at = (2 * z + kk) * r
                                w_ref[at : at + r, q * cols : (q + 1) * cols] = source[
                                    q ^ at_ref[0], step
                                ]

            gain_ref[...] = w_ref[:, gains_at:].astype(F32).T[:8]

        x = x_ref[0].astype(F32)
        inverse = lax.rsqrt(jnp.mean(x * x, axis=-1, keepdims=True) + EPSILON)
        first = (x * inverse * gain_ref[0:1]).astype(BF16)
        first_ref[0] = first
        cos, sin = cos_ref[0], sin_ref[0]
        kv = dot(first, w_ref[:, q_width:gains_at], ((1,), (0,))).T
        for h in range(kv_heads):
            at = h * HEAD_DIM
            if h < KV_HEADS:
                kv_ref[0, h] = turned(kv, at, cos, sin).astype(BF16)
            else:
                kv_ref[0, h] = kv[at : at + HEAD_DIM].astype(BF16)

        @pl.when(pl.program_id(0) < 2)
        def _():
            q = dot(first, w_ref[:, :q_width], ((1,), (0,))).T
            for h in range(HEADS):
                turned_q = turned(q, h * HEAD_DIM, cos, sin).astype(BF16)
                q_ref[0, h] = (turned_q.astype(F32) * 0.125).astype(BF16)

    table = pl.BlockSpec((1, half, rows), lambda i, s: (i, 0, 0))
    piece = pl.BlockSpec(mine.shape, lambda i, s: (0, 0, 0, 0))
    return pl.pallas_call(
        kernel,
        grid_spec=pltpu.PrefetchScalarGridSpec(
            num_scalar_prefetch=1,
            grid=(blocks,),
            in_specs=[
                pl.BlockSpec((1, rows, width), lambda i, s: (i, 0, 0)),
                piece,
                piece,
                table,
                table,
            ],
            out_specs=[
                pl.BlockSpec((1, rows, width), lambda i, s: (i, 0, 0)),
                pl.BlockSpec(
                    (1, HEADS, HEAD_DIM, rows), lambda i, s: (jnp.minimum(i, 1), 0, 0, 0)
                ),
                pl.BlockSpec((1, kv_heads, HEAD_DIM, rows), lambda i, s: (i, 0, 0, 0)),
                pl.BlockSpec((2 * nz * r, 4 * cols), lambda i, s: (0, 0)),
                pl.BlockSpec((8, width), lambda i, s: (0, 0)),
            ],
        ),
        out_shape=[
            jax.ShapeDtypeStruct((blocks, rows, width), BF16),
            jax.ShapeDtypeStruct((2, HEADS, HEAD_DIM, rows), BF16),
            jax.ShapeDtypeStruct((blocks, kv_heads, HEAD_DIM, rows), BF16),
            jax.ShapeDtypeStruct((2 * nz * r, 4 * cols), BF16),
            jax.ShapeDtypeStruct((8, width), F32),
        ],
        compiler_params=pltpu.CompilerParams(vmem_limit_bytes=56 * 2**20),
        cost_estimate=pl.CostEstimate(
            flops=8_000_000_000, bytes_accessed=25_000_000, transcendentals=0
        ),
    )(jnp.stack([c, f]).astype(jnp.int32), tokens_all, mine, other, cosine, sine)


def kernel_specs(blocks, rows):
    q_spec = pl.BlockSpec((2, GROUP, HEAD_DIM, rows), lambda g, *_: (0, g, 0, 0))
    k_spec = pl.BlockSpec((blocks, 1, HEAD_DIM, rows), lambda g, *_: (0, g, 0, 0))
    v_spec = pl.BlockSpec((blocks, 1, HEAD_DIM, rows), lambda g, *_: (0, KV_HEADS + g, 0, 0))
    stat_spec = pl.BlockSpec((2, 1, GROUP, rows), lambda g, *_: (0, g, 0, 0))
    seg_specs = [
        pl.BlockSpec((2, 1, rows), lambda g, *_: (0, 0, 0)),
        pl.BlockSpec((blocks, rows, 1), lambda g, *_: (0, 0, 0)),
        pl.BlockSpec((blocks, rows, 1), lambda g, *_: (0, 0, 0)),
    ]
    return q_spec, k_spec, v_spec, stat_spec, seg_specs


def attention_forward(q_blocks, slots, seg_q, seg_k, valid_k, q_t, kv_t):
    blocks, _, _, rows = kv_t.shape
    q_spec, k_spec, v_spec, stat_spec, seg_specs = kernel_specs(blocks, rows)
    reach = (WINDOW + rows - 2) // rows + 1
    return pl.pallas_call(
        forward_kernel,
        grid_spec=pltpu.PrefetchScalarGridSpec(
            num_scalar_prefetch=2,
            grid=(KV_HEADS,),
            in_specs=seg_specs + [q_spec, k_spec, v_spec],
            out_specs=[q_spec, stat_spec],
            scratch_shapes=[
                pltpu.VMEM((2, reach, rows, rows), F32),
                pltpu.VMEM((GROUP, HEAD_DIM, rows), F32),
                pltpu.VMEM((GROUP, rows), F32),
                pltpu.VMEM((GROUP, rows), F32),
            ],
        ),
        out_shape=[
            jax.ShapeDtypeStruct(q_t.shape, BF16),
            jax.ShapeDtypeStruct((2, KV_HEADS, GROUP, rows), F32),
        ],
        compiler_params=pltpu.CompilerParams(vmem_limit_bytes=40 * 2**20),
        cost_estimate=pl.CostEstimate(
            flops=20_000_000_000, bytes_accessed=6_000_000, transcendentals=0
        ),
    )(q_blocks, slots, seg_q, seg_k, valid_k, q_t, kv_t, kv_t)


def attention_backward(q_blocks, slots, seg_q, seg_k, valid_k, cos, sin, q_t, kv_t, o_t, do_t, lse):
    blocks, _, _, rows = kv_t.shape
    q_spec, k_spec, v_spec, stat_spec, seg_specs = kernel_specs(blocks, rows)
    reach = (WINDOW + rows - 2) // rows + 1
    table = pl.BlockSpec((2, HEAD_DIM // 2, rows), lambda g, *_: (0, 0, 0))
    dkv_spec = pl.BlockSpec((blocks, 2, 1, HEAD_DIM, rows), lambda g, *_: (0, 0, g, 0, 0))
    return pl.pallas_call(
        backward_kernel,
        grid_spec=pltpu.PrefetchScalarGridSpec(
            num_scalar_prefetch=2,
            grid=(KV_HEADS,),
            in_specs=seg_specs
            + [table, table, q_spec, k_spec, v_spec, q_spec, q_spec, stat_spec],
            out_specs=[q_spec, dkv_spec],
            scratch_shapes=[
                pltpu.VMEM((2, reach, rows, rows), F32),
                pltpu.VMEM((GROUP, HEAD_DIM, rows), F32),
                pltpu.VMEM((GROUP, rows), F32),
                pltpu.VMEM((blocks, HEAD_DIM, rows), F32),
                pltpu.VMEM((blocks, HEAD_DIM, rows), F32),
            ],
        ),
        out_shape=[
            jax.ShapeDtypeStruct(q_t.shape, BF16),
            jax.ShapeDtypeStruct((blocks, 2, KV_HEADS, HEAD_DIM, rows), BF16),
        ],
        compiler_params=pltpu.CompilerParams(vmem_limit_bytes=48 * 2**20),
        cost_estimate=pl.CostEstimate(
            flops=40_000_000_000, bytes_accessed=16_000_000, transcendentals=0
        ),
    )(q_blocks, slots, seg_q, seg_k, valid_k, cos, sin, q_t, kv_t, kv_t, o_t, do_t, lse)


def norm_forward(value_rows, gain):
    inverse = lax.rsqrt(jnp.mean(value_rows * value_rows, axis=-1, keepdims=True) + EPSILON)
    normed = value_rows * inverse
    return (normed * gain, normed, inverse)


def norm_backward(upstream, gain, normed, inverse):
    scaled = upstream * gain
    grad_in = inverse * (scaled - normed * jnp.mean(scaled * normed, axis=-1, keepdims=True))
    return (grad_in, jnp.sum(upstream * normed, axis=0))


def ein(spec, left, right):
    return jnp.einsum(spec, left, right, preferred_element_type=F32)


def turn(v, cosine, sine):
    half = HEAD_DIM // 2
    a, b = v[:, :, :half], v[:, :, half:]
    return jnp.concatenate([a * cosine - b * sine, a * sine + b * cosine], axis=2)


def per_device(
    tokens, cotangent, segments, valid, norm_one, w_query, w_key, w_value, w_out,
    norm_two, w_gate, w_up, w_down,
):
    c = lax.axis_index("ctx")
    n = lax.axis_size("fsdp")
    f = lax.axis_index("fsdp")
    row_count = tokens.shape[1]
    rows = row_count // 2
    width = tokens.shape[2]
    blocks = 8
    q_width, kv_width = w_query.shape[1], w_key.shape[1]
    ff = w_gate.shape[1]
    r = w_query.shape[0]
    c_ref = c.reshape(1).astype(jnp.int32)

    q_blocks = jnp.stack([c, blocks - 1 - c]).astype(jnp.int32)
    seg_blocks = segments[0].reshape(blocks, rows)
    valid_blocks = valid[0].reshape(blocks, rows)
    seg_q = jnp.stack([take(seg_blocks, q_blocks[0], 0), take(seg_blocks, q_blocks[1], 0)])
    live = jnp.stack([take(valid_blocks, q_blocks[0], 0), take(valid_blocks, q_blocks[1], 0)])
    seg_q = seg_q[:, None, :]
    seg_k = seg_blocks[:, :, None]
    valid_k = valid_blocks[:, :, None]
    owners = c ^ jnp.arange(4, dtype=jnp.int32)
    block_of = jnp.stack([owners, blocks - 1 - owners], axis=1)
    every = jnp.arange(blocks, dtype=jnp.int32)
    side = (every >= 4).astype(jnp.int32)
    slots = (c ^ jnp.where(every < 4, every, blocks - 1 - every)) * 2 + side
    slots = slots.astype(jnp.int32)
    places = block_of[:, :, None] * rows + jnp.arange(rows, dtype=jnp.int32)
    half = HEAD_DIM // 2
    freqs = jnp.exp(jnp.arange(half, dtype=F32) * (-math.log(ROPE_BASE) / half))
    angles = places.astype(F32).reshape(8, 1, rows) * freqs[None, :, None]
    cosine, sine = jnp.cos(angles), jnp.sin(angles)

    tokens_own = tokens[0].reshape(2, rows, width)
    tokens_x, tokens_y = swap_x(tokens_own), swap_y(tokens_own)
    gains = jnp.stack([norm_one, norm_two], axis=1)
    gains = jnp.concatenate([gains, jnp.zeros((r, 126), BF16)], axis=1)
    qkv_shard = jnp.concatenate([w_query, w_key, w_value, gains], axis=1)
    c4 = qkv_shard.shape[1] // 4
    qkv_z = z_fetch(lax.dynamic_slice_in_dim(qkv_shard, c * c4, c4, 1))
    out_w = lax.all_gather(w_out, "fsdp", axis=0, tiled=True)
    qkv_z, tokens_x, tokens_y = sync(qkv_z, tokens_x, tokens_y)
    qkv_x, qkv_y = swap_x(qkv_z), swap_y(qkv_z)
    gu_shard = after(pick_columns(c_ref, w_gate, w_up, n), qkv_z)
    gu_w = lax.all_gather(gu_shard, "fsdp", axis=0, tiled=True)
    d4 = w_down.shape[0] // 4
    down_shard = after(lax.dynamic_slice_in_dim(w_down, c * d4, d4, 0), gu_shard)
    down_w = lax.all_gather(down_shard, "fsdp", axis=0, tiled=True)
    cut = ff // 4
    qkv_x, qkv_y, tokens_x, tokens_y = sync(qkv_x, qkv_y, tokens_x, tokens_y)
    zh = qkv_z.shape[0] // 2
    qkv_d = jnp.concatenate([swap_y(qkv_x[:zh]), swap_x(qkv_y[zh:])])
    tokens_d = jnp.concatenate([swap_y(tokens_x[:1]), swap_x(tokens_y[1:])])
    qkv_mine = jnp.stack([qkv_z, qkv_x, qkv_y, qkv_d])
    qkv_other = core_swap(qkv_mine)
    tokens_all = jnp.stack([tokens_own, tokens_x, tokens_y, tokens_d])
    dy_own = cotangent[0].reshape(2, rows, width)
    dy_pieces = ctx_fetch_direct(after(dy_own, qkv_mine, tokens_d))

    first_all, q_t, kv_all, qkv_w, gain_rows = project(
        c, f, tokens_all.reshape(8, rows, width), qkv_mine, qkv_other, cosine, sine, q_width
    )
    gain_one, gain_two = gain_rows[0], gain_rows[1]
    first_all = first_all.reshape(4, 2, rows, width)
    qkv_w = qkv_w[:, : q_width + 2 * kv_width]
    inputs = tokens[0].astype(F32)
    _, unit_one, inverse_one = norm_forward(inputs, gain_one)
    o_t, lse = attention_forward(q_blocks, slots, seg_q, seg_k, valid_k, q_t, kv_all)
    o_t, out_w, dy_pieces, gu_w, down_w = sync(o_t, out_w, dy_pieces, gu_w, down_w)
    dy_all = jnp.stack(dy_pieces).reshape(-1, width)
    attended_t = o_t.reshape(2, width, rows)
    branch_attn = ein("bfr,fo->bro", attended_t, out_w).reshape(row_count, width)
    middle = inputs + branch_attn

    normed_two, unit_two, inverse_two = norm_forward(middle, gain_two)
    second_in = normed_two.astype(BF16)
    x_own = second_in.reshape(2, rows, width)
    x_x, x_y = swap_x(x_own), swap_y(x_own)
    d_hidden = ein("ro,fo->rf", dy_all, down_w)

    def gated(x, d_hidden):
        gu = ein("bri,if->brf", x, gu_w).reshape(-1, 2 * cut)
        gate_pre, up_pre = gu[:, :cut], gu[:, cut:]
        sig = jax.nn.sigmoid(gate_pre)
        swish = gate_pre * sig
        slope = sig * (1.0 + gate_pre * (1.0 - sig))
        d_gu = [(d_hidden * up_pre * slope).astype(BF16), (d_hidden * swish).astype(BF16)]
        return (swish * up_pre).astype(BF16), jnp.concatenate(d_gu, axis=1)

    def back(d_gu):
        return ein("rf,if->ri", d_gu, gu_w).astype(BF16).reshape(-1, 2, rows, width)

    hidden_0, d_gu_0 = gated(x_own, d_hidden[:row_count])
    x_x, x_y, hidden_0, d_gu_0 = lax.optimization_barrier((x_x, x_y, hidden_0, d_gu_0))
    x_d = jnp.concatenate([swap_y(x_x[:1]), swap_x(x_y[1:])])
    x_xy = jnp.concatenate([x_x, x_y])
    hidden_1, d_gu_1 = gated(x_xy, d_hidden[row_count : 3 * row_count])
    parts_1 = back(d_gu_1)
    x_d, parts_1 = lax.optimization_barrier((x_d, parts_1))
    hidden_2, d_gu_2 = gated(x_d, d_hidden[3 * row_count :])
    parts_2 = back(d_gu_2)
    d_gu_0 = after(d_gu_0, parts_2)
    parts_0 = back(d_gu_0)
    parts = [parts_0[0], parts_1[0], parts_1[1], parts_2[0]]
    got = scatter_first(parts)
    x_all = jnp.concatenate([x_own, x_xy, x_d]).reshape(-1, width)
    d_gu = jnp.concatenate([d_gu_0, d_gu_1, d_gu_2])
    hidden = jnp.concatenate([hidden_0, hidden_1, hidden_2])
    grad_gu = ein("ri,rf->if", x_all, d_gu).astype(BF16)
    got_low, got_high, grad_gu = lax.optimization_barrier((*got, grad_gu))
    d_second = scatter_last(*scatter_pass(parts, (got_low, got_high))).reshape(row_count, width)
    grad_d = ein("rf,ro->fo", after(hidden, grad_gu), dy_all).astype(BF16)
    ffn_parts = ein("rf,fo->ro", after(hidden, grad_d), down_w).astype(BF16)
    d_second, ffn_parts = lax.optimization_barrier((d_second, ffn_parts))
    ffn_parts = ffn_parts.reshape(4, 2, rows, width)
    ffn_parts = [ffn_parts[i] for i in range(4)]
    ffn_got = scatter_first(ffn_parts)
    own_gu = lax.psum_scatter(grad_gu, "fsdp", scatter_dimension=0, tiled=True)
    own_down = lax.psum_scatter(grad_d, "fsdp", scatter_dimension=0, tiled=True)

    k = f % 2
    nz = n // 2
    r4 = r // 4
    grad_output = cotangent[0].astype(F32)
    grad_mid_norm, grad_gain_two = norm_backward(d_second, gain_two, unit_two, inverse_two)
    grad_middle = grad_output + grad_mid_norm
    d_branch = grad_middle.astype(BF16).reshape(2, rows, width)
    do_t = ein("fo,bro->bfr", out_w, d_branch).astype(BF16).reshape(2, HEADS, HEAD_DIM, rows)
    whole_out = ein("bfr,bro->fo", attended_t, d_branch).astype(BF16).reshape(n, 4, r4, width)
    out_parts = [take(whole_out, c ^ i, 1) for i in range(4)]
    out_got = scatter_first(out_parts)
    d_q, dkv = attention_backward(
        q_blocks, slots, seg_q, seg_k, valid_k, cosine[:2], sine[:2], q_t, kv_all, o_t, do_t, lse
    )
    d_q, dkv, ffn_got, out_got = sync(d_q, dkv, ffn_got, out_got)
    dkv = dkv.reshape(4, 2, 2 * KV_HEADS, HEAD_DIM, rows)
    dkv = [dkv[i] for i in range(4)]
    dkv_got = scatter_first(dkv)
    q4, kv4 = q_width // 4, kv_width // 2

    def quarter(v, size, i):
        return lax.dynamic_slice_in_dim(v, (c ^ i) * size, size, 1)

    d_q = d_q.reshape(2, q_width, rows)
    dq_parts = [quarter(d_q, q4, i) for i in range(4)]
    out_sums = scatter_pass(out_parts, out_got)
    dkv_got, dq_parts, out_sums = sync(dkv_got, dq_parts, out_sums)
    dkv_own = scatter_last(*scatter_pass(dkv, dkv_got))
    dq_got = exchange_first(dq_parts)
    d_k = turn(dkv_own[:, :KV_HEADS], cosine[:2, None], -sine[:2, None]).astype(BF16)
    d_kv = jnp.concatenate([d_k, dkv_own[:, KV_HEADS:].astype(BF16)], axis=1)
    d_kv = d_kv.reshape(2, 2 * kv_width, rows)
    dkv_parts = [quarter(d_kv, kv4, i) for i in range(4)]
    dkv_parts, out_sums = sync(dkv_parts, out_sums)
    dkv_got = exchange_first(dkv_parts)
    own_out = scatter_last(*out_sums).astype(BF16)
    dq_got, dkv_got = sync(dq_got, dkv_got)
    dq_all = jnp.stack(exchange_second(dq_parts, *dq_got))
    dkv_all = jnp.stack(exchange_second(dkv_parts, *dkv_got))
    grad_q = ein("gbri,gbfr->if", first_all, dq_all).astype(BF16)
    grad_kv = ein("gbri,gbfr->if", first_all, dkv_all).astype(BF16)
    grad_qkv = jnp.concatenate([grad_q, grad_kv], axis=1).reshape(nz, 2, r, q4 + kv4)
    own_out = own_out.reshape(nz, 2, r4, width)
    grad_qkv, own_out, own_gu = sync(grad_qkv, own_out, own_gu)

    def pair_sum(v):
        got = core_swap(take(v, k ^ 1, 1))
        return (take(v, k, 1).astype(F32) + got.astype(F32)).astype(BF16)

    pair_qkv, pair_out = sync(pair_sum(grad_qkv), pair_sum(own_out))
    own_qkv = z_scatter(pair_qkv).astype(BF16)
    own_out = z_scatter(pair_out).astype(BF16)

    d_q, d_kv, ffn_got, own_gu, _ = sync(d_q, d_kv, ffn_got, own_gu, pair_qkv)
    branch_ffn = scatter_last(*scatter_pass(ffn_parts, ffn_got)).reshape(row_count, width)
    result = middle + branch_ffn
    gu_x, gu_y = swap_x(own_gu), swap_y(own_gu)
    d_first = ein("bfr,if->bri", d_q, qkv_w[:, :q_width]) + ein(
        "bfr,if->bri", d_kv, qkv_w[:, q_width:]
    )
    grad_in_norm, grad_gain_one = norm_backward(
        d_first.reshape(row_count, width), gain_one, unit_one, inverse_one
    )
    grad_inputs = grad_middle + grad_in_norm
    own_qkv, own_out, gu_x, gu_y, own_down = sync(own_qkv, own_out, gu_x, gu_y, own_down)
    hr = gu_x.shape[0] // 2
    gu_d = jnp.concatenate([swap_y(gu_x[:hr]), swap_x(gu_y[hr:])])
    grad_gate_w, grad_up_w = unpick_columns(c_ref, [own_gu, gu_x, gu_y, gu_d], n)
    grad_down_w = ctx_gather(own_down, 0).reshape(4 * d4, width).astype(F32)
    grad_out_w = ctx_gather(own_out, 0).reshape(r, width).astype(F32)
    grad_qkv = ctx_gather(own_qkv, 1).astype(F32)
    grad_q = grad_qkv[:, :, :q4].reshape(r, q_width)
    grad_kv = grad_qkv[:, :, q4:].reshape(r, 2 * kv_width)

    live_rows = live.reshape(row_count, 1).astype(F32)
    squares = jnp.stack(
        [
            jnp.sum(live_rows * member * member)
            for member in (result, grad_inputs, branch_attn, branch_ffn, middle)
        ]
        + [jnp.sum(live_rows)]
    )
    small = small_sum(jnp.concatenate([grad_gain_one, grad_gain_two, squares]))
    gain_sums = lax.dynamic_slice_in_dim(small[: 2 * width].reshape(2, width), f * r, r, 1)
    squares = small[2 * width :]
    spreads = jnp.sqrt(squares[:5] / (squares[5] * width))
    return (
        result[None].astype(BF16),
        grad_inputs[None].astype(BF16),
        gain_sums[0],
        grad_q,
        grad_kv[:, :kv_width],
        grad_kv[:, kv_width:],
        grad_out_w,
        gain_sums[1],
        grad_gate_w,
        grad_up_w,
        grad_down_w,
        spreads,
    )


def solution(mesh):
    rows, shard, vector = P("fsdp", "ctx", None), P("fsdp", None), P("fsdp")
    return jax.shard_map(
        per_device,
        mesh=mesh,
        in_specs=(
            rows, rows, shard, shard, vector, shard, shard, shard, shard, vector,
            shard, shard, shard,
        ),
        out_specs=(
            rows, rows, vector, shard, shard, shard, shard, vector, shard, shard, shard, P(),
        ),
        check_vma=False,
    )
```

time: 880 us -> 585 us (0.66)
  waiting for transfers between devices: 260 us -> 116 us
  starting transfers between devices: 215 us -> 108 us
  blocking collectives: 41.1 us -> 0 us
  local copies, waits for them, and re-layouts: 103 us -> 75.8 us
  Pallas kernels: 86.1 us -> 111 us
  between operations: 4.55 us -> 16.5 us
    ppermute x38 -> x28, waiting for transfers between devices: 127 us -> 45.5 us  [swap_x(): return lax.ppermute(v, 'ctx', [(i, i ^ 1) for i in range(4)])]
    ppermute x28 -> x7, starting transfers between devices: 68.4 us -> 8.26 us  [the longest x3 4.61 us: z_fetch(): lax.ppermute(piece, 'fsdp', [(i, (i + 2 * d) % n) for i in range(n)])]
    psum x1 -> x0, blocking collectives: 41.1 us -> none  [per_device(): lax.psum(jnp.concatenate([grad_gain_one, grad_gain_two, squares]), ('ctx'...]
    ppermute x28 -> x7, waiting for transfers between devices: 46 us -> 11.1 us  [the longest x3 8.12 us: z_fetch(): lax.ppermute(piece, 'fsdp', [(i, (i + 2 * d) % n) for i in range(n)])]
    ppermute x38 -> x28, starting transfers between devices: 71.3 us -> 47.5 us  [swap_y(): return lax.ppermute(v, 'ctx', [(i, i ^ 2) for i in range(4)])]
    pallas_call x0 -> x3, Pallas kernels: none -> 23.6 us  [the longest x1 17.5 us: project(): pl.pallas_call(kernel, grid_spec=pltpu.PrefetchScalarGridSpec(num_scalar_...]
    ppermute x38 -> x28, waiting for transfers between devices: 65.5 us -> 42.2 us  [swap_y(): return lax.ppermute(v, 'ctx', [(i, i ^ 2) for i in range(4)])]
    ppermute x12 -> x6, starting transfers between devices: 20.7 us -> 7.91 us  [z_scatter(): got = lax.ppermute(sent, 'fsdp', [(i, (i + 2 * d) % n) for i in range(n)])]
  transfers between devices with their start and end apart: 128 -> 77, of which waited for: 51 -> 29; matrix products, arithmetic and copies ran while one was open for 24% -> 32% of each run, Pallas kernels for 10% -> 19%
where the time goes in v2:
time: 585 us; the launch traced here: 578 us
  waiting for transfers between devices  116 us (20%)
  Pallas kernels  111 us (19%)
  starting transfers between devices  108 us (18%)
  matrix products  85.4 us (15%)
  local copies, waits for them, and re-layouts  75.8 us (13%)
  other arithmetic  66.5 us (11%)
  between operations  16.5 us (3%)
    dot_general x17, matrix products, ein(): return jnp.einsum(spec, left, right, preferred_element_type=F32)  85.4 us
    ppermute x28, starting transfers between devices, swap_y(): return lax.ppermute(v, 'ctx', [(i, i ^ 2) for i in range(4)])  47.5 us
    ppermute x28, waiting for transfers between devices, swap_x(): return lax.ppermute(v, 'ctx', [(i, i ^ 1) for i in range(4)])  45.5 us
    pallas_call x1, Pallas kernels, attention_backward(): pl.pallas_call(backward_kernel, grid_spec=pltpu.PrefetchScalarGridSpec(nu...  44.4 us
    ppermute x28, starting transfers between devices, swap_x(): return lax.ppermute(v, 'ctx', [(i, i ^ 1) for i in range(4)])  43.1 us
    pallas_call x1, Pallas kernels, attention_forward(): pl.pallas_call(forward_kernel, grid_spec=pltpu.PrefetchScalarGridSpec(num...  42.7 us
    ppermute x28, waiting for transfers between devices, swap_y(): return lax.ppermute(v, 'ctx', [(i, i ^ 2) for i in range(4)])  42.2 us
    pallas_call x1, Pallas kernels, project(): pl.pallas_call(kernel, grid_spec=pltpu.PrefetchScalarGridSpec(num_scalar_...  17.5 us
  transfers between devices with their start and end apart: 77, of which 29 were waited for; matrix products, arithmetic and copies ran while one was open for 32% of the time, Pallas kernels for 19%

profile of v2, /device:TPU:0, one launch (start us, length us, event | category | flops | bytes accessed | tf_op | source)
XLA Modules:
  0.0 578.4 jit_solution(12314169366016237937)
XLA Ops:
  26.0 8.1 %collective-permute-done.1 = bf16[160,512]{1,0:T(8,128)(2,1)} collective-permute-done((bf16[160,512]{1,0:T(8,128)(2,1)}, bf16[160,512]{1,0:T(8,128)(2,1)}, u32[]{:S(2)}, u32[]{:S(2)}) %collective-permute-start.1) | collective-permute-done | bytes 163872 | tf_op jit(solution)/shard_map/ppermute | solution.py:65
  40.0 13.2 %collective-permute-done.5 = bf16[4,160,512]{2,1,0:T(8,128)(2,1)S(1)} collective-permute-done((bf16[4,160,512]{2,1,0:T(8,128)(2,1)S(1)}, bf16[4,160,512]{2,1,0:T(8,128)(2,1)S(1)}, u32[]{:S(2)}, u32[]{:S(2)}) %collective-permute-start.5) | collective-permute-done | bytes 655392 | tf_op jit(solution)/shard_map/ppermute | solution.py:29
  77.6 10.3 %collective-permute-done.7 = bf16[1,216,1280]{2,1,0:T(8,128)(2,1)S(1)} collective-permute-done((bf16[1,216,1280]{2,1,0:T(8,128)(2,1)S(1)}, bf16[1,216,1280]{2,1,0:T(8,128)(2,1)S(1)}, u32[]{:S(2)}, u32[]{:S(2)}) %collective-permute-start.7) | collective-permute-done | bytes 552992 | tf_op jit(solution)/shard_map/ppermute | solution.py:33
  96.5 17.5 %shard_map.220 = (bf16[8,216,1280]{2,1,0:T(8,128)(2,1)}, bf16[2,20,64,216]{3,2,1,0:T(8,128)(2,1)}, bf16[8,10,64,216]{3,2,1,0:T(8,128)(2,1)}, bf16[1280,2048]{1,0:T(8,128)(2,1)}, f32[8,1280]{1,0:T(8,128)}) custom-call(s32[2]{0:T(128)} %pad_add_fusion.2.at_ref, bf16[8,216,1280]{2,1,0:T(8,128)(2,1)} %bitcast.355, ...), custom_call_target="tpu_custom_call" | custom-call | flops 8000000000 | bytes 25000000 | tf_op jit(solution)/shard_map/pallas_call | solution.py:408
  118.9 42.7 %shard_map.221 = (bf16[2,20,64,216]{3,2,1,0:T(8,128)(2,1)S(1)}, f32[2,5,4,216]{3,2,1,0:T(4,128)S(1)}) custom-call(s32[2]{0:T(128)S(1)} %pad_add_fusion.1.blocks_ref, s32[8]{0:T(128)S(1)} %fusion.110.slots_ref, s32[2,1,216]{2,1,0:T(1,128)S(1)} %broadcast_in_dim.62.seg_q_ref, s32[8,216,1]{2,1,0:T(8,128)S(1)} %broadcast_in_dim_reshape_squeeze.8.seg_k_ref, ...), custom_call_target="tpu_custom_call" | custom-call | flops 20000000000 | bytes 6000000 | tf_op jit(solution)/shard_map/pallas_call | solution.py:461
  163.1 6.1 %multiply_reduce_fusion.4 = (f32[432]{0:T(512)S(1)}, f32[432,1280]{1,0:T(8,128)S(1)}, f32[432]{0:T(512)}, f32[432,1280]{1,0:T(8,128)}) fusion(bf16[1,432,1280]{2,1,0:T(8,128)(2,1)} %param.13, bf16[432,1280]{1,0:T(8,128)(2,1)} %bitcast.386, bf16[1280,1280]{1,0:T(8,128)(2,1)} %all-gather.4.cloned.1.call-done), kind=kOutput, calls=%fused_computation.82 | convolution fusion | flops 1418894592 | bytes 9915776 | tf_op jit(solution)/shard_map/bfr,fo->bro/dot_general | solution.py:532
  170.8 6.6 %collective-permute-start.15 = (bf16[2,216,1280]{2,1,0:T(8,128)(2,1)S(1)}, bf16[2,216,1280]{2,1,0:T(8,128)(2,1)S(1)}, u32[]{:S(2)}, u32[]{:S(2)}) collective-permute-start(bf16[2,216,1280]{2,1,0:T(8,128)(2,1)S(1)} %bitcast.356), channel_id=1, source_target_pairs={{0,8},{8,0},{16,24},{24,16},{1,9},{9,1},{17,25},{25,17},{2,10},{10... | collective-permute-start | bytes 3317768 | tf_op jit(solution)/shard_map/ppermute | solution.py:29
  177.4 6.9 %collective-permute-start.16 = (bf16[2,216,1280]{2,1,0:T(8,128)(2,1)S(1)}, bf16[2,216,1280]{2,1,0:T(8,128)(2,1)S(1)}, u32[]{:S(2)}, u32[]{:S(2)}) collective-permute-start(bf16[2,216,1280]{2,1,0:T(8,128)(2,1)S(1)} %bitcast.357), channel_id=1, source_target_pairs={{0,16},{8,24},{16,0},{24,8},{1,17},{9,25},{17,1},{25,9},{2,18},{10... | collective-permute-start | bytes 3317768 | tf_op jit(solution)/shard_map/ppermute | solution.py:33
  187.0 4.9 fusion.129
  195.2 5.2 collective-permute-done.15
  200.5 6.9 %collective-permute-done.16 = bf16[2,216,1280]{2,1,0:T(8,128)(2,1)S(1)} collective-permute-done((bf16[2,216,1280]{2,1,0:T(8,128)(2,1)S(1)}, bf16[2,216,1280]{2,1,0:T(8,128)(2,1)S(1)}, u32[]{:S(2)}, u32[]{:S(2)}) %collective-permute-start.16) | collective-permute-done | bytes 1105952 | tf_op jit(solution)/shard_map/ppermute | solution.py:33
  216.2 4.7 convolution_convert_fusion.3
  242.2 13.8 %convolution_convert_fusion.1 = bf16[1280,1792]{1,0:T(8,128)(2,1)} fusion(bf16[1728,1280]{1,0:T(8,128)(2,1)S(1)} %bitcast.354, bf16[432,896]{1,0:T(8,128)(2,1)} %copy-done.55, bf16[432,896]{1,0:T(8,128)(2,1)} %copy-done.54, bf16[864,896]{1,0:T(8,128)(2,1)S(1)} %copy-done.45, bf16[864,896]{1,0:T(8,128)(2,1)S(1)} %copy-done.43, bf16[432,1792]{1,0:T(8,128)(2,1)} %copy-done.46), kind=kOutput, calls=%fused_computation.3 | convolution fusion | flops 7960494080 | bytes 15204352 | tf_op jit(solution)/shard_map/ri,rf->if/dot_general | solution.py:532
  268.3 9.0 %convolution_convert_fusion.2 = bf16[896,1280]{1,0:T(8,128)(2,1)} fusion(bf16[1728,896]{1,0:T(8,128)(2,1)} %pad_maximum_fusion.3, bf16[1728,1280]{1,0:T(8,128)(2,1)} %bitcast.353), kind=kOutput, calls=%fused_computation.24 | convolution fusion | flops 3964764160 | bytes 9814016 | tf_op jit(solution)/shard_map/rf,ro->fo/dot_general | solution.py:532
  277.2 9.5 %convolution_convert_fusion = bf16[1728,1280]{1,0:T(8,128)(2,1)} fusion(bf16[1728,896]{1,0:T(8,128)(2,1)} %pad_maximum_fusion.3, bf16[896,1280]{1,0:T(8,128)(2,1)} %all-gather.8.cloned.1.call-done), kind=kOutput, calls=%fused_computation.2 | convolution fusion | flops 3965829120 | bytes 9814016 | tf_op jit(solution)/shard_map/rf,fo->ro/dot_general | solution.py:532
  310.1 44.4 %shard_map.223 = (bf16[2,20,64,216]{3,2,1,0:T(8,128)(2,1)S(1)}, bf16[8,2,5,64,216]{4,3,2,1,0:T(8,128)(2,1)}) custom-call(s32[2]{0:T(128)S(1)} %pad_add_fusion.1.blocks_ref, s32[8]{0:T(128)S(1)} %fusion.110.slots_ref, s32[2,1,216]{2,1,0:T(1,128)S(1)} %broadcast_in_dim.62.seg_q_ref, s32[8,216,1]{2,1,0:T(8,128)S(1)} %broadcast_in_dim_reshape_squeeze.8.seg_k_ref, ...), custom_call_target="tpu_custom_call" | custom-call | flops 40000000000 | bytes 16000000 | tf_op jit(solution)/shard_map/pallas_call | solution.py:492
  357.6 7.2 %collective-permute-start.27 = (bf16[2,10,64,216]{3,2,1,0:T(8,128)(2,1)S(1)}, bf16[2,10,64,216]{3,2,1,0:T(8,128)(2,1)S(1)}, u32[]{:S(2)}, u32[]{:S(2)}) collective-permute-start(bf16[2,10,64,216]{3,2,1,0:T(8,128)(2,1)S(1)} %pad_maximum_fusion.19), channel_id=1, source_target_pairs={{0,8},{8,0},{16,24},{24,16},{1,9},{9,1},{17,25},{25,17},{2,10},{10... | collective-permute-start | bytes 1658888 | tf_op jit(solution)/shard_map/ppermute | solution.py:29
  364.9 6.6 %collective-permute-start.28 = (bf16[2,10,64,216]{3,2,1,0:T(8,128)(2,1)S(1)}, bf16[2,10,64,216]{3,2,1,0:T(8,128)(2,1)S(1)}, u32[]{:S(2)}, u32[]{:S(2)}) collective-permute-start(bf16[2,10,64,216]{3,2,1,0:T(8,128)(2,1)S(1)} %pad_maximum_fusion.20), channel_id=1, source_target_pairs={{0,16},{8,24},{16,0},{24,8},{1,17},{9,25},{17,1},{25,9},{2,18},{10... | collective-permute-start | bytes 1658888 | tf_op jit(solution)/shard_map/ppermute | solution.py:33
  373.9 8.9 %collective-permute-done.28 = bf16[2,10,64,216]{3,2,1,0:T(8,128)(2,1)S(1)} collective-permute-done((bf16[2,10,64,216]{3,2,1,0:T(8,128)(2,1)S(1)}, bf16[2,10,64,216]{3,2,1,0:T(8,128)(2,1)S(1)}, u32[]{:S(2)}, u32[]{:S(2)}) %collective-permute-start.28) | collective-permute-done | bytes 552992 | tf_op jit(solution)/shard_map/ppermute | solution.py:33
  450.2 5.6 multiply_reduce_fusion.1
  463.8 4.9 collective-permute-done.54
  471.9 10.3 %collective-permute-done.51 = bf16[160,480]{1,0:T(8,128)(2,1)S(1)} collective-permute-done((bf16[160,480]{1,0:T(8,128)(2,1)S(1)}, bf16[160,480]{1,0:T(8,128)(2,1)S(1)}, u32[]{:S(2)}, u32[]{:S(2)}) %collective-permute-start.51) | collective-permute-done | bytes 153632 | tf_op jit(solution)/shard_map/ppermute | solution.py:81
  497.6 9.6 %collective-permute-done.62 = bf16[40,1280]{1,0:T(8,128)(2,1)S(1)} collective-permute-done((bf16[40,1280]{1,0:T(8,128)(2,1)S(1)}, bf16[40,1280]{1,0:T(8,128)(2,1)S(1)}, u32[]{:S(2)}, u32[]{:S(2)}) %collective-permute-start.62) | collective-permute-done | bytes 102432 | tf_op jit(solution)/shard_map/ppermute | solution.py:29
  541.0 5.1 fusion.52
  (482 shorter events, 294.2 us)
Async XLA Ops:
  7.2 154.4 %all-gather.8.cloned.1.call-start = ((), (), s32[]{:S(2)}) async-start(), calls=%async_computation.4 | async-start | bytes 2580480 | tf_op jit(solution)/shard_map/all_gather | solution.py:591
  7.2 27.9 %collective-permute-start.3 = (bf16[2,216,1280]{2,1,0:T(8,128)(2,1)}, bf16[2,216,1280]{2,1,0:T(8,128)(2,1)S(1)}, u32[]{:S(2)}, u32[]{:S(2)}) collective-permute-start(bf16[2,216,1280]{2,1,0:T(8,128)(2,1)} %bitcast.359), channel_id=1, source_target_pairs={{0,8},{8,0},{16,24},{24,16},{1,9},{9,1},{17,25},{25,17},{2,10},{10... | collective-permute-start | bytes 3317768 | tf_op jit(solution)/shard_map/ppermute | solution.py:29
  36.3 125.3 %all-gather.4.cloned.1.call-start = ((), (), s32[]{:S(2)}) async-start(), calls=%async_computation.2 | async-start | bytes 3686400 | tf_op jit(solution)/shard_map/all_gather | solution.py:584
  37.1 124.6 %all-gather.6.cloned.1.call-start = ((), (), s32[]{:S(2)}) async-start(), calls=%async_computation.3 | async-start | bytes 5160960 | tf_op jit(solution)/shard_map/all_gather | solution.py:588
  37.8 397.0 %reduce-scatter.3.cloned.1.call-start = ((), (), s32[]{:S(2)}) async-start(), calls=%async_computation.5 | async-start | bytes 5160960 | tf_op jit(solution)/shard_map/reduce_scatter | solution.py:661
  68.1 28.4 %collective-permute-start.11 = (bf16[4,4,160,512]{3,2,1,0:T(8,128)(2,1)}, bf16[4,4,160,512]{3,2,1,0:T(8,128)(2,1)}, u32[]{:S(2)}, u32[]{:S(2)}) collective-permute-start(bf16[4,4,160,512]{3,2,1,0:T(8,128)(2,1)} %pad_maximum_fusion.4.mine_ref), channel_id=1, source_target_pairs={{0,1},{1,0},{2,3},{3,2},{4,5},{5,4},{6,7},{7,6},{8,9},{9,8},{10,11... | collective-permute-start | bytes 7864328 | tf_op jit(solution)/shard_map/ppermute | solution.py:25
  90.5 71.1 %collective-permute-start.12 = (bf16[2,216,1280]{2,1,0:T(8,128)(2,1)S(1)}, bf16[2,216,1280]{2,1,0:T(8,128)(2,1)}, u32[]{:S(2)}, u32[]{:S(2)}) collective-permute-start(bf16[2,216,1280]{2,1,0:T(8,128)(2,1)S(1)} %bitcast.343), channel_id=1, source_target_pairs={{0,8},{8,0},{16,24},{24,16},{1,9},{9,1},{17,25},{25,17},{2,10},{10... | collective-permute-start | bytes 3317768 | tf_op jit(solution)/shard_map/ppermute | solution.py:29
  91.1 70.5 %collective-permute-start.13 = (bf16[2,216,1280]{2,1,0:T(8,128)(2,1)S(1)}, bf16[2,216,1280]{2,1,0:T(8,128)(2,1)}, u32[]{:S(2)}, u32[]{:S(2)}) collective-permute-start(bf16[2,216,1280]{2,1,0:T(8,128)(2,1)S(1)} %bitcast.344), channel_id=1, source_target_pairs={{0,16},{8,24},{16,0},{24,8},{1,17},{9,25},{17,1},{25,9},{2,18},{10... | collective-permute-start | bytes 3317768 | tf_op jit(solution)/shard_map/ppermute | solution.py:33
  92.2 69.4 %collective-permute-start.14 = (bf16[2,216,1280]{2,1,0:T(8,128)(2,1)S(1)}, bf16[2,216,1280]{2,1,0:T(8,128)(2,1)}, u32[]{:S(2)}, u32[]{:S(2)}) collective-permute-start(bf16[2,216,1280]{2,1,0:T(8,128)(2,1)S(1)} %bitcast.345), channel_id=1, source_target_pairs={{0,24},{8,16},{16,8},{24,0},{1,25},{9,17},{17,9},{25,1},{2,26},{10... | collective-permute-start | bytes 3317768 | tf_op jit(solution)/shard_map/ppermute | solution.py:103
  170.8 29.6 %collective-permute-start.15 = (bf16[2,216,1280]{2,1,0:T(8,128)(2,1)S(1)}, bf16[2,216,1280]{2,1,0:T(8,128)(2,1)S(1)}, u32[]{:S(2)}, u32[]{:S(2)}) collective-permute-start(bf16[2,216,1280]{2,1,0:T(8,128)(2,1)S(1)} %bitcast.356), channel_id=1, source_target_pairs={{0,8},{8,0},{16,24},{24,16},{1,9},{9,1},{17,25},{25,17},{2,10},{10... | collective-permute-start | bytes 3317768 | tf_op jit(solution)/shard_map/ppermute | solution.py:29
  177.4 29.9 %collective-permute-start.16 = (bf16[2,216,1280]{2,1,0:T(8,128)(2,1)S(1)}, bf16[2,216,1280]{2,1,0:T(8,128)(2,1)S(1)}, u32[]{:S(2)}, u32[]{:S(2)}) collective-permute-start(bf16[2,216,1280]{2,1,0:T(8,128)(2,1)S(1)} %bitcast.357), channel_id=1, source_target_pairs={{0,16},{8,24},{16,0},{24,8},{1,17},{9,25},{17,1},{25,9},{2,18},{10... | collective-permute-start | bytes 3317768 | tf_op jit(solution)/shard_map/ppermute | solution.py:33
  267.8 220.3 %reduce-scatter.5.cloned.1.call-start = ((), (), s32[]{:S(2)}) async-start(), calls=%async_computation.6 | async-start | bytes 2580480 | tf_op jit(solution)/shard_map/reduce_scatter | solution.py:662
  303.6 50.9 %collective-permute-start.23 = (bf16[2,216,1280]{2,1,0:T(8,128)(2,1)S(1)}, bf16[2,216,1280]{2,1,0:T(8,128)(2,1)S(1)}, u32[]{:S(2)}, u32[]{:S(2)}) collective-permute-start(bf16[2,216,1280]{2,1,0:T(8,128)(2,1)S(1)} %pad_maximum_fusion.12), channel_id=1, source_target_pairs={{0,8},{8,0},{16,24},{24,16},{1,9},{9,1},{17,25},{25,17},{2,10},{10... | collective-permute-start | bytes 3317768 | tf_op jit(solution)/shard_map/ppermute | solution.py:29
  305.2 49.3 %collective-permute-start.24 = (bf16[2,216,1280]{2,1,0:T(8,128)(2,1)S(1)}, bf16[2,216,1280]{2,1,0:T(8,128)(2,1)S(1)}, u32[]{:S(2)}, u32[]{:S(2)}) collective-permute-start(bf16[2,216,1280]{2,1,0:T(8,128)(2,1)S(1)} %pad_maximum_fusion.13), channel_id=1, source_target_pairs={{0,16},{8,24},{16,0},{24,8},{1,17},{9,25},{17,1},{25,9},{2,18},{10... | collective-permute-start | bytes 3317768 | tf_op jit(solution)/shard_map/ppermute | solution.py:33
  307.3 47.2 %collective-permute-start.25 = (bf16[8,40,1280]{2,1,0:T(8,128)(2,1)}, bf16[8,40,1280]{2,1,0:T(8,128)(2,1)S(1)}, u32[]{:S(2)}, u32[]{:S(2)}) collective-permute-start(bf16[8,40,1280]{2,1,0:T(8,128)(2,1)} %pad_maximum_fusion.14), channel_id=1, source_target_pairs={{0,8},{8,0},{16,24},{24,16},{1,9},{9,1},{17,25},{25,17},{2,10},{10... | collective-permute-start | bytes 2457608 | tf_op jit(solution)/shard_map/ppermute | solution.py:29
  309.0 45.5 %collective-permute-start.26 = (bf16[8,40,1280]{2,1,0:T(8,128)(2,1)}, bf16[8,40,1280]{2,1,0:T(8,128)(2,1)S(1)}, u32[]{:S(2)}, u32[]{:S(2)}) collective-permute-start(bf16[8,40,1280]{2,1,0:T(8,128)(2,1)} %pad_maximum_fusion.15), channel_id=1, source_target_pairs={{0,16},{8,24},{16,0},{24,8},{1,17},{9,25},{17,1},{25,9},{2,18},{10... | collective-permute-start | bytes 2457608 | tf_op jit(solution)/shard_map/ppermute | solution.py:33
  400.7 31.6 %collective-permute-start.40 = (bf16[4,40,1280]{2,1,0:T(8,128)(2,1)}, bf16[4,40,1280]{2,1,0:T(8,128)(2,1)}, u32[]{:S(2)}, u32[]{:S(2)}) collective-permute-start(bf16[4,40,1280]{2,1,0:T(8,128)(2,1)} %get-tuple-element.163), channel_id=1, source_target_pairs={{0,8},{8,0},{16,24},{24,16},{1,9},{9,1},{17,25},{25,17},{2,10},{10... | collective-permute-start | bytes 1228808 | tf_op jit(solution)/shard_map/ppermute | solution.py:29
  402.4 31.2 %collective-permute-start.39 = (bf16[4,40,1280]{2,1,0:T(8,128)(2,1)}, bf16[4,40,1280]{2,1,0:T(8,128)(2,1)}, u32[]{:S(2)}, u32[]{:S(2)}) collective-permute-start(bf16[4,40,1280]{2,1,0:T(8,128)(2,1)} %get-tuple-element.161), channel_id=1, source_target_pairs={{0,16},{8,24},{16,0},{24,8},{1,17},{9,25},{17,1},{25,9},{2,18},{10... | collective-permute-start | bytes 1228808 | tf_op jit(solution)/shard_map/ppermute | solution.py:33
  447.3 35.8 %collective-permute-start.43 = (bf16[1,216,1280]{2,1,0:T(8,128)(2,1)}, bf16[1,216,1280]{2,1,0:T(8,128)(2,1)}, u32[]{:S(2)}, u32[]{:S(2)}) collective-permute-start(bf16[1,216,1280]{2,1,0:T(8,128)(2,1)} %fusion.79), channel_id=1, source_target_pairs={{0,16},{8,24},{16,0},{24,8},{1,17},{9,25},{17,1},{25,9},{2,18},{10... | collective-permute-start | bytes 1658888 | tf_op jit(solution)/shard_map/ppermute | solution.py:33
  486.7 50.0 %collective-permute-start.44 = (bf16[1,216,1280]{2,1,0:T(8,128)(2,1)}, bf16[1,216,1280]{2,1,0:T(8,128)(2,1)}, u32[]{:S(2)}, u32[]{:S(2)}) collective-permute-start(bf16[1,216,1280]{2,1,0:T(8,128)(2,1)} %get-tuple-element.206), channel_id=1, source_target_pairs={{0,8},{8,0},{16,24},{24,16},{1,9},{9,1},{17,25},{25,17},{2,10},{10... | collective-permute-start | bytes 1658888 | tf_op jit(solution)/shard_map/ppermute | solution.py:29
  517.6 39.5 %collective-permute-start.67 = (bf16[80,1792]{1,0:T(8,128)(2,1)}, bf16[80,1792]{1,0:T(8,128)(2,1)}, u32[]{:S(2)}, u32[]{:S(2)}) collective-permute-start(bf16[80,1792]{1,0:T(8,128)(2,1)} %slice.529), channel_id=1, source_target_pairs={{0,8},{8,0},{16,24},{24,16},{1,9},{9,1},{17,25},{25,17},{2,10},{10... | collective-permute-start | bytes 860168 | tf_op jit(solution)/shard_map/ppermute | solution.py:29
  519.2 37.9 %collective-permute-start.66 = (bf16[80,1792]{1,0:T(8,128)(2,1)}, bf16[80,1792]{1,0:T(8,128)(2,1)}, u32[]{:S(2)}, u32[]{:S(2)}) collective-permute-start(bf16[80,1792]{1,0:T(8,128)(2,1)} %slice.528), channel_id=1, source_target_pairs={{0,16},{8,24},{16,0},{24,8},{1,17},{9,25},{17,1},{25,9},{2,18},{10... | collective-permute-start | bytes 860168 | tf_op jit(solution)/shard_map/ppermute | solution.py:33
  533.1 29.9 %collective-permute-start.71 = (bf16[56,1280]{1,0:T(8,128)(2,1)}, bf16[56,1280]{1,0:T(8,128)(2,1)S(1)}, u32[]{:S(2)}, u32[]{:S(2)}) collective-permute-start(bf16[56,1280]{1,0:T(8,128)(2,1)} %slice.580), channel_id=1, source_target_pairs={{0,8},{8,0},{16,24},{24,16},{1,9},{9,1},{17,25},{25,17},{2,10},{10... | collective-permute-start | bytes 430088 | tf_op jit(solution)/shard_map/ppermute | solution.py:29
  535.1 27.9 %collective-permute-start.70 = (bf16[56,1280]{1,0:T(8,128)(2,1)}, bf16[56,1280]{1,0:T(8,128)(2,1)S(1)}, u32[]{:S(2)}, u32[]{:S(2)}) collective-permute-start(bf16[56,1280]{1,0:T(8,128)(2,1)} %slice.579), channel_id=1, source_target_pairs={{0,16},{8,24},{16,0},{24,8},{1,17},{9,25},{17,1},{25,9},{2,18},{10... | collective-permute-start | bytes 430088 | tf_op jit(solution)/shard_map/ppermute | solution.py:33
  (127 other events, 1291.0 us)
Sparse Core Ops, SparseCore 0:
  36.5 31.0 all-gather.7
  69.2 38.8 all-gather.3
  110.3 49.4 all-gather.5
  267.9 53.1 reduce-scatter.2
  400.8 35.4 reduce-scatter.4

commit v3 on v2

--- a/solution.py
+++ b/solution.py
@@ -16,6 +16,7 @@
 EPSILON = 1e-05
 MASKED = -1e30
 ROPE_BASE = 10000.0
+VMEM_LIMIT = 60 * 2**20
 BF16 = jnp.bfloat16
 F32 = jnp.float32
 
@@ -104,9 +105,9 @@
     return [piece, swap_x(piece), swap_y(piece), diagonal]
 
 
-def ctx_gather(piece, axis):
+def in_order(pieces, axis):
     c = lax.axis_index("ctx")
-    return place([(c ^ i, v) for i, v in enumerate(ctx_fetch(piece))], axis)
+    return place([(c ^ i, v) for i, v in enumerate(pieces)], axis)
 
 
 def scatter_first(parts):
@@ -118,11 +119,12 @@
 
 def scatter_pass(parts, got):
     half = parts[0].shape[0] // 2
+    rest = parts[0].shape[0] - half
     low_got, high_got = got[0].astype(F32), got[1].astype(F32)
     low_pass = (parts[2][:half].astype(F32) + low_got[half:]).astype(BF16)
-    high_pass = (parts[1][half:].astype(F32) + high_got[half:]).astype(BF16)
+    high_pass = (parts[1][half:].astype(F32) + high_got[rest:]).astype(BF16)
     low_own = parts[0][:half].astype(F32) + low_got[:half]
-    high_own = parts[0][half:].astype(F32) + high_got[:half]
+    high_own = parts[0][half:].astype(F32) + high_got[:rest]
     return low_own, high_own, low_pass, high_pass
 
 
@@ -137,19 +139,21 @@
     return swap_x(to_x), swap_y(to_y)
 
 
-def exchange_second(parts, got_x, got_y):
-    from_d = jnp.concatenate([swap_y(got_x[2:]), swap_x(got_y[2:])], axis=0)
-    return [parts[0], got_x[:2], got_y[:2], from_d]
-
-
-def small_sum(v):
+def exchange_second(got_x, got_y):
+    return swap_y(got_x[2:]), swap_x(got_y[2:])
+
+
+def z_sum(v):
     n = lax.axis_size("fsdp")
-    bit = 1
+    if n == 8:
+        return v + sum(
+            lax.ppermute(v, "fsdp", [(i, (i + 2 * d) % n) for i in range(n)]) for d in (1, 2, 3)
+        )
+    bit = 2
     while bit < n:
         v = v + lax.ppermute(v, "fsdp", [(i, i ^ bit) for i in range(n)])
         bit *= 2
-    v = v + swap_x(v)
-    return v + swap_y(v)
+    return v
 
 
 def pick_columns(c, gate, up, count):
@@ -214,8 +218,45 @@
             out_specs=[whole, whole],
         ),
         out_shape=[jax.ShapeDtypeStruct((r, ff), F32)] * 2,
-        compiler_params=pltpu.CompilerParams(vmem_limit_bytes=40 * 2**20),
+        compiler_params=pltpu.CompilerParams(vmem_limit_bytes=VMEM_LIMIT),
         cost_estimate=pl.CostEstimate(flops=0, bytes_accessed=12 * r * ff, transcendentals=0),
+    )(c, *pieces)
+
+
+def join_columns(c, pieces, q4, kv4):
+    r = pieces[0].shape[0]
+
+    def kernel(c_ref, *refs):
+        q_ref, k_ref, v_ref = refs[4:]
+        for own in range(4):
+
+            @pl.when(c_ref[0] == own)
+            def _():
+                for step in range(4):
+                    to = own ^ step
+                    piece = refs[step][...].astype(F32)
+                    q_ref[:, to * q4 : (to + 1) * q4] = piece[:, :q4]
+                    target = k_ref if to < 2 else v_ref
+                    at = (to % 2) * kv4
+                    target[:, at : at + kv4] = piece[:, q4:]
+
+    def whole(cols):
+        return pl.BlockSpec((r, cols), lambda i, s: (0, 0))
+
+    return pl.pallas_call(
+        kernel,
+        grid_spec=pltpu.PrefetchScalarGridSpec(
+            num_scalar_prefetch=1,
+            grid=(1,),
+            in_specs=[whole(q4 + kv4)] * 4,
+            out_specs=[whole(4 * q4), whole(2 * kv4), whole(2 * kv4)],
+        ),
+        out_shape=[
+            jax.ShapeDtypeStruct((r, cols), F32) for cols in (4 * q4, 2 * kv4, 2 * kv4)
+        ],
+        cost_estimate=pl.CostEstimate(
+            flops=0, bytes_accessed=24 * r * (q4 + kv4), transcendentals=0
+        ),
     )(c, *pieces)
 
 
@@ -257,7 +298,7 @@
 
 def forward_kernel(
     blocks_ref, slots_ref, seg_q_ref, seg_k_ref, valid_k_ref, q_ref, k_ref, v_ref,
-    o_ref, lse_ref, bias_ref, acc_ref, peak_ref, total_ref,
+    o_ref, lse_ref, bias_ref, scores_ref, acc_ref,
 ):
     rows = q_ref.shape[-1]
 
@@ -268,43 +309,45 @@
     for side in range(2):
         b = blocks_ref[side]
         lo = first_block(b, rows)
+
+        def score(kb, peaks):
+            keys = k_ref[slots_ref[kb], 0].T
+            bias = bias_ref[side, kb - lo]
+            higher = []
+            for h in range(GROUP):
+                s = dot(keys, q_ref[side, h], ((1,), (0,))) + bias
+                scores_ref[kb - lo, h] = s
+                higher.append(jnp.maximum(peaks[h], jnp.max(s, axis=0, keepdims=True)))
+            return tuple(higher)
+
+        peaks = lax.fori_loop(
+            lo, b + 1, score, (jnp.full((1, rows), -jnp.inf, F32),) * GROUP
+        )
         acc_ref[...] = jnp.zeros_like(acc_ref)
-        total_ref[...] = jnp.zeros_like(total_ref)
-        peak_ref[...] = jnp.full_like(peak_ref, -jnp.inf)
-
-        def body(kb, _):
-            slot = slots_ref[kb]
-            keys = k_ref[slot, 0].T
-            values_t = v_ref[slot, 0]
-            bias = bias_ref[side, kb - lo]
+
+        def mix(kb, totals):
+            values_t = v_ref[slots_ref[kb], 0]
+            more = []
             for h in range(GROUP):
-                query = q_ref[side, h]
-                s = dot(keys, query, ((1,), (0,))) + bias
-                peak_old = peak_ref[h : h + 1]
-                peak = jnp.maximum(peak_old, jnp.max(s, axis=0, keepdims=True))
-                p = jnp.exp(s - peak)
-                shrink = jnp.exp(peak_old - peak)
-                peak_ref[h : h + 1] = peak
-                total_ref[h : h + 1] = total_ref[h : h + 1] * shrink + jnp.sum(
-                    p, axis=0, keepdims=True
-                )
-                acc_ref[h] = acc_ref[h] * shrink + dot(values_t, p.astype(BF16), ((1,), (0,)))
-            return 0
-
-        body(b, 0)
-        lax.fori_loop(lo, b, body, 0)
+                p = jnp.exp(scores_ref[kb - lo, h] - peaks[h])
+                more.append(totals[h] + jnp.sum(p, axis=0, keepdims=True))
+                acc_ref[h] += dot(values_t, p.astype(BF16), ((1,), (0,)))
+            return tuple(more)
+
+        totals = lax.fori_loop(lo, b + 1, mix, (jnp.zeros((1, rows), F32),) * GROUP)
         for h in range(GROUP):
-            total = total_ref[h : h + 1]
-            o_ref[side, h] = (acc_ref[h] / total).astype(BF16)
-            lse_ref[side, 0, h : h + 1] = peak_ref[h : h + 1] + jnp.log(total)
+            o_ref[side, h] = (acc_ref[h] / totals[h]).astype(BF16)
+            lse_ref[side, 0, h : h + 1] = peaks[h] + jnp.log(totals[h])
 
 
 def backward_kernel(
     blocks_ref, slots_ref, seg_q_ref, seg_k_ref, valid_k_ref, cos_ref, sin_ref, q_ref, k_ref, v_ref,
     o_ref, do_ref, lse_ref,
-    dq_ref, dkv_ref, bias_ref, acc_ref, center_ref, dk_ref, dv_ref,
+    dq_ref, low_ref, high_ref, keep_ref,
+    bias_ref, acc_ref, center_ref, dk_ref, dv_ref, p_ref, ds_ref,
 ):
     rows = q_ref.shape[-1]
+    half = HEAD_DIM // 2
 
     @pl.when(pl.program_id(0) == 0)
     def _():
@@ -321,33 +364,48 @@
                 o_ref[side, h].astype(F32) * do_ref[side, h].astype(F32), axis=0, keepdims=True
             )
 
-        def body(kb, _):
+        def soft(kb, at):
             slot = slots_ref[kb]
-            keys_t = k_ref[slot, 0]
-            keys = keys_t.T
+            keys = k_ref[slot, 0].T
             values = v_ref[slot, 0].T
             bias = bias_ref[side, kb - lo]
             for h in range(GROUP):
-                query_t = q_ref[side, h]
-                grad_t = do_ref[side, h]
-                s = dot(keys, query_t, ((1,), (0,))) + bias
+                s = dot(keys, q_ref[side, h], ((1,), (0,))) + bias
                 p = jnp.exp(s - lse_ref[side, 0, h : h + 1])
-                dp = dot(values, grad_t, ((1,), (0,)))
-                ds = (p * (dp - center_ref[h : h + 1])).astype(BF16)
-                dv_ref[slot] += dot(grad_t, p.astype(BF16), ((1,), (1,)))
-                dk_ref[slot] += dot(query_t, ds, ((1,), (1,)))
-                acc_ref[h] += dot(keys_t, ds, ((1,), (0,)))
+                dp = dot(values, do_ref[side, h], ((1,), (0,)))
+                p_ref[at, h] = p.astype(BF16)
+                ds_ref[at, h] = (p * (dp - center_ref[h : h + 1])).astype(BF16)
+
+        def products(kb, at):
+            slot = slots_ref[kb]
+            dv = dot(do_ref[side, 0], p_ref[at, 0], ((1,), (1,)))
+            dk = dot(q_ref[side, 0], ds_ref[at, 0], ((1,), (1,)))
+            for h in range(1, GROUP):
+                dv += dot(do_ref[side, h], p_ref[at, h], ((1,), (1,)))
+                dk += dot(q_ref[side, h], ds_ref[at, h], ((1,), (1,)))
+            dv_ref[slot] += dv
+            dk_ref[slot] += dk
+            for h in range(GROUP):
+                acc_ref[h] += dot(k_ref[slot, 0], ds_ref[at, h], ((1,), (0,)))
+
+        soft(lo, 0)
+
+        def body(kb, _):
+            products(kb - 1, (kb - 1 - lo) % 2)
+            soft(kb, (kb - lo) % 2)
             return 0
 
-        lax.fori_loop(lo, b + 1, body, 0)
-        half = HEAD_DIM // 2
+        lax.fori_loop(lo + 1, b + 1, body, 0)
+        products(b, (b - lo) % 2)
         cos, sin = cos_ref[side], sin_ref[side]
         for h in range(GROUP):
-            a, b = acc_ref[h, :half] * 0.125, acc_ref[h, half:] * 0.125
-            turned = jnp.concatenate([a * cos + b * sin, b * cos - a * sin], axis=0)
+            a, b2 = acc_ref[h, :half] * 0.125, acc_ref[h, half:] * 0.125
+            turned = jnp.concatenate([a * cos + b2 * sin, b2 * cos - a * sin], axis=0)
             dq_ref[side, h] = turned.astype(BF16)
-    dkv_ref[:, 0, 0] = dk_ref[...].astype(BF16)
-    dkv_ref[:, 1, 0] = dv_ref[...].astype(BF16)
+    for target, slots in ((low_ref, (2, 6)), (high_ref, (5, 7)), (keep_ref, (0, 4, 1, 3))):
+        for i, slot in enumerate(slots):
+            target[i, 0, 0] = dk_ref[slot].astype(BF16)
+            target[i, 1, 0] = dv_ref[slot].astype(BF16)
 
 
 def project(c, f, tokens_all, mine, other, cosine, sine, q_width):
@@ -383,46 +441,50 @@
 
             gain_ref[...] = w_ref[:, gains_at:].astype(F32).T[:8]
 
-        x = x_ref[0].astype(F32)
+        x = x_ref[...].astype(F32)
         inverse = lax.rsqrt(jnp.mean(x * x, axis=-1, keepdims=True) + EPSILON)
-        first = (x * inverse * gain_ref[0:1]).astype(BF16)
-        first_ref[0] = first
-        cos, sin = cos_ref[0], sin_ref[0]
-        kv = dot(first, w_ref[:, q_width:gains_at], ((1,), (0,))).T
-        for h in range(kv_heads):
-            at = h * HEAD_DIM
-            if h < KV_HEADS:
-                kv_ref[0, h] = turned(kv, at, cos, sin).astype(BF16)
-            else:
-                kv_ref[0, h] = kv[at : at + HEAD_DIM].astype(BF16)
-
-        @pl.when(pl.program_id(0) < 2)
+        scaled = x * inverse * gain_ref[0:1][None]
+        first_ref[...] = scaled.astype(BF16)
+        first = scaled.reshape(2 * rows, width).astype(BF16)
+        both = dot(first, w_ref[:, q_width:gains_at], ((1,), (0,)))
+        for i in range(2):
+            cos, sin = cos_ref[i], sin_ref[i]
+            kv = both[i * rows : (i + 1) * rows].T
+            for h in range(kv_heads):
+                at = h * HEAD_DIM
+                if h < KV_HEADS:
+                    kv_ref[i, h] = turned(kv, at, cos, sin).astype(BF16)
+                else:
+                    kv_ref[i, h] = kv[at : at + HEAD_DIM].astype(BF16)
+
+        @pl.when(pl.program_id(0) == 0)
         def _():
-            q = dot(first, w_ref[:, :q_width], ((1,), (0,))).T
-            for h in range(HEADS):
-                turned_q = turned(q, h * HEAD_DIM, cos, sin).astype(BF16)
-                q_ref[0, h] = (turned_q.astype(F32) * 0.125).astype(BF16)
-
-    table = pl.BlockSpec((1, half, rows), lambda i, s: (i, 0, 0))
+            both = dot(first, w_ref[:, :q_width], ((1,), (0,)))
+            for i in range(2):
+                cos, sin = cos_ref[i], sin_ref[i]
+                q = both[i * rows : (i + 1) * rows].T
+                for h in range(HEADS):
+                    turned_q = turned(q, h * HEAD_DIM, cos, sin).astype(BF16)
+                    q_ref[i, h] = (turned_q.astype(F32) * 0.125).astype(BF16)
+
+    table = pl.BlockSpec((2, half, rows), lambda i, s: (i, 0, 0))
     piece = pl.BlockSpec(mine.shape, lambda i, s: (0, 0, 0, 0))
     return pl.pallas_call(
         kernel,
         grid_spec=pltpu.PrefetchScalarGridSpec(
             num_scalar_prefetch=1,
-            grid=(blocks,),
+            grid=(blocks // 2,),
             in_specs=[
-                pl.BlockSpec((1, rows, width), lambda i, s: (i, 0, 0)),
+                pl.BlockSpec((2, rows, width), lambda i, s: (i, 0, 0)),
                 piece,
                 piece,
                 table,
                 table,
             ],
             out_specs=[
-                pl.BlockSpec((1, rows, width), lambda i, s: (i, 0, 0)),
-                pl.BlockSpec(
-                    (1, HEADS, HEAD_DIM, rows), lambda i, s: (jnp.minimum(i, 1), 0, 0, 0)
-                ),
-                pl.BlockSpec((1, kv_heads, HEAD_DIM, rows), lambda i, s: (i, 0, 0, 0)),
+                pl.BlockSpec((2, rows, width), lambda i, s: (i, 0, 0)),
+                pl.BlockSpec((2, HEADS, HEAD_DIM, rows), lambda i, s: (0, 0, 0, 0)),
+                pl.BlockSpec((2, kv_heads, HEAD_DIM, rows), lambda i, s: (i, 0, 0, 0)),
                 pl.BlockSpec((2 * nz * r, 4 * cols), lambda i, s: (0, 0)),
                 pl.BlockSpec((8, width), lambda i, s: (0, 0)),
             ],
@@ -434,11 +496,38 @@
             jax.ShapeDtypeStruct((2 * nz * r, 4 * cols), BF16),
             jax.ShapeDtypeStruct((8, width), F32),
         ],
-        compiler_params=pltpu.CompilerParams(vmem_limit_bytes=56 * 2**20),
+        compiler_params=pltpu.CompilerParams(vmem_limit_bytes=VMEM_LIMIT),
         cost_estimate=pl.CostEstimate(
             flops=8_000_000_000, bytes_accessed=25_000_000, transcendentals=0
         ),
     )(jnp.stack([c, f]).astype(jnp.int32), tokens_all, mine, other, cosine, sine)
+
+
+def project_grad(first_all, dq_pieces, dkv_pieces):
+    _, rows, width = first_all.shape
+    q4, kv4 = dq_pieces[0].shape[1], dkv_pieces[0].shape[1]
+
+    def kernel(first_ref, *refs):
+        out_ref = refs[-1]
+        total = None
+        for i, (piece, at) in enumerate(
+            ((0, 0), (0, 1), (1, 0), (1, 1), (2, 0), (2, 1), (3, 0), (4, 0))
+        ):
+            turned = jnp.concatenate([refs[piece][at], refs[5 + piece][at]], axis=0)
+            term = dot(turned, first_ref[i], ((1,), (0,)))
+            total = term if total is None else total + term
+        out_ref[...] = total.T.astype(BF16)
+
+    operands = [first_all, *dq_pieces, *dkv_pieces]
+    return pl.pallas_call(
+        kernel,
+        grid=(1,),
+        in_specs=[fixed(v.shape) for v in operands],
+        out_specs=fixed((width, q4 + kv4)),
+        out_shape=jax.ShapeDtypeStruct((width, q4 + kv4), BF16),
+        compiler_params=pltpu.CompilerParams(vmem_limit_bytes=VMEM_LIMIT),
+        cost_estimate=BESIDE,
+    )(*operands)
 
 
 def kernel_specs(blocks, rows):
@@ -467,16 +556,15 @@
             out_specs=[q_spec, stat_spec],
             scratch_shapes=[
                 pltpu.VMEM((2, reach, rows, rows), F32),
+                pltpu.VMEM((reach, GROUP, rows, rows), F32),
                 pltpu.VMEM((GROUP, HEAD_DIM, rows), F32),
-                pltpu.VMEM((GROUP, rows), F32),
-                pltpu.VMEM((GROUP, rows), F32),
             ],
         ),
         out_shape=[
             jax.ShapeDtypeStruct(q_t.shape, BF16),
             jax.ShapeDtypeStruct((2, KV_HEADS, GROUP, rows), F32),
         ],
-        compiler_params=pltpu.CompilerParams(vmem_limit_bytes=40 * 2**20),
+        compiler_params=pltpu.CompilerParams(vmem_limit_bytes=VMEM_LIMIT),
         cost_estimate=pl.CostEstimate(
             flops=20_000_000_000, bytes_accessed=6_000_000, transcendentals=0
         ),
@@ -488,7 +576,13 @@
     q_spec, k_spec, v_spec, stat_spec, seg_specs = kernel_specs(blocks, rows)
     reach = (WINDOW + rows - 2) // rows + 1
     table = pl.BlockSpec((2, HEAD_DIM // 2, rows), lambda g, *_: (0, 0, 0))
-    dkv_spec = pl.BlockSpec((blocks, 2, 1, HEAD_DIM, rows), lambda g, *_: (0, 0, g, 0, 0))
+
+    def dkv_spec(count):
+        return pl.BlockSpec((count, 2, 1, HEAD_DIM, rows), lambda g, *_: (0, 0, g, 0, 0))
+
+    def dkv_shape(count):
+        return jax.ShapeDtypeStruct((count, 2, KV_HEADS, HEAD_DIM, rows), BF16)
+
     return pl.pallas_call(
         backward_kernel,
         grid_spec=pltpu.PrefetchScalarGridSpec(
@@ -496,24 +590,329 @@
             grid=(KV_HEADS,),
             in_specs=seg_specs
             + [table, table, q_spec, k_spec, v_spec, q_spec, q_spec, stat_spec],
-            out_specs=[q_spec, dkv_spec],
+            out_specs=[q_spec, dkv_spec(2), dkv_spec(2), dkv_spec(4)],
             scratch_shapes=[
                 pltpu.VMEM((2, reach, rows, rows), F32),
                 pltpu.VMEM((GROUP, HEAD_DIM, rows), F32),
                 pltpu.VMEM((GROUP, rows), F32),
                 pltpu.VMEM((blocks, HEAD_DIM, rows), F32),
                 pltpu.VMEM((blocks, HEAD_DIM, rows), F32),
+                pltpu.VMEM((2, GROUP, rows, rows), BF16),
+                pltpu.VMEM((2, GROUP, rows, rows), BF16),
             ],
         ),
         out_shape=[
             jax.ShapeDtypeStruct(q_t.shape, BF16),
-            jax.ShapeDtypeStruct((blocks, 2, KV_HEADS, HEAD_DIM, rows), BF16),
-        ],
-        compiler_params=pltpu.CompilerParams(vmem_limit_bytes=48 * 2**20),
+            dkv_shape(2),
+            dkv_shape(2),
+            dkv_shape(4),
+        ],
+        compiler_params=pltpu.CompilerParams(vmem_limit_bytes=VMEM_LIMIT),
+        cost_estimate=BESIDE,
+    )(q_blocks, slots, seg_q, seg_k, valid_k, cos, sin, q_t, kv_t, kv_t, o_t, do_t, lse)
+
+
+def feed_forward(x, dy_all, gu_w, down_w, first, held):
+    count, rows, width = x.shape
+    cut = down_w.shape[0]
+
+    def kernel(x_ref, dy_ref, gu_ref, down_ref, *refs):
+        all_ref, hidden_ref, d_gu_ref, part_ref = refs[-4:]
+        x_in = x_ref[0]
+        all_ref[0] = x_in
+        gu = dot(x_in, gu_ref[...], ((1,), (0,)))
+        d_hidden = dot(dy_ref[0], down_ref[...], ((1,), (1,)))
+        gate_pre, up_pre = gu[:, :cut], gu[:, cut:]
+        sig = jax.nn.sigmoid(gate_pre)
+        swish = gate_pre * sig
+        slope = sig * (1.0 + gate_pre * (1.0 - sig))
+        hidden_ref[0] = (swish * up_pre).astype(BF16)
+        d_gu_ref[0, :, :cut] = (d_hidden * up_pre * slope).astype(BF16)
+        d_gu_ref[0, :, cut:] = (d_hidden * swish).astype(BF16)
+        part_ref[0] = dot(d_gu_ref[0], gu_ref[...], ((1,), (1,))).astype(BF16)
+
+    def block(size):
+        return pl.BlockSpec((1, rows, size), lambda i: (first + i, 0, 0))
+
+    def own(size):
+        return pl.BlockSpec((1, rows, size), lambda i: (i, 0, 0))
+
+    held = () if held is None else held
+    return pl.pallas_call(
+        kernel,
+        grid=(count,),
+        in_specs=[
+            own(width),
+            block(width),
+            pl.BlockSpec(gu_w.shape, lambda i: (0, 0)),
+            pl.BlockSpec(down_w.shape, lambda i: (0, 0)),
+        ]
+        + [pl.BlockSpec(memory_space=pl.ANY)] * len(held),
+        out_specs=[block(width), block(cut), block(2 * cut), own(width)],
+        out_shape=[
+            jax.ShapeDtypeStruct((4, rows, width), BF16),
+            jax.ShapeDtypeStruct((4, rows, cut), BF16),
+            jax.ShapeDtypeStruct((4, rows, 2 * cut), BF16),
+            jax.ShapeDtypeStruct((count, rows, width), BF16),
+        ],
+        input_output_aliases={4 + i: i for i in range(len(held))},
+        compiler_params=pltpu.CompilerParams(vmem_limit_bytes=VMEM_LIMIT),
         cost_estimate=pl.CostEstimate(
-            flops=40_000_000_000, bytes_accessed=16_000_000, transcendentals=0
+            flops=10 * count * rows * width * cut,
+            bytes_accessed=2 * (gu_w.size + down_w.size + count * rows * (4 * width + 3 * cut)),
+            transcendentals=0,
         ),
-    )(q_blocks, slots, seg_q, seg_k, valid_k, cos, sin, q_t, kv_t, kv_t, o_t, do_t, lse)
+    )(x, dy_all, gu_w, down_w, *held)
+
+
+BESIDE = pl.CostEstimate(flops=0, bytes_accessed=0, transcendentals=0)
+
+
+def fixed(shape):
+    return pl.BlockSpec(shape, lambda *_: (0,) * len(shape))
+
+
+def transposed_product(left, right, tile):
+    depth, rows = left.shape
+    cols = right.shape[1]
+
+    def kernel(left_ref, right_ref, out_ref):
+        out_ref[...] = dot(left_ref[...], right_ref[...], ((0,), (0,))).astype(BF16)
+
+    return pl.pallas_call(
+        kernel,
+        grid=(rows // tile,),
+        in_specs=[pl.BlockSpec((depth, tile), lambda i: (0, i)), fixed(right.shape)],
+        out_specs=pl.BlockSpec((tile, cols), lambda i: (i, 0)),
+        out_shape=jax.ShapeDtypeStruct((rows, cols), BF16),
+        compiler_params=pltpu.CompilerParams(vmem_limit_bytes=VMEM_LIMIT),
+        cost_estimate=BESIDE,
+    )(left, right)
+
+
+def product(left, right, tile):
+    rows, depth = left.shape
+    cols = right.shape[1]
+
+    def kernel(left_ref, right_ref, out_ref):
+        out_ref[...] = dot(left_ref[...], right_ref[...], ((1,), (0,))).astype(BF16)
+
+    return pl.pallas_call(
+        kernel,
+        grid=(rows // tile,),
+        in_specs=[pl.BlockSpec((tile, depth), lambda i: (i, 0)), fixed(right.shape)],
+        out_specs=pl.BlockSpec((tile, cols), lambda i: (i, 0)),
+        out_shape=jax.ShapeDtypeStruct((rows, cols), BF16),
+        compiler_params=pltpu.CompilerParams(vmem_limit_bytes=VMEM_LIMIT),
+        cost_estimate=BESIDE,
+    )(left, right)
+
+
+def side_product(left_t, right):
+    def kernel(left_ref, right_ref, out_ref):
+        total = dot(left_ref[0], right_ref[0], ((1,), (0,)))
+        out_ref[...] = (total + dot(left_ref[1], right_ref[1], ((1,), (0,)))).astype(BF16)
+
+    shape = (left_t.shape[1], right.shape[2])
+    return pl.pallas_call(
+        kernel,
+        grid=(1,),
+        in_specs=[fixed(left_t.shape), fixed(right.shape)],
+        out_specs=fixed(shape),
+        out_shape=jax.ShapeDtypeStruct(shape, BF16),
+        compiler_params=pltpu.CompilerParams(vmem_limit_bytes=VMEM_LIMIT),
+        cost_estimate=BESIDE,
+    )(left_t, right)
+
+
+def add_sums(ref, first, sums):
+    row = lax.broadcasted_iota(jnp.int32, (8, 128), 0)
+    value = jnp.zeros((8, 128), F32)
+    for i, v in enumerate(sums):
+        value = jnp.where(row == i, v, value)
+
+    @pl.when(first)
+    def _():
+        ref[...] = jnp.zeros_like(ref)
+
+    ref[...] += value
+
+
+def side_spec(*shape):
+    return pl.BlockSpec((1, *shape), lambda i: (i, 0, 0))
+
+
+def out_project(tokens, attended_t, weights, gain, live):
+    sides, rows, width = tokens.shape
+
+    def kernel(x_ref, att_ref, w_ref, gain_ref, live_ref, middle_ref, second_ref, sums_ref):
+        branch = dot(att_ref[0], w_ref[...], ((0,), (0,)))
+        middle = x_ref[0].astype(F32) + branch
+        middle_ref[0] = middle
+        inverse = lax.rsqrt(jnp.mean(middle * middle, axis=-1, keepdims=True) + EPSILON)
+        second_ref[0] = (middle * inverse * gain_ref[...]).astype(BF16)
+        mask = live_ref[0]
+        sums = [jnp.sum(mask * branch * branch), jnp.sum(mask * middle * middle)]
+        add_sums(sums_ref, pl.program_id(0) == 0, sums)
+
+    return pl.pallas_call(
+        kernel,
+        grid=(sides,),
+        in_specs=[
+            side_spec(rows, width),
+            side_spec(width, rows),
+            fixed(weights.shape),
+            fixed((1, width)),
+            side_spec(rows, 1),
+        ],
+        out_specs=[side_spec(rows, width), side_spec(rows, width), fixed((8, 128))],
+        out_shape=[
+            jax.ShapeDtypeStruct(tokens.shape, F32),
+            jax.ShapeDtypeStruct(tokens.shape, BF16),
+            jax.ShapeDtypeStruct((8, 128), F32),
+        ],
+        compiler_params=pltpu.CompilerParams(vmem_limit_bytes=VMEM_LIMIT),
+        cost_estimate=BESIDE,
+    )(tokens, attended_t, weights, gain, live)
+
+
+def norm_back(upstream, gain, value):
+    inverse = lax.rsqrt(jnp.mean(value * value, axis=-1, keepdims=True) + EPSILON)
+    normed = value * inverse
+    scaled = upstream * gain
+    grad = inverse * (scaled - normed * jnp.mean(scaled * normed, axis=-1, keepdims=True))
+    return grad, jnp.sum(upstream * normed, axis=0, keepdims=True)
+
+
+def add_row(ref, first, row):
+    @pl.when(first)
+    def _():
+        ref[...] = jnp.zeros_like(ref)
+
+    ref[...] += row
+
+
+def middle_back(d_second, middle, cotangent, gain, weights):
+    sides, rows, width = middle.shape
+
+    def kernel(d_ref, m_ref, cot_ref, gain_ref, w_ref, gm_ref, branch_ref, do_ref, gain_grad_ref):
+        grad, gain_grad = norm_back(d_ref[0], gain_ref[...], m_ref[0])
+        grad_middle = cot_ref[0].astype(F32) + grad
+        gm_ref[0] = grad_middle
+        d_branch = grad_middle.astype(BF16)
+        branch_ref[0] = d_branch
+        do_ref[0] = dot(d_branch, w_ref[...], ((1,), (1,))).T.astype(BF16)
+        add_row(gain_grad_ref, pl.program_id(0) == 0, gain_grad)
+
+    return pl.pallas_call(
+        kernel,
+        grid=(sides,),
+        in_specs=[
+            side_spec(rows, width),
+            side_spec(rows, width),
+            side_spec(rows, width),
+            fixed((1, width)),
+            fixed(weights.shape),
+        ],
+        out_specs=[
+            side_spec(rows, width),
+            side_spec(rows, width),
+            side_spec(width, rows),
+            fixed((1, width)),
+        ],
+        out_shape=[
+            jax.ShapeDtypeStruct(middle.shape, F32),
+            jax.ShapeDtypeStruct(middle.shape, BF16),
+            jax.ShapeDtypeStruct((sides, width, rows), BF16),
+            jax.ShapeDtypeStruct((1, width), F32),
+        ],
+        compiler_params=pltpu.CompilerParams(vmem_limit_bytes=VMEM_LIMIT),
+        cost_estimate=BESIDE,
+    )(d_second, middle, cotangent, gain, weights)
+
+
+def first_back(d_q, d_kv, weights, tokens, grad_middle, gain, live):
+    sides, rows, width = tokens.shape
+    q_width, kv_width = d_q.shape[1], d_kv.shape[1]
+
+    def kernel(
+        dq_ref, dkv_ref, w_ref, x_ref, gm_ref, gain_ref, live_ref, out_ref, gain_grad_ref, sums_ref
+    ):
+        d_first = dot(dq_ref[0].T, w_ref[:, :q_width], ((1,), (1,)))
+        d_first += dot(dkv_ref[0].T, w_ref[:, q_width : q_width + kv_width], ((1,), (1,)))
+        grad, gain_grad = norm_back(d_first, gain_ref[...], x_ref[0].astype(F32))
+        total = gm_ref[0] + grad
+        out_ref[0] = total.astype(BF16)
+        add_row(gain_grad_ref, pl.program_id(0) == 0, gain_grad)
+        add_sums(sums_ref, pl.program_id(0) == 0, [jnp.sum(live_ref[0] * total * total)])
+
+    return pl.pallas_call(
+        kernel,
+        grid=(sides,),
+        in_specs=[
+            side_spec(q_width, rows),
+            side_spec(kv_width, rows),
+            fixed(weights.shape),
+            side_spec(rows, width),
+            side_spec(rows, width),
+            fixed((1, width)),
+            side_spec(rows, 1),
+        ],
+        out_specs=[side_spec(rows, width), fixed((1, width)), fixed((8, 128))],
+        out_shape=[
+            jax.ShapeDtypeStruct(tokens.shape, BF16),
+            jax.ShapeDtypeStruct((1, width), F32),
+            jax.ShapeDtypeStruct((8, 128), F32),
+        ],
+        compiler_params=pltpu.CompilerParams(vmem_limit_bytes=VMEM_LIMIT),
+        cost_estimate=BESIDE,
+    )(d_q, d_kv, weights, tokens, grad_middle, gain, live)
+
+
+def finish(middle, branch_ffn, live, gain_one, gain_two, early_sums, late_sums):
+    sides, rows, width = middle.shape
+
+    def kernel(m_ref, f_ref, live_ref, one_ref, two_ref, early_ref, late_ref, out_ref, small_ref):
+        result = m_ref[0] + f_ref[0]
+        out_ref[0] = result.astype(BF16)
+        mask = live_ref[0]
+        own = [jnp.sum(mask * result * result), jnp.sum(mask * f_ref[0] * f_ref[0]), jnp.sum(mask)]
+        first = pl.program_id(0) == 0
+        row = lax.broadcasted_iota(jnp.int32, (8, width), 0)
+        value = jnp.where(row == 2, own[0], 0.0)
+        value = jnp.where(row == 5, own[1], value)
+        value = jnp.where(row == 7, own[2], value)
+
+        @pl.when(first)
+        def _():
+            start = jnp.where(row == 0, one_ref[...], 0.0)
+            start = jnp.where(row == 1, two_ref[...], start)
+            start = jnp.where(row == 3, late_ref[0:1, 0:1], start)
+            start = jnp.where(row == 4, early_ref[0:1, 0:1], start)
+            small_ref[...] = jnp.where(row == 6, early_ref[1:2, 0:1], start)
+
+        small_ref[...] += value
+
+    return pl.pallas_call(
+        kernel,
+        grid=(sides,),
+        in_specs=[
+            side_spec(rows, width),
+            side_spec(rows, width),
+            side_spec(rows, 1),
+            fixed((1, width)),
+            fixed((1, width)),
+            fixed((8, 128)),
+            fixed((8, 128)),
+        ],
+        out_specs=[side_spec(rows, width), fixed((8, width))],
+        out_shape=[
+            jax.ShapeDtypeStruct(middle.shape, BF16),
+            jax.ShapeDtypeStruct((8, width), F32),
+        ],
+        compiler_params=pltpu.CompilerParams(vmem_limit_bytes=VMEM_LIMIT),
+        cost_estimate=BESIDE,
+    )(middle, branch_ffn, live, gain_one, gain_two, early_sums, late_sums)
 
 
 def norm_forward(value_rows, gain):
@@ -581,14 +980,14 @@
     qkv_shard = jnp.concatenate([w_query, w_key, w_value, gains], axis=1)
     c4 = qkv_shard.shape[1] // 4
     qkv_z = z_fetch(lax.dynamic_slice_in_dim(qkv_shard, c * c4, c4, 1))
-    out_w = lax.all_gather(w_out, "fsdp", axis=0, tiled=True)
+    d4 = w_down.shape[0] // 4
+    down_shard = lax.dynamic_slice_in_dim(w_down, c * d4, d4, 0)
+    out_down_shard = after(jnp.concatenate([w_out, down_shard]), qkv_z)
+    out_down = lax.all_gather(out_down_shard, "fsdp", axis=0)
     qkv_z, tokens_x, tokens_y = sync(qkv_z, tokens_x, tokens_y)
     qkv_x, qkv_y = swap_x(qkv_z), swap_y(qkv_z)
     gu_shard = after(pick_columns(c_ref, w_gate, w_up, n), qkv_z)
     gu_w = lax.all_gather(gu_shard, "fsdp", axis=0, tiled=True)
-    d4 = w_down.shape[0] // 4
-    down_shard = after(lax.dynamic_slice_in_dim(w_down, c * d4, d4, 0), gu_shard)
-    down_w = lax.all_gather(down_shard, "fsdp", axis=0, tiled=True)
     cut = ff // 4
     qkv_x, qkv_y, tokens_x, tokens_y = sync(qkv_x, qkv_y, tokens_x, tokens_y)
     zh = qkv_z.shape[0] // 2
@@ -603,82 +1002,61 @@
     first_all, q_t, kv_all, qkv_w, gain_rows = project(
         c, f, tokens_all.reshape(8, rows, width), qkv_mine, qkv_other, cosine, sine, q_width
     )
-    gain_one, gain_two = gain_rows[0], gain_rows[1]
+    gain_one, gain_two = gain_rows[0:1], gain_rows[1:2]
     first_all = first_all.reshape(4, 2, rows, width)
-    qkv_w = qkv_w[:, : q_width + 2 * kv_width]
-    inputs = tokens[0].astype(F32)
-    _, unit_one, inverse_one = norm_forward(inputs, gain_one)
     o_t, lse = attention_forward(q_blocks, slots, seg_q, seg_k, valid_k, q_t, kv_all)
-    o_t, out_w, dy_pieces, gu_w, down_w = sync(o_t, out_w, dy_pieces, gu_w, down_w)
-    dy_all = jnp.stack(dy_pieces).reshape(-1, width)
+    o_t, out_down, dy_pieces, gu_w = sync(o_t, out_down, dy_pieces, gu_w)
+    out_w = out_down[:, :r].reshape(n * r, width)
+    down_w = out_down[:, r:].reshape(cut, width)
+    (dy_all,) = sync(jnp.stack(dy_pieces).reshape(4, row_count, width))
     attended_t = o_t.reshape(2, width, rows)
-    branch_attn = ein("bfr,fo->bro", attended_t, out_w).reshape(row_count, width)
-    middle = inputs + branch_attn
-
-    normed_two, unit_two, inverse_two = norm_forward(middle, gain_two)
-    second_in = normed_two.astype(BF16)
-    x_own = second_in.reshape(2, rows, width)
+    live_rows = live.reshape(2, rows, 1).astype(F32)
+    middle, x_own, early_sums = out_project(tokens_own, attended_t, out_w, gain_two, live_rows)
+
     x_x, x_y = swap_x(x_own), swap_y(x_own)
-    d_hidden = ein("ro,fo->rf", dy_all, down_w)
-
-    def gated(x, d_hidden):
-        gu = ein("bri,if->brf", x, gu_w).reshape(-1, 2 * cut)
-        gate_pre, up_pre = gu[:, :cut], gu[:, cut:]
-        sig = jax.nn.sigmoid(gate_pre)
-        swish = gate_pre * sig
-        slope = sig * (1.0 + gate_pre * (1.0 - sig))
-        d_gu = [(d_hidden * up_pre * slope).astype(BF16), (d_hidden * swish).astype(BF16)]
-        return (swish * up_pre).astype(BF16), jnp.concatenate(d_gu, axis=1)
-
-    def back(d_gu):
-        return ein("rf,if->ri", d_gu, gu_w).astype(BF16).reshape(-1, 2, rows, width)
-
-    hidden_0, d_gu_0 = gated(x_own, d_hidden[:row_count])
-    x_x, x_y, hidden_0, d_gu_0 = lax.optimization_barrier((x_x, x_y, hidden_0, d_gu_0))
+    held = feed_forward(x_own.reshape(1, row_count, width), dy_all, gu_w, down_w, 0, None)
+    x_x, x_y, *held = sync(x_x, x_y, *held)
+    parts_0 = held.pop()
     x_d = jnp.concatenate([swap_y(x_x[:1]), swap_x(x_y[1:])])
-    x_xy = jnp.concatenate([x_x, x_y])
-    hidden_1, d_gu_1 = gated(x_xy, d_hidden[row_count : 3 * row_count])
-    parts_1 = back(d_gu_1)
-    x_d, parts_1 = lax.optimization_barrier((x_d, parts_1))
-    hidden_2, d_gu_2 = gated(x_d, d_hidden[3 * row_count :])
-    parts_2 = back(d_gu_2)
-    d_gu_0 = after(d_gu_0, parts_2)
-    parts_0 = back(d_gu_0)
-    parts = [parts_0[0], parts_1[0], parts_1[1], parts_2[0]]
+    x_xy = jnp.stack([x_x, x_y]).reshape(2, row_count, width)
+    held = feed_forward(x_xy, dy_all, gu_w, down_w, 1, held)
+    x_d, *held = sync(x_d, *held)
+    parts_1 = held.pop()
+    x_d = x_d.reshape(1, row_count, width)
+    *held, parts_2 = feed_forward(x_d, dy_all, gu_w, down_w, 3, held)
+    parts = [v.reshape(2, rows, width) for v in (parts_0[0], parts_1[0], parts_1[1], parts_2[0])]
     got = scatter_first(parts)
-    x_all = jnp.concatenate([x_own, x_xy, x_d]).reshape(-1, width)
-    d_gu = jnp.concatenate([d_gu_0, d_gu_1, d_gu_2])
-    hidden = jnp.concatenate([hidden_0, hidden_1, hidden_2])
-    grad_gu = ein("ri,rf->if", x_all, d_gu).astype(BF16)
-    got_low, got_high, grad_gu = lax.optimization_barrier((*got, grad_gu))
-    d_second = scatter_last(*scatter_pass(parts, (got_low, got_high))).reshape(row_count, width)
-    grad_d = ein("rf,ro->fo", after(hidden, grad_gu), dy_all).astype(BF16)
-    ffn_parts = ein("rf,fo->ro", after(hidden, grad_d), down_w).astype(BF16)
-    d_second, ffn_parts = lax.optimization_barrier((d_second, ffn_parts))
+    x_all, hidden, d_gu = [v.reshape(4 * row_count, -1) for v in held]
+    dy_all = dy_all.reshape(4 * row_count, width)
+    grad_gu = transposed_product(x_all, d_gu, 256)
+    ffn_parts = product(after(hidden, grad_gu), down_w, row_count)
+    got_low, got_high, grad_gu, ffn_parts = sync(*got, grad_gu, ffn_parts)
+    d_second = scatter_last(*scatter_pass(parts, (got_low, got_high)))
+    grad_d = transposed_product(after(hidden, ffn_parts), dy_all, cut)
+    d_second, grad_d = sync(d_second, grad_d)
     ffn_parts = ffn_parts.reshape(4, 2, rows, width)
     ffn_parts = [ffn_parts[i] for i in range(4)]
-    ffn_got = scatter_first(ffn_parts)
     own_gu = lax.psum_scatter(grad_gu, "fsdp", scatter_dimension=0, tiled=True)
     own_down = lax.psum_scatter(grad_d, "fsdp", scatter_dimension=0, tiled=True)
 
     k = f % 2
     nz = n // 2
     r4 = r // 4
-    grad_output = cotangent[0].astype(F32)
-    grad_mid_norm, grad_gain_two = norm_backward(d_second, gain_two, unit_two, inverse_two)
-    grad_middle = grad_output + grad_mid_norm
-    d_branch = grad_middle.astype(BF16).reshape(2, rows, width)
-    do_t = ein("fo,bro->bfr", out_w, d_branch).astype(BF16).reshape(2, HEADS, HEAD_DIM, rows)
-    whole_out = ein("bfr,bro->fo", attended_t, d_branch).astype(BF16).reshape(n, 4, r4, width)
-    out_parts = [take(whole_out, c ^ i, 1) for i in range(4)]
-    out_got = scatter_first(out_parts)
-    d_q, dkv = attention_backward(
+    grad_middle, d_branch, do_t, grad_gain_two = middle_back(
+        d_second, middle, dy_own, gain_two, out_w
+    )
+    do_t = do_t.reshape(2, HEADS, HEAD_DIM, rows)
+    whole_out = side_product(attended_t, d_branch)
+    do_t, ffn_parts, whole_out = sync(do_t, ffn_parts, whole_out)
+    ffn_got = scatter_first(ffn_parts)
+    d_q, dkv_low, dkv_high, dkv_keep = attention_backward(
         q_blocks, slots, seg_q, seg_k, valid_k, cosine[:2], sine[:2], q_t, kv_all, o_t, do_t, lse
     )
-    d_q, dkv, ffn_got, out_got = sync(d_q, dkv, ffn_got, out_got)
-    dkv = dkv.reshape(4, 2, 2 * KV_HEADS, HEAD_DIM, rows)
-    dkv = [dkv[i] for i in range(4)]
-    dkv_got = scatter_first(dkv)
+    d_q, dkv_low, dkv_high, dkv_keep, ffn_got = sync(d_q, dkv_low, dkv_high, dkv_keep, ffn_got)
+    dkv_got = swap_x(dkv_low), swap_y(dkv_high)
+    own_out = lax.psum_scatter(
+        after(whole_out, dkv_low, own_gu), "fsdp", scatter_dimension=0, tiled=True
+    )
     q4, kv4 = q_width // 4, kv_width // 2
 
     def quarter(v, size, i):
@@ -686,74 +1064,73 @@
 
     d_q = d_q.reshape(2, q_width, rows)
     dq_parts = [quarter(d_q, q4, i) for i in range(4)]
-    out_sums = scatter_pass(out_parts, out_got)
-    dkv_got, dq_parts, out_sums = sync(dkv_got, dq_parts, out_sums)
-    dkv_own = scatter_last(*scatter_pass(dkv, dkv_got))
+    ffn_sums = scatter_pass(ffn_parts, ffn_got)
+    dkv_got, dq_parts, ffn_sums = sync(dkv_got, dq_parts, ffn_sums)
+    kept = dkv_keep.astype(F32)
+    low_sums, high_sums = kept[:2] + dkv_got[0].astype(F32), kept[2:] + dkv_got[1].astype(F32)
+    from_y, from_x = swap_y(low_sums[1].astype(BF16)), swap_x(high_sums[1].astype(BF16))
+    dkv_own = jnp.stack([low_sums[0] + from_y.astype(F32), high_sums[0] + from_x.astype(F32)])
+    dkv_own = dkv_own.reshape(2, 2 * KV_HEADS, HEAD_DIM, rows)
     dq_got = exchange_first(dq_parts)
     d_k = turn(dkv_own[:, :KV_HEADS], cosine[:2, None], -sine[:2, None]).astype(BF16)
     d_kv = jnp.concatenate([d_k, dkv_own[:, KV_HEADS:].astype(BF16)], axis=1)
     d_kv = d_kv.reshape(2, 2 * kv_width, rows)
     dkv_parts = [quarter(d_kv, kv4, i) for i in range(4)]
-    dkv_parts, out_sums = sync(dkv_parts, out_sums)
     dkv_got = exchange_first(dkv_parts)
+    dq_got, dkv_got = sync(dq_got, dkv_got)
+    dq_pieces = [dq_parts[0], *dq_got, *exchange_second(*dq_got)]
+    dkv_pieces = [dkv_parts[0], *dkv_got, *exchange_second(*dkv_got)]
+    dq_pieces, dkv_pieces, own_gu, own_out = sync(dq_pieces, dkv_pieces, own_gu, own_out)
+    gu_x, gu_y = swap_x(own_gu), swap_y(own_gu)
+    own_out = own_out.reshape(4, r4, width)
+    out_parts = [take(own_out, c ^ i, 0) for i in range(4)]
+    out_got = scatter_first(out_parts)
+    grad_qkv = project_grad(first_all.reshape(8, rows, width), dq_pieces, dkv_pieces)
+    grad_qkv = grad_qkv.reshape(nz, 2, r, q4 + kv4)
+    got_half = core_swap(take(grad_qkv, k ^ 1, 1))
+    pair_qkv = (take(grad_qkv, k, 1).astype(F32) + got_half.astype(F32)).astype(BF16)
+    pair_qkv, d_q, d_kv, ffn_sums, gu_x, gu_y, out_got = sync(
+        pair_qkv, d_q, d_kv, ffn_sums, gu_x, gu_y, out_got
+    )
+    own_qkv = z_scatter(pair_qkv).astype(BF16)
+
+    branch_ffn = scatter_last(*ffn_sums)
+    grad_tokens, grad_gain_one, late_sums = first_back(
+        d_q, d_kv, qkv_w, tokens_own, grad_middle, gain_one, live_rows
+    )
+    out_sums = scatter_pass(out_parts, out_got)
+    own_qkv, branch_ffn, out_sums, grad_tokens, grad_gain_one, late_sums = sync(
+        own_qkv, branch_ffn, out_sums, grad_tokens, grad_gain_one, late_sums
+    )
+
+    qkv_pieces = ctx_fetch_direct(own_qkv)
     own_out = scatter_last(*out_sums).astype(BF16)
-    dq_got, dkv_got = sync(dq_got, dkv_got)
-    dq_all = jnp.stack(exchange_second(dq_parts, *dq_got))
-    dkv_all = jnp.stack(exchange_second(dkv_parts, *dkv_got))
-    grad_q = ein("gbri,gbfr->if", first_all, dq_all).astype(BF16)
-    grad_kv = ein("gbri,gbfr->if", first_all, dkv_all).astype(BF16)
-    grad_qkv = jnp.concatenate([grad_q, grad_kv], axis=1).reshape(nz, 2, r, q4 + kv4)
-    own_out = own_out.reshape(nz, 2, r4, width)
-    grad_qkv, own_out, own_gu = sync(grad_qkv, own_out, own_gu)
-
-    def pair_sum(v):
-        got = core_swap(take(v, k ^ 1, 1))
-        return (take(v, k, 1).astype(F32) + got.astype(F32)).astype(BF16)
-
-    pair_qkv, pair_out = sync(pair_sum(grad_qkv), pair_sum(own_out))
-    own_qkv = z_scatter(pair_qkv).astype(BF16)
-    own_out = z_scatter(pair_out).astype(BF16)
-
-    d_q, d_kv, ffn_got, own_gu, _ = sync(d_q, d_kv, ffn_got, own_gu, pair_qkv)
-    branch_ffn = scatter_last(*scatter_pass(ffn_parts, ffn_got)).reshape(row_count, width)
-    result = middle + branch_ffn
-    gu_x, gu_y = swap_x(own_gu), swap_y(own_gu)
-    d_first = ein("bfr,if->bri", d_q, qkv_w[:, :q_width]) + ein(
-        "bfr,if->bri", d_kv, qkv_w[:, q_width:]
+    result, small = finish(
+        middle, branch_ffn, live_rows, grad_gain_one, grad_gain_two, early_sums, late_sums
     )
-    grad_in_norm, grad_gain_one = norm_backward(
-        d_first.reshape(row_count, width), gain_one, unit_one, inverse_one
-    )
-    grad_inputs = grad_middle + grad_in_norm
-    own_qkv, own_out, gu_x, gu_y, own_down = sync(own_qkv, own_out, gu_x, gu_y, own_down)
+    small = small + core_swap(small)
+    own_out, qkv_pieces, small, gu_x, gu_y = sync(own_out, qkv_pieces, small, gu_x, gu_y)
     hr = gu_x.shape[0] // 2
     gu_d = jnp.concatenate([swap_y(gu_x[:hr]), swap_x(gu_y[hr:])])
+    small = z_sum(small)
+    grad_q, grad_k, grad_v = join_columns(c_ref, qkv_pieces, q4, kv4)
+    gu_d, small, own_down, own_out = sync(gu_d, small, own_down, own_out)
+    small = sum(ctx_fetch_direct(small))
+    out_pieces = ctx_fetch_direct(own_out)
+    down_pieces = ctx_fetch_direct(own_down)
     grad_gate_w, grad_up_w = unpick_columns(c_ref, [own_gu, gu_x, gu_y, gu_d], n)
-    grad_down_w = ctx_gather(own_down, 0).reshape(4 * d4, width).astype(F32)
-    grad_out_w = ctx_gather(own_out, 0).reshape(r, width).astype(F32)
-    grad_qkv = ctx_gather(own_qkv, 1).astype(F32)
-    grad_q = grad_qkv[:, :, :q4].reshape(r, q_width)
-    grad_kv = grad_qkv[:, :, q4:].reshape(r, 2 * kv_width)
-
-    live_rows = live.reshape(row_count, 1).astype(F32)
-    squares = jnp.stack(
-        [
-            jnp.sum(live_rows * member * member)
-            for member in (result, grad_inputs, branch_attn, branch_ffn, middle)
-        ]
-        + [jnp.sum(live_rows)]
-    )
-    small = small_sum(jnp.concatenate([grad_gain_one, grad_gain_two, squares]))
-    gain_sums = lax.dynamic_slice_in_dim(small[: 2 * width].reshape(2, width), f * r, r, 1)
-    squares = small[2 * width :]
+    grad_down_w = in_order(down_pieces, 0).reshape(4 * d4, width).astype(F32)
+    grad_out_w = in_order(out_pieces, 0).reshape(r, width).astype(F32)
+    gain_sums = lax.dynamic_slice_in_dim(small[:2], f * r, r, 1)
+    squares = small[2:8, 0]
     spreads = jnp.sqrt(squares[:5] / (squares[5] * width))
     return (
-        result[None].astype(BF16),
-        grad_inputs[None].astype(BF16),
+        result.reshape(1, row_count, width),
+        grad_tokens.reshape(1, row_count, width),
         gain_sums[0],
         grad_q,
-        grad_kv[:, :kv_width],
-        grad_kv[:, kv_width:],
+        grad_k,
+        grad_v,
         grad_out_w,
         gain_sums[1],
         grad_gate_w,

time: 585 us -> 501 us (0.86)
  matrix products: 85.4 us -> 0 us
  Pallas kernels: 111 us -> 194 us
  local copies, waits for them, and re-layouts: 75.8 us -> 47.3 us
  other arithmetic: 66.5 us -> 43.1 us
  starting transfers between devices: 108 us -> 86.3 us
    pallas_call x0 -> x13, Pallas kernels: none -> 111 us  [the longest x3 38.1 us: feed_forward(): pl.pallas_call(kernel, grid=(count,), in_specs=[own(width), block(width),...]
    dot_general x17 -> x0, matrix products: 85.4 us -> none  [ein(): return jnp.einsum(spec, left, right, preferred_element_type=F32)]
    pallas_call x1, Pallas kernels: 42.7 us -> 26.4 us  [attention_forward(): pl.pallas_call(forward_kernel, grid_spec=pltpu.PrefetchScalarGridSpec(num...]
    ppermute x28 -> x25, starting transfers between devices: 43.1 us -> 29.5 us  [swap_x(): return lax.ppermute(v, 'ctx', [(i, i ^ 1) for i in range(4)])]
    pallas_call x1, Pallas kernels: 44.4 us -> 32.6 us  [attention_backward(): pl.pallas_call(backward_kernel, grid_spec=pltpu.PrefetchScalarGridSpec(nu...]
    ppermute x28 -> x25, starting transfers between devices: 47.5 us -> 37.2 us  [swap_y(): return lax.ppermute(v, 'ctx', [(i, i ^ 2) for i in range(4)])]
    ppermute x6 -> x3, waiting for transfers between devices: 15.2 us -> 6.83 us  [z_scatter(): got = lax.ppermute(sent, 'fsdp', [(i, (i + 2 * d) % n) for i in range(n)])]
    reduce_sum x4 -> x0, other arithmetic: 7.64 us -> none  [the longest x2 6.36 us: per_device(): jnp.sum(live_rows * member * member)]
  transfers between devices with their start and end apart: 77 -> 72, of which waited for: 29 -> 30; matrix products, arithmetic and copies ran while one was open for 32% -> 14% of each run, Pallas kernels for 19% -> 35%
where the time goes in v3:
time: 501 us; the launch traced here: 497 us
  Pallas kernels  194 us (39%)
  waiting for transfers between devices  111 us (22%)
  starting transfers between devices  86.3 us (17%)
  local copies, waits for them, and re-layouts  47.3 us (9%)
  other arithmetic  43.1 us (9%)
  between operations  15.6 us (3%)
    ppermute x25, waiting for transfers between devices, swap_x(): return lax.ppermute(v, 'ctx', [(i, i ^ 1) for i in range(4)])  50.2 us
    pallas_call x3, Pallas kernels, feed_forward(): pl.pallas_call(kernel, grid=(count,), in_specs=[own(width), block(width),...  38.1 us
    ppermute x25, starting transfers between devices, swap_y(): return lax.ppermute(v, 'ctx', [(i, i ^ 2) for i in range(4)])  37.2 us
    ppermute x25, waiting for transfers between devices, swap_y(): return lax.ppermute(v, 'ctx', [(i, i ^ 2) for i in range(4)])  35.8 us
    pallas_call x1, Pallas kernels, attention_backward(): pl.pallas_call(backward_kernel, grid_spec=pltpu.PrefetchScalarGridSpec(nu...  32.6 us
    ppermute x25, starting transfers between devices, swap_x(): return lax.ppermute(v, 'ctx', [(i, i ^ 1) for i in range(4)])  29.5 us
    pallas_call x1, Pallas kernels, attention_forward(): pl.pallas_call(forward_kernel, grid_spec=pltpu.PrefetchScalarGridSpec(num...  26.4 us
    pallas_call x2, Pallas kernels, transposed_product(): pl.pallas_call(kernel, grid=(rows // tile,), in_specs=[pl.BlockSpec((dept...  22.4 us
  transfers between devices with their start and end apart: 72, of which 30 were waited for; matrix products, arithmetic and copies ran while one was open for 14% of the time, Pallas kernels for 35%

profile of v3, /device:TPU:0, one launch (start us, length us, event | category | flops | bytes accessed | tf_op | source)
XLA Modules:
  0.0 497.3 jit_solution(5550412928673441145)
XLA Ops:
  23.8 8.5 %collective-permute-done.1 = bf16[160,512]{1,0:T(8,128)(2,1)S(1)} collective-permute-done((bf16[160,512]{1,0:T(8,128)(2,1)}, bf16[160,512]{1,0:T(8,128)(2,1)S(1)}, u32[]{:S(2)}, u32[]{:S(2)}) %collective-permute-start.1) | collective-permute-done | bytes 163872 | tf_op jit(solution)/shard_map/ppermute | solution.py:66
  39.8 13.2 %collective-permute-done.5 = bf16[4,160,512]{2,1,0:T(8,128)(2,1)S(1)} collective-permute-done((bf16[4,160,512]{2,1,0:T(8,128)(2,1)S(1)}, bf16[4,160,512]{2,1,0:T(8,128)(2,1)S(1)}, u32[]{:S(2)}, u32[]{:S(2)}) %collective-permute-start.5) | collective-permute-done | bytes 655392 | tf_op jit(solution)/shard_map/ppermute | solution.py:30
  79.5 9.2 %collective-permute-done.7 = bf16[1,216,1280]{2,1,0:T(8,128)(2,1)S(1)} collective-permute-done((bf16[1,216,1280]{2,1,0:T(8,128)(2,1)S(1)}, bf16[1,216,1280]{2,1,0:T(8,128)(2,1)S(1)}, u32[]{:S(2)}, u32[]{:S(2)}) %collective-permute-start.7) | collective-permute-done | bytes 552992 | tf_op jit(solution)/shard_map/ppermute | solution.py:34
  98.3 15.4 %shard_map.220 = (bf16[8,216,1280]{2,1,0:T(8,128)(2,1)}, bf16[2,20,64,216]{3,2,1,0:T(8,128)(2,1)}, bf16[8,10,64,216]{3,2,1,0:T(8,128)(2,1)}, bf16[1280,2048]{1,0:T(8,128)(2,1)}, f32[8,1280]{1,0:T(8,128)}) custom-call(s32[2]{0:T(128)} %pad_add_fusion.2.at_ref, bf16[8,216,1280]{2,1,0:T(8,128)(2,1)} %bitcast.168, ...), custom_call_target="tpu_custom_call" | custom-call | flops 8000000000 | bytes 25000000 | tf_op jit(solution)/shard_map/pallas_call | solution.py:472
  113.7 26.4 %shard_map.221 = (bf16[2,20,64,216]{3,2,1,0:T(8,128)(2,1)}, f32[2,5,4,216]{3,2,1,0:T(4,128)}) custom-call(s32[2]{0:T(128)} %pad_add_fusion.1.blocks_ref, s32[8]{0:T(128)} %fusion.23.slots_ref, s32[2,1,216]{2,1,0:T(1,128)} %broadcast_in_dim.41.seg_q_ref, s32[8,216,1]{2,1,0:T(8,128)} %broadcast_in_dim_reshape_squeeze.8.seg_k_ref, ...), custom_call_target="tpu_custom_call" | custom-call | flops 20000000000 | bytes 6000000 | tf_op jit(solution)/shard_map/pallas_call | solution.py:550
  141.6 5.8 %all-gather.6.cloned.1.call-done = bf16[2176,1280]{1,0:T(8,128)(2,1)} async-done(((bf16[272,1280]{1,0:T(8,128)(2,1)}), bf16[2176,1280]{1,0:T(8,128)(2,1)}) %all-gather.6.cloned.1.call-update) | async-done | bytes 5570576 | tf_op jit(solution)/shard_map/all_gather | solution.py:986
  151.2 6.7 %shard_map.223 = (f32[2,216,1280]{2,1,0:T(8,128)}, bf16[2,216,1280]{2,1,0:T(8,128)(2,1)}, f32[8,128]{1,0:T(8,128)}) custom-call(bf16[2,216,1280]{2,1,0:T(8,128)(2,1)} %bitcast.151, bf16[2,1280,216]{2,1,0:T(8,128)(2,1)} %bitcast.147, bf16[1280,1280]{1,0:T(8,128)(2,1)} %bitcast.137, f32[1,1280]{1,0:T(1,128)} %get-tuple-element.355.gain_ref, ...), custom_call_target="tpu_custom_call" | custom-call | tf_op jit(solution)/shard_map/pallas_call | solution.py:758
  167.8 10.6 %shard_map.224 = (bf16[4,432,1280]{2,1,0:T(8,128)(2,1)}, bf16[4,432,896]{2,1,0:T(8,128)(2,1)}, bf16[4,432,1792]{2,1,0:T(8,128)(2,1)}, bf16[1,432,1280]{2,1,0:T(8,128)(2,1)}) custom-call(bf16[1,432,1280]{2,1,0:T(8,128)(2,1)} %bitcast.198, bf16[4,432,1280]{2,1,0:T(8,128)(2,1)} %pad_maximum_fusion.1.dy_ref, ...), custom_call_target="tpu_custom_call" | custom-call | flops 4954521600 | bytes 13627392 | tf_op jit(solution)/shard_map/pallas_call | solution.py:641
  178.4 6.3 %collective-permute-done.15 = bf16[2,216,1280]{2,1,0:T(8,128)(2,1)S(1)} collective-permute-done((bf16[2,216,1280]{2,1,0:T(8,128)(2,1)}, bf16[2,216,1280]{2,1,0:T(8,128)(2,1)S(1)}, u32[]{:S(2)}, u32[]{:S(2)}) %collective-permute-start.15) | collective-permute-done | bytes 1105952 | tf_op jit(solution)/shard_map/ppermute | solution.py:30
  190.4 17.0 %shard_map.225 = (bf16[4,432,1280]{2,1,0:T(8,128)(2,1)}, bf16[4,432,896]{2,1,0:T(8,128)(2,1)}, bf16[4,432,1792]{2,1,0:T(8,128)(2,1)}, bf16[2,432,1280]{2,1,0:T(8,128)(2,1)}) custom-call(bf16[2,432,1280]{2,1,0:T(8,128)(2,1)} %pad_maximum_fusion.3.x_ref, ...), custom_call_target="tpu_custom_call", output_to_operand_aliasing={{0}: (4, {}), {1}: (5, {}), {2}: (6, {})} | custom-call | flops 9909043200 | bytes 20373504 | tf_op jit(solution)/shard_map/pallas_call | solution.py:641
  208.5 10.6 %shard_map.226 = (bf16[4,432,1280]{2,1,0:T(8,128)(2,1)}, bf16[4,432,896]{2,1,0:T(8,128)(2,1)}, bf16[4,432,1792]{2,1,0:T(8,128)(2,1)}, bf16[1,432,1280]{2,1,0:T(8,128)(2,1)}) custom-call(bf16[1,432,1280]{2,1,0:T(8,128)(2,1)} %bitcast.167, bf16[4,432,1280]{2,1,0:T(8,128)(2,1)} %pad_maximum_fusion.1.dy_ref, ...), custom_call_target="tpu_custom_call", output_to_operand_aliasing={{0}: (4, {}), {1}: (5, {}), {2}: (6, {})} | custom-call | flops 4954521600 | bytes 13627392 | tf_op jit(solution)/shard_map/pallas_call | solution.py:641
  224.4 13.4 %shard_map.227 = bf16[1280,1792]{1,0:T(8,128)(2,1)} custom-call(bf16[1728,1280]{1,0:T(8,128)(2,1)} %bitcast.146, bf16[1728,1792]{1,0:T(8,128)(2,1)} %bitcast.141), custom_call_target="tpu_custom_call" | custom-call | tf_op jit(solution)/shard_map/pallas_call | solution.py:682
  237.8 8.4 %shard_map.228 = bf16[1728,1280]{1,0:T(8,128)(2,1)} custom-call(bf16[1728,896]{1,0:T(8,128)(2,1)} %bitcast.139, bf16[896,1280]{1,0:T(8,128)(2,1)} %bitcast.145), custom_call_target="tpu_custom_call" | custom-call | tf_op jit(solution)/shard_map/pallas_call | solution.py:700
  254.4 8.9 %shard_map.229 = bf16[896,1280]{1,0:T(8,128)(2,1)} custom-call(bf16[1728,896]{1,0:T(8,128)(2,1)} %bitcast.140, bf16[1728,1280]{1,0:T(8,128)(2,1)} %bitcast.136), custom_call_target="tpu_custom_call" | custom-call | tf_op jit(solution)/shard_map/pallas_call | solution.py:682
  271.9 8.0 %shard_map.230 = (f32[2,216,1280]{2,1,0:T(8,128)}, bf16[2,216,1280]{2,1,0:T(8,128)(2,1)}, bf16[2,1280,216]{2,1,0:T(8,128)(2,1)}, f32[1,1280]{1,0:T(1,128)}) custom-call(f32[2,216,1280]{2,1,0:T(8,128)} %pad_maximum_fusion.4.d_ref, f32[2,216,1280]{2,1,0:T(8,128)} %get-tuple-element.175.m_ref, bf16[2,216,1280]{2,1,0:T(8,128)(2,1)} %bitcast.174, ...), custom_call_target="tpu_custom_call" | custom-call | tf_op jit(solution)/shard_map/pallas_call | solution.py:807
  279.9 5.4 %shard_map.231 = bf16[1280,1280]{1,0:T(8,128)(2,1)} custom-call(bf16[2,1280,216]{2,1,0:T(8,128)(2,1)} %bitcast.148, bf16[2,216,1280]{2,1,0:T(8,128)(2,1)} %get-tuple-element.213.right_ref), custom_call_target="tpu_custom_call" | custom-call | tf_op jit(solution)/shard_map/pallas_call | solution.py:717
  293.9 32.6 %shard_map.232 = (bf16[2,20,64,216]{3,2,1,0:T(8,128)(2,1)}, bf16[2,2,5,64,216]{4,3,2,1,0:T(8,128)(2,1)}, bf16[2,2,5,64,216]{4,3,2,1,0:T(8,128)(2,1)}, bf16[4,2,5,64,216]{4,3,2,1,0:T(8,128)(2,1)}) custom-call(s32[2]{0:T(128)} %pad_add_fusion.1.blocks_ref, s32[8]{0:T(128)} %fusion.23.slots_ref, s32[2,1,216]{2,1,0:T(1,128)} %broadcast_in_dim.41.seg_q_ref, ...), custom_call_target="tpu_custom_call" | custom-call | tf_op jit(solution)/shard_map/pallas_call | solution.py:586
  326.6 5.2 %collective-permute-start.25 = (bf16[2,2,5,64,216]{4,3,2,1,0:T(8,128)(2,1)}, bf16[2,2,5,64,216]{4,3,2,1,0:T(8,128)(2,1)S(1)}, u32[]{:S(2)}, u32[]{:S(2)}) collective-permute-start(bf16[2,2,5,64,216]{4,3,2,1,0:T(8,128)(2,1)} %get-tuple-element.223), channel_id=1, source_target_pairs={{0,8},{8,0},{16,24},{24,16},{1,9},{9,1},{17,25},{25,17},{2,10},{10... | collective-permute-start | bytes 1658888 | tf_op jit(solution)/shard_map/ppermute | solution.py:30
  352.8 11.3 %collective-permute-done.30 = bf16[2,5,64,216]{3,2,1,0:T(8,128)(2,1)S(1)} collective-permute-done((bf16[2,5,64,216]{3,2,1,0:T(8,128)(2,1)S(1)}, bf16[2,5,64,216]{3,2,1,0:T(8,128)(2,1)S(1)}, u32[]{:S(2)}, u32[]{:S(2)}) %collective-permute-start.30) | collective-permute-done | bytes 276512 | tf_op jit(solution)/shard_map/ppermute | solution.py:30
  390.5 6.9 %shard_map.233 = bf16[1280,480]{1,0:T(8,128)(2,1)} custom-call(bf16[8,216,1280]{2,1,0:T(8,128)(2,1)} %get-tuple-element.176.first_ref, bf16[2,320,216]{2,1,0:T(8,128)(2,1)} %get-tuple-element.243.refs_0_, bf16[3,320,216]{2,1,0:T(8,128)(2,1)} %copy-done.28, bf16[3,320,216]{2,1,0:T(8,128)(2,1)} %copy-done.29, ...), custom_call_target="tpu_custom_call" | custom-call | tf_op jit(solution)/shard_map/pallas_call | solution.py:522
  411.7 9.3 %shard_map.234 = (bf16[2,216,1280]{2,1,0:T(8,128)(2,1)}, f32[1,1280]{1,0:T(1,128)}, f32[8,128]{1,0:T(8,128)}) custom-call(bf16[2,1280,216]{2,1,0:T(8,128)(2,1)} %bitcast.165, bf16[2,640,216]{2,1,0:T(8,128)(2,1)} %bitcast.156, bf16[1280,2048]{1,0:T(8,128)(2,1)} %get-tuple-element.268.w_ref, bf16[2,216,1280]{2,1,0:T(8,128)(2,1)} %bitcast.152, ...), custom_call_target="tpu_custom_call" | custom-call | tf_op jit(solution)/shard_map/pallas_call | solution.py:849
  420.9 6.8 %collective-permute-done.43 = bf16[160,480]{1,0:T(8,128)(2,1)} collective-permute-done((bf16[160,480]{1,0:T(8,128)(2,1)}, bf16[160,480]{1,0:T(8,128)(2,1)}, u32[]{:S(2)}, u32[]{:S(2)}) %collective-permute-start.43) | collective-permute-done | bytes 153632 | tf_op jit(solution)/shard_map/ppermute | solution.py:82
  444.0 5.9 %collective-permute-done.47 = bf16[20,1280]{1,0:T(8,128)(2,1)S(1)} collective-permute-done((bf16[20,1280]{1,0:T(8,128)(2,1)S(1)}, bf16[20,1280]{1,0:T(8,128)(2,1)S(1)}, u32[]{:S(2)}, u32[]{:S(2)}) %collective-permute-start.47) | collective-permute-done | bytes 51232 | tf_op jit(solution)/shard_map/ppermute | solution.py:34
  469.2 4.9 shard_map.237
  (369 shorter events, 224.9 us)
Async XLA Ops:
  7.2 134.4 %all-gather.4.cloned.1.call-start = ((), (), s32[]{:S(2)}) async-start(), calls=%async_computation.3 | async-start | bytes 5160960 | tf_op jit(solution)/shard_map/all_gather | solution.py:990
  7.2 27.6 %collective-permute-start.3 = (bf16[2,216,1280]{2,1,0:T(8,128)(2,1)}, bf16[2,216,1280]{2,1,0:T(8,128)(2,1)S(1)}, u32[]{:S(2)}, u32[]{:S(2)}) collective-permute-start(bf16[2,216,1280]{2,1,0:T(8,128)(2,1)} %bitcast.149), channel_id=1, source_target_pairs={{0,8},{8,0},{16,24},{24,16},{1,9},{9,1},{17,25},{25,17},{2,10},{10... | collective-permute-start | bytes 3317768 | tf_op jit(solution)/shard_map/ppermute | solution.py:30
  10.2 26.2 %collective-permute-start.4 = (bf16[2,216,1280]{2,1,0:T(8,128)(2,1)}, bf16[2,216,1280]{2,1,0:T(8,128)(2,1)}, u32[]{:S(2)}, u32[]{:S(2)}) collective-permute-start(bf16[2,216,1280]{2,1,0:T(8,128)(2,1)} %bitcast.150), channel_id=1, source_target_pairs={{0,16},{8,24},{16,0},{24,8},{1,17},{9,25},{17,1},{25,9},{2,18},{10... | collective-permute-start | bytes 3317768 | tf_op jit(solution)/shard_map/ppermute | solution.py:34
  36.4 111.0 %all-gather.6.cloned.1.call-start = ((), (), s32[]{:S(2)}) async-start(), calls=%async_computation.7 | async-start | bytes 6266880 | tf_op jit(solution)/shard_map/all_gather | solution.py:986
  37.5 289.0 %reduce-scatter.4.cloned.1.call-start = ((), (), s32[]{:S(2)}) async-start(), calls=%async_computation.4 | async-start | bytes 5160960 | tf_op jit(solution)/shard_map/reduce_scatter | solution.py:1039
  67.3 30.9 %collective-permute-start.11 = (bf16[4,4,160,512]{3,2,1,0:T(8,128)(2,1)}, bf16[4,4,160,512]{3,2,1,0:T(8,128)(2,1)}, u32[]{:S(2)}, u32[]{:S(2)}) collective-permute-start(bf16[4,4,160,512]{3,2,1,0:T(8,128)(2,1)} %pad_maximum_fusion.2.mine_ref), channel_id=1, source_target_pairs={{0,1},{1,0},{2,3},{3,2},{4,5},{5,4},{6,7},{7,6},{8,9},{9,8},{10,11... | collective-permute-start | bytes 7864328 | tf_op jit(solution)/shard_map/ppermute | solution.py:26
  91.2 50.3 %collective-permute-start.12 = (bf16[2,216,1280]{2,1,0:T(8,128)(2,1)S(1)}, bf16[2,216,1280]{2,1,0:T(8,128)(2,1)S(1)}, u32[]{:S(2)}, u32[]{:S(2)}) collective-permute-start(bf16[2,216,1280]{2,1,0:T(8,128)(2,1)S(1)} %bitcast.175), channel_id=1, source_target_pairs={{0,8},{8,0},{16,24},{24,16},{1,9},{9,1},{17,25},{25,17},{2,10},{10... | collective-permute-start | bytes 3317768 | tf_op jit(solution)/shard_map/ppermute | solution.py:30
  91.9 49.7 %collective-permute-start.13 = (bf16[2,216,1280]{2,1,0:T(8,128)(2,1)S(1)}, bf16[2,216,1280]{2,1,0:T(8,128)(2,1)}, u32[]{:S(2)}, u32[]{:S(2)}) collective-permute-start(bf16[2,216,1280]{2,1,0:T(8,128)(2,1)S(1)} %bitcast.176), channel_id=1, source_target_pairs={{0,16},{8,24},{16,0},{24,8},{1,17},{9,25},{17,1},{25,9},{2,18},{10... | collective-permute-start | bytes 3317768 | tf_op jit(solution)/shard_map/ppermute | solution.py:34
  92.7 48.9 %collective-permute-start.14 = (bf16[2,216,1280]{2,1,0:T(8,128)(2,1)S(1)}, bf16[2,216,1280]{2,1,0:T(8,128)(2,1)}, u32[]{:S(2)}, u32[]{:S(2)}) collective-permute-start(bf16[2,216,1280]{2,1,0:T(8,128)(2,1)S(1)} %bitcast.177), channel_id=1, source_target_pairs={{0,24},{8,16},{16,8},{24,0},{1,25},{9,17},{17,9},{25,1},{2,26},{10... | collective-permute-start | bytes 3317768 | tf_op jit(solution)/shard_map/ppermute | solution.py:104
  157.9 26.8 %collective-permute-start.15 = (bf16[2,216,1280]{2,1,0:T(8,128)(2,1)}, bf16[2,216,1280]{2,1,0:T(8,128)(2,1)S(1)}, u32[]{:S(2)}, u32[]{:S(2)}) collective-permute-start(bf16[2,216,1280]{2,1,0:T(8,128)(2,1)} %get-tuple-element.177), channel_id=1, source_target_pairs={{0,8},{8,0},{16,24},{24,16},{1,9},{9,1},{17,25},{25,17},{2,10},{10... | collective-permute-start | bytes 3317768 | tf_op jit(solution)/shard_map/ppermute | solution.py:30
  159.4 26.5 %collective-permute-start.16 = (bf16[2,216,1280]{2,1,0:T(8,128)(2,1)}, bf16[2,216,1280]{2,1,0:T(8,128)(2,1)S(1)}, u32[]{:S(2)}, u32[]{:S(2)}) collective-permute-start(bf16[2,216,1280]{2,1,0:T(8,128)(2,1)} %get-tuple-element.177), channel_id=1, source_target_pairs={{0,16},{8,24},{16,0},{24,8},{1,17},{9,25},{17,1},{25,9},{2,18},{10... | collective-permute-start | bytes 3317768 | tf_op jit(solution)/shard_map/ppermute | solution.py:34
  185.9 21.5 %collective-permute-start.18 = (bf16[1,216,1280]{2,1,0:T(8,128)(2,1)S(1)}, bf16[1,216,1280]{2,1,0:T(8,128)(2,1)S(1)}, u32[]{:S(2)}, u32[]{:S(2)}) collective-permute-start(bf16[1,216,1280]{2,1,0:T(8,128)(2,1)S(1)} %slice.286), channel_id=1, source_target_pairs={{0,8},{8,0},{16,24},{24,16},{1,9},{9,1},{17,25},{25,17},{2,10},{10... | collective-permute-start | bytes 1658888 | tf_op jit(solution)/shard_map/ppermute | solution.py:30
  187.4 20.0 %collective-permute-start.17 = (bf16[1,216,1280]{2,1,0:T(8,128)(2,1)}, bf16[1,216,1280]{2,1,0:T(8,128)(2,1)S(1)}, u32[]{:S(2)}, u32[]{:S(2)}) collective-permute-start(bf16[1,216,1280]{2,1,0:T(8,128)(2,1)} %slice.285), channel_id=1, source_target_pairs={{0,16},{8,24},{16,0},{24,8},{1,17},{9,25},{17,1},{25,9},{2,18},{10... | collective-permute-start | bytes 1658888 | tf_op jit(solution)/shard_map/ppermute | solution.py:34
  221.2 25.0 %collective-permute-start.19 = (bf16[2,216,1280]{2,1,0:T(8,128)(2,1)S(1)}, bf16[2,216,1280]{2,1,0:T(8,128)(2,1)S(1)}, u32[]{:S(2)}, u32[]{:S(2)}) collective-permute-start(bf16[2,216,1280]{2,1,0:T(8,128)(2,1)S(1)} %pad_maximum_fusion.7), channel_id=1, source_target_pairs={{0,8},{8,0},{16,24},{24,16},{1,9},{9,1},{17,25},{25,17},{2,10},{10... | collective-permute-start | bytes 3317768 | tf_op jit(solution)/shard_map/ppermute | solution.py:30
  223.8 24.8 %collective-permute-start.20 = (bf16[2,216,1280]{2,1,0:T(8,128)(2,1)}, bf16[2,216,1280]{2,1,0:T(8,128)(2,1)S(1)}, u32[]{:S(2)}, u32[]{:S(2)}) collective-permute-start(bf16[2,216,1280]{2,1,0:T(8,128)(2,1)} %pad_maximum_fusion.8), channel_id=1, source_target_pairs={{0,16},{8,24},{16,0},{24,8},{1,17},{9,25},{17,1},{25,9},{2,18},{10... | collective-permute-start | bytes 3317768 | tf_op jit(solution)/shard_map/ppermute | solution.py:34
  248.6 139.9 %reduce-scatter.6.cloned.1.call-start = ((), (), s32[]{:S(2)}) async-start(), calls=%async_computation.5 | async-start | bytes 3686400 | tf_op jit(solution)/shard_map/reduce_scatter | solution.py:1057
  286.8 39.6 %collective-permute-start.23 = (bf16[2,216,1280]{2,1,0:T(8,128)(2,1)S(1)}, bf16[2,216,1280]{2,1,0:T(8,128)(2,1)S(1)}, u32[]{:S(2)}, u32[]{:S(2)}) collective-permute-start(bf16[2,216,1280]{2,1,0:T(8,128)(2,1)S(1)} %pad_maximum_fusion.9), channel_id=1, source_target_pairs={{0,8},{8,0},{16,24},{24,16},{1,9},{9,1},{17,25},{25,17},{2,10},{10... | collective-permute-start | bytes 3317768 | tf_op jit(solution)/shard_map/ppermute | solution.py:30
  289.4 37.0 %collective-permute-start.24 = (bf16[2,216,1280]{2,1,0:T(8,128)(2,1)}, bf16[2,216,1280]{2,1,0:T(8,128)(2,1)S(1)}, u32[]{:S(2)}, u32[]{:S(2)}) collective-permute-start(bf16[2,216,1280]{2,1,0:T(8,128)(2,1)} %pad_maximum_fusion.10), channel_id=1, source_target_pairs={{0,16},{8,24},{16,0},{24,8},{1,17},{9,25},{17,1},{25,9},{2,18},{10... | collective-permute-start | bytes 3317768 | tf_op jit(solution)/shard_map/ppermute | solution.py:34
  326.5 137.0 %reduce-scatter.8.cloned.1.call-start = ((), (), s32[]{:S(2)}) async-start(), calls=%async_computation.6 | async-start | bytes 2580480 | tf_op jit(solution)/shard_map/reduce_scatter | solution.py:1040
  347.7 22.0 %collective-permute-start.27 = (bf16[3,320,216]{2,1,0:T(8,128)(2,1)S(1)}, bf16[3,320,216]{2,1,0:T(8,128)(2,1)S(1)}, u32[]{:S(2)}, u32[]{:S(2)}) collective-permute-start(bf16[3,320,216]{2,1,0:T(8,128)(2,1)S(1)} %pad_maximum_fusion.16), channel_id=1, source_target_pairs={{0,8},{8,0},{16,24},{24,16},{1,9},{9,1},{17,25},{25,17},{2,10},{10... | collective-permute-start | bytes 1244168 | tf_op jit(solution)/shard_map/ppermute | solution.py:30
  405.4 22.4 %collective-permute-start.43 = (bf16[160,480]{1,0:T(8,128)(2,1)}, bf16[160,480]{1,0:T(8,128)(2,1)}, u32[]{:S(2)}, u32[]{:S(2)}) collective-permute-start(bf16[160,480]{1,0:T(8,128)(2,1)} %get-tuple-element.334), channel_id=1, source_target_pairs={{0,4},{1,5},{2,6},{3,7},{4,0},{5,1},{6,2},{7,3},{8,12},{9,13},{10,... | collective-permute-start | bytes 460808 | tf_op jit(solution)/shard_map/ppermute | solution.py:82
  406.6 21.2 %collective-permute-start.42 = (bf16[160,480]{1,0:T(8,128)(2,1)}, bf16[160,480]{1,0:T(8,128)(2,1)}, u32[]{:S(2)}, u32[]{:S(2)}) collective-permute-start(bf16[160,480]{1,0:T(8,128)(2,1)} %get-tuple-element.332), channel_id=1, source_target_pairs={{0,2},{1,3},{2,4},{3,5},{4,6},{5,7},{6,0},{7,1},{8,10},{9,11},{10,... | collective-permute-start | bytes 460808 | tf_op jit(solution)/shard_map/ppermute | solution.py:82
  408.6 20.3 %collective-permute-start.46 = (bf16[1,216,1280]{2,1,0:T(8,128)(2,1)}, bf16[1,216,1280]{2,1,0:T(8,128)(2,1)}, u32[]{:S(2)}, u32[]{:S(2)}) collective-permute-start(bf16[1,216,1280]{2,1,0:T(8,128)(2,1)} %get-tuple-element.263), channel_id=1, source_target_pairs={{0,8},{8,0},{16,24},{24,16},{1,9},{9,1},{17,25},{25,17},{2,10},{10... | collective-permute-start | bytes 1658888 | tf_op jit(solution)/shard_map/ppermute | solution.py:30
  409.1 21.0 %collective-permute-start.45 = (bf16[1,216,1280]{2,1,0:T(8,128)(2,1)}, bf16[1,216,1280]{2,1,0:T(8,128)(2,1)}, u32[]{:S(2)}, u32[]{:S(2)}) collective-permute-start(bf16[1,216,1280]{2,1,0:T(8,128)(2,1)} %get-tuple-element.261), channel_id=1, source_target_pairs={{0,16},{8,24},{16,0},{24,8},{1,17},{9,25},{17,1},{25,9},{2,18},{10... | collective-permute-start | bytes 1658888 | tf_op jit(solution)/shard_map/ppermute | solution.py:34
  (97 other events, 811.9 us)
Sparse Core Ops, SparseCore 0:
  36.6 50.9 all-gather.3
  89.8 57.5 all-gather.5
  248.8 50.6 reduce-scatter.3
  326.6 46.7 reduce-scatter.5
  382.8 39.6 reduce-scatter.7

commit v4 on v3

--- a/solution.py
+++ b/solution.py
@@ -139,10 +139,6 @@
     return swap_x(to_x), swap_y(to_y)
 
 
-def exchange_second(got_x, got_y):
-    return swap_y(got_x[2:]), swap_x(got_y[2:])
-
-
 def z_sum(v):
     n = lax.axis_size("fsdp")
     if n == 8:
@@ -268,7 +264,7 @@
         (seg_q == seg_k)
         & (distance >= 0)
         & (distance < WINDOW)
-        & ((valid_k == 1) | (distance == 0))
+        & ((valid_k == 1.0) | (distance == 0))
     )
     return jnp.where(allowed, 0.0, MASKED).astype(F32)
 
@@ -280,6 +276,11 @@
 
 def dot(a, b, dims):
     return lax.dot_general(a, b, (dims, ((), ())), preferred_element_type=F32)
+
+
+def column(row):
+    size = row.shape[1]
+    return jnp.broadcast_to(row, (size, size)).T
 
 
 def fill_bias(blocks_ref, seg_q_ref, seg_k_ref, valid_k_ref, bias_ref, rows):
@@ -289,7 +290,7 @@
 
         def body(kb, _):
             bias_ref[side, kb - lo] = pair_bias(
-                b, kb, rows, seg_q_ref[side], seg_k_ref[kb], valid_k_ref[kb]
+                b, kb, rows, seg_q_ref[side], column(seg_k_ref[kb]), column(valid_k_ref[kb])
             )
             return 0
 
@@ -408,9 +409,10 @@
             target[i, 1, 0] = dv_ref[slot].astype(BF16)
 
 
-def project(c, f, tokens_all, mine, other, cosine, sine, q_width):
-    blocks, rows, width = tokens_all.shape
-    _, nz, r, cols = mine.shape
+def project(c, f, tokens, mine, other, cosine, sine, q_width):
+    _, rows, width = tokens[0].shape
+    blocks = 8
+    _, nz, r, cols = mine[0].shape
     half = HEAD_DIM // 2
     kv_heads = 2 * KV_HEADS
     gains_at = q_width + kv_heads * HEAD_DIM
@@ -419,29 +421,48 @@
         a, b = flat_t[at : at + half], flat_t[at + half : at + HEAD_DIM]
         return jnp.concatenate([a * cos - b * sin, a * sin + b * cos], axis=0)
 
-    def kernel(
-        at_ref, x_ref, mine_ref, other_ref, cos_ref, sin_ref,
-        first_ref, q_ref, kv_ref, w_ref, gain_ref,
-    ):
+    def kernel(at_ref, *refs):
+        token_refs, mine_refs, other_refs = refs[:5], refs[5:7], refs[7:9]
+        cos_ref, sin_ref, first_ref, q_ref, kv_ref, w_ref, gain_ref, x_ref = refs[9:]
+
         @pl.when(pl.program_id(0) == 0)
         def _():
             for core in range(2):
-
-                @pl.when(at_ref[1] % 2 == core)
-                def _():
-                    for z in range(nz):
-                        step = (at_ref[1] // 2 - z + nz) % nz
-                        for q in range(4):
+                for q in range(4):
+                    step = q ^ at_ref[0]
+
+                    def fill(index, which, core=core, q=q):
+                        for z in range(nz):
+                            z_step = (at_ref[1] // 2 - z + nz) % nz
                             for kk in range(2):
-                                source = mine_ref if kk == core else other_ref
+                                source = mine_refs if kk == core else other_refs
                                 at = (2 * z + kk) * r
-                                w_ref[at : at + r, q * cols : (q + 1) * cols] = source[
-                                    q ^ at_ref[0], step
+                                w_ref[at : at + r, q * cols : (q + 1) * cols] = source[which][
+                                    index, z_step
                                 ]
 
+                    @pl.when((at_ref[1] % 2 == core) & (step < 3))
+                    def _(step=step, fill=fill):
+                        fill(step, 0)
+
+                    @pl.when((at_ref[1] % 2 == core) & (step == 3))
+                    def _(fill=fill):
+                        fill(0, 1)
+
             gain_ref[...] = w_ref[:, gains_at:].astype(F32).T[:8]
 
-        x = x_ref[...].astype(F32)
+        for i in range(3):
+
+            @pl.when(pl.program_id(0) == i)
+            def _(i=i):
+                x_ref[...] = token_refs[i][...].astype(F32)
+
+        @pl.when(pl.program_id(0) == 3)
+        def _():
+            x_ref[0] = token_refs[3][0].astype(F32)
+            x_ref[1] = token_refs[4][0].astype(F32)
+
+        x = x_ref[...]
         inverse = lax.rsqrt(jnp.mean(x * x, axis=-1, keepdims=True) + EPSILON)
         scaled = x * inverse * gain_ref[0:1][None]
         first_ref[...] = scaled.astype(BF16)
@@ -468,26 +489,21 @@
                     q_ref[i, h] = (turned_q.astype(F32) * 0.125).astype(BF16)
 
     table = pl.BlockSpec((2, half, rows), lambda i, s: (i, 0, 0))
-    piece = pl.BlockSpec(mine.shape, lambda i, s: (0, 0, 0, 0))
+    operands = [*tokens, *mine, *other]
     return pl.pallas_call(
         kernel,
         grid_spec=pltpu.PrefetchScalarGridSpec(
             num_scalar_prefetch=1,
             grid=(blocks // 2,),
-            in_specs=[
-                pl.BlockSpec((2, rows, width), lambda i, s: (i, 0, 0)),
-                piece,
-                piece,
-                table,
-                table,
-            ],
+            in_specs=[fixed(v.shape) for v in operands] + [table, table],
             out_specs=[
                 pl.BlockSpec((2, rows, width), lambda i, s: (i, 0, 0)),
-                pl.BlockSpec((2, HEADS, HEAD_DIM, rows), lambda i, s: (0, 0, 0, 0)),
+                fixed((2, HEADS, HEAD_DIM, rows)),
                 pl.BlockSpec((2, kv_heads, HEAD_DIM, rows), lambda i, s: (i, 0, 0, 0)),
-                pl.BlockSpec((2 * nz * r, 4 * cols), lambda i, s: (0, 0)),
-                pl.BlockSpec((8, width), lambda i, s: (0, 0)),
+                fixed((2 * nz * r, 4 * cols)),
+                fixed((8, width)),
             ],
+            scratch_shapes=[pltpu.VMEM((2, rows, width), F32)],
         ),
         out_shape=[
             jax.ShapeDtypeStruct((blocks, rows, width), BF16),
@@ -500,25 +516,26 @@
         cost_estimate=pl.CostEstimate(
             flops=8_000_000_000, bytes_accessed=25_000_000, transcendentals=0
         ),
-    )(jnp.stack([c, f]).astype(jnp.int32), tokens_all, mine, other, cosine, sine)
-
-
-def project_grad(first_all, dq_pieces, dkv_pieces):
+    )(jnp.stack([c, f]).astype(jnp.int32), *operands, cosine, sine)
+
+
+def project_grad(first_all, dq_pieces, dkv_pieces, diagonal):
     _, rows, width = first_all.shape
     q4, kv4 = dq_pieces[0].shape[1], dkv_pieces[0].shape[1]
 
     def kernel(first_ref, *refs):
         out_ref = refs[-1]
         total = None
-        for i, (piece, at) in enumerate(
-            ((0, 0), (0, 1), (1, 0), (1, 1), (2, 0), (2, 1), (3, 0), (4, 0))
-        ):
-            turned = jnp.concatenate([refs[piece][at], refs[5 + piece][at]], axis=0)
+        for i in range(8):
+            if i < 6:
+                turned = jnp.concatenate([refs[i // 2][i % 2], refs[3 + i // 2][i % 2]], axis=0)
+            else:
+                turned = refs[i][0]
             term = dot(turned, first_ref[i], ((1,), (0,)))
             total = term if total is None else total + term
         out_ref[...] = total.T.astype(BF16)
 
-    operands = [first_all, *dq_pieces, *dkv_pieces]
+    operands = [first_all, *dq_pieces, *dkv_pieces, *diagonal]
     return pl.pallas_call(
         kernel,
         grid=(1,),
@@ -537,8 +554,8 @@
     stat_spec = pl.BlockSpec((2, 1, GROUP, rows), lambda g, *_: (0, g, 0, 0))
     seg_specs = [
         pl.BlockSpec((2, 1, rows), lambda g, *_: (0, 0, 0)),
-        pl.BlockSpec((blocks, rows, 1), lambda g, *_: (0, 0, 0)),
-        pl.BlockSpec((blocks, rows, 1), lambda g, *_: (0, 0, 0)),
+        pl.BlockSpec((blocks, 1, rows), lambda g, *_: (0, 0, 0)),
+        pl.BlockSpec((blocks, 1, rows), lambda g, *_: (0, 0, 0)),
     ]
     return q_spec, k_spec, v_spec, stat_spec, seg_specs
 
@@ -742,11 +759,12 @@
     return pl.BlockSpec((1, *shape), lambda i: (i, 0, 0))
 
 
-def out_project(tokens, attended_t, weights, gain, live):
+def out_project(tokens, attended_t, weights, gain, live, r):
     sides, rows, width = tokens.shape
 
     def kernel(x_ref, att_ref, w_ref, gain_ref, live_ref, middle_ref, second_ref, sums_ref):
-        branch = dot(att_ref[0], w_ref[...], ((0,), (0,)))
+        w_out = w_ref[:, :r].reshape(width, width)
+        branch = dot(att_ref[0], w_out, ((0,), (0,)))
         middle = x_ref[0].astype(F32) + branch
         middle_ref[0] = middle
         inverse = lax.rsqrt(jnp.mean(middle * middle, axis=-1, keepdims=True) + EPSILON)
@@ -958,9 +976,9 @@
     valid_blocks = valid[0].reshape(blocks, rows)
     seg_q = jnp.stack([take(seg_blocks, q_blocks[0], 0), take(seg_blocks, q_blocks[1], 0)])
     live = jnp.stack([take(valid_blocks, q_blocks[0], 0), take(valid_blocks, q_blocks[1], 0)])
-    seg_q = seg_q[:, None, :]
-    seg_k = seg_blocks[:, :, None]
-    valid_k = valid_blocks[:, :, None]
+    seg_q = seg_q[:, None, :].astype(F32)
+    seg_k = seg_blocks[:, None, :].astype(F32)
+    valid_k = valid_blocks[:, None, :].astype(F32)
     owners = c ^ jnp.arange(4, dtype=jnp.int32)
     block_of = jnp.stack([owners, blocks - 1 - owners], axis=1)
     every = jnp.arange(blocks, dtype=jnp.int32)
@@ -989,18 +1007,30 @@
     gu_shard = after(pick_columns(c_ref, w_gate, w_up, n), qkv_z)
     gu_w = lax.all_gather(gu_shard, "fsdp", axis=0, tiled=True)
     cut = ff // 4
-    qkv_x, qkv_y, tokens_x, tokens_y = sync(qkv_x, qkv_y, tokens_x, tokens_y)
+    live_rows = live.reshape(2, rows, 1).astype(F32)
+    qkv_x, qkv_y, tokens_x, tokens_y, cosine, sine, live_rows = sync(
+        qkv_x, qkv_y, tokens_x, tokens_y, cosine, sine, live_rows
+    )
     zh = qkv_z.shape[0] // 2
-    qkv_d = jnp.concatenate([swap_y(qkv_x[:zh]), swap_x(qkv_y[zh:])])
-    tokens_d = jnp.concatenate([swap_y(tokens_x[:1]), swap_x(tokens_y[1:])])
-    qkv_mine = jnp.stack([qkv_z, qkv_x, qkv_y, qkv_d])
+    qkv_mine = jnp.stack([qkv_z, qkv_x, qkv_y])
+    qkv_d = swap_y(qkv_x[:zh]), swap_x(qkv_y[zh:])
+    tokens_d = swap_y(tokens_x[:1]), swap_x(tokens_y[1:])
     qkv_other = core_swap(qkv_mine)
-    tokens_all = jnp.stack([tokens_own, tokens_x, tokens_y, tokens_d])
+    qkv_d, tokens_d, qkv_other = sync(qkv_d, tokens_d, qkv_other)
+    qkv_d = jnp.concatenate(qkv_d)[None]
+    qkv_other_d = core_swap(qkv_d)
     dy_own = cotangent[0].reshape(2, rows, width)
-    dy_pieces = ctx_fetch_direct(after(dy_own, qkv_mine, tokens_d))
+    dy_pieces = ctx_fetch_direct(after(dy_own, qkv_other_d))
 
     first_all, q_t, kv_all, qkv_w, gain_rows = project(
-        c, f, tokens_all.reshape(8, rows, width), qkv_mine, qkv_other, cosine, sine, q_width
+        c,
+        f,
+        (tokens_own, tokens_x, tokens_y, *tokens_d),
+        (qkv_mine, qkv_d),
+        (qkv_other, qkv_other_d),
+        cosine,
+        sine,
+        q_width,
     )
     gain_one, gain_two = gain_rows[0:1], gain_rows[1:2]
     first_all = first_all.reshape(4, 2, rows, width)
@@ -1008,10 +1038,12 @@
     o_t, out_down, dy_pieces, gu_w = sync(o_t, out_down, dy_pieces, gu_w)
     out_w = out_down[:, :r].reshape(n * r, width)
     down_w = out_down[:, r:].reshape(cut, width)
-    (dy_all,) = sync(jnp.stack(dy_pieces).reshape(4, row_count, width))
+    dy_all, out_w = sync(jnp.stack(dy_pieces).reshape(4, row_count, width), out_w)
     attended_t = o_t.reshape(2, width, rows)
-    live_rows = live.reshape(2, rows, 1).astype(F32)
-    middle, x_own, early_sums = out_project(tokens_own, attended_t, out_w, gain_two, live_rows)
+    out_rows = out_down if r % 16 == 0 else out_w.reshape(n, r, width)
+    middle, x_own, early_sums = out_project(
+        tokens_own, attended_t, out_rows, gain_two, live_rows, r
+    )
 
     x_x, x_y = swap_x(x_own), swap_y(x_own)
     held = feed_forward(x_own.reshape(1, row_count, width), dy_all, gu_w, down_w, 0, None)
@@ -1077,47 +1109,50 @@
     d_kv = d_kv.reshape(2, 2 * kv_width, rows)
     dkv_parts = [quarter(d_kv, kv4, i) for i in range(4)]
     dkv_got = exchange_first(dkv_parts)
-    dq_got, dkv_got = sync(dq_got, dkv_got)
-    dq_pieces = [dq_parts[0], *dq_got, *exchange_second(*dq_got)]
-    dkv_pieces = [dkv_parts[0], *dkv_got, *exchange_second(*dkv_got)]
-    dq_pieces, dkv_pieces, own_gu, own_out = sync(dq_pieces, dkv_pieces, own_gu, own_out)
-    gu_x, gu_y = swap_x(own_gu), swap_y(own_gu)
+    dq_got, dkv_got, ffn_sums = sync(dq_got, dkv_got, ffn_sums)
+    diagonal = (
+        swap_y(jnp.concatenate([dq_got[0][2:], dkv_got[0][2:]], axis=1)),
+        swap_x(jnp.concatenate([dq_got[1][2:], dkv_got[1][2:]], axis=1)),
+    )
+    ffn_last = swap_y(ffn_sums[2]), swap_x(ffn_sums[3])
+    dq_pieces = [dq_parts[0], *dq_got]
+    dkv_pieces = [dkv_parts[0], *dkv_got]
+    diagonal, own_out = sync(diagonal, own_out)
     own_out = own_out.reshape(4, r4, width)
     out_parts = [take(own_out, c ^ i, 0) for i in range(4)]
     out_got = scatter_first(out_parts)
-    grad_qkv = project_grad(first_all.reshape(8, rows, width), dq_pieces, dkv_pieces)
+    grad_qkv = project_grad(first_all.reshape(8, rows, width), dq_pieces, dkv_pieces, diagonal)
     grad_qkv = grad_qkv.reshape(nz, 2, r, q4 + kv4)
     got_half = core_swap(take(grad_qkv, k ^ 1, 1))
     pair_qkv = (take(grad_qkv, k, 1).astype(F32) + got_half.astype(F32)).astype(BF16)
-    pair_qkv, d_q, d_kv, ffn_sums, gu_x, gu_y, out_got = sync(
-        pair_qkv, d_q, d_kv, ffn_sums, gu_x, gu_y, out_got
-    )
+    pair_qkv, d_q, d_kv, ffn_last, own_gu, out_got = sync(
+        pair_qkv, d_q, d_kv, ffn_last, own_gu, out_got
+    )
+    branch_ffn = jnp.concatenate([v + g.astype(F32) for v, g in zip(ffn_sums[:2], ffn_last)])
     own_qkv = z_scatter(pair_qkv).astype(BF16)
 
-    branch_ffn = scatter_last(*ffn_sums)
+    gu_x, gu_y = swap_x(own_gu), swap_y(own_gu)
+    out_sums = scatter_pass(out_parts, out_got)
     grad_tokens, grad_gain_one, late_sums = first_back(
         d_q, d_kv, qkv_w, tokens_own, grad_middle, gain_one, live_rows
     )
-    out_sums = scatter_pass(out_parts, out_got)
-    own_qkv, branch_ffn, out_sums, grad_tokens, grad_gain_one, late_sums = sync(
-        own_qkv, branch_ffn, out_sums, grad_tokens, grad_gain_one, late_sums
-    )
-
-    qkv_pieces = ctx_fetch_direct(own_qkv)
-    own_out = scatter_last(*out_sums).astype(BF16)
     result, small = finish(
         middle, branch_ffn, live_rows, grad_gain_one, grad_gain_two, early_sums, late_sums
     )
+    own_qkv, small, gu_x, gu_y, out_sums = sync(own_qkv, small, gu_x, gu_y, out_sums)
+
     small = small + core_swap(small)
-    own_out, qkv_pieces, small, gu_x, gu_y = sync(own_out, qkv_pieces, small, gu_x, gu_y)
+    own_out = scatter_last(*out_sums).astype(BF16)
+    qkv_pieces = ctx_fetch_direct(own_qkv)
+    small, own_out, gu_x, gu_y = sync(small, own_out, gu_x, gu_y)
+    small = z_sum(small)
     hr = gu_x.shape[0] // 2
     gu_d = jnp.concatenate([swap_y(gu_x[:hr]), swap_x(gu_y[hr:])])
-    small = z_sum(small)
+    small, own_down, gu_d, own_out = sync(small, own_down, gu_d, own_out)
+    small = sum(ctx_fetch_direct(small))
+    down_pieces = ctx_fetch_direct(own_down)
+    out_pieces = ctx_fetch_direct(own_out)
     grad_q, grad_k, grad_v = join_columns(c_ref, qkv_pieces, q4, kv4)
-    gu_d, small, own_down, own_out = sync(gu_d, small, own_down, own_out)
-    small = sum(ctx_fetch_direct(small))
-    out_pieces = ctx_fetch_direct(own_out)
-    down_pieces = ctx_fetch_direct(own_down)
     grad_gate_w, grad_up_w = unpick_columns(c_ref, [own_gu, gu_x, gu_y, gu_d], n)
     grad_down_w = in_order(down_pieces, 0).reshape(4 * d4, width).astype(F32)
     grad_out_w = in_order(out_pieces, 0).reshape(r, width).astype(F32)

time: 501 us -> 486 us (0.970)
  other arithmetic: 43.1 us -> 36.5 us
    ppermute x25 -> x24, waiting for transfers between devices: 50.2 us -> 39.1 us  [swap_x(): return lax.ppermute(v, 'ctx', [(i, i ^ 1) for i in range(4)])]
    ppermute x25 -> x24, waiting for transfers between devices: 35.8 us -> 42.2 us  [swap_y(): return lax.ppermute(v, 'ctx', [(i, i ^ 2) for i in range(4)])]
    another operation x10 -> x6, other arithmetic: 9.91 us -> 3.96 us  [the longest x1 3.57 us: per_device(): jnp.stack(dy_pieces).reshape(4, row_count, width)]
    ppermute x25 -> x24, starting transfers between devices: 37.2 us -> 32 us  [swap_y(): return lax.ppermute(v, 'ctx', [(i, i ^ 2) for i in range(4)])]
    ppermute x25 -> x24, starting transfers between devices: 29.5 us -> 31.4 us  [swap_x(): return lax.ppermute(v, 'ctx', [(i, i ^ 1) for i in range(4)])]
    unnamed x99 -> x98, local copies, waits for them, and re-layouts: 11.4 us -> 13 us
  transfers between devices with their start and end apart: 72 -> 71, of which waited for: 30 -> 31; matrix products, arithmetic and copies ran while one was open for 14% -> 13% of each run, Pallas kernels for 35% -> 37%
where the time goes in v4:
time: 486 us; the launch traced here: 483 us
  Pallas kernels  195 us (40%)
  waiting for transfers between devices  110 us (23%)
  starting transfers between devices  81.7 us (17%)
  local copies, waits for them, and re-layouts  44 us (9%)
  other arithmetic  36.5 us (8%)
  between operations  15.8 us (3%)
    ppermute x24, waiting for transfers between devices, swap_y(): return lax.ppermute(v, 'ctx', [(i, i ^ 2) for i in range(4)])  42.2 us
    ppermute x24, waiting for transfers between devices, swap_x(): return lax.ppermute(v, 'ctx', [(i, i ^ 1) for i in range(4)])  39.1 us
    pallas_call x3, Pallas kernels, feed_forward(): pl.pallas_call(kernel, grid=(count,), in_specs=[own(width), block(width),...  38.1 us
    pallas_call x1, Pallas kernels, attention_backward(): pl.pallas_call(backward_kernel, grid_spec=pltpu.PrefetchScalarGridSpec(nu...  32.4 us
    ppermute x24, starting transfers between devices, swap_y(): return lax.ppermute(v, 'ctx', [(i, i ^ 2) for i in range(4)])  32 us
    ppermute x24, starting transfers between devices, swap_x(): return lax.ppermute(v, 'ctx', [(i, i ^ 1) for i in range(4)])  31.4 us
    pallas_call x1, Pallas kernels, attention_forward(): pl.pallas_call(forward_kernel, grid_spec=pltpu.PrefetchScalarGridSpec(num...  26.2 us
    pallas_call x2, Pallas kernels, transposed_product(): pl.pallas_call(kernel, grid=(rows // tile,), in_specs=[pl.BlockSpec((dept...  22.3 us
  transfers between devices with their start and end apart: 71, of which 31 were waited for; matrix products, arithmetic and copies ran while one was open for 13% of the time, Pallas kernels for 37%

profile of v4, /device:TPU:0, one launch (start us, length us, event | category | flops | bytes accessed | tf_op | source)
XLA Modules:
  0.0 482.6 jit_solution(4608590278542361088)
XLA Ops:
  23.8 8.5 %collective-permute-done.1 = bf16[160,512]{1,0:T(8,128)(2,1)S(1)} collective-permute-done((bf16[160,512]{1,0:T(8,128)(2,1)}, bf16[160,512]{1,0:T(8,128)(2,1)S(1)}, u32[]{:S(2)}, u32[]{:S(2)}) %collective-permute-start.1) | collective-permute-done | bytes 163872 | tf_op jit(solution)/shard_map/ppermute | solution.py:66
  43.1 10.6 %collective-permute-done.5 = bf16[4,160,512]{2,1,0:T(8,128)(2,1)S(1)} collective-permute-done((bf16[4,160,512]{2,1,0:T(8,128)(2,1)S(1)}, bf16[4,160,512]{2,1,0:T(8,128)(2,1)S(1)}, u32[]{:S(2)}, u32[]{:S(2)}) %collective-permute-start.5) | collective-permute-done | bytes 655392 | tf_op jit(solution)/shard_map/ppermute | solution.py:30
  60.0 16.6 %collective-permute-done.7 = bf16[2,160,512]{2,1,0:T(8,128)(2,1)S(1)} collective-permute-done((bf16[2,160,512]{2,1,0:T(8,128)(2,1)S(1)}, bf16[2,160,512]{2,1,0:T(8,128)(2,1)S(1)}, u32[]{:S(2)}, u32[]{:S(2)}) %collective-permute-start.7) | collective-permute-done | bytes 327712 | tf_op jit(solution)/shard_map/ppermute | solution.py:34
  88.6 16.2 %shard_map.220 = (bf16[8,216,1280]{2,1,0:T(8,128)(2,1)}, bf16[2,20,64,216]{3,2,1,0:T(8,128)(2,1)}, bf16[8,10,64,216]{3,2,1,0:T(8,128)(2,1)}, bf16[1280,2048]{1,0:T(8,128)(2,1)}, f32[8,1280]{1,0:T(8,128)}) custom-call(s32[2]{0:T(128)} %get-tuple-element.361.at_ref, bf16[2,216,1280]{2,1,0:T(8,128)(2,1)} %bitcast.164, bf16[2,216,1280]{2,1,0:T(8,128)(2,1)} %copy-done.36, ...), custom_call_target="tpu_custom_call" | custom-call | flops 8000000000 | bytes 25000000 | tf_op jit(solution)/shard_map/pallas_call | solution.py:493
  104.8 26.2 %shard_map.221 = (bf16[2,20,64,216]{3,2,1,0:T(8,128)(2,1)}, f32[2,5,4,216]{3,2,1,0:T(4,128)}) custom-call(s32[2]{0:T(128)} %get-tuple-element.360.blocks_ref, s32[8]{0:T(128)} %fusion.25.slots_ref, f32[2,1,216]{2,1,0:T(1,128)} %add_convert_fusion.5.seg_q_ref, f32[8,1,216]{2,1,0:T(1,128)} %convert_element_type.215.seg_k_ref, ...), custom_call_target="tpu_custom_call" | custom-call | flops 20000000000 | bytes 6000000 | tf_op jit(solution)/shard_map/pallas_call | solution.py:567
  136.7 10.7 %all-gather.6.cloned.1.call-done = bf16[2176,1280]{1,0:T(8,128)(2,1)} async-done(((bf16[272,1280]{1,0:T(8,128)(2,1)}), bf16[2176,1280]{1,0:T(8,128)(2,1)}) %all-gather.6.cloned.1.call-update) | async-done | bytes 5570576 | tf_op jit(solution)/shard_map/all_gather | solution.py:1004
  147.4 7.3 %shard_map.223 = (f32[2,216,1280]{2,1,0:T(8,128)}, bf16[2,216,1280]{2,1,0:T(8,128)(2,1)}, f32[8,128]{1,0:T(8,128)}) custom-call(bf16[2,216,1280]{2,1,0:T(8,128)(2,1)} %bitcast.165, bf16[2,1280,216]{2,1,0:T(8,128)(2,1)} %bitcast.148, bf16[8,272,1280]{2,1,0:T(8,128)(2,1)} %bitcast.139, f32[1,1280]{1,0:T(1,128)} %get-tuple-element.349.gain_ref, ...), custom_call_target="tpu_custom_call" | custom-call | tf_op jit(solution)/shard_map/pallas_call | solution.py:776
  168.5 10.6 %shard_map.224 = (bf16[4,432,1280]{2,1,0:T(8,128)(2,1)}, bf16[4,432,896]{2,1,0:T(8,128)(2,1)}, bf16[4,432,1792]{2,1,0:T(8,128)(2,1)}, bf16[1,432,1280]{2,1,0:T(8,128)(2,1)}) custom-call(bf16[1,432,1280]{2,1,0:T(8,128)(2,1)} %bitcast.195, bf16[4,432,1280]{2,1,0:T(8,128)(2,1)} %pad_maximum_fusion.dy_ref, ...), custom_call_target="tpu_custom_call" | custom-call | flops 4954521600 | bytes 13627392 | tf_op jit(solution)/shard_map/pallas_call | solution.py:658
  187.2 17.0 %shard_map.225 = (bf16[4,432,1280]{2,1,0:T(8,128)(2,1)}, bf16[4,432,896]{2,1,0:T(8,128)(2,1)}, bf16[4,432,1792]{2,1,0:T(8,128)(2,1)}, bf16[2,432,1280]{2,1,0:T(8,128)(2,1)}) custom-call(bf16[2,432,1280]{2,1,0:T(8,128)(2,1)} %pad_maximum_fusion.1.x_ref, ...), custom_call_target="tpu_custom_call", output_to_operand_aliasing={{0}: (4, {}), {1}: (5, {}), {2}: (6, {})} | custom-call | flops 9909043200 | bytes 20373504 | tf_op jit(solution)/shard_map/pallas_call | solution.py:658
  205.3 10.6 %shard_map.226 = (bf16[4,432,1280]{2,1,0:T(8,128)(2,1)}, bf16[4,432,896]{2,1,0:T(8,128)(2,1)}, bf16[4,432,1792]{2,1,0:T(8,128)(2,1)}, bf16[1,432,1280]{2,1,0:T(8,128)(2,1)}) custom-call(bf16[1,432,1280]{2,1,0:T(8,128)(2,1)} %bitcast.161, bf16[4,432,1280]{2,1,0:T(8,128)(2,1)} %pad_maximum_fusion.dy_ref, ...), custom_call_target="tpu_custom_call", output_to_operand_aliasing={{0}: (4, {}), {1}: (5, {}), {2}: (6, {})} | custom-call | flops 4954521600 | bytes 13627392 | tf_op jit(solution)/shard_map/pallas_call | solution.py:658
  221.2 13.4 %shard_map.227 = bf16[1280,1792]{1,0:T(8,128)(2,1)} custom-call(bf16[1728,1280]{1,0:T(8,128)(2,1)} %bitcast.146, bf16[1728,1792]{1,0:T(8,128)(2,1)} %bitcast.138), custom_call_target="tpu_custom_call" | custom-call | tf_op jit(solution)/shard_map/pallas_call | solution.py:699
  234.6 8.4 %shard_map.228 = bf16[1728,1280]{1,0:T(8,128)(2,1)} custom-call(bf16[1728,896]{1,0:T(8,128)(2,1)} %bitcast.136, bf16[896,1280]{1,0:T(8,128)(2,1)} %bitcast.145), custom_call_target="tpu_custom_call" | custom-call | tf_op jit(solution)/shard_map/pallas_call | solution.py:717
  251.0 8.9 %shard_map.229 = bf16[896,1280]{1,0:T(8,128)(2,1)} custom-call(bf16[1728,896]{1,0:T(8,128)(2,1)} %bitcast.137, bf16[1728,1280]{1,0:T(8,128)(2,1)} %bitcast.135), custom_call_target="tpu_custom_call" | custom-call | tf_op jit(solution)/shard_map/pallas_call | solution.py:699
  260.0 4.6 fusion.28
  267.7 8.0 %shard_map.230 = (f32[2,216,1280]{2,1,0:T(8,128)}, bf16[2,216,1280]{2,1,0:T(8,128)(2,1)}, bf16[2,1280,216]{2,1,0:T(8,128)(2,1)}, f32[1,1280]{1,0:T(1,128)}) custom-call(f32[2,216,1280]{2,1,0:T(8,128)} %pad_maximum_fusion.2.d_ref, f32[2,216,1280]{2,1,0:T(8,128)} %get-tuple-element.180.m_ref, bf16[2,216,1280]{2,1,0:T(8,128)(2,1)} %bitcast.172, ...), custom_call_target="tpu_custom_call" | custom-call | tf_op jit(solution)/shard_map/pallas_call | solution.py:825
  275.8 5.4 %shard_map.231 = bf16[1280,1280]{1,0:T(8,128)(2,1)} custom-call(bf16[2,1280,216]{2,1,0:T(8,128)(2,1)} %bitcast.149, bf16[2,216,1280]{2,1,0:T(8,128)(2,1)} %get-tuple-element.219.right_ref), custom_call_target="tpu_custom_call" | custom-call | tf_op jit(solution)/shard_map/pallas_call | solution.py:734
  289.7 32.4 %shard_map.232 = (bf16[2,20,64,216]{3,2,1,0:T(8,128)(2,1)}, bf16[2,2,5,64,216]{4,3,2,1,0:T(8,128)(2,1)}, bf16[2,2,5,64,216]{4,3,2,1,0:T(8,128)(2,1)}, bf16[4,2,5,64,216]{4,3,2,1,0:T(8,128)(2,1)}) custom-call(s32[2]{0:T(128)} %get-tuple-element.360.blocks_ref, s32[8]{0:T(128)} %fusion.25.slots_ref, f32[2,1,216]{2,1,0:T(1,128)} %add_convert_fusion.5.seg_q_ref, ...), custom_call_target="tpu_custom_call" | custom-call | tf_op jit(solution)/shard_map/pallas_call | solution.py:603
  322.4 5.1 %collective-permute-start.26 = (bf16[2,2,5,64,216]{4,3,2,1,0:T(8,128)(2,1)}, bf16[2,2,5,64,216]{4,3,2,1,0:T(8,128)(2,1)S(1)}, u32[]{:S(2)}, u32[]{:S(2)}) collective-permute-start(bf16[2,2,5,64,216]{4,3,2,1,0:T(8,128)(2,1)} %get-tuple-element.229), channel_id=1, source_target_pairs={{0,8},{8,0},{16,24},{24,16},{1,9},{9,1},{17,25},{25,17},{2,10},{10... | collective-permute-start | bytes 1658888 | tf_op jit(solution)/shard_map/ppermute | solution.py:30
  327.5 4.5 collective-permute-start.27
  348.8 11.4 %collective-permute-done.31 = bf16[2,5,64,216]{3,2,1,0:T(8,128)(2,1)S(1)} collective-permute-done((bf16[2,5,64,216]{3,2,1,0:T(8,128)(2,1)S(1)}, bf16[2,5,64,216]{3,2,1,0:T(8,128)(2,1)S(1)}, u32[]{:S(2)}, u32[]{:S(2)}) %collective-permute-start.31) | collective-permute-done | bytes 276512 | tf_op jit(solution)/shard_map/ppermute | solution.py:30
  382.2 6.8 %shard_map.233 = bf16[1280,480]{1,0:T(8,128)(2,1)} custom-call(bf16[8,216,1280]{2,1,0:T(8,128)(2,1)} %get-tuple-element.246.first_ref, bf16[2,320,216]{2,1,0:T(8,128)(2,1)} %get-tuple-element.247.refs_0_, bf16[3,320,216]{2,1,0:T(8,128)(2,1)} %copy-done.25, bf16[3,320,216]{2,1,0:T(8,128)(2,1)} %copy-done.26, bf16[2,160,216]{2,1,0:T(8,128)(2,1)} %get-tuple-element.329.refs_3_, ...), custom_call_target="tpu_custom_call" | custom-call | tf_op jit(solution)/shard_map/pallas_call | solution.py:539
  405.6 9.2 %shard_map.234 = (bf16[2,216,1280]{2,1,0:T(8,128)(2,1)}, f32[1,1280]{1,0:T(1,128)}, f32[8,128]{1,0:T(8,128)}) custom-call(bf16[2,1280,216]{2,1,0:T(8,128)(2,1)} %bitcast.159, bf16[2,640,216]{2,1,0:T(8,128)(2,1)} %bitcast.152, bf16[1280,2048]{1,0:T(8,128)(2,1)} %get-tuple-element.265.w_ref, bf16[2,216,1280]{2,1,0:T(8,128)(2,1)} %bitcast.166, ...), custom_call_target="tpu_custom_call" | custom-call | tf_op jit(solution)/shard_map/pallas_call | solution.py:867
  438.1 4.5 collective-permute-done.59.refs_3_
  453.6 4.9 %shard_map.237 = (f32[160,3584]{1,0:T(8,128)}, f32[160,3584]{1,0:T(8,128)}) custom-call(s32[1]{0:T(128)} %bitcast.1.c_ref, bf16[160,1792]{1,0:T(8,128)(2,1)} %reduce-scatter.4.cloned.1.call-done.refs_0_, bf16[160,1792]{1,0:T(8,128)(2,1)} %collective-permute-done.44.refs_1_, bf16[160,1792]{1,0:T(8,128)(2,1)} %collective-permute-done.45.refs_2_, ...), custom_call_target="tpu_custom_call" | custom-call | bytes 6881280 | tf_op jit(solution)/shard_map/pallas_call | solution.py:208
  (365 shorter events, 204.9 us)
Async XLA Ops:
  7.2 129.5 %all-gather.4.cloned.1.call-start = ((), (), s32[]{:S(2)}) async-start(), calls=%async_computation.3 | async-start | bytes 5160960 | tf_op jit(solution)/shard_map/all_gather | solution.py:1008
  7.2 27.6 %collective-permute-start.3 = (bf16[2,216,1280]{2,1,0:T(8,128)(2,1)}, bf16[2,216,1280]{2,1,0:T(8,128)(2,1)S(1)}, u32[]{:S(2)}, u32[]{:S(2)}) collective-permute-start(bf16[2,216,1280]{2,1,0:T(8,128)(2,1)} %bitcast.162), channel_id=1, source_target_pairs={{0,8},{8,0},{16,24},{24,16},{1,9},{9,1},{17,25},{25,17},{2,10},{10... | collective-permute-start | bytes 3317768 | tf_op jit(solution)/shard_map/ppermute | solution.py:30
  10.2 26.2 %collective-permute-start.4 = (bf16[2,216,1280]{2,1,0:T(8,128)(2,1)}, bf16[2,216,1280]{2,1,0:T(8,128)(2,1)}, u32[]{:S(2)}, u32[]{:S(2)}) collective-permute-start(bf16[2,216,1280]{2,1,0:T(8,128)(2,1)} %bitcast.163), channel_id=1, source_target_pairs={{0,16},{8,24},{16,0},{24,8},{1,17},{9,25},{17,1},{25,9},{2,18},{10... | collective-permute-start | bytes 3317768 | tf_op jit(solution)/shard_map/ppermute | solution.py:34
  36.4 111.0 %all-gather.6.cloned.1.call-start = ((), (), s32[]{:S(2)}) async-start(), calls=%async_computation.7 | async-start | bytes 6266880 | tf_op jit(solution)/shard_map/all_gather | solution.py:1004
  37.5 284.6 %reduce-scatter.4.cloned.1.call-start = ((), (), s32[]{:S(2)}) async-start(), calls=%async_computation.4 | async-start | bytes 5160960 | tf_op jit(solution)/shard_map/reduce_scatter | solution.py:1071
  54.4 25.3 %collective-permute-start.11 = (bf16[3,4,160,512]{3,2,1,0:T(8,128)(2,1)S(1)}, bf16[3,4,160,512]{3,2,1,0:T(8,128)(2,1)S(1)}, u32[]{:S(2)}, u32[]{:S(2)}) collective-permute-start(bf16[3,4,160,512]{3,2,1,0:T(8,128)(2,1)S(1)} %pad_maximum_fusion.4.refs_5_), channel_id=1, source_target_pairs={{0,1},{1,0},{2,3},{3,2},{4,5},{5,4},{6,7},{7,6},{8,9},{9,8},{10,11... | collective-permute-start | bytes 5898248 | tf_op jit(solution)/shard_map/ppermute | solution.py:26
  54.5 24.3 %collective-permute-start.9 = (bf16[1,216,1280]{2,1,0:T(8,128)(2,1)S(1)}, bf16[1,216,1280]{2,1,0:T(8,128)(2,1)S(1)}, u32[]{:S(2)}, u32[]{:S(2)}) collective-permute-start(bf16[1,216,1280]{2,1,0:T(8,128)(2,1)S(1)} %slice.277), channel_id=1, source_target_pairs={{0,16},{8,24},{16,0},{24,8},{1,17},{9,25},{17,1},{25,9},{2,18},{10... | collective-permute-start | bytes 1658888 | tf_op jit(solution)/shard_map/ppermute | solution.py:34
  57.1 21.7 %collective-permute-start.10 = (bf16[1,216,1280]{2,1,0:T(8,128)(2,1)S(1)}, bf16[1,216,1280]{2,1,0:T(8,128)(2,1)S(1)}, u32[]{:S(2)}, u32[]{:S(2)}) collective-permute-start(bf16[1,216,1280]{2,1,0:T(8,128)(2,1)S(1)} %slice.278), channel_id=1, source_target_pairs={{0,8},{8,0},{16,24},{24,16},{1,9},{9,1},{17,25},{25,17},{2,10},{10... | collective-permute-start | bytes 1658888 | tf_op jit(solution)/shard_map/ppermute | solution.py:30
  85.1 47.4 %collective-permute-start.13 = (bf16[2,216,1280]{2,1,0:T(8,128)(2,1)S(1)}, bf16[2,216,1280]{2,1,0:T(8,128)(2,1)S(1)}, u32[]{:S(2)}, u32[]{:S(2)}) collective-permute-start(bf16[2,216,1280]{2,1,0:T(8,128)(2,1)S(1)} %bitcast.173), channel_id=1, source_target_pairs={{0,8},{8,0},{16,24},{24,16},{1,9},{9,1},{17,25},{25,17},{2,10},{10... | collective-permute-start | bytes 3317768 | tf_op jit(solution)/shard_map/ppermute | solution.py:30
  86.5 50.1 %collective-permute-start.14 = (bf16[2,216,1280]{2,1,0:T(8,128)(2,1)S(1)}, bf16[2,216,1280]{2,1,0:T(8,128)(2,1)S(1)}, u32[]{:S(2)}, u32[]{:S(2)}) collective-permute-start(bf16[2,216,1280]{2,1,0:T(8,128)(2,1)S(1)} %bitcast.174), channel_id=1, source_target_pairs={{0,16},{8,24},{16,0},{24,8},{1,17},{9,25},{17,1},{25,9},{2,18},{10... | collective-permute-start | bytes 3317768 | tf_op jit(solution)/shard_map/ppermute | solution.py:34
  87.0 49.6 %collective-permute-start.15 = (bf16[2,216,1280]{2,1,0:T(8,128)(2,1)S(1)}, bf16[2,216,1280]{2,1,0:T(8,128)(2,1)}, u32[]{:S(2)}, u32[]{:S(2)}) collective-permute-start(bf16[2,216,1280]{2,1,0:T(8,128)(2,1)S(1)} %bitcast.175), channel_id=1, source_target_pairs={{0,24},{8,16},{16,8},{24,0},{1,25},{9,17},{17,9},{25,1},{2,26},{10... | collective-permute-start | bytes 3317768 | tf_op jit(solution)/shard_map/ppermute | solution.py:104
  154.7 26.8 %collective-permute-start.16 = (bf16[2,216,1280]{2,1,0:T(8,128)(2,1)}, bf16[2,216,1280]{2,1,0:T(8,128)(2,1)S(1)}, u32[]{:S(2)}, u32[]{:S(2)}) collective-permute-start(bf16[2,216,1280]{2,1,0:T(8,128)(2,1)} %get-tuple-element.181), channel_id=1, source_target_pairs={{0,8},{8,0},{16,24},{24,16},{1,9},{9,1},{17,25},{25,17},{2,10},{10... | collective-permute-start | bytes 3317768 | tf_op jit(solution)/shard_map/ppermute | solution.py:30
  156.3 26.5 %collective-permute-start.17 = (bf16[2,216,1280]{2,1,0:T(8,128)(2,1)}, bf16[2,216,1280]{2,1,0:T(8,128)(2,1)S(1)}, u32[]{:S(2)}, u32[]{:S(2)}) collective-permute-start(bf16[2,216,1280]{2,1,0:T(8,128)(2,1)} %get-tuple-element.181), channel_id=1, source_target_pairs={{0,16},{8,24},{16,0},{24,8},{1,17},{9,25},{17,1},{25,9},{2,18},{10... | collective-permute-start | bytes 3317768 | tf_op jit(solution)/shard_map/ppermute | solution.py:34
  182.8 21.5 %collective-permute-start.19 = (bf16[1,216,1280]{2,1,0:T(8,128)(2,1)S(1)}, bf16[1,216,1280]{2,1,0:T(8,128)(2,1)S(1)}, u32[]{:S(2)}, u32[]{:S(2)}) collective-permute-start(bf16[1,216,1280]{2,1,0:T(8,128)(2,1)S(1)} %slice.286), channel_id=1, source_target_pairs={{0,8},{8,0},{16,24},{24,16},{1,9},{9,1},{17,25},{25,17},{2,10},{10... | collective-permute-start | bytes 1658888 | tf_op jit(solution)/shard_map/ppermute | solution.py:30
  218.0 25.0 %collective-permute-start.20 = (bf16[2,216,1280]{2,1,0:T(8,128)(2,1)S(1)}, bf16[2,216,1280]{2,1,0:T(8,128)(2,1)S(1)}, u32[]{:S(2)}, u32[]{:S(2)}) collective-permute-start(bf16[2,216,1280]{2,1,0:T(8,128)(2,1)S(1)} %pad_maximum_fusion.6), channel_id=1, source_target_pairs={{0,8},{8,0},{16,24},{24,16},{1,9},{9,1},{17,25},{25,17},{2,10},{10... | collective-permute-start | bytes 3317768 | tf_op jit(solution)/shard_map/ppermute | solution.py:30
  220.7 24.8 %collective-permute-start.21 = (bf16[2,216,1280]{2,1,0:T(8,128)(2,1)}, bf16[2,216,1280]{2,1,0:T(8,128)(2,1)S(1)}, u32[]{:S(2)}, u32[]{:S(2)}) collective-permute-start(bf16[2,216,1280]{2,1,0:T(8,128)(2,1)} %pad_maximum_fusion.7), channel_id=1, source_target_pairs={{0,16},{8,24},{16,0},{24,8},{1,17},{9,25},{17,1},{25,9},{2,18},{10... | collective-permute-start | bytes 3317768 | tf_op jit(solution)/shard_map/ppermute | solution.py:34
  245.5 136.7 %reduce-scatter.6.cloned.1.call-start = ((), (), s32[]{:S(2)}) async-start(), calls=%async_computation.5 | async-start | bytes 3686400 | tf_op jit(solution)/shard_map/reduce_scatter | solution.py:1089
  282.6 39.4 %collective-permute-start.24 = (bf16[2,216,1280]{2,1,0:T(8,128)(2,1)S(1)}, bf16[2,216,1280]{2,1,0:T(8,128)(2,1)S(1)}, u32[]{:S(2)}, u32[]{:S(2)}) collective-permute-start(bf16[2,216,1280]{2,1,0:T(8,128)(2,1)S(1)} %pad_maximum_fusion.8), channel_id=1, source_target_pairs={{0,8},{8,0},{16,24},{24,16},{1,9},{9,1},{17,25},{25,17},{2,10},{10... | collective-permute-start | bytes 3317768 | tf_op jit(solution)/shard_map/ppermute | solution.py:30
  285.2 36.9 %collective-permute-start.25 = (bf16[2,216,1280]{2,1,0:T(8,128)(2,1)}, bf16[2,216,1280]{2,1,0:T(8,128)(2,1)S(1)}, u32[]{:S(2)}, u32[]{:S(2)}) collective-permute-start(bf16[2,216,1280]{2,1,0:T(8,128)(2,1)} %pad_maximum_fusion.9), channel_id=1, source_target_pairs={{0,16},{8,24},{16,0},{24,8},{1,17},{9,25},{17,1},{25,9},{2,18},{10... | collective-permute-start | bytes 3317768 | tf_op jit(solution)/shard_map/ppermute | solution.py:34
  322.1 125.2 %reduce-scatter.8.cloned.1.call-start = ((), (), s32[]{:S(2)}) async-start(), calls=%async_computation.6 | async-start | bytes 2580480 | tf_op jit(solution)/shard_map/reduce_scatter | solution.py:1072
  343.8 22.0 %collective-permute-start.28 = (bf16[3,320,216]{2,1,0:T(8,128)(2,1)S(1)}, bf16[3,320,216]{2,1,0:T(8,128)(2,1)S(1)}, u32[]{:S(2)}, u32[]{:S(2)}) collective-permute-start(bf16[3,320,216]{2,1,0:T(8,128)(2,1)S(1)} %pad_maximum_fusion.15), channel_id=1, source_target_pairs={{0,8},{8,0},{16,24},{24,16},{1,9},{9,1},{17,25},{25,17},{2,10},{10... | collective-permute-start | bytes 1244168 | tf_op jit(solution)/shard_map/ppermute | solution.py:30
  396.5 25.1 %collective-permute-start.44 = (bf16[160,1792]{1,0:T(8,128)(2,1)S(1)}, bf16[160,1792]{1,0:T(8,128)(2,1)}, u32[]{:S(2)}, u32[]{:S(2)}) collective-permute-start(bf16[160,1792]{1,0:T(8,128)(2,1)S(1)} %copy-done.31), channel_id=1, source_target_pairs={{0,8},{8,0},{16,24},{24,16},{1,9},{9,1},{17,25},{25,17},{2,10},{10... | collective-permute-start | bytes 1720328 | tf_op jit(solution)/shard_map/ppermute | solution.py:30
  397.6 24.1 %collective-permute-start.45 = (bf16[160,1792]{1,0:T(8,128)(2,1)S(1)}, bf16[160,1792]{1,0:T(8,128)(2,1)}, u32[]{:S(2)}, u32[]{:S(2)}) collective-permute-start(bf16[160,1792]{1,0:T(8,128)(2,1)S(1)} %copy-done.31), channel_id=1, source_target_pairs={{0,16},{8,24},{16,0},{24,8},{1,17},{9,25},{17,1},{25,9},{2,18},{10... | collective-permute-start | bytes 1720328 | tf_op jit(solution)/shard_map/ppermute | solution.py:34
  400.2 20.3 %collective-permute-start.42 = (bf16[160,480]{1,0:T(8,128)(2,1)}, bf16[160,480]{1,0:T(8,128)(2,1)}, u32[]{:S(2)}, u32[]{:S(2)}) collective-permute-start(bf16[160,480]{1,0:T(8,128)(2,1)} %get-tuple-element.328), channel_id=1, source_target_pairs={{0,4},{1,5},{2,6},{3,7},{4,0},{5,1},{6,2},{7,3},{8,12},{9,13},{10,... | collective-permute-start | bytes 460808 | tf_op jit(solution)/shard_map/ppermute | solution.py:82
  (96 other events, 783.9 us)
Sparse Core Ops, SparseCore 0:
  36.6 50.9 all-gather.3
  89.7 57.5 all-gather.5
  245.6 50.6 reduce-scatter.3
  322.2 46.6 reduce-scatter.5
  375.5 38.0 reduce-scatter.7

commit v5 on v4

--- a/solution.py
+++ b/solution.py
@@ -152,20 +152,23 @@
     return v
 
 
-def pick_columns(c, gate, up, count):
+def pick_columns(c, out, gate, up, count):
     r, ff = gate.shape
+    width = out.shape[1]
     group = ff // count
     strip = group // 4
 
-    def kernel(c_ref, gate_ref, up_ref, out_ref):
+    def kernel(c_ref, w_ref, gate_ref, up_ref, out_ref):
+        out_ref[:, :width] = w_ref[...]
         for own in range(4):
 
             @pl.when(c_ref[0] == own)
             def _():
                 for j in range(count):
                     at = j * group + own * strip
-                    out_ref[:, j * strip : (j + 1) * strip] = gate_ref[:, at : at + strip]
-                    to = ff // 4 + j * strip
+                    to = width + j * strip
+                    out_ref[:, to : to + strip] = gate_ref[:, at : at + strip]
+                    to += ff // 4
                     out_ref[:, to : to + strip] = up_ref[:, at : at + strip]
 
     whole = pl.BlockSpec((r, ff), lambda i, s: (0, 0))
@@ -174,12 +177,12 @@
         grid_spec=pltpu.PrefetchScalarGridSpec(
             num_scalar_prefetch=1,
             grid=(1,),
-            in_specs=[whole, whole],
-            out_specs=pl.BlockSpec((r, ff // 2), lambda i, s: (0, 0)),
+            in_specs=[pl.BlockSpec((r, width), lambda i, s: (0, 0)), whole, whole],
+            out_specs=pl.BlockSpec((r, width + ff // 2), lambda i, s: (0, 0)),
         ),
-        out_shape=jax.ShapeDtypeStruct((r, ff // 2), BF16),
+        out_shape=jax.ShapeDtypeStruct((r, width + ff // 2), BF16),
         cost_estimate=pl.CostEstimate(flops=0, bytes_accessed=6 * r * ff, transcendentals=0),
-    )(c, gate, up)
+    )(c, out, gate, up)
 
 
 def unpick_columns(c, pieces, count):
@@ -632,9 +635,11 @@
 def feed_forward(x, dy_all, gu_w, down_w, first, held):
     count, rows, width = x.shape
     cut = down_w.shape[0]
+    side = rows // 2
+    held = () if held is None else tuple(held)
 
     def kernel(x_ref, dy_ref, gu_ref, down_ref, *refs):
-        all_ref, hidden_ref, d_gu_ref, part_ref = refs[-4:]
+        all_ref, hidden_ref, d_gu_ref, *part_refs = refs[len(held) :]
         x_in = x_ref[0]
         all_ref[0] = x_in
         gu = dot(x_in, gu_ref[...], ((1,), (0,)))
@@ -646,32 +651,59 @@
         hidden_ref[0] = (swish * up_pre).astype(BF16)
         d_gu_ref[0, :, :cut] = (d_hidden * up_pre * slope).astype(BF16)
         d_gu_ref[0, :, cut:] = (d_hidden * swish).astype(BF16)
-        part_ref[0] = dot(d_gu_ref[0], gu_ref[...], ((1,), (1,))).astype(BF16)
+        part = dot(d_gu_ref[0], gu_ref[...], ((1,), (1,)))
+        low, high = part[:side].astype(BF16), part[side:].astype(BF16)
+        if first == 0:
+            part_refs[0][0] = low
+            part_refs[0][1] = high
+        elif first == 3:
+            part_refs[0][0] = low
+            part_refs[1][0] = high
+        else:
+            to_x, to_y, x_high, y_low = part_refs
+
+            @pl.when(pl.program_id(0) == 0)
+            def _():
+                to_x[0] = low
+                x_high[0] = high
+
+            @pl.when(pl.program_id(0) == 1)
+            def _():
+                y_low[0] = low
+                to_y[0] = high
 
     def block(size):
         return pl.BlockSpec((1, rows, size), lambda i: (first + i, 0, 0))
 
-    def own(size):
-        return pl.BlockSpec((1, rows, size), lambda i: (i, 0, 0))
-
-    held = () if held is None else held
+    def at(index):
+        return pl.BlockSpec((1, side, width), lambda i: (index, 0, 0))
+
+    def sums(size):
+        return jax.ShapeDtypeStruct((size, side, width), BF16)
+
+    if first == 0:
+        part_specs, part_shapes = [fixed((2, side, width))], [sums(2)]
+    elif first == 3:
+        part_specs, part_shapes = [at(1), at(1)], [sums(2), sums(2)]
+    else:
+        part_specs, part_shapes = [at(0)] * 4, [sums(2), sums(2), sums(1), sums(1)]
     return pl.pallas_call(
         kernel,
         grid=(count,),
         in_specs=[
-            own(width),
+            pl.BlockSpec((1, rows, width), lambda i: (i, 0, 0)),
             block(width),
-            pl.BlockSpec(gu_w.shape, lambda i: (0, 0)),
-            pl.BlockSpec(down_w.shape, lambda i: (0, 0)),
+            fixed(gu_w.shape),
+            fixed(down_w.shape),
         ]
         + [pl.BlockSpec(memory_space=pl.ANY)] * len(held),
-        out_specs=[block(width), block(cut), block(2 * cut), own(width)],
+        out_specs=[block(width), block(cut), block(2 * cut)] + part_specs,
         out_shape=[
             jax.ShapeDtypeStruct((4, rows, width), BF16),
             jax.ShapeDtypeStruct((4, rows, cut), BF16),
             jax.ShapeDtypeStruct((4, rows, 2 * cut), BF16),
-            jax.ShapeDtypeStruct((count, rows, width), BF16),
-        ],
+        ]
+        + part_shapes,
         input_output_aliases={4 + i: i for i in range(len(held))},
         compiler_params=pltpu.CompilerParams(vmem_limit_bytes=VMEM_LIMIT),
         cost_estimate=pl.CostEstimate(
@@ -707,22 +739,34 @@
     )(left, right)
 
 
-def product(left, right, tile):
-    rows, depth = left.shape
-    cols = right.shape[1]
-
-    def kernel(left_ref, right_ref, out_ref):
-        out_ref[...] = dot(left_ref[...], right_ref[...], ((1,), (0,))).astype(BF16)
-
+def ffn_product(hidden, down_w, side):
+    rows, cut = hidden.shape
+    width = down_w.shape[1]
+
+    def kernel(left_ref, right_ref, to_x, to_y, keep):
+        total = dot(left_ref[...], right_ref[...], ((1,), (0,)))
+        low, high = total[:side].astype(BF16), total[side:].astype(BF16)
+        places = (
+            ((keep, 0), (keep, 1)), ((to_x, 0), (keep, 3)),
+            ((keep, 2), (to_y, 0)), ((to_x, 1), (to_y, 1)),
+        )
+        for i, ((low_ref, low_at), (high_ref, high_at)) in enumerate(places):
+
+            @pl.when(pl.program_id(0) == i)
+            def _():
+                low_ref[low_at] = low
+                high_ref[high_at] = high
+
+    sizes = (2, 2, 4)
     return pl.pallas_call(
         kernel,
-        grid=(rows // tile,),
-        in_specs=[pl.BlockSpec((tile, depth), lambda i: (i, 0)), fixed(right.shape)],
-        out_specs=pl.BlockSpec((tile, cols), lambda i: (i, 0)),
-        out_shape=jax.ShapeDtypeStruct((rows, cols), BF16),
+        grid=(4,),
+        in_specs=[pl.BlockSpec((rows // 4, cut), lambda i: (i, 0)), fixed(down_w.shape)],
+        out_specs=[fixed((size, side, width)) for size in sizes],
+        out_shape=[jax.ShapeDtypeStruct((size, side, width), BF16) for size in sizes],
         compiler_params=pltpu.CompilerParams(vmem_limit_bytes=VMEM_LIMIT),
         cost_estimate=BESIDE,
-    )(left, right)
+    )(hidden, down_w)
 
 
 def side_product(left_t, right):
@@ -759,12 +803,11 @@
     return pl.BlockSpec((1, *shape), lambda i: (i, 0, 0))
 
 
-def out_project(tokens, attended_t, weights, gain, live, r):
+def out_project(tokens, attended_t, weights, gain, live):
     sides, rows, width = tokens.shape
 
     def kernel(x_ref, att_ref, w_ref, gain_ref, live_ref, middle_ref, second_ref, sums_ref):
-        w_out = w_ref[:, :r].reshape(width, width)
-        branch = dot(att_ref[0], w_out, ((0,), (0,)))
+        branch = dot(att_ref[0], w_ref[...], ((0,), (0,)))
         middle = x_ref[0].astype(F32) + branch
         middle_ref[0] = middle
         inverse = lax.rsqrt(jnp.mean(middle * middle, axis=-1, keepdims=True) + EPSILON)
@@ -779,7 +822,7 @@
         in_specs=[
             side_spec(rows, width),
             side_spec(width, rows),
-            fixed(weights.shape),
+            fixed((width, width)),
             fixed((1, width)),
             side_spec(rows, 1),
         ],
@@ -813,8 +856,19 @@
 def middle_back(d_second, middle, cotangent, gain, weights):
     sides, rows, width = middle.shape
 
-    def kernel(d_ref, m_ref, cot_ref, gain_ref, w_ref, gm_ref, branch_ref, do_ref, gain_grad_ref):
-        grad, gain_grad = norm_back(d_ref[0], gain_ref[...], m_ref[0])
+    def kernel(
+        low_ref, from_y_ref, high_ref, from_x_ref, m_ref, cot_ref, gain_ref, w_ref,
+        gm_ref, branch_ref, do_ref, gain_grad_ref, d_ref,
+    ):
+        @pl.when(pl.program_id(0) == 0)
+        def _():
+            d_ref[...] = low_ref[0] + from_y_ref[0].astype(F32)
+
+        @pl.when(pl.program_id(0) == 1)
+        def _():
+            d_ref[...] = high_ref[0] + from_x_ref[0].astype(F32)
+
+        grad, gain_grad = norm_back(d_ref[...], gain_ref[...], m_ref[0])
         grad_middle = cot_ref[0].astype(F32) + grad
         gm_ref[0] = grad_middle
         d_branch = grad_middle.astype(BF16)
@@ -825,12 +879,12 @@
     return pl.pallas_call(
         kernel,
         grid=(sides,),
-        in_specs=[
-            side_spec(rows, width),
+        in_specs=[fixed((1, rows, width))] * 4
+        + [
             side_spec(rows, width),
             side_spec(rows, width),
             fixed((1, width)),
-            fixed(weights.shape),
+            fixed((width, width)),
         ],
         out_specs=[
             side_spec(rows, width),
@@ -844,9 +898,10 @@
             jax.ShapeDtypeStruct((sides, width, rows), BF16),
             jax.ShapeDtypeStruct((1, width), F32),
         ],
+        scratch_shapes=[pltpu.VMEM((rows, width), F32)],
         compiler_params=pltpu.CompilerParams(vmem_limit_bytes=VMEM_LIMIT),
         cost_estimate=BESIDE,
-    )(d_second, middle, cotangent, gain, weights)
+    )(*d_second, middle, cotangent, gain, weights)
 
 
 def first_back(d_q, d_kv, weights, tokens, grad_middle, gain, live):
@@ -1000,12 +1055,11 @@
     qkv_z = z_fetch(lax.dynamic_slice_in_dim(qkv_shard, c * c4, c4, 1))
     d4 = w_down.shape[0] // 4
     down_shard = lax.dynamic_slice_in_dim(w_down, c * d4, d4, 0)
-    out_down_shard = after(jnp.concatenate([w_out, down_shard]), qkv_z)
-    out_down = lax.all_gather(out_down_shard, "fsdp", axis=0)
     qkv_z, tokens_x, tokens_y = sync(qkv_z, tokens_x, tokens_y)
     qkv_x, qkv_y = swap_x(qkv_z), swap_y(qkv_z)
-    gu_shard = after(pick_columns(c_ref, w_gate, w_up, n), qkv_z)
-    gu_w = lax.all_gather(gu_shard, "fsdp", axis=0, tiled=True)
+    picked = after(pick_columns(c_ref, w_out, w_gate, w_up, n), qkv_z)
+    out_gu = lax.all_gather(picked, "fsdp", axis=0, tiled=True)
+    down_w = lax.all_gather(after(down_shard, qkv_z), "fsdp", axis=0, tiled=True)
     cut = ff // 4
     live_rows = live.reshape(2, rows, 1).astype(F32)
     qkv_x, qkv_y, tokens_x, tokens_y, cosine, sine, live_rows = sync(
@@ -1035,39 +1089,38 @@
     gain_one, gain_two = gain_rows[0:1], gain_rows[1:2]
     first_all = first_all.reshape(4, 2, rows, width)
     o_t, lse = attention_forward(q_blocks, slots, seg_q, seg_k, valid_k, q_t, kv_all)
-    o_t, out_down, dy_pieces, gu_w = sync(o_t, out_down, dy_pieces, gu_w)
-    out_w = out_down[:, :r].reshape(n * r, width)
-    down_w = out_down[:, r:].reshape(cut, width)
-    dy_all, out_w = sync(jnp.stack(dy_pieces).reshape(4, row_count, width), out_w)
+    o_t, out_gu, dy_pieces, down_w = sync(o_t, out_gu, dy_pieces, down_w)
+    dy_all, gu_w = sync(
+        jnp.stack(dy_pieces).reshape(4, row_count, width), out_gu[:, width:]
+    )
     attended_t = o_t.reshape(2, width, rows)
-    out_rows = out_down if r % 16 == 0 else out_w.reshape(n, r, width)
-    middle, x_own, early_sums = out_project(
-        tokens_own, attended_t, out_rows, gain_two, live_rows, r
-    )
+    middle, x_own, early_sums = out_project(tokens_own, attended_t, out_gu, gain_two, live_rows)
 
     x_x, x_y = swap_x(x_own), swap_y(x_own)
     held = feed_forward(x_own.reshape(1, row_count, width), dy_all, gu_w, down_w, 0, None)
     x_x, x_y, *held = sync(x_x, x_y, *held)
-    parts_0 = held.pop()
+    own_part = held.pop()
     x_d = jnp.concatenate([swap_y(x_x[:1]), swap_x(x_y[1:])])
     x_xy = jnp.stack([x_x, x_y]).reshape(2, row_count, width)
     held = feed_forward(x_xy, dy_all, gu_w, down_w, 1, held)
     x_d, *held = sync(x_d, *held)
-    parts_1 = held.pop()
+    y_low, x_high = held.pop(), held.pop()
     x_d = x_d.reshape(1, row_count, width)
-    *held, parts_2 = feed_forward(x_d, dy_all, gu_w, down_w, 3, held)
-    parts = [v.reshape(2, rows, width) for v in (parts_0[0], parts_1[0], parts_1[1], parts_2[0])]
-    got = scatter_first(parts)
+    *held, to_x, to_y = feed_forward(x_d, dy_all, gu_w, down_w, 3, held)
+    got = swap_x(to_x), swap_y(to_y)
     x_all, hidden, d_gu = [v.reshape(4 * row_count, -1) for v in held]
     dy_all = dy_all.reshape(4 * row_count, width)
     grad_gu = transposed_product(x_all, d_gu, 256)
-    ffn_parts = product(after(hidden, grad_gu), down_w, row_count)
+    ffn_parts = ffn_product(after(hidden, grad_gu), down_w, rows)
     got_low, got_high, grad_gu, ffn_parts = sync(*got, grad_gu, ffn_parts)
-    d_second = scatter_last(*scatter_pass(parts, (got_low, got_high)))
+    got_low, got_high = got_low.astype(F32), got_high.astype(F32)
+    low_own = own_part[:1].astype(F32) + got_low[:1]
+    high_own = own_part[1:].astype(F32) + got_high[:1]
+    from_y = swap_y((y_low.astype(F32) + got_low[1:]).astype(BF16))
+    from_x = swap_x((x_high.astype(F32) + got_high[1:]).astype(BF16))
     grad_d = transposed_product(after(hidden, ffn_parts), dy_all, cut)
+    d_second = low_own, from_y, high_own, from_x
     d_second, grad_d = sync(d_second, grad_d)
-    ffn_parts = ffn_parts.reshape(4, 2, rows, width)
-    ffn_parts = [ffn_parts[i] for i in range(4)]
     own_gu = lax.psum_scatter(grad_gu, "fsdp", scatter_dimension=0, tiled=True)
     own_down = lax.psum_scatter(grad_d, "fsdp", scatter_dimension=0, tiled=True)
 
@@ -1075,12 +1128,13 @@
     nz = n // 2
     r4 = r // 4
     grad_middle, d_branch, do_t, grad_gain_two = middle_back(
-        d_second, middle, dy_own, gain_two, out_w
+        d_second, middle, dy_own, gain_two, out_gu
     )
     do_t = do_t.reshape(2, HEADS, HEAD_DIM, rows)
     whole_out = side_product(attended_t, d_branch)
     do_t, ffn_parts, whole_out = sync(do_t, ffn_parts, whole_out)
-    ffn_got = scatter_first(ffn_parts)
+    ffn_to_x, ffn_to_y, ffn_keep = ffn_parts
+    ffn_got = swap_x(ffn_to_x), swap_y(ffn_to_y)
     d_q, dkv_low, dkv_high, dkv_keep = attention_backward(
         q_blocks, slots, seg_q, seg_k, valid_k, cosine[:2], sine[:2], q_t, kv_all, o_t, do_t, lse
     )
@@ -1096,7 +1150,13 @@
 
     d_q = d_q.reshape(2, q_width, rows)
     dq_parts = [quarter(d_q, q4, i) for i in range(4)]
-    ffn_sums = scatter_pass(ffn_parts, ffn_got)
+    ffn_low, ffn_high = ffn_got[0].astype(F32), ffn_got[1].astype(F32)
+    ffn_sums = (
+        ffn_keep[:1].astype(F32) + ffn_low[:1],
+        ffn_keep[1:2].astype(F32) + ffn_high[:1],
+        (ffn_keep[2:3].astype(F32) + ffn_low[1:]).astype(BF16),
+        (ffn_keep[3:].astype(F32) + ffn_high[1:]).astype(BF16),
+    )
     dkv_got, dq_parts, ffn_sums = sync(dkv_got, dq_parts, ffn_sums)
     kept = dkv_keep.astype(F32)
     low_sums, high_sums = kept[:2] + dkv_got[0].astype(F32), kept[2:] + dkv_got[1].astype(F32)

time: 486 us -> 476 us (0.979)
  local copies, waits for them, and re-layouts: 44 us -> 35.2 us
  other arithmetic: 36.5 us -> 30.5 us
    slice x4 -> x1, local copies, waits for them, and re-layouts: 11.8 us -> 4.72 us  [per_device(): out_gu[:, width:]]
    ppermute x24, waiting for transfers between devices: 39.1 us -> 44.1 us  [swap_x(): return lax.ppermute(v, 'ctx', [(i, i ^ 1) for i in range(4)])]
    unnamed x98 -> x86, local copies, waits for them, and re-layouts: 13 us -> 12.1 us
  transfers between devices with their start and end apart: 71 -> 71, of which waited for: 31 -> 32; matrix products, arithmetic and copies ran while one was open for 13% -> 11% of each run, Pallas kernels for 37% -> 38%
where the time goes in v5:
time: 476 us; the launch traced here: 473 us
  Pallas kernels  198 us (42%)
  waiting for transfers between devices  112 us (24%)
  starting transfers between devices  81.4 us (17%)
  local copies, waits for them, and re-layouts  35.2 us (7%)
  other arithmetic  30.5 us (6%)
  between operations  15.6 us (3%)
    ppermute x24, waiting for transfers between devices, swap_x(): return lax.ppermute(v, 'ctx', [(i, i ^ 1) for i in range(4)])  44.1 us
    ppermute x24, waiting for transfers between devices, swap_y(): return lax.ppermute(v, 'ctx', [(i, i ^ 2) for i in range(4)])  40.1 us
    pallas_call x3, Pallas kernels, feed_forward(): pl.pallas_call(kernel, grid=(count,), in_specs=[pl.BlockSpec((1, rows, wi...  39.7 us
    ppermute x24, starting transfers between devices, swap_y(): return lax.ppermute(v, 'ctx', [(i, i ^ 2) for i in range(4)])  32.6 us
    pallas_call x1, Pallas kernels, attention_backward(): pl.pallas_call(backward_kernel, grid_spec=pltpu.PrefetchScalarGridSpec(nu...  32.4 us
    ppermute x24, starting transfers between devices, swap_x(): return lax.ppermute(v, 'ctx', [(i, i ^ 1) for i in range(4)])  30.1 us
    pallas_call x1, Pallas kernels, attention_forward(): pl.pallas_call(forward_kernel, grid_spec=pltpu.PrefetchScalarGridSpec(num...  26.2 us
    pallas_call x2, Pallas kernels, transposed_product(): pl.pallas_call(kernel, grid=(rows // tile,), in_specs=[pl.BlockSpec((dept...  22.4 us
  transfers between devices with their start and end apart: 71, of which 32 were waited for; matrix products, arithmetic and copies ran while one was open for 11% of the time, Pallas kernels for 38%

profile of v5, /device:TPU:0, one launch (start us, length us, event | category | flops | bytes accessed | tf_op | source)
XLA Modules:
  0.0 472.6 jit_solution(2267077387664557376)
XLA Ops:
  23.8 8.5 %collective-permute-done.1 = bf16[160,512]{1,0:T(8,128)(2,1)S(1)} collective-permute-done((bf16[160,512]{1,0:T(8,128)(2,1)}, bf16[160,512]{1,0:T(8,128)(2,1)S(1)}, u32[]{:S(2)}, u32[]{:S(2)}) %collective-permute-start.1) | collective-permute-done | bytes 163872 | tf_op jit(solution)/shard_map/ppermute | solution.py:66
  45.3 10.6 %collective-permute-done.5 = bf16[4,160,512]{2,1,0:T(8,128)(2,1)S(1)} collective-permute-done((bf16[4,160,512]{2,1,0:T(8,128)(2,1)S(1)}, bf16[4,160,512]{2,1,0:T(8,128)(2,1)S(1)}, u32[]{:S(2)}, u32[]{:S(2)}) %collective-permute-start.5) | collective-permute-done | bytes 655392 | tf_op jit(solution)/shard_map/ppermute | solution.py:30
  63.6 15.3 %collective-permute-done.7 = bf16[2,160,512]{2,1,0:T(8,128)(2,1)S(1)} collective-permute-done((bf16[2,160,512]{2,1,0:T(8,128)(2,1)S(1)}, bf16[2,160,512]{2,1,0:T(8,128)(2,1)S(1)}, u32[]{:S(2)}, u32[]{:S(2)}) %collective-permute-start.7) | collective-permute-done | bytes 327712 | tf_op jit(solution)/shard_map/ppermute | solution.py:34
  91.1 16.3 %shard_map.220 = (bf16[8,216,1280]{2,1,0:T(8,128)(2,1)}, bf16[2,20,64,216]{3,2,1,0:T(8,128)(2,1)}, bf16[8,10,64,216]{3,2,1,0:T(8,128)(2,1)}, bf16[1280,2048]{1,0:T(8,128)(2,1)}, f32[8,1280]{1,0:T(8,128)}) custom-call(s32[2]{0:T(128)} %get-tuple-element.381.at_ref, bf16[2,216,1280]{2,1,0:T(8,128)(2,1)} %bitcast.149, bf16[2,216,1280]{2,1,0:T(8,128)(2,1)} %copy-done.28, ...), custom_call_target="tpu_custom_call" | custom-call | flops 8000000000 | bytes 25000000 | tf_op jit(solution)/shard_map/pallas_call | solution.py:496
  107.4 26.2 %shard_map.221 = (bf16[2,20,64,216]{3,2,1,0:T(8,128)(2,1)}, f32[2,5,4,216]{3,2,1,0:T(4,128)}) custom-call(s32[2]{0:T(128)} %get-tuple-element.380.blocks_ref, s32[8]{0:T(128)} %fusion.23.slots_ref, f32[2,1,216]{2,1,0:T(1,128)} %add_convert_fusion.5.seg_q_ref, f32[8,1,216]{2,1,0:T(1,128)} %convert_element_type.201.seg_k_ref, ...), custom_call_target="tpu_custom_call" | custom-call | flops 20000000000 | bytes 6000000 | tf_op jit(solution)/shard_map/pallas_call | solution.py:570
  138.8 8.3 %all-gather.3.cloned.1.call-done.w_ref = bf16[1280,3072]{1,0:T(8,128)(2,1)} async-done(((bf16[160,3072]{1,0:T(8,128)(2,1)}), bf16[1280,3072]{1,0:T(8,128)(2,1)}) %all-gather.3.cloned.1.call-update) | async-done | bytes 7864336 | tf_op jit(solution)/shard_map/all_gather | solution.py:1061
  147.1 6.5 %shard_map.223 = (f32[2,216,1280]{2,1,0:T(8,128)}, bf16[2,216,1280]{2,1,0:T(8,128)(2,1)}, f32[8,128]{1,0:T(8,128)}) custom-call(bf16[2,216,1280]{2,1,0:T(8,128)(2,1)} %bitcast.150, bf16[2,1280,216]{2,1,0:T(8,128)(2,1)} %bitcast.133, bf16[1280,3072]{1,0:T(8,128)(2,1)} %all-gather.3.cloned.1.call-done.w_ref, f32[1,1280]{1,0:T(1,128)} %get-tuple-element.369.gain_ref, ...), custom_call_target="tpu_custom_call" | custom-call | tf_op jit(solution)/shard_map/pallas_call | solution.py:819
  156.7 4.7 slice.219.gu_ref
  165.0 10.6 %shard_map.224 = (bf16[4,432,1280]{2,1,0:T(8,128)(2,1)}, bf16[4,432,896]{2,1,0:T(8,128)(2,1)}, bf16[4,432,1792]{2,1,0:T(8,128)(2,1)}, bf16[2,216,1280]{2,1,0:T(8,128)(2,1)}) custom-call(bf16[1,432,1280]{2,1,0:T(8,128)(2,1)} %bitcast.173, bf16[4,432,1280]{2,1,0:T(8,128)(2,1)} %pad_maximum_fusion.dy_ref, bf16[1280,1792]{1,0:T(8,128)(2,1)} %slice.219.gu_ref, ...), custom_call_target="tpu_custom_call" | custom-call | flops 4954521600 | bytes 13627392 | tf_op jit(solution)/shard_map/pallas_call | solution.py:690
  175.5 4.9 %collective-permute-done.16 = bf16[2,216,1280]{2,1,0:T(8,128)(2,1)S(1)} collective-permute-done((bf16[2,216,1280]{2,1,0:T(8,128)(2,1)}, bf16[2,216,1280]{2,1,0:T(8,128)(2,1)S(1)}, u32[]{:S(2)}, u32[]{:S(2)}) %collective-permute-start.16) | collective-permute-done | bytes 1105952 | tf_op jit(solution)/shard_map/ppermute | solution.py:30
  186.2 18.6 %shard_map.225 = (bf16[4,432,1280]{2,1,0:T(8,128)(2,1)}, bf16[4,432,896]{2,1,0:T(8,128)(2,1)}, bf16[4,432,1792]{2,1,0:T(8,128)(2,1)}, bf16[2,216,1280]{2,1,0:T(8...) custom-call(bf16[2,432,1280]{2,1,0:T(8,128)(2,1)} %pad_maximum_fusio, ...), custom_call_target="tpu_custom_call", output_to_operand_aliasing={{0}: (4, {}), {1}: (5, {}), {2}: (6, {})} | custom-call | flops 9909043200 | bytes 20373504 | tf_op jit(solution)/shard_map/pallas_call | solution.py:690
  206.0 10.5 %shard_map.226 = (bf16[4,432,1280]{2,1,0:T(8,128)(2,1)}, bf16[4,432,896]{2,1,0:T(8,128)(2,1)}, bf16[4,432,1792]{2,1,0:T(8,128)(2,1)}, bf16[2,216,1280]{2,1,0:T(8,128)(2,1)}, bf16[2,216,1280]{2,1,0:T(8,128)(2,1)}) custom-call(bf16[1,432,1280]{2,1,0:T(8,128)(2,1)} %bitcast.146, ...), custom_call_target="tpu_custom_call", output_to_operand_aliasing={{0}: (4, {}), {1}: (5, {}), {2}: (6, {}), {3}: (7, {}), {4}... | custom-call | flops 4954521600 | bytes 13627392 | tf_op jit(solution)/shard_map/pallas_call | solution.py:690
  218.5 13.5 %shard_map.227 = bf16[1280,1792]{1,0:T(8,128)(2,1)} custom-call(bf16[1728,1280]{1,0:T(8,128)(2,1)} %bitcast.132, bf16[1728,1792]{1,0:T(8,128)(2,1)} %bitcast.131), custom_call_target="tpu_custom_call" | custom-call | tf_op jit(solution)/shard_map/pallas_call | solution.py:731
  232.0 9.7 %shard_map.228 = (bf16[2,216,1280]{2,1,0:T(8,128)(2,1)}, bf16[2,216,1280]{2,1,0:T(8,128)(2,1)}, bf16[4,216,1280]{2,1,0:T(8,128)(2,1)}) custom-call(bf16[1728,896]{1,0:T(8,128)(2,1)} %bitcast.129, bf16[896,1280]{1,0:T(8,128)(2,1)} %all-gather.5.cloned.1.call-done.down_ref.right_ref), custom_call_target="tpu_custom_call" | custom-call | tf_op jit(solution)/shard_map/pallas_call | solution.py:761
  248.4 8.9 %shard_map.229 = bf16[896,1280]{1,0:T(8,128)(2,1)} custom-call(bf16[1728,896]{1,0:T(8,128)(2,1)} %bitcast.130, bf16[1728,1280]{1,0:T(8,128)(2,1)} %bitcast.128), custom_call_target="tpu_custom_call" | custom-call | tf_op jit(solution)/shard_map/pallas_call | solution.py:731
  260.4 8.6 %shard_map.230 = (f32[2,216,1280]{2,1,0:T(8,128)}, bf16[2,216,1280]{2,1,0:T(8,128)(2,1)}, bf16[2,1280,216]{2,1,0:T(8,128)(2,1)}, f32[1,1280]{1,0:T(1,128)}) custom-call(f32[1,216,1280]{2,1,0:T(8,128)} %get-tuple-element.243.low_ref, bf16[1,216,1280]{2,1,0:T(8,128)(2,1)} %copy-done.21, f32[1,216,1280]{2,1,0:T(8,128)} %get-tuple-element.245.high_ref, ...), custom_call_target="tpu_custom_call" | custom-call | tf_op jit(solution)/shard_map/pallas_call | solution.py:879
  269.1 5.3 %shard_map.231 = bf16[1280,1280]{1,0:T(8,128)(2,1)} custom-call(bf16[2,1280,216]{2,1,0:T(8,128)(2,1)} %bitcast.134, bf16[2,216,1280]{2,1,0:T(8,128)(2,1)} %get-tuple-element.248.right_ref), custom_call_target="tpu_custom_call" | custom-call | tf_op jit(solution)/shard_map/pallas_call | solution.py:778
  279.1 32.4 %shard_map.232 = (bf16[2,20,64,216]{3,2,1,0:T(8,128)(2,1)}, bf16[2,2,5,64,216]{4,3,2,1,0:T(8,128)(2,1)}, bf16[2,2,5,64,216]{4,3,2,1,0:T(8,128)(2,1)}, bf16[4,2,5,64,216]{4,3,2,1,0:T(8,128)(2,1)}) custom-call(s32[2]{0:T(128)} %get-tuple-element.380.blocks_ref, s32[8]{0:T(128)} %fusion.23.slots_ref, f32[2,1,216]{2,1,0:T(1,128)} %add_convert_fusion.5.seg_q_ref, ...), custom_call_target="tpu_custom_call" | custom-call | tf_op jit(solution)/shard_map/pallas_call | solution.py:606
  311.8 5.4 %collective-permute-start.26 = (bf16[2,2,5,64,216]{4,3,2,1,0:T(8,128)(2,1)}, bf16[2,2,5,64,216]{4,3,2,1,0:T(8,128)(2,1)S(1)}, u32[]{:S(2)}, u32[]{:S(2)}) collective-permute-start(bf16[2,2,5,64,216]{4,3,2,1,0:T(8,128)(2,1)} %get-tuple-element.257), channel_id=1, source_target_pairs={{0,8},{8,0},{16,24},{24,16},{1,9},{9,1},{17,25},{25,17},{2,10},{10... | collective-permute-start | bytes 1658888 | tf_op jit(solution)/shard_map/ppermute | solution.py:30
  317.2 5.0 %collective-permute-start.27 = (bf16[2,2,5,64,216]{4,3,2,1,0:T(8,128)(2,1)S(1)}, bf16[2,2,5,64,216]{4,3,2,1,0:T(8,128)(2,1)S(1)}, u32[]{:S(2)}, u32[]{:S(2)}) collective-permute-start(bf16[2,2,5,64,216]{4,3,2,1,0:T(8,128)(2,1)S(1)} %copy-done.39), channel_id=1, source_target_pairs={{0,16},{8,24},{16,0},{24,8},{1,17},{9,25},{17,1},{25,9},{2,18},{10... | collective-permute-start | bytes 1658888 | tf_op jit(solution)/shard_map/ppermute | solution.py:34
  338.1 10.9 %collective-permute-done.31 = bf16[2,5,64,216]{3,2,1,0:T(8,128)(2,1)S(1)} collective-permute-done((bf16[2,5,64,216]{3,2,1,0:T(8,128)(2,1)S(1)}, bf16[2,5,64,216]{3,2,1,0:T(8,128)(2,1)S(1)}, u32[]{:S(2)}, u32[]{:S(2)}) %collective-permute-start.31) | collective-permute-done | bytes 276512 | tf_op jit(solution)/shard_map/ppermute | solution.py:30
  372.6 6.8 %shard_map.233 = bf16[1280,480]{1,0:T(8,128)(2,1)} custom-call(bf16[8,216,1280]{2,1,0:T(8,128)(2,1)} %get-tuple-element.274.first_ref, bf16[2,320,216]{2,1,0:T(8,128)(2,1)} %get-tuple-element.275.refs_0_, bf16[3,320,216]{2,1,0:T(8,128)(2,1)} %copy-done.15, bf16[3,320,216]{2,1,0:T(8,128)(2,1)} %copy-done.16, bf16[2,160,216]{2,1,0:T(8,128)(2,1)} %get-tuple-element.349.refs_3_, ...), custom_call_target="tpu_custom_call" | custom-call | tf_op jit(solution)/shard_map/pallas_call | solution.py:542
  396.4 9.2 %shard_map.234 = (bf16[2,216,1280]{2,1,0:T(8,128)(2,1)}, f32[1,1280]{1,0:T(1,128)}, f32[8,128]{1,0:T(8,128)}) custom-call(bf16[2,1280,216]{2,1,0:T(8,128)(2,1)} %bitcast.144, bf16[2,640,216]{2,1,0:T(8,128)(2,1)} %bitcast.137, bf16[1280,2048]{1,0:T(8,128)(2,1)} %get-tuple-element.293.w_ref, bf16[2,216,1280]{2,1,0:T(8,128)(2,1)} %bitcast.151, ...), custom_call_target="tpu_custom_call" | custom-call | tf_op jit(solution)/shard_map/pallas_call | solution.py:922
  443.7 4.9 %shard_map.237 = (f32[160,3584]{1,0:T(8,128)}, f32[160,3584]{1,0:T(8,128)}) custom-call(s32[1]{0:T(128)} %bitcast.1.c_ref, bf16[160,1792]{1,0:T(8,128)(2,1)} %reduce-scatter.4.cloned.1.call-done.refs_0_, bf16[160,1792]{1,0:T(8,128)(2,1)} %collective-permute-done.44.refs_1_, bf16[160,1792]{1,0:T(8,128)(2,1)} %collective-permute-done.45.refs_2_, ...), custom_call_target="tpu_custom_call" | custom-call | bytes 6881280 | tf_op jit(solution)/shard_map/pallas_call | solution.py:211
  (339 shorter events, 195.1 us)
Async XLA Ops:
  7.2 127.9 %all-gather.5.cloned.1.call-start = ((), (), s32[]{:S(2)}) async-start(), calls=%async_computation.4 | async-start | bytes 2580480 | tf_op jit(solution)/shard_map/all_gather | solution.py:1062
  7.2 27.6 %collective-permute-start.3 = (bf16[2,216,1280]{2,1,0:T(8,128)(2,1)}, bf16[2,216,1280]{2,1,0:T(8,128)(2,1)S(1)}, u32[]{:S(2)}, u32[]{:S(2)}) collective-permute-start(bf16[2,216,1280]{2,1,0:T(8,128)(2,1)} %bitcast.147), channel_id=1, source_target_pairs={{0,8},{8,0},{16,24},{24,16},{1,9},{9,1},{17,25},{25,17},{2,10},{10... | collective-permute-start | bytes 3317768 | tf_op jit(solution)/shard_map/ppermute | solution.py:30
  10.2 26.2 %collective-permute-start.4 = (bf16[2,216,1280]{2,1,0:T(8,128)(2,1)}, bf16[2,216,1280]{2,1,0:T(8,128)(2,1)}, u32[]{:S(2)}, u32[]{:S(2)}) collective-permute-start(bf16[2,216,1280]{2,1,0:T(8,128)(2,1)} %bitcast.148), channel_id=1, source_target_pairs={{0,16},{8,24},{16,0},{24,8},{1,17},{9,25},{17,1},{25,9},{2,18},{10... | collective-permute-start | bytes 3317768 | tf_op jit(solution)/shard_map/ppermute | solution.py:34
  36.4 110.7 %all-gather.3.cloned.1.call-start = ((), (), s32[]{:S(2)}) async-start(), calls=%async_computation.3 | async-start | bytes 8847360 | tf_op jit(solution)/shard_map/all_gather | solution.py:1061
  39.6 271.9 %reduce-scatter.4.cloned.1.call-start = ((), (), s32[]{:S(2)}) async-start(), calls=%async_computation.5 | async-start | bytes 5160960 | tf_op jit(solution)/shard_map/reduce_scatter | solution.py:1124
  56.8 25.4 %collective-permute-start.11 = (bf16[3,4,160,512]{3,2,1,0:T(8,128)(2,1)S(1)}, bf16[3,4,160,512]{3,2,1,0:T(8,128)(2,1)S(1)}, u32[]{:S(2)}, u32[]{:S(2)}) collective-permute-start(bf16[3,4,160,512]{3,2,1,0:T(8,128)(2,1)S(1)} %pad_maximum_fusion.3.refs_5_), channel_id=1, source_target_pairs={{0,1},{1,0},{2,3},{3,2},{4,5},{5,4},{6,7},{7,6},{8,9},{9,8},{10,11... | collective-permute-start | bytes 5898248 | tf_op jit(solution)/shard_map/ppermute | solution.py:26
  58.2 23.1 %collective-permute-start.9 = (bf16[1,216,1280]{2,1,0:T(8,128)(2,1)S(1)}, bf16[1,216,1280]{2,1,0:T(8,128)(2,1)S(1)}, u32[]{:S(2)}, u32[]{:S(2)}) collective-permute-start(bf16[1,216,1280]{2,1,0:T(8,128)(2,1)S(1)} %slice.214), channel_id=1, source_target_pairs={{0,16},{8,24},{16,0},{24,8},{1,17},{9,25},{17,1},{25,9},{2,18},{10... | collective-permute-start | bytes 1658888 | tf_op jit(solution)/shard_map/ppermute | solution.py:34
  60.9 20.4 %collective-permute-start.10 = (bf16[1,216,1280]{2,1,0:T(8,128)(2,1)S(1)}, bf16[1,216,1280]{2,1,0:T(8,128)(2,1)S(1)}, u32[]{:S(2)}, u32[]{:S(2)}) collective-permute-start(bf16[1,216,1280]{2,1,0:T(8,128)(2,1)S(1)} %slice.215), channel_id=1, source_target_pairs={{0,8},{8,0},{16,24},{24,16},{1,9},{9,1},{17,25},{25,17},{2,10},{10... | collective-permute-start | bytes 1658888 | tf_op jit(solution)/shard_map/ppermute | solution.py:30
  87.6 47.5 %collective-permute-start.13 = (bf16[2,216,1280]{2,1,0:T(8,128)(2,1)S(1)}, bf16[2,216,1280]{2,1,0:T(8,128)(2,1)S(1)}, u32[]{:S(2)}, u32[]{:S(2)}) collective-permute-start(bf16[2,216,1280]{2,1,0:T(8,128)(2,1)S(1)} %bitcast.153), channel_id=1, source_target_pairs={{0,8},{8,0},{16,24},{24,16},{1,9},{9,1},{17,25},{25,17},{2,10},{10... | collective-permute-start | bytes 3317768 | tf_op jit(solution)/shard_map/ppermute | solution.py:30
  88.7 50.1 %collective-permute-start.14 = (bf16[2,216,1280]{2,1,0:T(8,128)(2,1)S(1)}, bf16[2,216,1280]{2,1,0:T(8,128)(2,1)S(1)}, u32[]{:S(2)}, u32[]{:S(2)}) collective-permute-start(bf16[2,216,1280]{2,1,0:T(8,128)(2,1)S(1)} %bitcast.154), channel_id=1, source_target_pairs={{0,16},{8,24},{16,0},{24,8},{1,17},{9,25},{17,1},{25,9},{2,18},{10... | collective-permute-start | bytes 3317768 | tf_op jit(solution)/shard_map/ppermute | solution.py:34
  89.2 49.6 %collective-permute-start.15 = (bf16[2,216,1280]{2,1,0:T(8,128)(2,1)S(1)}, bf16[2,216,1280]{2,1,0:T(8,128)(2,1)}, u32[]{:S(2)}, u32[]{:S(2)}) collective-permute-start(bf16[2,216,1280]{2,1,0:T(8,128)(2,1)S(1)} %bitcast.155), channel_id=1, source_target_pairs={{0,24},{8,16},{16,8},{24,0},{1,25},{9,17},{17,9},{25,1},{2,26},{10... | collective-permute-start | bytes 3317768 | tf_op jit(solution)/shard_map/ppermute | solution.py:104
  153.7 26.8 %collective-permute-start.16 = (bf16[2,216,1280]{2,1,0:T(8,128)(2,1)}, bf16[2,216,1280]{2,1,0:T(8,128)(2,1)S(1)}, u32[]{:S(2)}, u32[]{:S(2)}) collective-permute-start(bf16[2,216,1280]{2,1,0:T(8,128)(2,1)} %get-tuple-element.195), channel_id=1, source_target_pairs={{0,8},{8,0},{16,24},{24,16},{1,9},{9,1},{17,25},{25,17},{2,10},{10... | collective-permute-start | bytes 3317768 | tf_op jit(solution)/shard_map/ppermute | solution.py:30
  155.2 26.5 %collective-permute-start.17 = (bf16[2,216,1280]{2,1,0:T(8,128)(2,1)}, bf16[2,216,1280]{2,1,0:T(8,128)(2,1)S(1)}, u32[]{:S(2)}, u32[]{:S(2)}) collective-permute-start(bf16[2,216,1280]{2,1,0:T(8,128)(2,1)} %get-tuple-element.195), channel_id=1, source_target_pairs={{0,16},{8,24},{16,0},{24,8},{1,17},{9,25},{17,1},{25,9},{2,18},{10... | collective-permute-start | bytes 3317768 | tf_op jit(solution)/shard_map/ppermute | solution.py:34
  181.7 23.1 %collective-permute-start.19 = (bf16[1,216,1280]{2,1,0:T(8,128)(2,1)S(1)}, bf16[1,216,1280]{2,1,0:T(8,128)(2,1)S(1)}, u32[]{:S(2)}, u32[]{:S(2)}) collective-permute-start(bf16[1,216,1280]{2,1,0:T(8,128)(2,1)S(1)} %slice.222), channel_id=1, source_target_pairs={{0,8},{8,0},{16,24},{24,16},{1,9},{9,1},{17,25},{25,17},{2,10},{10... | collective-permute-start | bytes 1658888 | tf_op jit(solution)/shard_map/ppermute | solution.py:30
  183.2 21.7 %collective-permute-start.18 = (bf16[1,216,1280]{2,1,0:T(8,128)(2,1)}, bf16[1,216,1280]{2,1,0:T(8,128)(2,1)S(1)}, u32[]{:S(2)}, u32[]{:S(2)}) collective-permute-start(bf16[1,216,1280]{2,1,0:T(8,128)(2,1)} %slice.221), channel_id=1, source_target_pairs={{0,16},{8,24},{16,0},{24,8},{1,17},{9,25},{17,1},{25,9},{2,18},{10... | collective-permute-start | bytes 1658888 | tf_op jit(solution)/shard_map/ppermute | solution.py:34
  216.5 25.2 %collective-permute-start.20 = (bf16[2,216,1280]{2,1,0:T(8,128)(2,1)}, bf16[2,216,1280]{2,1,0:T(8,128)(2,1)S(1)}, u32[]{:S(2)}, u32[]{:S(2)}) collective-permute-start(bf16[2,216,1280]{2,1,0:T(8,128)(2,1)} %get-tuple-element.226), channel_id=1, source_target_pairs={{0,8},{8,0},{16,24},{24,16},{1,9},{9,1},{17,25},{25,17},{2,10},{10... | collective-permute-start | bytes 3317768 | tf_op jit(solution)/shard_map/ppermute | solution.py:30
  218.0 24.8 %collective-permute-start.21 = (bf16[2,216,1280]{2,1,0:T(8,128)(2,1)}, bf16[2,216,1280]{2,1,0:T(8,128)(2,1)S(1)}, u32[]{:S(2)}, u32[]{:S(2)}) collective-permute-start(bf16[2,216,1280]{2,1,0:T(8,128)(2,1)} %get-tuple-element.227), channel_id=1, source_target_pairs={{0,16},{8,24},{16,0},{24,8},{1,17},{9,25},{17,1},{25,9},{2,18},{10... | collective-permute-start | bytes 3317768 | tf_op jit(solution)/shard_map/ppermute | solution.py:34
  242.8 129.2 %reduce-scatter.6.cloned.1.call-start = ((), (), s32[]{:S(2)}) async-start(), calls=%async_computation.6 | async-start | bytes 3686400 | tf_op jit(solution)/shard_map/reduce_scatter | solution.py:1143
  274.4 37.0 %collective-permute-start.24 = (bf16[2,216,1280]{2,1,0:T(8,128)(2,1)}, bf16[2,216,1280]{2,1,0:T(8,128)(2,1)S(1)}, u32[]{:S(2)}, u32[]{:S(2)}) collective-permute-start(bf16[2,216,1280]{2,1,0:T(8,128)(2,1)} %get-tuple-element.255), channel_id=1, source_target_pairs={{0,8},{8,0},{16,24},{24,16},{1,9},{9,1},{17,25},{25,17},{2,10},{10... | collective-permute-start | bytes 3317768 | tf_op jit(solution)/shard_map/ppermute | solution.py:30
  275.0 36.4 %collective-permute-start.25 = (bf16[2,216,1280]{2,1,0:T(8,128)(2,1)S(1)}, bf16[2,216,1280]{2,1,0:T(8,128)(2,1)S(1)}, u32[]{:S(2)}, u32[]{:S(2)}) collective-permute-start(bf16[2,216,1280]{2,1,0:T(8,128)(2,1)S(1)} %copy-done.38), channel_id=1, source_target_pairs={{0,16},{8,24},{16,0},{24,8},{1,17},{9,25},{17,1},{25,9},{2,18},{10... | collective-permute-start | bytes 3317768 | tf_op jit(solution)/shard_map/ppermute | solution.py:34
  311.5 125.9 %reduce-scatter.8.cloned.1.call-start = ((), (), s32[]{:S(2)}) async-start(), calls=%async_computation.7 | async-start | bytes 2580480 | tf_op jit(solution)/shard_map/reduce_scatter | solution.py:1125
  332.9 22.3 %collective-permute-start.28 = (bf16[3,320,216]{2,1,0:T(8,128)(2,1)S(1)}, bf16[3,320,216]{2,1,0:T(8,128)(2,1)S(1)}, u32[]{:S(2)}, u32[]{:S(2)}) collective-permute-start(bf16[3,320,216]{2,1,0:T(8,128)(2,1)S(1)} %pad_maximum_fusion.9), channel_id=1, source_target_pairs={{0,8},{8,0},{16,24},{24,16},{1,9},{9,1},{17,25},{25,17},{2,10},{10... | collective-permute-start | bytes 1244168 | tf_op jit(solution)/shard_map/ppermute | solution.py:30
  386.4 25.3 %collective-permute-start.44 = (bf16[160,1792]{1,0:T(8,128)(2,1)}, bf16[160,1792]{1,0:T(8,128)(2,1)}, u32[]{:S(2)}, u32[]{:S(2)}) collective-permute-start(bf16[160,1792]{1,0:T(8,128)(2,1)} %reduce-scatter.4.cloned.1.call-done.refs_0_), channel_id=1, source_target_pairs={{0,8},{8,0},{16,24},{24,16},{1,9},{9,1},{17,25},{25,17},{2,10},{10... | collective-permute-start | bytes 1720328 | tf_op jit(solution)/shard_map/ppermute | solution.py:30
  388.1 23.7 %collective-permute-start.45 = (bf16[160,1792]{1,0:T(8,128)(2,1)}, bf16[160,1792]{1,0:T(8,128)(2,1)}, u32[]{:S(2)}, u32[]{:S(2)}) collective-permute-start(bf16[160,1792]{1,0:T(8,128)(2,1)} %reduce-scatter.4.cloned.1.call-done.refs_0_), channel_id=1, source_target_pairs={{0,16},{8,24},{16,0},{24,8},{1,17},{9,25},{17,1},{25,9},{2,18},{10... | collective-permute-start | bytes 1720328 | tf_op jit(solution)/shard_map/ppermute | solution.py:34
  (90 other events, 745.4 us)
Sparse Core Ops, SparseCore 0:
  36.6 30.9 all-gather.4
  69.7 77.3 all-gather.2
  242.9 50.4 reduce-scatter.3
  311.6 47.2 reduce-scatter.5
  366.1 38.2 reduce-scatter.7

commit v6 on v5

--- a/solution.py
+++ b/solution.py
@@ -945,11 +945,23 @@
 def finish(middle, branch_ffn, live, gain_one, gain_two, early_sums, late_sums):
     sides, rows, width = middle.shape
 
-    def kernel(m_ref, f_ref, live_ref, one_ref, two_ref, early_ref, late_ref, out_ref, small_ref):
-        result = m_ref[0] + f_ref[0]
+    def kernel(
+        m_ref, low_ref, high_ref, from_y_ref, from_x_ref, live_ref, one_ref, two_ref, early_ref,
+        late_ref, out_ref, small_ref, f_ref,
+    ):
+        @pl.when(pl.program_id(0) == 0)
+        def _():
+            f_ref[...] = low_ref[0] + from_y_ref[0].astype(F32)
+
+        @pl.when(pl.program_id(0) == 1)
+        def _():
+            f_ref[...] = high_ref[0] + from_x_ref[0].astype(F32)
+
+        ffn = f_ref[...]
+        result = m_ref[0] + ffn
         out_ref[0] = result.astype(BF16)
         mask = live_ref[0]
-        own = [jnp.sum(mask * result * result), jnp.sum(mask * f_ref[0] * f_ref[0]), jnp.sum(mask)]
+        own = [jnp.sum(mask * result * result), jnp.sum(mask * ffn * ffn), jnp.sum(mask)]
         first = pl.program_id(0) == 0
         row = lax.broadcasted_iota(jnp.int32, (8, width), 0)
         value = jnp.where(row == 2, own[0], 0.0)
@@ -971,7 +983,10 @@
         grid=(sides,),
         in_specs=[
             side_spec(rows, width),
-            side_spec(rows, width),
+            fixed((1, rows, width)),
+            fixed((1, rows, width)),
+            fixed((1, rows, width)),
+            fixed((1, rows, width)),
             side_spec(rows, 1),
             fixed((1, width)),
             fixed((1, width)),
@@ -983,9 +998,10 @@
             jax.ShapeDtypeStruct(middle.shape, BF16),
             jax.ShapeDtypeStruct((8, width), F32),
         ],
+        scratch_shapes=[pltpu.VMEM((rows, width), F32)],
         compiler_params=pltpu.CompilerParams(vmem_limit_bytes=VMEM_LIMIT),
         cost_estimate=BESIDE,
-    )(middle, branch_ffn, live, gain_one, gain_two, early_sums, late_sums)
+    )(middle, *branch_ffn, live, gain_one, gain_two, early_sums, late_sums)
 
 
 def norm_forward(value_rows, gain):
@@ -1062,8 +1078,8 @@
     down_w = lax.all_gather(after(down_shard, qkv_z), "fsdp", axis=0, tiled=True)
     cut = ff // 4
     live_rows = live.reshape(2, rows, 1).astype(F32)
-    qkv_x, qkv_y, tokens_x, tokens_y, cosine, sine, live_rows = sync(
-        qkv_x, qkv_y, tokens_x, tokens_y, cosine, sine, live_rows
+    qkv_x, qkv_y, tokens_x, tokens_y, cosine, sine, cos_own, sin_own, live_rows = sync(
+        qkv_x, qkv_y, tokens_x, tokens_y, cosine, sine, cosine[:2], sine[:2], live_rows
     )
     zh = qkv_z.shape[0] // 2
     qkv_mine = jnp.stack([qkv_z, qkv_x, qkv_y])
@@ -1136,7 +1152,7 @@
     ffn_to_x, ffn_to_y, ffn_keep = ffn_parts
     ffn_got = swap_x(ffn_to_x), swap_y(ffn_to_y)
     d_q, dkv_low, dkv_high, dkv_keep = attention_backward(
-        q_blocks, slots, seg_q, seg_k, valid_k, cosine[:2], sine[:2], q_t, kv_all, o_t, do_t, lse
+        q_blocks, slots, seg_q, seg_k, valid_k, cos_own, sin_own, q_t, kv_all, o_t, do_t, lse
     )
     d_q, dkv_low, dkv_high, dkv_keep, ffn_got = sync(d_q, dkv_low, dkv_high, dkv_keep, ffn_got)
     dkv_got = swap_x(dkv_low), swap_y(dkv_high)
@@ -1164,7 +1180,7 @@
     dkv_own = jnp.stack([low_sums[0] + from_y.astype(F32), high_sums[0] + from_x.astype(F32)])
     dkv_own = dkv_own.reshape(2, 2 * KV_HEADS, HEAD_DIM, rows)
     dq_got = exchange_first(dq_parts)
-    d_k = turn(dkv_own[:, :KV_HEADS], cosine[:2, None], -sine[:2, None]).astype(BF16)
+    d_k = turn(dkv_own[:, :KV_HEADS], cos_own[:, None], -sin_own[:, None]).astype(BF16)
     d_kv = jnp.concatenate([d_k, dkv_own[:, KV_HEADS:].astype(BF16)], axis=1)
     d_kv = d_kv.reshape(2, 2 * kv_width, rows)
     dkv_parts = [quarter(d_kv, kv4, i) for i in range(4)]
@@ -1188,7 +1204,6 @@
     pair_qkv, d_q, d_kv, ffn_last, own_gu, out_got = sync(
         pair_qkv, d_q, d_kv, ffn_last, own_gu, out_got
     )
-    branch_ffn = jnp.concatenate([v + g.astype(F32) for v, g in zip(ffn_sums[:2], ffn_last)])
     own_qkv = z_scatter(pair_qkv).astype(BF16)
 
     gu_x, gu_y = swap_x(own_gu), swap_y(own_gu)
@@ -1197,7 +1212,7 @@
         d_q, d_kv, qkv_w, tokens_own, grad_middle, gain_one, live_rows
     )
     result, small = finish(
-        middle, branch_ffn, live_rows, grad_gain_one, grad_gain_two, early_sums, late_sums
+        middle, (*ffn_sums[:2], *ffn_last), live_rows, grad_gain_one, grad_gain_two, early_sums, late_sums
     )
     own_qkv, small, gu_x, gu_y, out_sums = sync(own_qkv, small, gu_x, gu_y, out_sums)
 
@@ -1210,8 +1225,8 @@
     gu_d = jnp.concatenate([swap_y(gu_x[:hr]), swap_x(gu_y[hr:])])
     small, own_down, gu_d, own_out = sync(small, own_down, gu_d, own_out)
     small = sum(ctx_fetch_direct(small))
-    down_pieces = ctx_fetch_direct(own_down)
-    out_pieces = ctx_fetch_direct(own_out)
+    last = ctx_fetch_direct(jnp.concatenate([own_out, own_down]))
+    out_pieces, down_pieces = [v[:r4] for v in last], [v[r4:] for v in last]
     grad_q, grad_k, grad_v = join_columns(c_ref, qkv_pieces, q4, kv4)
     grad_gate_w, grad_up_w = unpick_columns(c_ref, [own_gu, gu_x, gu_y, gu_d], n)
     grad_down_w = in_order(down_pieces, 0).reshape(4 * d4, width).astype(F32)

time: 476 us -> 467 us (0.981)
  other arithmetic: 30.5 us -> 23.2 us
    ppermute x24 -> x23, waiting for transfers between devices: 44.1 us -> 40.3 us  [swap_x(): return lax.ppermute(v, 'ctx', [(i, i ^ 1) for i in range(4)])]
    ppermute x24 -> x23, starting transfers between devices: 30.1 us -> 28.2 us  [swap_x(): return lax.ppermute(v, 'ctx', [(i, i ^ 1) for i in range(4)])]
    ppermute x24 -> x23, waiting for transfers between devices: 40.1 us -> 41.3 us  [swap_y(): return lax.ppermute(v, 'ctx', [(i, i ^ 2) for i in range(4)])]
    unnamed x86 -> x99, local copies, waits for them, and re-layouts: 12.1 us -> 12.9 us
    ppermute x24 -> x23, starting transfers between devices: 32.6 us -> 32.6 us  [swap_y(): return lax.ppermute(v, 'ctx', [(i, i ^ 2) for i in range(4)])]
  transfers between devices with their start and end apart: 71 -> 68, of which waited for: 32 -> 33; matrix products, arithmetic and copies ran while one was open for 11% -> 9% of each run, Pallas kernels for 38% -> 39%
where the time goes in v6:
time: 467 us; the launch traced here: 464 us
  Pallas kernels  198 us (42%)
  waiting for transfers between devices  113 us (24%)
  starting transfers between devices  78.9 us (17%)
  local copies, waits for them, and re-layouts  34.8 us (7%)
  other arithmetic  23.2 us (5%)
  between operations  15.8 us (3%)
    ppermute x23, waiting for transfers between devices, swap_y(): return lax.ppermute(v, 'ctx', [(i, i ^ 2) for i in range(4)])  41.3 us
    ppermute x23, waiting for transfers between devices, swap_x(): return lax.ppermute(v, 'ctx', [(i, i ^ 1) for i in range(4)])  40.3 us
    pallas_call x3, Pallas kernels, feed_forward(): pl.pallas_call(kernel, grid=(count,), in_specs=[pl.BlockSpec((1, rows, wi...  39.7 us
    ppermute x23, starting transfers between devices, swap_y(): return lax.ppermute(v, 'ctx', [(i, i ^ 2) for i in range(4)])  32.6 us
    pallas_call x1, Pallas kernels, attention_backward(): pl.pallas_call(backward_kernel, grid_spec=pltpu.PrefetchScalarGridSpec(nu...  32.4 us
    ppermute x23, starting transfers between devices, swap_x(): return lax.ppermute(v, 'ctx', [(i, i ^ 1) for i in range(4)])  28.2 us
    pallas_call x1, Pallas kernels, attention_forward(): pl.pallas_call(forward_kernel, grid_spec=pltpu.PrefetchScalarGridSpec(num...  26.2 us
    pallas_call x2, Pallas kernels, transposed_product(): pl.pallas_call(kernel, grid=(rows // tile,), in_specs=[pl.BlockSpec((dept...  22.4 us
  transfers between devices with their start and end apart: 68, of which 33 were waited for; matrix products, arithmetic and copies ran while one was open for 9% of the time, Pallas kernels for 39%

profile of v6, /device:TPU:0, one launch (start us, length us, event | category | flops | bytes accessed | tf_op | source)
XLA Modules:
  0.0 463.7 jit_solution(17145447969966533388)
XLA Ops:
  23.8 8.5 %collective-permute-done.1 = bf16[160,512]{1,0:T(8,128)(2,1)S(1)} collective-permute-done((bf16[160,512]{1,0:T(8,128)(2,1)}, bf16[160,512]{1,0:T(8,128)(2,1)S(1)}, u32[]{:S(2)}, u32[]{:S(2)}) %collective-permute-start.1) | collective-permute-done | bytes 163872 | tf_op jit(solution)/shard_map/ppermute | solution.py:66
  46.5 9.2 %collective-permute-done.5 = bf16[4,160,512]{2,1,0:T(8,128)(2,1)S(1)} collective-permute-done((bf16[4,160,512]{2,1,0:T(8,128)(2,1)S(1)}, bf16[4,160,512]{2,1,0:T(8,128)(2,1)S(1)}, u32[]{:S(2)}, u32[]{:S(2)}) %collective-permute-start.5) | collective-permute-done | bytes 655392 | tf_op jit(solution)/shard_map/ppermute | solution.py:30
  63.2 15.4 %collective-permute-done.7 = bf16[2,160,512]{2,1,0:T(8,128)(2,1)S(1)} collective-permute-done((bf16[2,160,512]{2,1,0:T(8,128)(2,1)S(1)}, bf16[2,160,512]{2,1,0:T(8,128)(2,1)S(1)}, u32[]{:S(2)}, u32[]{:S(2)}) %collective-permute-start.7) | collective-permute-done | bytes 327712 | tf_op jit(solution)/shard_map/ppermute | solution.py:34
  90.8 16.3 %shard_map.220 = (bf16[8,216,1280]{2,1,0:T(8,128)(2,1)}, bf16[2,20,64,216]{3,2,1,0:T(8,128)(2,1)}, bf16[8,10,64,216]{3,2,1,0:T(8,128)(2,1)}, bf16[1280,2048]{1,0:T(8,128)(2,1)}, f32[8,1280]{1,0:T(8,128)}) custom-call(s32[2]{0:T(128)} %get-tuple-element.383.at_ref, bf16[2,216,1280]{2,1,0:T(8,128)(2,1)} %bitcast.161, bf16[2,216,1280]{2,1,0:T(8,128)(2,1)} %copy-done.34, ...), custom_call_target="tpu_custom_call" | custom-call | flops 8000000000 | bytes 25000000 | tf_op jit(solution)/shard_map/pallas_call | solution.py:496
  107.1 26.2 %shard_map.221 = (bf16[2,20,64,216]{3,2,1,0:T(8,128)(2,1)}, f32[2,5,4,216]{3,2,1,0:T(4,128)}) custom-call(s32[2]{0:T(128)} %get-tuple-element.382.blocks_ref, s32[8]{0:T(128)} %fusion.29.slots_ref, f32[2,1,216]{2,1,0:T(1,128)} %add_convert_fusion.5.seg_q_ref, f32[8,1,216]{2,1,0:T(1,128)} %convert_element_type.195.seg_k_ref, ...), custom_call_target="tpu_custom_call" | custom-call | flops 20000000000 | bytes 6000000 | tf_op jit(solution)/shard_map/pallas_call | solution.py:570
  138.6 8.5 %all-gather.3.cloned.1.call-done.w_ref = bf16[1280,3072]{1,0:T(8,128)(2,1)} async-done(((bf16[160,3072]{1,0:T(8,128)(2,1)}), bf16[1280,3072]{1,0:T(8,128)(2,1)}) %all-gather.3.cloned.1.call-update) | async-done | bytes 7864336 | tf_op jit(solution)/shard_map/all_gather | solution.py:1077
  147.1 6.5 %shard_map.223 = (f32[2,216,1280]{2,1,0:T(8,128)}, bf16[2,216,1280]{2,1,0:T(8,128)(2,1)}, f32[8,128]{1,0:T(8,128)}) custom-call(bf16[2,216,1280]{2,1,0:T(8,128)(2,1)} %bitcast.162, bf16[2,1280,216]{2,1,0:T(8,128)(2,1)} %bitcast.145, bf16[1280,3072]{1,0:T(8,128)(2,1)} %all-gather.3.cloned.1.call-done.w_ref, f32[1,1280]{1,0:T(1,128)} %get-tuple-element.371.gain_ref, ...), custom_call_target="tpu_custom_call" | custom-call | tf_op jit(solution)/shard_map/pallas_call | solution.py:819
  164.9 10.6 %shard_map.224 = (bf16[4,432,1280]{2,1,0:T(8,128)(2,1)}, bf16[4,432,896]{2,1,0:T(8,128)(2,1)}, bf16[4,432,1792]{2,1,0:T(8,128)(2,1)}, bf16[2,216,1280]{2,1,0:T(8,128)(2,1)}) custom-call(bf16[1,432,1280]{2,1,0:T(8,128)(2,1)} %bitcast.185, bf16[4,432,1280]{2,1,0:T(8,128)(2,1)} %pad_maximum_fusion.dy_ref, bf16[1280,1792]{1,0:T(8,128)(2,1)} %slice.235.gu_ref, ...), custom_call_target="tpu_custom_call" | custom-call | flops 4954521600 | bytes 13627392 | tf_op jit(solution)/shard_map/pallas_call | solution.py:690
  175.5 4.9 %collective-permute-done.16 = bf16[2,216,1280]{2,1,0:T(8,128)(2,1)S(1)} collective-permute-done((bf16[2,216,1280]{2,1,0:T(8,128)(2,1)}, bf16[2,216,1280]{2,1,0:T(8,128)(2,1)S(1)}, u32[]{:S(2)}, u32[]{:S(2)}) %collective-permute-start.16) | collective-permute-done | bytes 1105952 | tf_op jit(solution)/shard_map/ppermute | solution.py:30
  186.2 18.6 %shard_map.225 = (bf16[4,432,1280]{2,1,0:T(8,128)(2,1)}, bf16[4,432,896]{2,1,0:T(8,128)(2,1)}, bf16[4,432,1792]{2,1,0:T(8,128)(2,1)}, bf16[2,216,1280]{2,1,0:T(8...) custom-call(bf16[2,432,1280]{2,1,0:T(8,128)(2,1)} %pad_maximum_fusio, ...), custom_call_target="tpu_custom_call", output_to_operand_aliasing={{0}: (4, {}), {1}: (5, {}), {2}: (6, {})} | custom-call | flops 9909043200 | bytes 20373504 | tf_op jit(solution)/shard_map/pallas_call | solution.py:690
  205.9 10.5 %shard_map.226 = (bf16[4,432,1280]{2,1,0:T(8,128)(2,1)}, bf16[4,432,896]{2,1,0:T(8,128)(2,1)}, bf16[4,432,1792]{2,1,0:T(8,128)(2,1)}, bf16[2,216,1280]{2,1,0:T(8,128)(2,1)}, bf16[2,216,1280]{2,1,0:T(8,128)(2,1)}) custom-call(bf16[1,432,1280]{2,1,0:T(8,128)(2,1)} %bitcast.158, ...), custom_call_target="tpu_custom_call", output_to_operand_aliasing={{0}: (4, {}), {1}: (5, {}), {2}: (6, {}), {3}: (7, {}), {4}... | custom-call | flops 4954521600 | bytes 13627392 | tf_op jit(solution)/shard_map/pallas_call | solution.py:690
  218.5 13.5 %shard_map.227 = bf16[1280,1792]{1,0:T(8,128)(2,1)} custom-call(bf16[1728,1280]{1,0:T(8,128)(2,1)} %bitcast.144, bf16[1728,1792]{1,0:T(8,128)(2,1)} %bitcast.143), custom_call_target="tpu_custom_call" | custom-call | tf_op jit(solution)/shard_map/pallas_call | solution.py:731
  232.0 9.7 %shard_map.228 = (bf16[2,216,1280]{2,1,0:T(8,128)(2,1)}, bf16[2,216,1280]{2,1,0:T(8,128)(2,1)}, bf16[4,216,1280]{2,1,0:T(8,128)(2,1)}) custom-call(bf16[1728,896]{1,0:T(8,128)(2,1)} %bitcast.141, bf16[896,1280]{1,0:T(8,128)(2,1)} %all-gather.5.cloned.1.call-done.down_ref.right_ref), custom_call_target="tpu_custom_call" | custom-call | tf_op jit(solution)/shard_map/pallas_call | solution.py:761
  248.4 8.9 %shard_map.229 = bf16[896,1280]{1,0:T(8,128)(2,1)} custom-call(bf16[1728,896]{1,0:T(8,128)(2,1)} %bitcast.142, bf16[1728,1280]{1,0:T(8,128)(2,1)} %bitcast.140), custom_call_target="tpu_custom_call" | custom-call | tf_op jit(solution)/shard_map/pallas_call | solution.py:731
  260.4 8.6 %shard_map.230 = (f32[2,216,1280]{2,1,0:T(8,128)}, bf16[2,216,1280]{2,1,0:T(8,128)(2,1)}, bf16[2,1280,216]{2,1,0:T(8,128)(2,1)}, f32[1,1280]{1,0:T(1,128)}) custom-call(f32[1,216,1280]{2,1,0:T(8,128)} %get-tuple-element.247.low_ref, bf16[1,216,1280]{2,1,0:T(8,128)(2,1)} %copy-done.25, f32[1,216,1280]{2,1,0:T(8,128)} %get-tuple-element.249.high_ref, ...), custom_call_target="tpu_custom_call" | custom-call | tf_op jit(solution)/shard_map/pallas_call | solution.py:879
  269.0 5.3 %shard_map.231 = bf16[1280,1280]{1,0:T(8,128)(2,1)} custom-call(bf16[2,1280,216]{2,1,0:T(8,128)(2,1)} %bitcast.146, bf16[2,216,1280]{2,1,0:T(8,128)(2,1)} %get-tuple-element.252.right_ref), custom_call_target="tpu_custom_call" | custom-call | tf_op jit(solution)/shard_map/pallas_call | solution.py:778
  276.1 32.4 %shard_map.232 = (bf16[2,20,64,216]{3,2,1,0:T(8,128)(2,1)}, bf16[2,2,5,64,216]{4,3,2,1,0:T(8,128)(2,1)}, bf16[2,2,5,64,216]{4,3,2,1,0:T(8,128)(2,1)}, bf16[4,2,5,64,216]{4,3,2,1,0:T(8,128)(2,1)}) custom-call(s32[2]{0:T(128)} %get-tuple-element.382.blocks_ref, s32[8]{0:T(128)} %fusion.29.slots_ref, f32[2,1,216]{2,1,0:T(1,128)} %add_convert_fusion.5.seg_q_ref, ...), custom_call_target="tpu_custom_call" | custom-call | tf_op jit(solution)/shard_map/pallas_call | solution.py:606
  309.4 5.4 %collective-permute-start.26 = (bf16[2,2,5,64,216]{4,3,2,1,0:T(8,128)(2,1)}, bf16[2,2,5,64,216]{4,3,2,1,0:T(8,128)(2,1)S(1)}, u32[]{:S(2)}, u32[]{:S(2)}) collective-permute-start(bf16[2,2,5,64,216]{4,3,2,1,0:T(8,128)(2,1)} %get-tuple-element.261), channel_id=1, source_target_pairs={{0,8},{8,0},{16,24},{24,16},{1,9},{9,1},{17,25},{25,17},{2,10},{10... | collective-permute-start | bytes 1658888 | tf_op jit(solution)/shard_map/ppermute | solution.py:30
  335.6 11.0 %collective-permute-done.31 = bf16[2,5,64,216]{3,2,1,0:T(8,128)(2,1)S(1)} collective-permute-done((bf16[2,5,64,216]{3,2,1,0:T(8,128)(2,1)S(1)}, bf16[2,5,64,216]{3,2,1,0:T(8,128)(2,1)S(1)}, u32[]{:S(2)}, u32[]{:S(2)}) %collective-permute-start.31) | collective-permute-done | bytes 276512 | tf_op jit(solution)/shard_map/ppermute | solution.py:30
  354.9 5.0 %collective-permute-done.33.refs_5_ = bf16[3,160,216]{2,1,0:T(8,128)(2,1)S(1)} collective-permute-done((bf16[3,160,216]{2,1,0:T(8,128)(2,1)S(1)}, bf16[3,160,216]{2,1,0:T(8,128)(2,1)S(1)}, u32[]{:S(2)}, u32[]{:S(2)}) %collective-permute-start.33) | collective-permute-done | bytes 207392 | tf_op jit(solution)/shard_map/ppermute | solution.py:34
  369.2 6.9 %shard_map.233 = bf16[1280,480]{1,0:T(8,128)(2,1)} custom-call(bf16[8,216,1280]{2,1,0:T(8,128)(2,1)} %get-tuple-element.279.first_ref, bf16[2,320,216]{2,1,0:T(8,128)(2,1)} %get-tuple-element.280.refs_0_, bf16[3,320,216]{2,1,0:T(8,128)(2,1)} %copy-done.17, bf16[3,320,216]{2,1,0:T(8,128)(2,1)} %copy-done.18, bf16[2,160,216]{2,1,0:T(8,128)(2,1)} %get-tuple-element.353.refs_3_, ...), custom_call_target="tpu_custom_call" | custom-call | tf_op jit(solution)/shard_map/pallas_call | solution.py:542
  389.0 9.2 %shard_map.234 = (bf16[2,216,1280]{2,1,0:T(8,128)(2,1)}, f32[1,1280]{1,0:T(1,128)}, f32[8,128]{1,0:T(8,128)}) custom-call(bf16[2,1280,216]{2,1,0:T(8,128)(2,1)} %bitcast.156, bf16[2,640,216]{2,1,0:T(8,128)(2,1)} %bitcast.149, bf16[1280,2048]{1,0:T(8,128)(2,1)} %get-tuple-element.297.w_ref, bf16[2,216,1280]{2,1,0:T(8,128)(2,1)} %bitcast.163, ...), custom_call_target="tpu_custom_call" | custom-call | tf_op jit(solution)/shard_map/pallas_call | solution.py:922
  438.3 4.9 %shard_map.237 = (f32[160,3584]{1,0:T(8,128)}, f32[160,3584]{1,0:T(8,128)}) custom-call(s32[1]{0:T(128)} %bitcast.1.c_ref, bf16[160,1792]{1,0:T(8,128)(2,1)} %reduce-scatter.4.cloned.1.call-done.refs_0_, bf16[160,1792]{1,0:T(8,128)(2,1)} %copy-done.9, bf16[160,1792]{1,0:T(8,128)(2,1)} %copy-done.10, bf16[160,1792]{1,0:T(8,128)(2,1)} %pad_maximum_fusion.7.refs_3_), custom_call_target="tpu_custom_call" | custom-call | bytes 6881280 | tf_op jit(solution)/shard_map/pallas_call | solution.py:211
  447.6 6.7 %collective-permute-done.62 = bf16[152,1280]{1,0:T(8,128)(2,1)S(1)} collective-permute-done((bf16[152,1280]{1,0:T(8,128)(2,1)S(1)}, bf16[152,1280]{1,0:T(8,128)(2,1)S(1)}, u32[]{:S(2)}, u32[]{:S(2)}) %collective-permute-start.62) | collective-permute-done | bytes 389152 | tf_op jit(solution)/shard_map/ppermute | solution.py:104
  (345 shorter events, 185.0 us)
Async XLA Ops:
  7.2 127.6 %all-gather.5.cloned.1.call-start = ((), (), s32[]{:S(2)}) async-start(), calls=%async_computation.4 | async-start | bytes 2580480 | tf_op jit(solution)/shard_map/all_gather | solution.py:1078
  7.2 27.6 %collective-permute-start.3 = (bf16[2,216,1280]{2,1,0:T(8,128)(2,1)}, bf16[2,216,1280]{2,1,0:T(8,128)(2,1)S(1)}, u32[]{:S(2)}, u32[]{:S(2)}) collective-permute-start(bf16[2,216,1280]{2,1,0:T(8,128)(2,1)} %bitcast.159), channel_id=1, source_target_pairs={{0,8},{8,0},{16,24},{24,16},{1,9},{9,1},{17,25},{25,17},{2,10},{10... | collective-permute-start | bytes 3317768 | tf_op jit(solution)/shard_map/ppermute | solution.py:30
  10.2 26.2 %collective-permute-start.4 = (bf16[2,216,1280]{2,1,0:T(8,128)(2,1)}, bf16[2,216,1280]{2,1,0:T(8,128)(2,1)}, u32[]{:S(2)}, u32[]{:S(2)}) collective-permute-start(bf16[2,216,1280]{2,1,0:T(8,128)(2,1)} %bitcast.160), channel_id=1, source_target_pairs={{0,16},{8,24},{16,0},{24,8},{1,17},{9,25},{17,1},{25,9},{2,18},{10... | collective-permute-start | bytes 3317768 | tf_op jit(solution)/shard_map/ppermute | solution.py:34
  36.4 110.7 %all-gather.3.cloned.1.call-start = ((), (), s32[]{:S(2)}) async-start(), calls=%async_computation.3 | async-start | bytes 8847360 | tf_op jit(solution)/shard_map/all_gather | solution.py:1077
  39.6 268.9 %reduce-scatter.4.cloned.1.call-start = ((), (), s32[]{:S(2)}) async-start(), calls=%async_computation.5 | async-start | bytes 5160960 | tf_op jit(solution)/shard_map/reduce_scatter | solution.py:1140
  56.5 25.4 %collective-permute-start.11 = (bf16[3,4,160,512]{3,2,1,0:T(8,128)(2,1)S(1)}, bf16[3,4,160,512]{3,2,1,0:T(8,128)(2,1)S(1)}, u32[]{:S(2)}, u32[]{:S(2)}) collective-permute-start(bf16[3,4,160,512]{3,2,1,0:T(8,128)(2,1)S(1)} %pad_maximum_fusion.2.refs_5_), channel_id=1, source_target_pairs={{0,1},{1,0},{2,3},{3,2},{4,5},{5,4},{6,7},{7,6},{8,9},{9,8},{10,11... | collective-permute-start | bytes 5898248 | tf_op jit(solution)/shard_map/ppermute | solution.py:26
  57.8 23.3 %collective-permute-start.9 = (bf16[1,216,1280]{2,1,0:T(8,128)(2,1)S(1)}, bf16[1,216,1280]{2,1,0:T(8,128)(2,1)S(1)}, u32[]{:S(2)}, u32[]{:S(2)}) collective-permute-start(bf16[1,216,1280]{2,1,0:T(8,128)(2,1)S(1)} %slice.232), channel_id=1, source_target_pairs={{0,16},{8,24},{16,0},{24,8},{1,17},{9,25},{17,1},{25,9},{2,18},{10... | collective-permute-start | bytes 1658888 | tf_op jit(solution)/shard_map/ppermute | solution.py:34
  60.5 20.6 %collective-permute-start.10 = (bf16[1,216,1280]{2,1,0:T(8,128)(2,1)S(1)}, bf16[1,216,1280]{2,1,0:T(8,128)(2,1)S(1)}, u32[]{:S(2)}, u32[]{:S(2)}) collective-permute-start(bf16[1,216,1280]{2,1,0:T(8,128)(2,1)S(1)} %slice.233), channel_id=1, source_target_pairs={{0,8},{8,0},{16,24},{24,16},{1,9},{9,1},{17,25},{25,17},{2,10},{10... | collective-permute-start | bytes 1658888 | tf_op jit(solution)/shard_map/ppermute | solution.py:30
  87.3 47.5 %collective-permute-start.13 = (bf16[2,216,1280]{2,1,0:T(8,128)(2,1)S(1)}, bf16[2,216,1280]{2,1,0:T(8,128)(2,1)S(1)}, u32[]{:S(2)}, u32[]{:S(2)}) collective-permute-start(bf16[2,216,1280]{2,1,0:T(8,128)(2,1)S(1)} %bitcast.165), channel_id=1, source_target_pairs={{0,8},{8,0},{16,24},{24,16},{1,9},{9,1},{17,25},{25,17},{2,10},{10... | collective-permute-start | bytes 3317768 | tf_op jit(solution)/shard_map/ppermute | solution.py:30
  88.4 50.1 %collective-permute-start.14 = (bf16[2,216,1280]{2,1,0:T(8,128)(2,1)S(1)}, bf16[2,216,1280]{2,1,0:T(8,128)(2,1)S(1)}, u32[]{:S(2)}, u32[]{:S(2)}) collective-permute-start(bf16[2,216,1280]{2,1,0:T(8,128)(2,1)S(1)} %bitcast.166), channel_id=1, source_target_pairs={{0,16},{8,24},{16,0},{24,8},{1,17},{9,25},{17,1},{25,9},{2,18},{10... | collective-permute-start | bytes 3317768 | tf_op jit(solution)/shard_map/ppermute | solution.py:34
  88.9 49.6 %collective-permute-start.15 = (bf16[2,216,1280]{2,1,0:T(8,128)(2,1)S(1)}, bf16[2,216,1280]{2,1,0:T(8,128)(2,1)}, u32[]{:S(2)}, u32[]{:S(2)}) collective-permute-start(bf16[2,216,1280]{2,1,0:T(8,128)(2,1)S(1)} %bitcast.167), channel_id=1, source_target_pairs={{0,24},{8,16},{16,8},{24,0},{1,25},{9,17},{17,9},{25,1},{2,26},{10... | collective-permute-start | bytes 3317768 | tf_op jit(solution)/shard_map/ppermute | solution.py:104
  153.6 26.8 %collective-permute-start.16 = (bf16[2,216,1280]{2,1,0:T(8,128)(2,1)}, bf16[2,216,1280]{2,1,0:T(8,128)(2,1)S(1)}, u32[]{:S(2)}, u32[]{:S(2)}) collective-permute-start(bf16[2,216,1280]{2,1,0:T(8,128)(2,1)} %get-tuple-element.199), channel_id=1, source_target_pairs={{0,8},{8,0},{16,24},{24,16},{1,9},{9,1},{17,25},{25,17},{2,10},{10... | collective-permute-start | bytes 3317768 | tf_op jit(solution)/shard_map/ppermute | solution.py:30
  155.2 26.5 %collective-permute-start.17 = (bf16[2,216,1280]{2,1,0:T(8,128)(2,1)}, bf16[2,216,1280]{2,1,0:T(8,128)(2,1)S(1)}, u32[]{:S(2)}, u32[]{:S(2)}) collective-permute-start(bf16[2,216,1280]{2,1,0:T(8,128)(2,1)} %get-tuple-element.199), channel_id=1, source_target_pairs={{0,16},{8,24},{16,0},{24,8},{1,17},{9,25},{17,1},{25,9},{2,18},{10... | collective-permute-start | bytes 3317768 | tf_op jit(solution)/shard_map/ppermute | solution.py:34
  181.7 23.1 %collective-permute-start.19 = (bf16[1,216,1280]{2,1,0:T(8,128)(2,1)S(1)}, bf16[1,216,1280]{2,1,0:T(8,128)(2,1)S(1)}, u32[]{:S(2)}, u32[]{:S(2)}) collective-permute-start(bf16[1,216,1280]{2,1,0:T(8,128)(2,1)S(1)} %slice.238), channel_id=1, source_target_pairs={{0,8},{8,0},{16,24},{24,16},{1,9},{9,1},{17,25},{25,17},{2,10},{10... | collective-permute-start | bytes 1658888 | tf_op jit(solution)/shard_map/ppermute | solution.py:30
  183.1 21.7 %collective-permute-start.18 = (bf16[1,216,1280]{2,1,0:T(8,128)(2,1)}, bf16[1,216,1280]{2,1,0:T(8,128)(2,1)S(1)}, u32[]{:S(2)}, u32[]{:S(2)}) collective-permute-start(bf16[1,216,1280]{2,1,0:T(8,128)(2,1)} %slice.237), channel_id=1, source_target_pairs={{0,16},{8,24},{16,0},{24,8},{1,17},{9,25},{17,1},{25,9},{2,18},{10... | collective-permute-start | bytes 1658888 | tf_op jit(solution)/shard_map/ppermute | solution.py:34
  216.4 25.2 %collective-permute-start.20 = (bf16[2,216,1280]{2,1,0:T(8,128)(2,1)}, bf16[2,216,1280]{2,1,0:T(8,128)(2,1)S(1)}, u32[]{:S(2)}, u32[]{:S(2)}) collective-permute-start(bf16[2,216,1280]{2,1,0:T(8,128)(2,1)} %get-tuple-element.230), channel_id=1, source_target_pairs={{0,8},{8,0},{16,24},{24,16},{1,9},{9,1},{17,25},{25,17},{2,10},{10... | collective-permute-start | bytes 3317768 | tf_op jit(solution)/shard_map/ppermute | solution.py:30
  217.9 24.8 %collective-permute-start.21 = (bf16[2,216,1280]{2,1,0:T(8,128)(2,1)}, bf16[2,216,1280]{2,1,0:T(8,128)(2,1)S(1)}, u32[]{:S(2)}, u32[]{:S(2)}) collective-permute-start(bf16[2,216,1280]{2,1,0:T(8,128)(2,1)} %get-tuple-element.231), channel_id=1, source_target_pairs={{0,16},{8,24},{16,0},{24,8},{1,17},{9,25},{17,1},{25,9},{2,18},{10... | collective-permute-start | bytes 3317768 | tf_op jit(solution)/shard_map/ppermute | solution.py:34
  242.7 125.7 %reduce-scatter.6.cloned.1.call-start = ((), (), s32[]{:S(2)}) async-start(), calls=%async_computation.6 | async-start | bytes 3686400 | tf_op jit(solution)/shard_map/reduce_scatter | solution.py:1159
  274.3 34.1 %collective-permute-start.24 = (bf16[2,216,1280]{2,1,0:T(8,128)(2,1)}, bf16[2,216,1280]{2,1,0:T(8,128)(2,1)S(1)}, u32[]{:S(2)}, u32[]{:S(2)}) collective-permute-start(bf16[2,216,1280]{2,1,0:T(8,128)(2,1)} %get-tuple-element.259), channel_id=1, source_target_pairs={{0,8},{8,0},{16,24},{24,16},{1,9},{9,1},{17,25},{25,17},{2,10},{10... | collective-permute-start | bytes 3317768 | tf_op jit(solution)/shard_map/ppermute | solution.py:30
  275.0 33.5 %collective-permute-start.25 = (bf16[2,216,1280]{2,1,0:T(8,128)(2,1)S(1)}, bf16[2,216,1280]{2,1,0:T(8,128)(2,1)S(1)}, u32[]{:S(2)}, u32[]{:S(2)}) collective-permute-start(bf16[2,216,1280]{2,1,0:T(8,128)(2,1)S(1)} %copy-done.44), channel_id=1, source_target_pairs={{0,16},{8,24},{16,0},{24,8},{1,17},{9,25},{17,1},{25,9},{2,18},{10... | collective-permute-start | bytes 3317768 | tf_op jit(solution)/shard_map/ppermute | solution.py:34
  308.6 122.7 %reduce-scatter.8.cloned.1.call-start = ((), (), s32[]{:S(2)}) async-start(), calls=%async_computation.7 | async-start | bytes 2580480 | tf_op jit(solution)/shard_map/reduce_scatter | solution.py:1141
  330.4 22.7 %collective-permute-start.28 = (bf16[3,320,216]{2,1,0:T(8,128)(2,1)S(1)}, bf16[3,320,216]{2,1,0:T(8,128)(2,1)S(1)}, u32[]{:S(2)}, u32[]{:S(2)}) collective-permute-start(bf16[3,320,216]{2,1,0:T(8,128)(2,1)S(1)} %pad_maximum_fusion.8), channel_id=1, source_target_pairs={{0,8},{8,0},{16,24},{24,16},{1,9},{9,1},{17,25},{25,17},{2,10},{10... | collective-permute-start | bytes 1244168 | tf_op jit(solution)/shard_map/ppermute | solution.py:30
  382.9 22.6 %collective-permute-start.44 = (bf16[160,1792]{1,0:T(8,128)(2,1)S(1)}, bf16[160,1792]{1,0:T(8,128)(2,1)S(1)}, u32[]{:S(2)}, u32[]{:S(2)}) collective-permute-start(bf16[160,1792]{1,0:T(8,128)(2,1)S(1)} %copy-done.24), channel_id=1, source_target_pairs={{0,8},{8,0},{16,24},{24,16},{1,9},{9,1},{17,25},{25,17},{2,10},{10... | collective-permute-start | bytes 1720328 | tf_op jit(solution)/shard_map/ppermute | solution.py:30
  384.7 20.9 %collective-permute-start.45 = (bf16[160,1792]{1,0:T(8,128)(2,1)S(1)}, bf16[160,1792]{1,0:T(8,128)(2,1)S(1)}, u32[]{:S(2)}, u32[]{:S(2)}) collective-permute-start(bf16[160,1792]{1,0:T(8,128)(2,1)S(1)} %copy-done.24), channel_id=1, source_target_pairs={{0,16},{8,24},{16,0},{24,8},{1,17},{9,25},{17,1},{25,9},{2,18},{10... | collective-permute-start | bytes 1720328 | tf_op jit(solution)/shard_map/ppermute | solution.py:34
  (93 other events, 792.5 us)
Sparse Core Ops, SparseCore 0:
  36.6 31.0 all-gather.4
  69.9 77.1 all-gather.2
  242.8 50.4 reduce-scatter.3
  308.7 47.1 reduce-scatter.5
  358.6 36.9 reduce-scatter.7

commit v7 on v6

--- a/solution.py
+++ b/solution.py
@@ -1105,9 +1105,9 @@
     gain_one, gain_two = gain_rows[0:1], gain_rows[1:2]
     first_all = first_all.reshape(4, 2, rows, width)
     o_t, lse = attention_forward(q_blocks, slots, seg_q, seg_k, valid_k, q_t, kv_all)
-    o_t, out_gu, dy_pieces, down_w = sync(o_t, out_gu, dy_pieces, down_w)
-    dy_all, gu_w = sync(
-        jnp.stack(dy_pieces).reshape(4, row_count, width), out_gu[:, width:]
+    o_t, out_gu, dy_pieces = sync(o_t, out_gu, dy_pieces)
+    dy_all, gu_w, down_w = sync(
+        jnp.stack(dy_pieces).reshape(4, row_count, width), out_gu[:, width:], down_w
     )
     attended_t = o_t.reshape(2, width, rows)
     middle, x_own, early_sums = out_project(tokens_own, attended_t, out_gu, gain_two, live_rows)

time: 467 us -> 461 us (0.987)
  waiting for transfers between devices: 113 us -> 99.7 us
  starting transfers between devices: 78.9 us -> 83.7 us
    all_gather x1, waiting for transfers between devices: 8.52 us -> 0.01 us  [per_device(): out_gu = lax.all_gather(picked, 'fsdp', axis=0, tiled=True)]
    unnamed x99 -> x93, local copies, waits for them, and re-layouts: 12.9 us -> 9.34 us
  transfers between devices with their start and end apart: 68 -> 68, of which waited for: 33 -> 32; matrix products, arithmetic and copies ran while one was open for 9% -> 10% of each run, Pallas kernels for 39% -> 41%
where the time goes in v7:
time: 461 us; the launch traced here: 456 us
  Pallas kernels  199 us (43%)
  waiting for transfers between devices  99.7 us (22%)
  starting transfers between devices  83.7 us (18%)
  local copies, waits for them, and re-layouts  33.5 us (7%)
  other arithmetic  25 us (5%)
  between operations  15.6 us (3%)
    ppermute x23, waiting for transfers between devices, swap_y(): return lax.ppermute(v, 'ctx', [(i, i ^ 2) for i in range(4)])  41.3 us
    pallas_call x3, Pallas kernels, feed_forward(): pl.pallas_call(kernel, grid=(count,), in_specs=[pl.BlockSpec((1, rows, wi...  39.5 us
    ppermute x23, waiting for transfers between devices, swap_x(): return lax.ppermute(v, 'ctx', [(i, i ^ 1) for i in range(4)])  36.6 us
    ppermute x23, starting transfers between devices, swap_y(): return lax.ppermute(v, 'ctx', [(i, i ^ 2) for i in range(4)])  33.8 us
    pallas_call x1, Pallas kernels, attention_backward(): pl.pallas_call(backward_kernel, grid_spec=pltpu.PrefetchScalarGridSpec(nu...  32.4 us
    ppermute x23, starting transfers between devices, swap_x(): return lax.ppermute(v, 'ctx', [(i, i ^ 1) for i in range(4)])  29.8 us
    pallas_call x1, Pallas kernels, attention_forward(): pl.pallas_call(forward_kernel, grid_spec=pltpu.PrefetchScalarGridSpec(num...  26.2 us
    pallas_call x2, Pallas kernels, transposed_product(): pl.pallas_call(kernel, grid=(rows // tile,), in_specs=[pl.BlockSpec((dept...  22.5 us
  transfers between devices with their start and end apart: 68, of which 32 were waited for; matrix products, arithmetic and copies ran while one was open for 10% of the time, Pallas kernels for 41%

profile of v7, /device:TPU:0, one launch (start us, length us, event | category | flops | bytes accessed | tf_op | source)
XLA Modules:
  0.0 456.4 jit_solution(8651208516433139280)
XLA Ops:
  23.8 8.5 %collective-permute-done.1 = bf16[160,512]{1,0:T(8,128)(2,1)S(1)} collective-permute-done((bf16[160,512]{1,0:T(8,128)(2,1)}, bf16[160,512]{1,0:T(8,128)(2,1)S(1)}, u32[]{:S(2)}, u32[]{:S(2)}) %collective-permute-start.1) | collective-permute-done | bytes 163872 | tf_op jit(solution)/shard_map/ppermute | solution.py:66
  43.2 9.1 %collective-permute-done.5 = bf16[4,160,512]{2,1,0:T(8,128)(2,1)S(1)} collective-permute-done((bf16[4,160,512]{2,1,0:T(8,128)(2,1)S(1)}, bf16[4,160,512]{2,1,0:T(8,128)(2,1)S(1)}, u32[]{:S(2)}, u32[]{:S(2)}) %collective-permute-start.5) | collective-permute-done | bytes 655392 | tf_op jit(solution)/shard_map/ppermute | solution.py:30
  63.5 14.0 %collective-permute-done.7 = bf16[2,160,512]{2,1,0:T(8,128)(2,1)S(1)} collective-permute-done((bf16[2,160,512]{2,1,0:T(8,128)(2,1)}, bf16[2,160,512]{2,1,0:T(8,128)(2,1)S(1)}, u32[]{:S(2)}, u32[]{:S(2)}) %collective-permute-start.7) | collective-permute-done | bytes 327712 | tf_op jit(solution)/shard_map/ppermute | solution.py:34
  90.0 16.3 %shard_map.220 = (bf16[8,216,1280]{2,1,0:T(8,128)(2,1)}, bf16[2,20,64,216]{3,2,1,0:T(8,128)(2,1)}, bf16[8,10,64,216]{3,2,1,0:T(8,128)(2,1)}, bf16[1280,2048]{1,0:T(8,128)(2,1)}, f32[8,1280]{1,0:T(8,128)}) custom-call(s32[2]{0:T(128)} %get-tuple-element.383.at_ref, bf16[2,216,1280]{2,1,0:T(8,128)(2,1)} %bitcast.161, bf16[2,216,1280]{2,1,0:T(8,128)(2,1)} %copy-done.34, ...), custom_call_target="tpu_custom_call" | custom-call | flops 8000000000 | bytes 25000000 | tf_op jit(solution)/shard_map/pallas_call | solution.py:496
  106.2 26.2 %shard_map.221 = (bf16[2,20,64,216]{3,2,1,0:T(8,128)(2,1)}, f32[2,5,4,216]{3,2,1,0:T(4,128)}) custom-call(s32[2]{0:T(128)} %get-tuple-element.382.blocks_ref, s32[8]{0:T(128)} %fusion.29.slots_ref, f32[2,1,216]{2,1,0:T(1,128)} %add_convert_fusion.5.seg_q_ref, f32[8,1,216]{2,1,0:T(1,128)} %convert_element_type.195.seg_k_ref, ...), custom_call_target="tpu_custom_call" | custom-call | flops 20000000000 | bytes 6000000 | tf_op jit(solution)/shard_map/pallas_call | solution.py:570
  137.7 6.9 %shard_map.223 = (f32[2,216,1280]{2,1,0:T(8,128)}, bf16[2,216,1280]{2,1,0:T(8,128)(2,1)}, f32[8,128]{1,0:T(8,128)}) custom-call(bf16[2,216,1280]{2,1,0:T(8,128)(2,1)} %bitcast.162, bf16[2,1280,216]{2,1,0:T(8,128)(2,1)} %bitcast.145, bf16[1280,3072]{1,0:T(8,128)(2,1)} %all-gather.3.cloned.1.call-done.w_ref, f32[1,1280]{1,0:T(1,128)} %get-tuple-element.371.gain_ref, ...), custom_call_target="tpu_custom_call" | custom-call | tf_op jit(solution)/shard_map/pallas_call | solution.py:819
  149.3 4.7 %slice.235.gu_ref = bf16[1280,1792]{1,0:T(8,128)(2,1)} slice(bf16[1280,3072]{1,0:T(8,128)(2,1)} %all-gather.3.cloned.1.call-done.w_ref), slice={[0:1280], [1280:3072]} | slice | bytes 9175040 | tf_op jit(solution)/shard_map/slice | solution.py:1110
  157.6 10.6 %shard_map.224 = (bf16[4,432,1280]{2,1,0:T(8,128)(2,1)}, bf16[4,432,896]{2,1,0:T(8,128)(2,1)}, bf16[4,432,1792]{2,1,0:T(8,128)(2,1)}, bf16[2,216,1280]{2,1,0:T(8,128)(2,1)}) custom-call(bf16[1,432,1280]{2,1,0:T(8,128)(2,1)} %bitcast.185, bf16[4,432,1280]{2,1,0:T(8,128)(2,1)} %pad_maximum_fusion.dy_ref, bf16[1280,1792]{1,0:T(8,128)(2,1)} %slice.235.gu_ref, ...), custom_call_target="tpu_custom_call" | custom-call | flops 4954521600 | bytes 13627392 | tf_op jit(solution)/shard_map/pallas_call | solution.py:690
  178.6 18.4 %shard_map.225 = (bf16[4,432,1280]{2,1,0:T(8,128)(2,1)}, bf16[4,432,896]{2,1,0:T(8,128)(2,1)}, bf16[4,432,1792]{2,1,0:T(8,128)(2,1)}, bf16[2,216,1280]{2,1,0:T(8...) custom-call(bf16[2,432,1280]{2,1,0:T(8,128)(2,1)} %pad_maximum_fusio, ...), custom_call_target="tpu_custom_call", output_to_operand_aliasing={{0}: (4, {}), {1}: (5, {}), {2}: (6, {})} | custom-call | flops 9909043200 | bytes 20373504 | tf_op jit(solution)/shard_map/pallas_call | solution.py:690
  198.2 10.5 %shard_map.226 = (bf16[4,432,1280]{2,1,0:T(8,128)(2,1)}, bf16[4,432,896]{2,1,0:T(8,128)(2,1)}, bf16[4,432,1792]{2,1,0:T(8,128)(2,1)}, bf16[2,216,1280]{2,1,0:T(8,128)(2,1)}, bf16[2,216,1280]{2,1,0:T(8,128)(2,1)}) custom-call(bf16[1,432,1280]{2,1,0:T(8,128)(2,1)} %bitcast.158, ...), custom_call_target="tpu_custom_call", output_to_operand_aliasing={{0}: (4, {}), {1}: (5, {}), {2}: (6, {}), {3}: (7, {}), {4}... | custom-call | flops 4954521600 | bytes 13627392 | tf_op jit(solution)/shard_map/pallas_call | solution.py:690
  210.0 13.5 %shard_map.227 = bf16[1280,1792]{1,0:T(8,128)(2,1)} custom-call(bf16[1728,1280]{1,0:T(8,128)(2,1)} %bitcast.144, bf16[1728,1792]{1,0:T(8,128)(2,1)} %bitcast.143), custom_call_target="tpu_custom_call" | custom-call | tf_op jit(solution)/shard_map/pallas_call | solution.py:731
  223.5 9.7 %shard_map.228 = (bf16[2,216,1280]{2,1,0:T(8,128)(2,1)}, bf16[2,216,1280]{2,1,0:T(8,128)(2,1)}, bf16[4,216,1280]{2,1,0:T(8,128)(2,1)}) custom-call(bf16[1728,896]{1,0:T(8,128)(2,1)} %bitcast.141, bf16[896,1280]{1,0:T(8,128)(2,1)} %all-gather.5.cloned.1.call-done.down_ref.right_ref), custom_call_target="tpu_custom_call" | custom-call | tf_op jit(solution)/shard_map/pallas_call | solution.py:761
  240.1 9.0 %shard_map.229 = bf16[896,1280]{1,0:T(8,128)(2,1)} custom-call(bf16[1728,896]{1,0:T(8,128)(2,1)} %bitcast.142, bf16[1728,1280]{1,0:T(8,128)(2,1)} %bitcast.140), custom_call_target="tpu_custom_call" | custom-call | tf_op jit(solution)/shard_map/pallas_call | solution.py:731
  251.3 8.8 %shard_map.230 = (f32[2,216,1280]{2,1,0:T(8,128)}, bf16[2,216,1280]{2,1,0:T(8,128)(2,1)}, bf16[2,1280,216]{2,1,0:T(8,128)(2,1)}, f32[1,1280]{1,0:T(1,128)}) custom-call(f32[1,216,1280]{2,1,0:T(8,128)} %get-tuple-element.247.low_ref, bf16[1,216,1280]{2,1,0:T(8,128)(2,1)} %copy-done.24, f32[1,216,1280]{2,1,0:T(8,128)} %get-tuple-element.249.high_ref, ...), custom_call_target="tpu_custom_call" | custom-call | tf_op jit(solution)/shard_map/pallas_call | solution.py:879
  260.1 5.3 %shard_map.231 = bf16[1280,1280]{1,0:T(8,128)(2,1)} custom-call(bf16[2,1280,216]{2,1,0:T(8,128)(2,1)} %bitcast.146, bf16[2,216,1280]{2,1,0:T(8,128)(2,1)} %get-tuple-element.252.right_ref), custom_call_target="tpu_custom_call" | custom-call | tf_op jit(solution)/shard_map/pallas_call | solution.py:778
  267.7 32.4 %shard_map.232 = (bf16[2,20,64,216]{3,2,1,0:T(8,128)(2,1)}, bf16[2,2,5,64,216]{4,3,2,1,0:T(8,128)(2,1)}, bf16[2,2,5,64,216]{4,3,2,1,0:T(8,128)(2,1)}, bf16[4,2,5,64,216]{4,3,2,1,0:T(8,128)(2,1)}) custom-call(s32[2]{0:T(128)} %get-tuple-element.382.blocks_ref, s32[8]{0:T(128)} %fusion.29.slots_ref, f32[2,1,216]{2,1,0:T(1,128)} %add_convert_fusion.5.seg_q_ref, ...), custom_call_target="tpu_custom_call" | custom-call | tf_op jit(solution)/shard_map/pallas_call | solution.py:606
  301.0 4.9 %collective-permute-start.26 = (bf16[2,2,5,64,216]{4,3,2,1,0:T(8,128)(2,1)}, bf16[2,2,5,64,216]{4,3,2,1,0:T(8,128)(2,1)S(1)}, u32[]{:S(2)}, u32[]{:S(2)}) collective-permute-start(bf16[2,2,5,64,216]{4,3,2,1,0:T(8,128)(2,1)} %get-tuple-element.261), channel_id=1, source_target_pairs={{0,8},{8,0},{16,24},{24,16},{1,9},{9,1},{17,25},{25,17},{2,10},{10... | collective-permute-start | bytes 1658888 | tf_op jit(solution)/shard_map/ppermute | solution.py:30
  306.0 4.8 %collective-permute-start.27 = (bf16[2,2,5,64,216]{4,3,2,1,0:T(8,128)(2,1)S(1)}, bf16[2,2,5,64,216]{4,3,2,1,0:T(8,128)(2,1)S(1)}, u32[]{:S(2)}, u32[]{:S(2)}) collective-permute-start(bf16[2,2,5,64,216]{4,3,2,1,0:T(8,128)(2,1)S(1)} %copy-done.45), channel_id=1, source_target_pairs={{0,16},{8,24},{16,0},{24,8},{1,17},{9,25},{17,1},{25,9},{2,18},{10... | collective-permute-start | bytes 1658888 | tf_op jit(solution)/shard_map/ppermute | solution.py:34
  327.7 10.0 %collective-permute-done.31 = bf16[2,5,64,216]{3,2,1,0:T(8,128)(2,1)S(1)} collective-permute-done((bf16[2,5,64,216]{3,2,1,0:T(8,128)(2,1)S(1)}, bf16[2,5,64,216]{3,2,1,0:T(8,128)(2,1)S(1)}, u32[]{:S(2)}, u32[]{:S(2)}) %collective-permute-start.31) | collective-permute-done | bytes 276512 | tf_op jit(solution)/shard_map/ppermute | solution.py:30
  346.2 4.6 %collective-permute-done.33.refs_5_ = bf16[3,160,216]{2,1,0:T(8,128)(2,1)S(1)} collective-permute-done((bf16[3,160,216]{2,1,0:T(8,128)(2,1)S(1)}, bf16[3,160,216]{2,1,0:T(8,128)(2,1)S(1)}, u32[]{:S(2)}, u32[]{:S(2)}) %collective-permute-start.33) | collective-permute-done | bytes 207392 | tf_op jit(solution)/shard_map/ppermute | solution.py:34
  360.0 6.8 %shard_map.233 = bf16[1280,480]{1,0:T(8,128)(2,1)} custom-call(bf16[8,216,1280]{2,1,0:T(8,128)(2,1)} %get-tuple-element.279.first_ref, bf16[2,320,216]{2,1,0:T(8,128)(2,1)} %get-tuple-element.280.refs_0_, bf16[3,320,216]{2,1,0:T(8,128)(2,1)} %copy-done.16, bf16[3,320,216]{2,1,0:T(8,128)(2,1)} %copy-done.17, bf16[2,160,216]{2,1,0:T(8,128)(2,1)} %get-tuple-element.353.refs_3_, ...), custom_call_target="tpu_custom_call" | custom-call | tf_op jit(solution)/shard_map/pallas_call | solution.py:542
  381.6 9.2 %shard_map.234 = (bf16[2,216,1280]{2,1,0:T(8,128)(2,1)}, f32[1,1280]{1,0:T(1,128)}, f32[8,128]{1,0:T(8,128)}) custom-call(bf16[2,1280,216]{2,1,0:T(8,128)(2,1)} %bitcast.156, bf16[2,640,216]{2,1,0:T(8,128)(2,1)} %bitcast.149, bf16[1280,2048]{1,0:T(8,128)(2,1)} %get-tuple-element.297.w_ref, bf16[2,216,1280]{2,1,0:T(8,128)(2,1)} %bitcast.163, ...), custom_call_target="tpu_custom_call" | custom-call | tf_op jit(solution)/shard_map/pallas_call | solution.py:922
  430.8 4.9 %shard_map.237 = (f32[160,3584]{1,0:T(8,128)}, f32[160,3584]{1,0:T(8,128)}) custom-call(s32[1]{0:T(128)} %bitcast.1.c_ref, bf16[160,1792]{1,0:T(8,128)(2,1)} %reduce-scatter.4.cloned.1.call-done.refs_0_, bf16[160,1792]{1,0:T(8,128)(2,1)} %copy-done.8, bf16[160,1792]{1,0:T(8,128)(2,1)} %copy-done.9, bf16[160,1792]{1,0:T(8,128)(2,1)} %pad_maximum_fusion.7.refs_3_), custom_call_target="tpu_custom_call" | custom-call | bytes 6881280 | tf_op jit(solution)/shard_map/pallas_call | solution.py:211
  440.0 6.9 %collective-permute-done.62 = bf16[152,1280]{1,0:T(8,128)(2,1)S(1)} collective-permute-done((bf16[152,1280]{1,0:T(8,128)(2,1)S(1)}, bf16[152,1280]{1,0:T(8,128)(2,1)S(1)}, u32[]{:S(2)}, u32[]{:S(2)}) %collective-permute-start.62) | collective-permute-done | bytes 389152 | tf_op jit(solution)/shard_map/ppermute | solution.py:104
  (339 shorter events, 184.4 us)
Async XLA Ops:
  7.2 130.5 %all-gather.3.cloned.1.call-start = ((), (), s32[]{:S(2)}) async-start(), calls=%async_computation.3 | async-start | bytes 8847360 | tf_op jit(solution)/shard_map/all_gather | solution.py:1077
  7.2 27.6 %collective-permute-start.3 = (bf16[2,216,1280]{2,1,0:T(8,128)(2,1)}, bf16[2,216,1280]{2,1,0:T(8,128)(2,1)S(1)}, u32[]{:S(2)}, u32[]{:S(2)}) collective-permute-start(bf16[2,216,1280]{2,1,0:T(8,128)(2,1)} %bitcast.159), channel_id=1, source_target_pairs={{0,8},{8,0},{16,24},{24,16},{1,9},{9,1},{17,25},{25,17},{2,10},{10... | collective-permute-start | bytes 3317768 | tf_op jit(solution)/shard_map/ppermute | solution.py:30
  10.2 26.2 %collective-permute-start.4 = (bf16[2,216,1280]{2,1,0:T(8,128)(2,1)}, bf16[2,216,1280]{2,1,0:T(8,128)(2,1)}, u32[]{:S(2)}, u32[]{:S(2)}) collective-permute-start(bf16[2,216,1280]{2,1,0:T(8,128)(2,1)} %bitcast.160), channel_id=1, source_target_pairs={{0,16},{8,24},{16,0},{24,8},{1,17},{9,25},{17,1},{25,9},{2,18},{10... | collective-permute-start | bytes 3317768 | tf_op jit(solution)/shard_map/ppermute | solution.py:34
  36.4 121.1 %all-gather.5.cloned.1.call-start = ((), (), s32[]{:S(2)}) async-start(), calls=%async_computation.4 | async-start | bytes 2580480 | tf_op jit(solution)/shard_map/all_gather | solution.py:1078
  54.5 26.9 %collective-permute-start.11 = (bf16[3,4,160,512]{3,2,1,0:T(8,128)(2,1)}, bf16[3,4,160,512]{3,2,1,0:T(8,128)(2,1)}, u32[]{:S(2)}, u32[]{:S(2)}) collective-permute-start(bf16[3,4,160,512]{3,2,1,0:T(8,128)(2,1)} %pad_maximum_fusion.2.refs_5_), channel_id=1, source_target_pairs={{0,1},{1,0},{2,3},{3,2},{4,5},{5,4},{6,7},{7,6},{8,9},{9,8},{10,11... | collective-permute-start | bytes 5898248 | tf_op jit(solution)/shard_map/ppermute | solution.py:26
  55.4 25.3 %collective-permute-start.9 = (bf16[1,216,1280]{2,1,0:T(8,128)(2,1)}, bf16[1,216,1280]{2,1,0:T(8,128)(2,1)}, u32[]{:S(2)}, u32[]{:S(2)}) collective-permute-start(bf16[1,216,1280]{2,1,0:T(8,128)(2,1)} %slice.232), channel_id=1, source_target_pairs={{0,16},{8,24},{16,0},{24,8},{1,17},{9,25},{17,1},{25,9},{2,18},{10... | collective-permute-start | bytes 1658888 | tf_op jit(solution)/shard_map/ppermute | solution.py:34
  58.8 21.9 %collective-permute-start.10 = (bf16[1,216,1280]{2,1,0:T(8,128)(2,1)}, bf16[1,216,1280]{2,1,0:T(8,128)(2,1)}, u32[]{:S(2)}, u32[]{:S(2)}) collective-permute-start(bf16[1,216,1280]{2,1,0:T(8,128)(2,1)} %slice.233), channel_id=1, source_target_pairs={{0,8},{8,0},{16,24},{24,16},{1,9},{9,1},{17,25},{25,17},{2,10},{10... | collective-permute-start | bytes 1658888 | tf_op jit(solution)/shard_map/ppermute | solution.py:30
  84.0 216.2 %reduce-scatter.4.cloned.1.call-start = ((), (), s32[]{:S(2)}) async-start(), calls=%async_computation.5 | async-start | bytes 5160960 | tf_op jit(solution)/shard_map/reduce_scatter | solution.py:1140
  86.4 47.5 %collective-permute-start.13 = (bf16[2,216,1280]{2,1,0:T(8,128)(2,1)S(1)}, bf16[2,216,1280]{2,1,0:T(8,128)(2,1)S(1)}, u32[]{:S(2)}, u32[]{:S(2)}) collective-permute-start(bf16[2,216,1280]{2,1,0:T(8,128)(2,1)S(1)} %bitcast.165), channel_id=1, source_target_pairs={{0,8},{8,0},{16,24},{24,16},{1,9},{9,1},{17,25},{25,17},{2,10},{10... | collective-permute-start | bytes 3317768 | tf_op jit(solution)/shard_map/ppermute | solution.py:30
  87.5 50.2 %collective-permute-start.14 = (bf16[2,216,1280]{2,1,0:T(8,128)(2,1)S(1)}, bf16[2,216,1280]{2,1,0:T(8,128)(2,1)S(1)}, u32[]{:S(2)}, u32[]{:S(2)}) collective-permute-start(bf16[2,216,1280]{2,1,0:T(8,128)(2,1)S(1)} %bitcast.166), channel_id=1, source_target_pairs={{0,16},{8,24},{16,0},{24,8},{1,17},{9,25},{17,1},{25,9},{2,18},{10... | collective-permute-start | bytes 3317768 | tf_op jit(solution)/shard_map/ppermute | solution.py:34
  88.0 49.7 %collective-permute-start.15 = (bf16[2,216,1280]{2,1,0:T(8,128)(2,1)S(1)}, bf16[2,216,1280]{2,1,0:T(8,128)(2,1)}, u32[]{:S(2)}, u32[]{:S(2)}) collective-permute-start(bf16[2,216,1280]{2,1,0:T(8,128)(2,1)S(1)} %bitcast.167), channel_id=1, source_target_pairs={{0,24},{8,16},{16,8},{24,0},{1,25},{9,17},{17,9},{25,1},{2,26},{10... | collective-permute-start | bytes 3317768 | tf_op jit(solution)/shard_map/ppermute | solution.py:104
  144.7 25.3 %collective-permute-start.16 = (bf16[2,216,1280]{2,1,0:T(8,128)(2,1)}, bf16[2,216,1280]{2,1,0:T(8,128)(2,1)S(1)}, u32[]{:S(2)}, u32[]{:S(2)}) collective-permute-start(bf16[2,216,1280]{2,1,0:T(8,128)(2,1)} %get-tuple-element.198), channel_id=1, source_target_pairs={{0,8},{8,0},{16,24},{24,16},{1,9},{9,1},{17,25},{25,17},{2,10},{10... | collective-permute-start | bytes 3317768 | tf_op jit(solution)/shard_map/ppermute | solution.py:30
  145.7 27.6 %collective-permute-start.17 = (bf16[2,216,1280]{2,1,0:T(8,128)(2,1)}, bf16[2,216,1280]{2,1,0:T(8,128)(2,1)S(1)}, u32[]{:S(2)}, u32[]{:S(2)}) collective-permute-start(bf16[2,216,1280]{2,1,0:T(8,128)(2,1)} %get-tuple-element.198), channel_id=1, source_target_pairs={{0,16},{8,24},{16,0},{24,8},{1,17},{9,25},{17,1},{25,9},{2,18},{10... | collective-permute-start | bytes 3317768 | tf_op jit(solution)/shard_map/ppermute | solution.py:34
  173.4 23.7 %collective-permute-start.19 = (bf16[1,216,1280]{2,1,0:T(8,128)(2,1)S(1)}, bf16[1,216,1280]{2,1,0:T(8,128)(2,1)S(1)}, u32[]{:S(2)}, u32[]{:S(2)}) collective-permute-start(bf16[1,216,1280]{2,1,0:T(8,128)(2,1)S(1)} %slice.238), channel_id=1, source_target_pairs={{0,8},{8,0},{16,24},{24,16},{1,9},{9,1},{17,25},{25,17},{2,10},{10... | collective-permute-start | bytes 1658888 | tf_op jit(solution)/shard_map/ppermute | solution.py:30
  175.4 21.7 %collective-permute-start.18 = (bf16[1,216,1280]{2,1,0:T(8,128)(2,1)}, bf16[1,216,1280]{2,1,0:T(8,128)(2,1)S(1)}, u32[]{:S(2)}, u32[]{:S(2)}) collective-permute-start(bf16[1,216,1280]{2,1,0:T(8,128)(2,1)} %slice.237), channel_id=1, source_target_pairs={{0,16},{8,24},{16,0},{24,8},{1,17},{9,25},{17,1},{25,9},{2,18},{10... | collective-permute-start | bytes 1658888 | tf_op jit(solution)/shard_map/ppermute | solution.py:34
  208.7 24.5 %collective-permute-start.20 = (bf16[2,216,1280]{2,1,0:T(8,128)(2,1)}, bf16[2,216,1280]{2,1,0:T(8,128)(2,1)S(1)}, u32[]{:S(2)}, u32[]{:S(2)}) collective-permute-start(bf16[2,216,1280]{2,1,0:T(8,128)(2,1)} %get-tuple-element.230), channel_id=1, source_target_pairs={{0,8},{8,0},{16,24},{24,16},{1,9},{9,1},{17,25},{25,17},{2,10},{10... | collective-permute-start | bytes 3317768 | tf_op jit(solution)/shard_map/ppermute | solution.py:30
  209.7 24.0 %collective-permute-start.21 = (bf16[2,216,1280]{2,1,0:T(8,128)(2,1)}, bf16[2,216,1280]{2,1,0:T(8,128)(2,1)S(1)}, u32[]{:S(2)}, u32[]{:S(2)}) collective-permute-start(bf16[2,216,1280]{2,1,0:T(8,128)(2,1)} %get-tuple-element.231), channel_id=1, source_target_pairs={{0,16},{8,24},{16,0},{24,8},{1,17},{9,25},{17,1},{25,9},{2,18},{10... | collective-permute-start | bytes 3317768 | tf_op jit(solution)/shard_map/ppermute | solution.py:34
  233.7 125.6 %reduce-scatter.6.cloned.1.call-start = ((), (), s32[]{:S(2)}) async-start(), calls=%async_computation.6 | async-start | bytes 3686400 | tf_op jit(solution)/shard_map/reduce_scatter | solution.py:1159
  265.4 34.7 %collective-permute-start.24 = (bf16[2,216,1280]{2,1,0:T(8,128)(2,1)}, bf16[2,216,1280]{2,1,0:T(8,128)(2,1)S(1)}, u32[]{:S(2)}, u32[]{:S(2)}) collective-permute-start(bf16[2,216,1280]{2,1,0:T(8,128)(2,1)} %get-tuple-element.259), channel_id=1, source_target_pairs={{0,8},{8,0},{16,24},{24,16},{1,9},{9,1},{17,25},{25,17},{2,10},{10... | collective-permute-start | bytes 3317768 | tf_op jit(solution)/shard_map/ppermute | solution.py:30
  266.6 33.6 %collective-permute-start.25 = (bf16[2,216,1280]{2,1,0:T(8,128)(2,1)S(1)}, bf16[2,216,1280]{2,1,0:T(8,128)(2,1)S(1)}, u32[]{:S(2)}, u32[]{:S(2)}) collective-permute-start(bf16[2,216,1280]{2,1,0:T(8,128)(2,1)S(1)} %copy-done.44), channel_id=1, source_target_pairs={{0,16},{8,24},{16,0},{24,8},{1,17},{9,25},{17,1},{25,9},{2,18},{10... | collective-permute-start | bytes 3317768 | tf_op jit(solution)/shard_map/ppermute | solution.py:34
  300.3 123.5 %reduce-scatter.8.cloned.1.call-start = ((), (), s32[]{:S(2)}) async-start(), calls=%async_computation.7 | async-start | bytes 2580480 | tf_op jit(solution)/shard_map/reduce_scatter | solution.py:1141
  321.4 22.5 %collective-permute-start.28 = (bf16[3,320,216]{2,1,0:T(8,128)(2,1)S(1)}, bf16[3,320,216]{2,1,0:T(8,128)(2,1)S(1)}, u32[]{:S(2)}, u32[]{:S(2)}) collective-permute-start(bf16[3,320,216]{2,1,0:T(8,128)(2,1)S(1)} %pad_maximum_fusion.8), channel_id=1, source_target_pairs={{0,8},{8,0},{16,24},{24,16},{1,9},{9,1},{17,25},{25,17},{2,10},{10... | collective-permute-start | bytes 1244168 | tf_op jit(solution)/shard_map/ppermute | solution.py:30
  374.8 23.4 %collective-permute-start.44 = (bf16[160,1792]{1,0:T(8,128)(2,1)S(1)}, bf16[160,1792]{1,0:T(8,128)(2,1)S(1)}, u32[]{:S(2)}, u32[]{:S(2)}) collective-permute-start(bf16[160,1792]{1,0:T(8,128)(2,1)S(1)} %copy-done.23), channel_id=1, source_target_pairs={{0,8},{8,0},{16,24},{24,16},{1,9},{9,1},{17,25},{25,17},{2,10},{10... | collective-permute-start | bytes 1720328 | tf_op jit(solution)/shard_map/ppermute | solution.py:30
  375.4 22.7 %collective-permute-start.45 = (bf16[160,1792]{1,0:T(8,128)(2,1)S(1)}, bf16[160,1792]{1,0:T(8,128)(2,1)S(1)}, u32[]{:S(2)}, u32[]{:S(2)}) collective-permute-start(bf16[160,1792]{1,0:T(8,128)(2,1)S(1)} %copy-done.23), channel_id=1, source_target_pairs={{0,16},{8,24},{16,0},{24,8},{1,17},{9,25},{17,1},{25,9},{2,18},{10... | collective-permute-start | bytes 1720328 | tf_op jit(solution)/shard_map/ppermute | solution.py:34
  (90 other events, 858.4 us)
Sparse Core Ops, SparseCore 0:
  36.6 78.0 all-gather.2
  116.9 29.3 all-gather.4
  233.8 54.3 reduce-scatter.3
  300.4 49.3 reduce-scatter.5
  352.4 38.4 reduce-scatter.7
